TPU v7x, 32 devices: a whole 2x2x4 slice. The times are simulated.
32 devices in a mesh: leaf: 4 (over y, x), row: 8 (over z, core).
Axes of the slice: x: 2, y: 2, z: 4, core: 2. Of those that a mesh axis runs over, the one named last changes fastest.
Arguments:
- right_side: bfloat16 [4, 32, 256, 512], P('leaf', 'row'), may hold values from -6 to 6
- panels: bfloat16 [4, 4, 32, 512, 512], P(None, 'leaf', 'row'), may hold values from -0.1875 to 0.1875
- tile_counts: int32 [4, 4, 32], P(None, 'leaf', 'row'), may hold values from 0 to 512, as said below
- diag_leaf: bfloat16 [4, 512, 512], P('leaf')
- diag_pair: bfloat16 [2, 512, 512], replicated
- diag_root: bfloat16 [2, 512, 512], replicated
- sup_rows: int32 [4], replicated, may hold values from 0 to 31, as said below
Outputs:
- solution: bfloat16 [4, 4, 256, 512], P(None, 'leaf')
- updated_side: bfloat16 [32, 256, 512], P('row')
Inputs may be any that keep to these rules, and one draw needn't show every extreme that they name: `sup_rows`: 4 distinct block rows, one a level. `tile_counts`: 0 marks a tile with no valid columns.
All inputs are finite; a program needn't handle non-finite values.
Results may differ from a plain program's by a relative error of at most 0.0062.
Values may be sent and summed in bfloat16 or wider, within the bound.
No kernel may reach another device: no remote copies, remote signals or barrier semaphores. Data moves between devices by JAX's collectives and lax.ppermute only.
A program may use at most 128 MiB of HBM per device.

v0:
```python
import jax
import jax.numpy as jnp
from jax import lax
from jax.sharding import PartitionSpec as P


def swapped(shard, axis, apart):
    return lax.ppermute(shard, axis, [(i, i ^ 1 << apart) for i in range(lax.axis_size(axis))])


def from_root(block, axis, owner):
    block = jnp.where(lax.axis_index(axis) == owner, block, jnp.zeros_like(block))
    return lax.psum(block, axis)


def merge_pairs(partial_result, depth):
    merged = partial_result + swapped(partial_result, "leaf", 0)
    if depth > 1:
        merged = merged + swapped(merged, "leaf", 1)
    return merged


def solve_owned(merged, inverse, is_owner):

    def compute(values):
        return jnp.dot(
            values.astype(jnp.bfloat16), inverse, preferred_element_type=jnp.float32
        ).astype(jnp.bfloat16)

    def nothing(values):
        return jnp.zeros(values.shape, jnp.bfloat16)

    return lax.cond(is_owner, compute, nothing, merged)


def publish(current_solved, owner_row):
    return from_root(current_solved, "row", owner_row)


def on_device(right_side, panels, tile_counts, diag_leaf, diag_pair, diag_root, sup_rows):
    leaf_position = lax.axis_index("leaf")
    row_index = lax.axis_index("row")
    levels = panels.shape[0]
    rows_here = panels.shape[2]
    tile_width = panels.shape[3]
    share_parts = right_side[0].astype(jnp.float32)
    totals = jnp.zeros(share_parts.shape, jnp.float32)
    tile_ids = row_index * rows_here + jnp.arange(rows_here, dtype=jnp.int32)
    columns = jnp.arange(tile_width, dtype=jnp.int32)
    solved = []
    for panel_height in range(levels):
        target_row = sup_rows[panel_height]
        owner_row = target_row // rows_here
        local_tile = target_row % rows_here
        is_owner = owner_row == row_index
        partial_result = lax.dynamic_index_in_dim(
            share_parts, local_tile, 0, keepdims=False
        ) - lax.dynamic_index_in_dim(totals, local_tile, 0, keepdims=False)
        if panel_height == 0:
            current_solved = publish(solve_owned(partial_result, diag_leaf[0], is_owner), owner_row)
        elif panel_height == 1:
            inverse = lax.dynamic_index_in_dim(diag_pair, leaf_position // 2, 0, keepdims=False)
            current_solved = publish(
                solve_owned(merge_pairs(partial_result, 1), inverse, is_owner), owner_row
            )
        else:
            inverse = diag_root[panel_height - 2]
            current_solved = publish(
                solve_owned(merge_pairs(partial_result, 2), inverse, is_owner), owner_row
            )
        solved.append(current_solved)
        structure = jnp.logical_not(
            jnp.any(tile_ids[:, None] == sup_rows[: panel_height + 1][None, :], axis=1)
        )
        col_mask = (
            (columns[None, :] < tile_counts[panel_height, 0][:, None]) & structure[:, None]
        ).astype(jnp.float32)
        update_term = jnp.einsum(
            "pi,bis->bps",
            current_solved,
            panels[panel_height, 0],
            preferred_element_type=jnp.float32,
        )
        totals = totals + update_term * col_mask[:, None, :]
    solution = jnp.stack(solved)[:, None]
    quarter = lax.psum_scatter(
        share_parts - totals, "leaf", scatter_dimension=1, tiled=True
    ).astype(jnp.bfloat16)
    updated_side = lax.all_gather(quarter, "leaf", axis=1, tiled=True)
    return (solution, updated_side)


def solution(mesh):
    placed = (
        P("leaf", "row", None, None),
        P(None, "leaf", "row", None, None),
        P(None, "leaf", "row"),
        P("leaf", None, None),
        P(),
        P(),
        P(),
    )
    return jax.shard_map(
        on_device,
        mesh=mesh,
        in_specs=placed,
        out_specs=(P(None, "leaf", None, None), P("row", None, None)),
        check_vma=False,
    )
```

profile of v0, /device:TPU:0, one launch (start us, length us, event | category | flops | bytes accessed | tf_op | source)
XLA Modules:
  0.0 388.2 jit_solution(14850098007651455530)
XLA Ops:
  7.2 1.4 fusion.47
  11.2 0.7 broadcast_select_fusion.3
  13.7 2.9 convert_element_type.85
  16.6 0.6 compare_not_fusion
  17.2 0.1 fusion.40
  17.3 53.3 %all-reduce.5.cloned.1.call-done = bf16[256,512]{1,0:T(8,128)(2,1)} async-done(((bf16[256,512]{1,0:T(8,128)(2,1)}), bf16[256,512]{1,0:T(8,128)(2,1)}) %all-reduce.5.cloned.1.call-update) | async-done | bytes 262160 | tf_op jit(solution)/shard_map/psum | solution.py:13
  70.6 2.4 fusion.27
  73.0 1.1 fusion.34
  74.1 1.5 collective-permute-start
  78.2 0.2 compare_reduce_fusion.2
  78.4 7.7 %collective-permute-done = f32[256,512]{1,0:T(8,128)S(1)} collective-permute-done((f32[256,512]{1,0:T(8,128)S(1)}, f32[256,512]{1,0:T(8,128)S(1)}, u32[]{:S(2)}, u32[]{:S(2)}) %collective-permute-start) | collective-permute-done | bytes 524320 | tf_op jit(solution)/shard_map/ppermute | solution.py:8
  86.2 1.3 conditional.5
  86.2 1.3 convolution_convert_fusion.3
  87.5 0.7 broadcast_select_fusion.2
  88.3 0.1 fusion.42
  88.4 53.5 %all-reduce.7.cloned.1.call-done = bf16[256,512]{1,0:T(8,128)(2,1)} async-done(((bf16[256,512]{1,0:T(8,128)(2,1)}), bf16[256,512]{1,0:T(8,128)(2,1)}) %all-reduce.7.cloned.1.call-update) | async-done | bytes 262160 | tf_op jit(solution)/shard_map/psum | solution.py:13
  141.9 2.4 multiply_add_fusion.1
  144.3 1.3 copy-done
  145.6 1.2 fusion.33
  146.8 1.5 collective-permute-start.1
  148.4 10.5 %collective-permute-done.1 = f32[256,512]{1,0:T(8,128)S(1)} collective-permute-done((f32[256,512]{1,0:T(8,128)S(1)}, f32[256,512]{1,0:T(8,128)S(1)}, u32[]{:S(2)}, u32[]{:S(2)}) %collective-permute-start.1) | collective-permute-done | bytes 524320 | tf_op jit(solution)/shard_map/ppermute | solution.py:8
  158.9 0.1 add.115
  159.0 1.5 collective-permute-start.2
  162.9 0.2 compare_reduce_fusion.1
  163.1 7.0 %collective-permute-done.2 = f32[256,512]{1,0:T(8,128)S(1)} collective-permute-done((f32[256,512]{1,0:T(8,128)S(1)}, f32[256,512]{1,0:T(8,128)S(1)}, u32[]{:S(2)}, u32[]{:S(2)}) %collective-permute-start.2) | collective-permute-done | bytes 524320 | tf_op jit(solution)/shard_map/ppermute | solution.py:8
  170.1 0.3 conditional.6
  170.1 0.3 convolution_convert_fusion.1
  170.4 0.7 broadcast_select_fusion.1
  171.1 0.0 all-reduce.11.cloned.1.call-start
  171.2 0.1 fusion.44
  171.3 55.5 %all-reduce.9.cloned.1.call-done = bf16[256,512]{1,0:T(8,128)(2,1)} async-done(((bf16[256,512]{1,0:T(8,128)(2,1)}), bf16[256,512]{1,0:T(8,128)(2,1)}) %all-reduce.9.cloned.1.call-update) | async-done | bytes 262160 | tf_op jit(solution)/shard_map/psum | solution.py:13
  226.7 3.0 multiply_add_fusion
  229.8 1.1 fusion.32
  230.9 1.5 collective-permute-start.3
  232.4 10.5 %collective-permute-done.3 = f32[256,512]{1,0:T(8,128)S(1)} collective-permute-done((f32[256,512]{1,0:T(8,128)S(1)}, f32[256,512]{1,0:T(8,128)S(1)}, u32[]{:S(2)}, u32[]{:S(2)}) %collective-permute-start.3) | collective-permute-done | bytes 524320 | tf_op jit(solution)/shard_map/ppermute | solution.py:8
  242.9 0.9 add.119
  243.8 1.5 collective-permute-start.4
  245.9 0.2 compare_reduce_fusion
  246.1 9.1 %collective-permute-done.4 = f32[256,512]{1,0:T(8,128)} collective-permute-done((f32[256,512]{1,0:T(8,128)}, f32[256,512]{1,0:T(8,128)}, u32[]{:S(2)}, u32[]{:S(2)}) %collective-permute-start.4) | collective-permute-done | bytes 524320 | tf_op jit(solution)/shard_map/ppermute | solution.py:8
  255.2 0.7 broadcast_select_fusion
  256.0 0.1 fusion.46
  256.1 55.8 %all-reduce.11.cloned.1.call-done = bf16[256,512]{1,0:T(8,128)(2,1)} async-done(((bf16[256,512]{1,0:T(8,128)(2,1)}), bf16[256,512]{1,0:T(8,128)(2,1)}) %all-reduce.11.cloned.1.call-update) | async-done | bytes 262160 | tf_op jit(solution)/shard_map/psum | solution.py:13
  311.9 3.7 bitcast_subtract_fusion
  315.8 34.3 %reduce-scatter.2.cloned.1.call-done = f32[4,64,512]{2,1,0:T(8,128)} async-done(((f32[4,256,512]{2,1,0:T(8,128)}), f32[4,64,512]{2,1,0:T(8,128)}) %reduce-scatter.2.cloned.1.call-update) | async-done | bytes 524304 | tf_op jit(solution)/shard_map/reduce_scatter | solution.py:86
  350.0 1.8 convert_element_type.94
  351.9 1.1 maximum_bitcast_fusion
  353.0 26.1 %all-gather.2.cloned.1.call-done = bf16[4,256,512]{2,1,0:T(8,128)(2,1)} async-done(((bf16[4,64,512]{2,1,0:T(8,128)(2,1)}), bf16[4,256,512]{2,1,0:T(8,128)(2,1)}) %all-gather.2.cloned.1.call-update) | async-done | bytes 1048592 | tf_op jit(solution)/shard_map/all_gather | solution.py:89
  379.1 2.3 copy.27
  (37 shorter events, 0.5 us)
Async XLA Ops:
  7.2 63.4 %all-reduce.5.cloned.1.call-start = ((), (), s32[]{:S(2)}) async-start(), calls=%async_computation.1 | async-start | bytes 524288 | tf_op jit(solution)/shard_map/psum | solution.py:13
  11.2 6.0 %copy-start.8 = (s32[4,1,4]{2,1,0:T(1,128)S(1)}, s32[4,1,4]{2,1,0:T(1,128)}, u32[]{:S(2)}) copy-start(s32[4,1,4]{2,1,0:T(1,128)} %param.17) | copy-start | bytes 196
  12.0 129.9 %all-reduce.7.cloned.1.call-start = ((), (), s32[]{:S(2)}) async-start(), calls=%async_computation.2 | async-start | bytes 524288 | tf_op jit(solution)/shard_map/psum | solution.py:13
  17.3 60.9 %copy-start.7 = (s32[4]{0:T(128)S(1)}, s32[4]{0:T(128)}, u32[]{:S(2)}) copy-start(s32[4]{0:T(128)} %param.21) | copy-start | bytes 52
  74.1 12.0 %collective-permute-start = (f32[256,512]{1,0:T(8,128)S(1)}, f32[256,512]{1,0:T(8,128)S(1)}, u32[]{:S(2)}, u32[]{:S(2)}) collective-permute-start(f32[256,512]{1,0:T(8,128)S(1)} %fusion.34), channel_id=1, source_target_pairs={{0,8},{8,0},{16,24},{24,16},{1,9},{9,1},{17,25},{25,17},{2,10},{10... | collective-permute-start | bytes 1572872 | tf_op jit(solution)/shard_map/ppermute | solution.py:8
  88.3 138.5 %all-reduce.9.cloned.1.call-start = ((), (), s32[]{:S(2)}) async-start(), calls=%async_computation.3 | async-start | bytes 524288 | tf_op jit(solution)/shard_map/psum | solution.py:13
  144.3 1.3 copy-start
  145.6 24.5 %copy-start.2 = (bf16[2,512,512]{2,1,0:T(8,128)(2,1)S(1)}, bf16[2,512,512]{2,1,0:T(8,128)(2,1)}, u32[]{:S(2)}) copy-start(bf16[2,512,512]{2,1,0:T(8,128)(2,1)} %param.20) | copy-start | bytes 3145732
  146.8 12.0 %collective-permute-start.1 = (f32[256,512]{1,0:T(8,128)S(1)}, f32[256,512]{1,0:T(8,128)S(1)}, u32[]{:S(2)}, u32[]{:S(2)}) collective-permute-start(f32[256,512]{1,0:T(8,128)S(1)} %fusion.33), channel_id=1, source_target_pairs={{0,8},{8,0},{16,24},{24,16},{1,9},{9,1},{17,25},{25,17},{2,10},{10... | collective-permute-start | bytes 1572872 | tf_op jit(solution)/shard_map/ppermute | solution.py:8
  159.0 11.1 %collective-permute-start.2 = (f32[256,512]{1,0:T(8,128)S(1)}, f32[256,512]{1,0:T(8,128)S(1)}, u32[]{:S(2)}, u32[]{:S(2)}) collective-permute-start(f32[256,512]{1,0:T(8,128)S(1)} %add.115), channel_id=1, source_target_pairs={{0,16},{8,24},{16,0},{24,8},{1,17},{9,25},{17,1},{25,9},{2,18},{10... | collective-permute-start | bytes 1572872 | tf_op jit(solution)/shard_map/ppermute | solution.py:8
  171.1 140.8 %all-reduce.11.cloned.1.call-start = ((), (), s32[]{:S(2)}) async-start(), calls=%async_computation.4 | async-start | bytes 524288 | tf_op jit(solution)/shard_map/psum | solution.py:13
  230.9 81.0 %copy-start.1 = (bf16[1,4,256,512]{3,2,1,0:T(8,128)(2,1)S(1)}, bf16[1,4,256,512]{3,2,1,0:T(8,128)(2,1)}, u32[]{:S(2)}) copy-start(bf16[1,4,256,512]{3,2,1,0:T(8,128)(2,1)} %param.15) | copy-start | bytes 3145732
  230.9 12.0 %collective-permute-start.3 = (f32[256,512]{1,0:T(8,128)S(1)}, f32[256,512]{1,0:T(8,128)S(1)}, u32[]{:S(2)}, u32[]{:S(2)}) collective-permute-start(f32[256,512]{1,0:T(8,128)S(1)} %fusion.32), channel_id=1, source_target_pairs={{0,8},{8,0},{16,24},{24,16},{1,9},{9,1},{17,25},{25,17},{2,10},{10... | collective-permute-start | bytes 1572872 | tf_op jit(solution)/shard_map/ppermute | solution.py:8
  243.8 11.4 %collective-permute-start.4 = (f32[256,512]{1,0:T(8,128)}, f32[256,512]{1,0:T(8,128)}, u32[]{:S(2)}, u32[]{:S(2)}) collective-permute-start(f32[256,512]{1,0:T(8,128)} %add.119), channel_id=1, source_target_pairs={{0,16},{8,24},{16,0},{24,8},{1,17},{9,25},{17,1},{25,9},{2,18},{10... | collective-permute-start | bytes 1572872 | tf_op jit(solution)/shard_map/ppermute | solution.py:8
  256.0 94.1 %reduce-scatter.2.cloned.1.call-start = ((), (), s32[]{:S(2)}) async-start(), calls=%async_computation.5 | async-start | bytes 2621440 | tf_op jit(solution)/shard_map/reduce_scatter | solution.py:86
  315.7 36.2 %copy-start.3 = (bf16[256,512]{1,0:T(8,128)(2,1)S(1)}, bf16[256,512]{1,0:T(8,128)(2,1)}, u32[]{:S(2)}) copy-start(bf16[256,512]{1,0:T(8,128)(2,1)} %all-reduce.5.cloned.1.call-done) | copy-start | bytes 786436
  315.7 36.2 %copy-start.4 = (bf16[256,512]{1,0:T(8,128)(2,1)S(1)}, bf16[256,512]{1,0:T(8,128)(2,1)}, u32[]{:S(2)}) copy-start(bf16[256,512]{1,0:T(8,128)(2,1)} %all-reduce.7.cloned.1.call-done) | copy-start | bytes 786436
  315.7 36.2 %copy-start.5 = (bf16[256,512]{1,0:T(8,128)(2,1)S(1)}, bf16[256,512]{1,0:T(8,128)(2,1)}, u32[]{:S(2)}) copy-start(bf16[256,512]{1,0:T(8,128)(2,1)} %all-reduce.9.cloned.1.call-done) | copy-start | bytes 786436
  315.7 36.2 %copy-start.6 = (bf16[256,512]{1,0:T(8,128)(2,1)S(1)}, bf16[256,512]{1,0:T(8,128)(2,1)}, u32[]{:S(2)}) copy-start(bf16[256,512]{1,0:T(8,128)(2,1)} %all-reduce.11.cloned.1.call-done) | copy-start | bytes 786436
  315.7 63.4 %all-gather.2.cloned.1.call-start = ((), (), s32[]{:S(2)}) async-start(), calls=%async_computation.6 | async-start | bytes 1310720 | tf_op jit(solution)/shard_map/all_gather | solution.py:89
Sparse Core Ops, SparseCore 0:
  12.1 58.4 all-reduce.4
  88.4 53.4 all-reduce.6
  171.3 55.4 all-reduce.8
  256.1 55.7 all-reduce.10
  315.8 34.1 reduce-scatter.1
  352.4 26.6 all-gather.1
where the time goes:
time: 388 us
  waiting for transfers between devices  323 us (83%)
  between operations  24.1 us (6%)
  other arithmetic  14.6 us (4%)
  matrix products  13.2 us (3%)
  starting transfers between devices  7.86 us (2%)
  local copies, waits for them, and re-layouts  5.05 us (1%)
    psum x4, waiting for transfers between devices, from_root(): return lax.psum(block, axis)  218 us
    ppermute x5, waiting for transfers between devices, swapped(): lax.ppermute(shard, axis, [(i, i ^ 1 << apart) for i in range(lax.axis_si...  44.8 us
    reduce_scatter x1, waiting for transfers between devices, on_device(): lax.psum_scatter(share_parts - totals, 'leaf', scatter_dimension=1, tiled...  34.3 us
    all_gather x1, waiting for transfers between devices, on_device(): updated_side = lax.all_gather(quarter, 'leaf', axis=1, tiled=True)  26.1 us
    dot_general x4, matrix products, on_device(): jnp.einsum('pi,bis->bps', current_solved, panels[panel_height, 0], prefer...  11.5 us
  transfers between devices with their start and end apart: 11, of which 11 were waited for; matrix products, arithmetic and copies ran while one was open for 1% of the time, Pallas kernels for 0%

commit v1 on v0

v1 whole, which is shorter than its diff:
```python
import jax
import jax.numpy as jnp
from jax import lax
from jax.sharding import PartitionSpec as P

F32 = jnp.float32
BF16 = jnp.bfloat16


def swap(block, axis, bits):
    return lax.ppermute(block, axis, [(i, i ^ bits) for i in range(lax.axis_size(axis))])


def dot(a, b):
    return jnp.dot(a, b, preferred_element_type=F32)


def piece(array, index, size, axis):
    return lax.dynamic_slice_in_dim(array, index * size, size, axis)


def placed(pieces, me, axis):
    size = pieces[0].shape[axis]
    shape = list(pieces[0].shape)
    shape[axis] = size * len(pieces)
    out = jnp.zeros(shape, pieces[0].dtype)
    for m, block in enumerate(pieces):
        out = lax.dynamic_update_slice_in_dim(out, block, (me ^ m) * size, axis)
    return out


def on_device(right_side, panels, tile_counts, diag_leaf, diag_pair, diag_root, sup_rows):
    right, panels, counts = right_side[0], panels[:, 0], tile_counts[:, 0]
    levels, here, width, _ = panels.shape
    n_row, n_leaf = lax.axis_size("row"), lax.axis_size("leaf")
    chips = min(n_row // 2, 4)
    leaf, row = lax.axis_index("leaf"), lax.axis_index("row")
    core, chip = row & 1, (row >> 1) & (chips - 1)
    outer = [1 << b for b in range(n_row.bit_length()) if 2 * chips <= 1 << b < n_row]
    half_r, half_w = right.shape[1] // 2, width // 2
    part_r, part_w = half_r // chips, width // chips

    ids = row * here + jnp.arange(here, dtype=jnp.int32)
    columns = jnp.arange(width, dtype=jnp.int32)
    masks = []
    for level in range(levels):
        free = jnp.all(ids[:, None] != sup_rows[None, : level + 1], axis=1)
        masks.append((columns[None, :] < counts[level][:, None]) & free[:, None])
    owned = [sup_rows[level] // here == row for level in range(levels)]
    local = [sup_rows[level] % here for level in range(levels)]

    def side(level):
        block = lax.dynamic_index_in_dim(right, local[level], 0, keepdims=False)
        return jnp.where(owned[level], block, jnp.zeros_like(block))

    def tile(of, level):
        block = lax.dynamic_index_in_dim(panels[of], local[level], 0, keepdims=False)
        mask = lax.dynamic_index_in_dim(masks[of], local[level], 0, keepdims=False)
        return jnp.where(mask[None, :] & owned[level], block, jnp.zeros_like(block))

    def spread(block):
        for bits in outer:
            block = block + swap(block, "row", bits)
        return block

    def halved(blocks, size):
        stack = jnp.stack(blocks)
        mine, other = piece(stack, core, size, 1), piece(stack, 1 - core, size, 1)
        return spread(mine + swap(other, "row", 1))

    def chip_scatter(block, size, axis):
        total = piece(block, chip, size, axis)
        for m in range(1, chips):
            total = total + swap(piece(block, chip ^ m, size, axis), "row", 2 * m)
        return total

    def chip_gather(block, axis):
        return placed([block] + [swap(block, "row", 2 * m) for m in range(1, chips)], chip, axis)

    def chip_spread(block):
        m = 1
        while m < chips:
            block = block + swap(block, "row", 2 * m)
            m *= 2
        return block

    def core_gather(block, axis):
        return placed([block, swap(block, "row", 1)], core, axis)

    sides = halved([side(level) for level in range(levels)], half_r)
    tiles = halved([tile(0, 1), tile(2, 3)], half_w)
    both = jnp.stack([tile(0, 2), tile(1, 2), tile(0, 3), tile(1, 3)])
    both = spread(both + swap(both, "row", 1))

    b0 = chip_spread(sides[0])
    level1 = chip_scatter(jnp.concatenate([tiles[0], sides[1]]), part_w, 1)
    p01 = core_gather(level1[:half_w], 0)
    b1 = level1[half_w:]

    x0 = dot(b0, diag_leaf[0]).astype(BF16)
    t1 = b1.astype(F32) - dot(x0, p01)
    m1 = (t1 + swap(t1, "leaf", 1)).astype(BF16)
    m1 = chip_gather(m1, 1)
    x1 = dot(m1, lax.dynamic_index_in_dim(diag_pair, leaf // 2, 0, keepdims=False)).astype(BF16)

    t2 = sides[2].astype(F32) - dot(x0, both[0]) - dot(x1, both[1])
    t3 = sides[3].astype(F32) - dot(x0, both[2]) - dot(x1, both[3])
    t23 = chip_scatter(jnp.concatenate([t2, t3], 1).astype(BF16), part_r, 0)
    total = t23.astype(F32)
    for m in range(1, n_leaf):
        total = total + swap(t23, "leaf", m).astype(F32)
    m23 = chip_gather(total.astype(BF16), 0)

    p23 = tiles[1].astype(F32)
    m = 1
    while m < n_leaf:
        p23 = p23 + swap(p23.astype(BF16), "leaf", m).astype(F32)
        m *= 2
    p23 = core_gather(chip_spread(p23.astype(BF16)), 0)

    x2 = dot(m23[:, :width], diag_root[0]).astype(BF16)
    x3 = dot((m23[:, width:].astype(F32) - dot(x2, p23)).astype(BF16), diag_root[1]).astype(BF16)

    x01 = core_gather(jnp.stack([x0, x1]), 1)
    x23 = core_gather(jnp.stack([x2, x3]), 1)

    def leaf_scatter(blocks, dims):
        first, second = dims
        keep = [piece(blocks, (leaf & (1 << first)) | (i << second), 1, 0) for i in range(2)]
        give = [piece(blocks, ((leaf ^ (1 << first)) & (1 << first)) | (i << second), 1, 0) for i in range(2)]
        got = swap(jnp.concatenate(give), "leaf", 1 << first)
        kept = (jnp.concatenate(keep).astype(F32) + got.astype(F32)).astype(BF16)
        bit = (leaf >> second) & 1
        mine, other = piece(kept, bit, 1, 0), piece(kept, 1 - bit, 1, 0)
        return (mine.astype(F32) + swap(other, "leaf", 1 << second).astype(F32)).astype(BF16)[0]

    sum2 = leaf_scatter(jnp.where(masks[2][:, None, :], panels[2], jnp.zeros_like(panels[2])), (0, 1))
    sum3 = leaf_scatter(jnp.where(masks[3][:, None, :], panels[3], jnp.zeros_like(panels[3])), (1, 0))

    update = right.astype(F32)
    for level in range(2):
        term = jnp.einsum("pi,bis->bps", x01[level], panels[level], preferred_element_type=F32)
        update = update - jnp.where(masks[level][:, None, :], term, jnp.zeros_like(term))
    update = update.astype(BF16)
    partial = piece(update, leaf, 1, 0)[0].astype(F32)
    for m in range(1, n_leaf):
        partial = partial + swap(piece(update, leaf ^ m, 1, 0)[0], "leaf", m).astype(F32)

    done = (partial - dot(x23[0], sum2) - dot(x23[1], sum3)).astype(BF16)[None]
    updated = placed([done] + [swap(done, "leaf", m) for m in range(1, n_leaf)], leaf, 0)
    return jnp.concatenate([x01, x23])[:, None], updated


def solution(mesh):
    return jax.shard_map(
        on_device,
        mesh=mesh,
        in_specs=(
            P("leaf", "row", None, None),
            P(None, "leaf", "row", None, None),
            P(None, "leaf", "row"),
            P("leaf", None, None),
            P(),
            P(),
            P(),
        ),
        out_specs=(P(None, "leaf", None, None), P("row", None, None)),
        check_vma=False,
    )
```

time: 388 us -> 185 us (0.48)
  waiting for transfers between devices: 323 us -> 62.3 us
  starting transfers between devices: 7.86 us -> 47.1 us
  local copies, waits for them, and re-layouts: 5.05 us -> 20.9 us
  between operations: 24.1 us -> 11.8 us
  other arithmetic: 14.6 us -> 26 us
    psum x4 -> x0, waiting for transfers between devices: 218 us -> none  [from_root(): return lax.psum(block, axis)]
    ppermute x5 -> x39, starting transfers between devices: 7.61 us -> 47.1 us  [swap(): lax.ppermute(block, axis, [(i, i ^ bits) for i in range(lax.axis_size(axi...]
    reduce_scatter x1 -> x0, waiting for transfers between devices: 34.3 us -> none  [on_device(): lax.psum_scatter(share_parts - totals, 'leaf', scatter_dimension=1, tiled...]
    all_gather x1 -> x0, waiting for transfers between devices: 26.1 us -> none  [on_device(): updated_side = lax.all_gather(quarter, 'leaf', axis=1, tiled=True)]
    ppermute x5 -> x39, waiting for transfers between devices: 44.8 us -> 62.3 us  [swap(): lax.ppermute(block, axis, [(i, i ^ bits) for i in range(lax.axis_size(axi...]
    slice x1 -> x3, local copies, waits for them, and re-layouts: 1.4 us -> 7.5 us  [the longest x1 5.39 us: tile(): panels[of]]
    add x3 -> x8, other arithmetic: 0.95 us -> 6.57 us  [the longest x2 2.59 us: halved(): return spread(mine + swap(other, 'row', 1))]
    dynamic_slice x0 -> x5, local copies, waits for them, and re-layouts: none -> 5.28 us  [piece(): return lax.dynamic_slice_in_dim(array, index * size, size, axis)]
  transfers between devices with their start and end apart: 11 -> 39, of which waited for: 11 -> 16; matrix products, arithmetic and copies ran while one was open for 1% -> 23% of each run, Pallas kernels for 0% -> 0%
where the time goes in v1:
time: 185 us
  waiting for transfers between devices  62.3 us (34%)
  starting transfers between devices  47.1 us (25%)
  other arithmetic  26 us (14%)
  local copies, waits for them, and re-layouts  20.9 us (11%)
  matrix products  16.4 us (9%)
  between operations  11.8 us (6%)
    ppermute x39, waiting for transfers between devices, swap(): lax.ppermute(block, axis, [(i, i ^ bits) for i in range(lax.axis_size(axi...  62.3 us
    ppermute x39, starting transfers between devices, swap(): lax.ppermute(block, axis, [(i, i ^ bits) for i in range(lax.axis_size(axi...  47.1 us
    dot_general x11, matrix products, dot(): return jnp.dot(a, b, preferred_element_type=F32)  9.59 us
    dot_general x2, matrix products, on_device(): jnp.einsum('pi,bis->bps', x01[level], panels[level], preferred_element_ty...  6.84 us
    slice x1, local copies, waits for them, and re-layouts, tile(): panels[of]  5.39 us
    dynamic_slice x5, local copies, waits for them, and re-layouts, piece(): return lax.dynamic_slice_in_dim(array, index * size, size, axis)  5.28 us
    unnamed x64, local copies, waits for them, and re-layouts  4.68 us
  transfers between devices with their start and end apart: 39, of which 16 were waited for; matrix products, arithmetic and copies ran while one was open for 23% of the time, Pallas kernels for 0%

profile of v1, /device:TPU:0, one launch (start us, length us, event | category | flops | bytes accessed | tf_op | source)
XLA Modules:
  0.0 184.6 jit_solution(9256801478857724567)
XLA Ops:
  0.6 1.5 fusion.88
  13.1 5.4 %fusion.86 = (bf16[1,1,4,512,512]{4,3,2,1,0:T(8,128)(2,1)}, bf16[1,1,4,512,512]{4,3,2,1,0:T(8,128)(2,1)}, bf16[1,1,4,512,512]{4,3,2,1,0:T(8,128)(2,1)S(1)}) fusion(bf16[4,1,4,512,512]{4,3,2,1,0:T(8,128)(2,1)} %param.8), kind=kLoop, calls=%fused_computation.203 | loop fusion | bytes 12582912 | tf_op jit(solution)/shard_map/slice | solution.py:57
  18.9 1.9 %bitcast_select_fusion.6 = bf16[1,512,512]{2,1,0:T(8,128)(2,1)} fusion(bf16[1,1,4,512,512]{4,3,2,1,0:T(8,128)(2,1)} %get-tuple-element.20, s32[]{:T(128)S(6)} %select_n.342, pred[512]{0:T(512)(128)(4,1)S(1)} %fusion.80), kind=kLoop, calls=%fused_computation.59 | loop fusion | flops 262144 | bytes 1049092 | tf_op jit(solution)/shard_map/jit(_where)/select_n | solution.py:59
  29.2 1.6 pad_maximum_fusion
  30.9 2.5 %bitcast_select_fusion.1 = (bf16[4,512,512]{2,1,0:T(8,128)(2,1)S(1)}, bf16[4,512,512]{2,1,0:T(8,128)(2,1)S(1)}) fusion(pred[4,512]{1,0:T(4,128)(4,1)S(1)} %get-tuple-element.73, bf16[4,1,4,512,512]{4,3,2,1,0:T(8,128)(2,1)} %param.8, pred[4,512]{1,0:T(4,128)(4,1)S(1)} %get-tuple-element.74), kind=kLoop, calls=%fused_computation.5 | loop fusion | flops 2097152 | bytes 8392704 | tf_op jit(solution)/shard_map/jit(_where)/select_n | solution.py:137
  34.8 1.4 fusion.17
  41.2 3.0 %collective-permute-start.4 = (bf16[384,128]{1,0:T(8,128)(2,1)}, bf16[384,128]{1,0:T(8,128)(2,1)}, u32[]{:S(2)}, u32[]{:S(2)}) collective-permute-start(bf16[384,128]{1,0:T(8,128)(2,1)} %get-tuple-element.48), channel_id=1, source_target_pairs={{0,2},{1,3},{2,0},{3,1},{4,6},{5,7},{6,4},{7,5},{8,10},{9,11},{10,... | collective-permute-start | bytes 294920 | tf_op jit(solution)/shard_map/ppermute | solution.py:11
  44.2 2.6 %collective-permute-start.5 = (bf16[384,128]{1,0:T(8,128)(2,1)}, bf16[384,128]{1,0:T(8,128)(2,1)}, u32[]{:S(2)}, u32[]{:S(2)}) collective-permute-start(bf16[384,128]{1,0:T(8,128)(2,1)} %get-tuple-element.49), channel_id=1, source_target_pairs={{0,4},{1,5},{2,6},{3,7},{4,0},{5,1},{6,2},{7,3},{8,12},{9,13},{10,... | collective-permute-start | bytes 294920 | tf_op jit(solution)/shard_map/ppermute | solution.py:11
  47.9 1.7 collective-permute-start.32
  50.2 4.9 %collective-permute-done.5 = bf16[384,128]{1,0:T(8,128)(2,1)} collective-permute-done((bf16[384,128]{1,0:T(8,128)(2,1)}, bf16[384,128]{1,0:T(8,128)(2,1)}, u32[]{:S(2)}, u32[]{:S(2)}) %collective-permute-start.5) | collective-permute-done | bytes 98336 | tf_op jit(solution)/shard_map/ppermute | solution.py:11
  57.8 2.7 %collective-permute-start.2 = (bf16[128,512]{1,0:T(8,128)(2,1)S(1)}, bf16[128,512]{1,0:T(8,128)(2,1)S(1)}, u32[]{:S(2)}, u32[]{:S(2)}) collective-permute-start(bf16[128,512]{1,0:T(8,128)(2,1)S(1)} %fusion.82), channel_id=1, source_target_pairs={{0,4},{1,5},{2,6},{3,7},{4,0},{5,1},{6,2},{7,3},{8,12},{9,13},{10,... | collective-permute-start | bytes 393224 | tf_op jit(solution)/shard_map/ppermute | solution.py:11
  61.9 1.5 collective-permute-start.23
  64.2 3.3 %collective-permute-done.2 = bf16[128,512]{1,0:T(8,128)(2,1)S(1)} collective-permute-done((bf16[128,512]{1,0:T(8,128)(2,1)S(1)}, bf16[128,512]{1,0:T(8,128)(2,1)S(1)}, u32[]{:S(2)}, u32[]{:S(2)}) %collective-permute-start.2) | collective-permute-done | bytes 131104 | tf_op jit(solution)/shard_map/ppermute | solution.py:11
  69.7 1.6 collective-permute-start.8
  71.3 2.3 %pad_maximum_fusion.3 = bf16[2,512,512]{2,1,0:T(8,128)(2,1)} fusion(bf16[1,512,512]{2,1,0:T(8,128)(2,1)} %get-tuple-element.27, bf16[1,512,512]{2,1,0:T(8,128)(2,1)} %get-tuple-element.28), kind=kLoop, calls=%fused_computation.24 | loop fusion | flops 524288 | bytes 2097152 | tf_op jit(solution)/shard_map/concatenate | solution.py:131
  73.5 1.5 collective-permute-start.34
  75.1 4.6 %collective-permute-done.8 = f32[128,128]{1,0:T(8,128)S(1)} collective-permute-done((f32[128,128]{1,0:T(8,128)S(1)}, f32[128,128]{1,0:T(8,128)S(1)}, u32[]{:S(2)}, u32[]{:S(2)}) %collective-permute-start.8) | collective-permute-done | bytes 65568 | tf_op jit(solution)/shard_map/ppermute | solution.py:11
  80.4 1.6 collective-permute-start.24
  82.0 1.6 collective-permute-done.9
  83.7 2.1 %collective-permute-start.10 = (bf16[128,128]{1,0:T(8,128)(2,1)S(1)}, bf16[128,128]{1,0:T(8,128)(2,1)S(1)}, u32[]{:S(2)}, u32[]{:S(2)}) collective-permute-start(bf16[128,128]{1,0:T(8,128)(2,1)S(1)} %get-tuple-element.16), channel_id=1, source_target_pairs={{0,4},{1,5},{2,6},{3,7},{4,0},{5,1},{6,2},{7,3},{8,12},{9,13},{10,... | collective-permute-start | bytes 98312 | tf_op jit(solution)/shard_map/ppermute | solution.py:11
  85.8 3.0 %collective-permute-done.10 = bf16[128,128]{1,0:T(8,128)(2,1)S(1)} collective-permute-done((bf16[128,128]{1,0:T(8,128)(2,1)S(1)}, bf16[128,128]{1,0:T(8,128)(2,1)S(1)}, u32[]{:S(2)}, u32[]{:S(2)}) %collective-permute-start.10) | collective-permute-done | bytes 32800 | tf_op jit(solution)/shard_map/ppermute | solution.py:11
  88.7 3.3 %collective-permute-start.11 = (bf16[128,128]{1,0:T(8,128)(2,1)S(1)}, bf16[128,128]{1,0:T(8,128)(2,1)S(1)}, u32[]{:S(2)}, u32[]{:S(2)}) collective-permute-start(bf16[128,128]{1,0:T(8,128)(2,1)S(1)} %get-tuple-element.16), channel_id=1, source_target_pairs={{0,6},{1,7},{2,4},{3,5},{4,2},{5,3},{6,0},{7,1},{8,14},{9,15},{10,... | collective-permute-start | bytes 98312 | tf_op jit(solution)/shard_map/ppermute | solution.py:11
  92.0 2.4 %collective-permute-done.11 = bf16[128,128]{1,0:T(8,128)(2,1)S(1)} collective-permute-done((bf16[128,128]{1,0:T(8,128)(2,1)S(1)}, bf16[128,128]{1,0:T(8,128)(2,1)S(1)}, u32[]{:S(2)}, u32[]{:S(2)}) %collective-permute-start.11) | collective-permute-done | bytes 32800 | tf_op jit(solution)/shard_map/ppermute | solution.py:11
  94.9 9.0 %collective-permute-done.24 = bf16[256,512]{1,0:T(8,128)(2,1)S(1)} collective-permute-done((bf16[256,512]{1,0:T(8,128)(2,1)S(1)}, bf16[256,512]{1,0:T(8,128)(2,1)S(1)}, u32[]{:S(2)}, u32[]{:S(2)}) %collective-permute-start.24) | collective-permute-done | bytes 262176 | tf_op jit(solution)/shard_map/ppermute | solution.py:11
  104.1 1.6 add_convert_fusion.1
  106.6 1.5 collective-permute-start.33
  109.3 1.5 collective-permute-done.25
  110.9 1.6 collective-permute-start.26
  112.5 1.9 %fusion.85 = bf16[4,512,512]{2,1,0:T(8,128)(2,1)S(1)} fusion(bf16[4,512,512]{2,1,0:T(8,128)(2,1)} %collective-permute-done.13, bf16[1,512,512]{2,1,0:T(8,128)(2,1)S(1)} %copy-done.14, bf16[1,512,512]{2,1,0:T(8,128)(2,1)S(1)} %copy-done.10, bf16[1,512,512]{2,1,0:T(8,128)(2,1)S(1)} %copy-done.12, bf16[1,512,512]{2,1,0:T(8,128)(2,1)S(1)} %copy-done.8), kind=kLoop, calls=%fused_computation.202 | loop fusion | flops 4194304 | bytes 6291456 | tf_op jit(solution)/shard_map/add | solution.py:93
  116.4 1.6 collective-permute-start.14
  118.4 2.5 %collective-permute-start.16 = (bf16[32,1024]{1,0:T(8,128)(2,1)S(1)}, bf16[32,1024]{1,0:T(8,128)(2,1)S(1)}, u32[]{:S(2)}, u32[]{:S(2)}) collective-permute-start(bf16[32,1024]{1,0:T(8,128)(2,1)S(1)} %get-tuple-element.57), channel_id=1, source_target_pairs={{0,6},{1,7},{2,4},{3,5},{4,2},{5,3},{6,0},{7,1},{8,14},{9,15},{10,... | collective-permute-start | bytes 196616 | tf_op jit(solution)/shard_map/ppermute | solution.py:11
  120.9 5.8 %collective-permute-done.26 = bf16[256,512]{1,0:T(8,128)(2,1)S(1)} collective-permute-done((bf16[256,512]{1,0:T(8,128)(2,1)S(1)}, bf16[256,512]{1,0:T(8,128)(2,1)S(1)}, u32[]{:S(2)}, u32[]{:S(2)}) %collective-permute-start.26) | collective-permute-done | bytes 262176 | tf_op jit(solution)/shard_map/ppermute | solution.py:11
  130.0 1.7 collective-permute-start.19
  131.7 3.6 %fusion.4 = f32[256,4,512]{2,0,1:T(8,128)} fusion(bf16[2,256,512]{2,1,0:T(8,128)(2,1)S(1)} %constant_dynamic-update-slice_fusion.12, bf16[4,1,4,512,512]{4,3,2,1,0:T(8,128)(2,1)} %param.8), kind=kOutput, calls=%fused_computation.8 | convolution fusion | flops 536870912 | bytes 4456448 | tf_op jit(solution)/shard_map/pi,bis->bps/dot_general | solution.py:142
  136.0 1.4 collective-permute-start.20
  137.5 1.6 collective-permute-start.21
  139.1 1.5 collective-permute-start.22
  140.6 3.1 %collective-permute-done.21 = bf16[32,1024]{1,0:T(8,128)(2,1)S(1)} collective-permute-done((bf16[32,1024]{1,0:T(8,128)(2,1)S(1)}, bf16[32,1024]{1,0:T(8,128)(2,1)S(1)}, u32[]{:S(2)}, u32[]{:S(2)}) %collective-permute-start.21) | collective-permute-done | bytes 65568 | tf_op jit(solution)/shard_map/ppermute | solution.py:11
  143.7 1.5 collective-permute-done.22
  145.4 2.1 %fusion.8 = bf16[1,128,512]{2,1,0:T(8,128)(2,1)} fusion(bf16[2,512,512]{2,1,0:T(8,128)(2,1)} %param.12, bf16[128,1024]{1,0:T(8,128)(2,1)S(1)} %constant_dynamic-update-slice_fusion.7, bf16[128,512]{1,0:T(8,128)(2,1)S(1)} %convolution_convert_fusion.1, bf16[512,512]{1,0:T(8,128)(2,1)S(1)} %constant_dynamic-update-slice_fusion.5), kind=kOutput, calls=%fused_computation.20 | convolution fusion | flops 134479872 | bytes 1441792 | tf_op jit(solution)/shard_map/dot_general | solution.py:15
  148.6 3.2 %fusion.1 = bf16[4,256,512]{2,1,0:T(8,128)(2,1)S(1)} fusion(f32[256,4,512]{2,0,1:T(8,128)} %fusion.4, bf16[1,4,256,512]{3,2,1,0:T(8,128)(2,1)} %param.7, pred[4,512]{1,0:T(4,128)(4,1)S(1)} %fusion.68, pred[4,512]{1,0:T(4,128)(4,1)S(1)} %fusion.66, bf16[2,256,512]{2,1,0:T(8,128)(2,1)S(1)} %copy-done.18, bf16[4,1,4,512,512]{4,3,2,1,0:T(8,128)(2,1)} %param.8), kind=kOutput, calls=%fused_computation.3 | convolution fusion | flops 540016640 | bytes 6557696 | tf_op jit(solution)/shard_map/pi,bis->bps/dot_general | solution.py:142
  151.9 1.6 collective-permute-start.29
  156.9 4.2 %collective-permute-done.29 = bf16[256,512]{1,0:T(8,128)(2,1)S(1)} collective-permute-done((bf16[256,512]{1,0:T(8,128)(2,1)S(1)}, bf16[256,512]{1,0:T(8,128)(2,1)S(1)}, u32[]{:S(2)}, u32[]{:S(2)}) %collective-permute-start.29) | collective-permute-done | bytes 262176 | tf_op jit(solution)/shard_map/ppermute | solution.py:11
  161.0 6.5 %collective-permute-done.30 = bf16[256,512]{1,0:T(8,128)(2,1)S(1)} collective-permute-done((bf16[256,512]{1,0:T(8,128)(2,1)S(1)}, bf16[256,512]{1,0:T(8,128)(2,1)S(1)}, u32[]{:S(2)}, u32[]{:S(2)}) %collective-permute-start.30) | collective-permute-done | bytes 262176 | tf_op jit(solution)/shard_map/ppermute | solution.py:11
  167.7 1.5 constant_dynamic-update-slice_fusion.2
  171.1 1.7 collective-permute-start.38
  173.8 4.7 %collective-permute-done.36 = bf16[1,256,512]{2,1,0:T(8,128)(2,1)S(1)} collective-permute-done((bf16[1,256,512]{2,1,0:T(8,128)(2,1)S(1)}, bf16[1,256,512]{2,1,0:T(8,128)(2,1)S(1)}, u32[]{:S(2)}, u32[]{:S(2)}) %collective-permute-start.36) | collective-permute-done | bytes 262176 | tf_op jit(solution)/shard_map/ppermute | solution.py:11
  178.5 5.0 %collective-permute-done.37 = bf16[1,256,512]{2,1,0:T(8,128)(2,1)S(1)} collective-permute-done((bf16[1,256,512]{2,1,0:T(8,128)(2,1)S(1)}, bf16[1,256,512]{2,1,0:T(8,128)(2,1)S(1)}, u32[]{:S(2)}, u32[]{:S(2)}) %collective-permute-start.37) | collective-permute-done | bytes 262176 | tf_op jit(solution)/shard_map/ppermute | solution.py:11
  (178 shorter events, 42.9 us)
Async XLA Ops:
  0.6 93.8 %copy-start = (bf16[2,512,512]{2,1,0:T(8,128)(2,1)S(1)}, bf16[2,512,512]{2,1,0:T(8,128)(2,1)}, u32[]{:S(2)}) copy-start(bf16[2,512,512]{2,1,0:T(8,128)(2,1)} %param.11) | copy-start | bytes 3145732
  23.6 11.2 %collective-permute-start.3 = (bf16[2,256,512]{2,1,0:T(8,128)(2,1)}, bf16[2,256,512]{2,1,0:T(8,128)(2,1)}, u32[]{:S(2)}, u32[]{:S(2)}) collective-permute-start(bf16[2,256,512]{2,1,0:T(8,128)(2,1)} %fusion.15), channel_id=1, source_target_pairs={{0,1},{1,0},{2,3},{3,2},{4,5},{5,4},{6,7},{7,6},{8,9},{9,8},{10,11... | collective-permute-start | bytes 1572872 | tf_op jit(solution)/shard_map/ppermute | solution.py:11
  27.8 9.9 %collective-permute-start = (bf16[4,128,512]{2,1,0:T(8,128)(2,1)}, bf16[4,128,512]{2,1,0:T(8,128)(2,1)}, u32[]{:S(2)}, u32[]{:S(2)}) collective-permute-start(bf16[4,128,512]{2,1,0:T(8,128)(2,1)} %constant_dynamic-slice_fusion.16), channel_id=1, source_target_pairs={{0,1},{1,0},{2,3},{3,2},{4,5},{5,4},{6,7},{7,6},{8,9},{9,8},{10,11... | collective-permute-start | bytes 1572872 | tf_op jit(solution)/shard_map/ppermute | solution.py:11
  30.8 81.7 %collective-permute-start.13 = (bf16[4,512,512]{2,1,0:T(8,128)(2,1)}, bf16[4,512,512]{2,1,0:T(8,128)(2,1)}, u32[]{:S(2)}, u32[]{:S(2)}) collective-permute-start(bf16[4,512,512]{2,1,0:T(8,128)(2,1)} %pad_maximum_fusion), channel_id=1, source_target_pairs={{0,1},{1,0},{2,3},{3,2},{4,5},{5,4},{6,7},{7,6},{8,9},{9,8},{10,11... | collective-permute-start | bytes 6291464 | tf_op jit(solution)/shard_map/ppermute | solution.py:11
  41.2 8.4 %collective-permute-start.4 = (bf16[384,128]{1,0:T(8,128)(2,1)}, bf16[384,128]{1,0:T(8,128)(2,1)}, u32[]{:S(2)}, u32[]{:S(2)}) collective-permute-start(bf16[384,128]{1,0:T(8,128)(2,1)} %get-tuple-element.48), channel_id=1, source_target_pairs={{0,2},{1,3},{2,0},{3,1},{4,6},{5,7},{6,4},{7,5},{8,10},{9,11},{10,... | collective-permute-start | bytes 294920 | tf_op jit(solution)/shard_map/ppermute | solution.py:11
  44.2 11.0 %collective-permute-start.5 = (bf16[384,128]{1,0:T(8,128)(2,1)}, bf16[384,128]{1,0:T(8,128)(2,1)}, u32[]{:S(2)}, u32[]{:S(2)}) collective-permute-start(bf16[384,128]{1,0:T(8,128)(2,1)} %get-tuple-element.49), channel_id=1, source_target_pairs={{0,4},{1,5},{2,6},{3,7},{4,0},{5,1},{6,2},{7,3},{8,12},{9,13},{10,... | collective-permute-start | bytes 294920 | tf_op jit(solution)/shard_map/ppermute | solution.py:11
  46.8 8.4 %collective-permute-start.6 = (bf16[384,128]{1,0:T(8,128)(2,1)}, bf16[384,128]{1,0:T(8,128)(2,1)}, u32[]{:S(2)}, u32[]{:S(2)}) collective-permute-start(bf16[384,128]{1,0:T(8,128)(2,1)} %get-tuple-element.50), channel_id=1, source_target_pairs={{0,6},{1,7},{2,4},{3,5},{4,2},{5,3},{6,0},{7,1},{8,14},{9,15},{10,... | collective-permute-start | bytes 294920 | tf_op jit(solution)/shard_map/ppermute | solution.py:11
  47.9 56.2 %collective-permute-start.32 = (bf16[2,512,512]{2,1,0:T(8,128)(2,1)}, bf16[2,512,512]{2,1,0:T(8,128)(2,1)}, u32[]{:S(2)}, u32[]{:S(2)}) collective-permute-start(bf16[2,512,512]{2,1,0:T(8,128)(2,1)} %pad_maximum_fusion.2), channel_id=1, source_target_pairs={{0,8},{8,0},{16,24},{24,16},{1,9},{9,1},{17,25},{25,17},{2,10},{10... | collective-permute-start | bytes 3145736 | tf_op jit(solution)/shard_map/ppermute | solution.py:11
  49.6 7.3 %collective-permute-start.1 = (bf16[128,512]{1,0:T(8,128)(2,1)}, bf16[128,512]{1,0:T(8,128)(2,1)S(1)}, u32[]{:S(2)}, u32[]{:S(2)}) collective-permute-start(bf16[128,512]{1,0:T(8,128)(2,1)} %get-tuple-element.47), channel_id=1, source_target_pairs={{0,2},{1,3},{2,0},{3,1},{4,6},{5,7},{6,4},{7,5},{8,10},{9,11},{10,... | collective-permute-start | bytes 393224 | tf_op jit(solution)/shard_map/ppermute | solution.py:11
  56.9 6.5 %collective-permute-start.7 = (bf16[256,128]{1,0:T(8,128)(2,1)}, bf16[256,128]{1,0:T(8,128)(2,1)}, u32[]{:S(2)}, u32[]{:S(2)}) collective-permute-start(bf16[256,128]{1,0:T(8,128)(2,1)} %get-tuple-element.58), channel_id=1, source_target_pairs={{0,1},{1,0},{2,3},{3,2},{4,5},{5,4},{6,7},{7,6},{8,9},{9,8},{10,11... | collective-permute-start | bytes 196616 | tf_op jit(solution)/shard_map/ppermute | solution.py:11
  57.8 9.7 %collective-permute-start.2 = (bf16[128,512]{1,0:T(8,128)(2,1)S(1)}, bf16[128,512]{1,0:T(8,128)(2,1)S(1)}, u32[]{:S(2)}, u32[]{:S(2)}) collective-permute-start(bf16[128,512]{1,0:T(8,128)(2,1)S(1)} %fusion.82), channel_id=1, source_target_pairs={{0,4},{1,5},{2,6},{3,7},{4,0},{5,1},{6,2},{7,3},{8,12},{9,13},{10,... | collective-permute-start | bytes 393224 | tf_op jit(solution)/shard_map/ppermute | solution.py:11
  61.9 18.5 %copy-start.4 = (bf16[2,256,512]{2,1,0:T(8,128)(2,1)S(1)}, bf16[2,256,512]{2,1,0:T(8,128)(2,1)}, u32[]{:S(2)}) copy-start(bf16[2,256,512]{2,1,0:T(8,128)(2,1)} %copy-done.3) | copy-start | bytes 1572868
  61.9 18.5 %collective-permute-start.23 = (bf16[256,512]{1,0:T(8,128)(2,1)}, bf16[256,512]{1,0:T(8,128)(2,1)S(1)}, u32[]{:S(2)}, u32[]{:S(2)}) collective-permute-start(bf16[256,512]{1,0:T(8,128)(2,1)} %get-tuple-element.42), channel_id=1, source_target_pairs={{0,8},{8,0},{16,24},{24,16},{1,9},{9,1},{17,25},{25,17},{2,10},{10... | collective-permute-start | bytes 786440 | tf_op jit(solution)/shard_map/ppermute | solution.py:11
  69.7 9.9 %collective-permute-start.8 = (f32[128,128]{1,0:T(8,128)S(1)}, f32[128,128]{1,0:T(8,128)S(1)}, u32[]{:S(2)}, u32[]{:S(2)}) collective-permute-start(f32[128,128]{1,0:T(8,128)S(1)} %convert_subtract_fusion.3), channel_id=1, source_target_pairs={{0,8},{8,0},{16,24},{24,16},{1,9},{9,1},{17,25},{25,17},{2,10},{10... | collective-permute-start | bytes 196616 | tf_op jit(solution)/shard_map/ppermute | solution.py:11
  73.5 34.6 %collective-permute-start.34 = (bf16[2,512,512]{2,1,0:T(8,128)(2,1)}, bf16[2,512,512]{2,1,0:T(8,128)(2,1)S(1)}, u32[]{:S(2)}, u32[]{:S(2)}) collective-permute-start(bf16[2,512,512]{2,1,0:T(8,128)(2,1)} %pad_maximum_fusion.3), channel_id=1, source_target_pairs={{0,16},{8,24},{16,0},{24,8},{1,17},{9,25},{17,1},{25,9},{2,18},{10... | collective-permute-start | bytes 3145736 | tf_op jit(solution)/shard_map/ppermute | solution.py:11
  79.7 24.4 %copy-start.21 = (bf16[1,512,512]{2,1,0:T(8,128)(2,1)S(1)}, bf16[1,512,512]{2,1,0:T(8,128)(2,1)}, u32[]{:S(2)}) copy-start(bf16[1,512,512]{2,1,0:T(8,128)(2,1)} %get-tuple-element.22) | copy-start | bytes 1572868
  79.7 24.4 %copy-start.22 = (bf16[1,512,512]{2,1,0:T(8,128)(2,1)S(1)}, bf16[1,512,512]{2,1,0:T(8,128)(2,1)}, u32[]{:S(2)}) copy-start(bf16[1,512,512]{2,1,0:T(8,128)(2,1)} %get-tuple-element.25) | copy-start | bytes 1572868
  79.7 4.0 %collective-permute-start.9 = (bf16[128,128]{1,0:T(8,128)(2,1)S(1)}, bf16[128,128]{1,0:T(8,128)(2,1)S(1)}, u32[]{:S(2)}, u32[]{:S(2)}) collective-permute-start(bf16[128,128]{1,0:T(8,128)(2,1)S(1)} %get-tuple-element.16), channel_id=1, source_target_pairs={{0,2},{1,3},{2,0},{3,1},{4,6},{5,7},{6,4},{7,5},{8,10},{9,11},{10,... | collective-permute-start | bytes 98312 | tf_op jit(solution)/shard_map/ppermute | solution.py:11
  80.4 23.4 %collective-permute-start.24 = (bf16[256,512]{1,0:T(8,128)(2,1)S(1)}, bf16[256,512]{1,0:T(8,128)(2,1)S(1)}, u32[]{:S(2)}, u32[]{:S(2)}) collective-permute-start(bf16[256,512]{1,0:T(8,128)(2,1)S(1)} %fusion.41), channel_id=1, source_target_pairs={{0,16},{8,24},{16,0},{24,8},{1,17},{9,25},{17,1},{25,9},{2,18},{10... | collective-permute-start | bytes 786440 | tf_op jit(solution)/shard_map/ppermute | solution.py:11
  83.7 5.1 %collective-permute-start.10 = (bf16[128,128]{1,0:T(8,128)(2,1)S(1)}, bf16[128,128]{1,0:T(8,128)(2,1)S(1)}, u32[]{:S(2)}, u32[]{:S(2)}) collective-permute-start(bf16[128,128]{1,0:T(8,128)(2,1)S(1)} %get-tuple-element.16), channel_id=1, source_target_pairs={{0,4},{1,5},{2,6},{3,7},{4,0},{5,1},{6,2},{7,3},{8,12},{9,13},{10,... | collective-permute-start | bytes 98312 | tf_op jit(solution)/shard_map/ppermute | solution.py:11
  88.7 5.7 %collective-permute-start.11 = (bf16[128,128]{1,0:T(8,128)(2,1)S(1)}, bf16[128,128]{1,0:T(8,128)(2,1)S(1)}, u32[]{:S(2)}, u32[]{:S(2)}) collective-permute-start(bf16[128,128]{1,0:T(8,128)(2,1)S(1)} %get-tuple-element.16), channel_id=1, source_target_pairs={{0,6},{1,7},{2,4},{3,5},{4,2},{5,3},{6,0},{7,1},{8,14},{9,15},{10,... | collective-permute-start | bytes 98312 | tf_op jit(solution)/shard_map/ppermute | solution.py:11
  94.8 14.5 %collective-permute-start.12 = (bf16[2,128,512]{2,1,0:T(8,128)(2,1)S(1)}, bf16[2,128,512]{2,1,0:T(8,128)(2,1)S(1)}, u32[]{:S(2)}, u32[]{:S(2)}) collective-permute-start(bf16[2,128,512]{2,1,0:T(8,128)(2,1)S(1)} %get-tuple-element.51), channel_id=1, source_target_pairs={{0,1},{1,0},{2,3},{3,2},{4,5},{5,4},{6,7},{7,6},{8,9},{9,8},{10,11... | collective-permute-start | bytes 786440 | tf_op jit(solution)/shard_map/ppermute | solution.py:11
  104.0 6.8 %collective-permute-start.25 = (bf16[256,512]{1,0:T(8,128)(2,1)S(1)}, bf16[256,512]{1,0:T(8,128)(2,1)S(1)}, u32[]{:S(2)}, u32[]{:S(2)}) collective-permute-start(bf16[256,512]{1,0:T(8,128)(2,1)S(1)} %add_convert_fusion.4), channel_id=1, source_target_pairs={{0,2},{1,3},{2,0},{3,1},{4,6},{5,7},{6,4},{7,5},{8,10},{9,11},{10,... | collective-permute-start | bytes 786440 | tf_op jit(solution)/shard_map/ppermute | solution.py:11
  106.6 48.9 %collective-permute-start.33 = (bf16[1,512,512]{2,1,0:T(8,128)(2,1)}, bf16[1,512,512]{2,1,0:T(8,128)(2,1)}, u32[]{:S(2)}, u32[]{:S(2)}) collective-permute-start(bf16[1,512,512]{2,1,0:T(8,128)(2,1)} %constant_dynamic-slice_fusion.5), channel_id=1, source_target_pairs={{0,16},{8,24},{16,0},{24,8},{1,17},{9,25},{17,1},{25,9},{2,18},{10... | collective-permute-start | bytes 1572872 | tf_op jit(solution)/shard_map/ppermute | solution.py:11
  109.3 22.4 %copy-start.17 = (bf16[2,256,512]{2,1,0:T(8,128)(2,1)}, bf16[2,256,512]{2,1,0:T(8,128)(2,1)S(1)}, u32[]{:S(2)}) copy-start(bf16[2,256,512]{2,1,0:T(8,128)(2,1)S(1)} %constant_dynamic-update-slice_fusion.12) | copy-start | bytes 1572868
  110.9 15.8 %collective-permute-start.26 = (bf16[256,512]{1,0:T(8,128)(2,1)S(1)}, bf16[256,512]{1,0:T(8,128)(2,1)S(1)}, u32[]{:S(2)}, u32[]{:S(2)}) collective-permute-start(bf16[256,512]{1,0:T(8,128)(2,1)S(1)} %add.293), channel_id=1, source_target_pairs={{0,4},{1,5},{2,6},{3,7},{4,0},{5,1},{6,2},{7,3},{8,12},{9,13},{10,... | collective-permute-start | bytes 786440 | tf_op jit(solution)/shard_map/ppermute | solution.py:11
  116.4 10.5 %collective-permute-start.14 = (bf16[32,1024]{1,0:T(8,128)(2,1)S(1)}, bf16[32,1024]{1,0:T(8,128)(2,1)S(1)}, u32[]{:S(2)}, u32[]{:S(2)}) collective-permute-start(bf16[32,1024]{1,0:T(8,128)(2,1)S(1)} %get-tuple-element.55), channel_id=1, source_target_pairs={{0,2},{1,3},{2,0},{3,1},{4,6},{5,7},{6,4},{7,5},{8,10},{9,11},{10,... | collective-permute-start | bytes 196616 | tf_op jit(solution)/shard_map/ppermute | solution.py:11
  118.0 10.1 %collective-permute-start.15 = (bf16[32,1024]{1,0:T(8,128)(2,1)S(1)}, bf16[32,1024]{1,0:T(8,128)(2,1)S(1)}, u32[]{:S(2)}, u32[]{:S(2)}) collective-permute-start(bf16[32,1024]{1,0:T(8,128)(2,1)S(1)} %get-tuple-element.56), channel_id=1, source_target_pairs={{0,4},{1,5},{2,6},{3,7},{4,0},{5,1},{6,2},{7,3},{8,12},{9,13},{10,... | collective-permute-start | bytes 196616 | tf_op jit(solution)/shard_map/ppermute | solution.py:11
  118.4 9.7 %collective-permute-start.16 = (bf16[32,1024]{1,0:T(8,128)(2,1)S(1)}, bf16[32,1024]{1,0:T(8,128)(2,1)S(1)}, u32[]{:S(2)}, u32[]{:S(2)}) collective-permute-start(bf16[32,1024]{1,0:T(8,128)(2,1)S(1)} %get-tuple-element.57), channel_id=1, source_target_pairs={{0,6},{1,7},{2,4},{3,5},{4,2},{5,3},{6,0},{7,1},{8,14},{9,15},{10,... | collective-permute-start | bytes 196616 | tf_op jit(solution)/shard_map/ppermute | solution.py:11
  126.8 10.6 %collective-permute-start.27 = (bf16[256,512]{1,0:T(8,128)(2,1)S(1)}, bf16[256,512]{1,0:T(8,128)(2,1)S(1)}, u32[]{:S(2)}, u32[]{:S(2)}) collective-permute-start(bf16[256,512]{1,0:T(8,128)(2,1)S(1)} %get-tuple-element.12), channel_id=1, source_target_pairs={{0,1},{1,0},{2,3},{3,2},{4,5},{5,4},{6,7},{7,6},{8,9},{9,8},{10,11... | collective-permute-start | bytes 786440 | tf_op jit(solution)/shard_map/ppermute | solution.py:11
  128.2 17.0 %copy-start.30 = (bf16[2,512,512]{2,1,0:T(8,128)(2,1)S(1)}, bf16[2,512,512]{2,1,0:T(8,128)(2,1)}, u32[]{:S(2)}) copy-start(bf16[2,512,512]{2,1,0:T(8,128)(2,1)} %param.12) | copy-start | bytes 3145732
  128.2 7.2 %collective-permute-start.17 = (bf16[32,1024]{1,0:T(8,128)(2,1)S(1)}, bf16[32,1024]{1,0:T(8,128)(2,1)S(1)}, u32[]{:S(2)}, u32[]{:S(2)}) collective-permute-start(bf16[32,1024]{1,0:T(8,128)(2,1)S(1)} %fusion.60), channel_id=1, source_target_pairs={{0,8},{8,0},{16,24},{24,16},{1,9},{9,1},{17,25},{25,17},{2,10},{10... | collective-permute-start | bytes 196616 | tf_op jit(solution)/shard_map/ppermute | solution.py:11
  128.8 7.1 %collective-permute-start.18 = (bf16[32,1024]{1,0:T(8,128)(2,1)S(1)}, bf16[32,1024]{1,0:T(8,128)(2,1)S(1)}, u32[]{:S(2)}, u32[]{:S(2)}) collective-permute-start(bf16[32,1024]{1,0:T(8,128)(2,1)S(1)} %fusion.60), channel_id=1, source_target_pairs={{0,16},{8,24},{16,0},{24,8},{1,17},{9,25},{17,1},{25,9},{2,18},{10... | collective-permute-start | bytes 196616 | tf_op jit(solution)/shard_map/ppermute | solution.py:11
  130.0 5.9 %collective-permute-start.19 = (bf16[32,1024]{1,0:T(8,128)(2,1)S(1)}, bf16[32,1024]{1,0:T(8,128)(2,1)S(1)}, u32[]{:S(2)}, u32[]{:S(2)}) collective-permute-start(bf16[32,1024]{1,0:T(8,128)(2,1)S(1)} %fusion.60), channel_id=1, source_target_pairs={{0,24},{8,16},{16,8},{24,0},{1,25},{9,17},{17,9},{25,1},{2,26},{10... | collective-permute-start | bytes 196616 | tf_op jit(solution)/shard_map/ppermute | solution.py:11
  135.4 32.2 %collective-permute-start.35 = (bf16[1,512,512]{2,1,0:T(8,128)(2,1)}, bf16[1,512,512]{2,1,0:T(8,128)(2,1)}, u32[]{:S(2)}, u32[]{:S(2)}) collective-permute-start(bf16[1,512,512]{2,1,0:T(8,128)(2,1)} %constant_dynamic-slice_fusion), channel_id=1, source_target_pairs={{0,8},{8,0},{16,24},{24,16},{1,9},{9,1},{17,25},{25,17},{2,10},{10... | collective-permute-start | bytes 1572872 | tf_op jit(solution)/shard_map/ppermute | solution.py:11
  136.0 4.6 %collective-permute-start.20 = (bf16[32,1024]{1,0:T(8,128)(2,1)S(1)}, bf16[32,1024]{1,0:T(8,128)(2,1)S(1)}, u32[]{:S(2)}, u32[]{:S(2)}) collective-permute-start(bf16[32,1024]{1,0:T(8,128)(2,1)S(1)} %get-tuple-element.14), channel_id=1, source_target_pairs={{0,2},{1,3},{2,0},{3,1},{4,6},{5,7},{6,4},{7,5},{8,10},{9,11},{10,... | collective-permute-start | bytes 196616 | tf_op jit(solution)/shard_map/ppermute | solution.py:11
  137.5 11.1 %copy-start.18 = (bf16[2,256,512]{2,1,0:T(8,128)(2,1)S(1)}, bf16[2,256,512]{2,1,0:T(8,128)(2,1)}, u32[]{:S(2)}) copy-start(bf16[2,256,512]{2,1,0:T(8,128)(2,1)} %copy-done.17) | copy-start | bytes 1572868
  137.5 6.2 %collective-permute-start.21 = (bf16[32,1024]{1,0:T(8,128)(2,1)S(1)}, bf16[32,1024]{1,0:T(8,128)(2,1)S(1)}, u32[]{:S(2)}, u32[]{:S(2)}) collective-permute-start(bf16[32,1024]{1,0:T(8,128)(2,1)S(1)} %get-tuple-element.14), channel_id=1, source_target_pairs={{0,4},{1,5},{2,6},{3,7},{4,0},{5,1},{6,2},{7,3},{8,12},{9,13},{10,... | collective-permute-start | bytes 196616 | tf_op jit(solution)/shard_map/ppermute | solution.py:11
  139.1 6.1 %collective-permute-start.22 = (bf16[32,1024]{1,0:T(8,128)(2,1)S(1)}, bf16[32,1024]{1,0:T(8,128)(2,1)S(1)}, u32[]{:S(2)}, u32[]{:S(2)}) collective-permute-start(bf16[32,1024]{1,0:T(8,128)(2,1)S(1)} %get-tuple-element.14), channel_id=1, source_target_pairs={{0,6},{1,7},{2,4},{3,5},{4,2},{5,3},{6,0},{7,1},{8,14},{9,15},{10,... | collective-permute-start | bytes 196616 | tf_op jit(solution)/shard_map/ppermute | solution.py:11
  148.5 6.3 %collective-permute-start.28 = (bf16[2,128,512]{2,1,0:T(8,128)(2,1)S(1)}, bf16[2,128,512]{2,1,0:T(8,128)(2,1)S(1)}, u32[]{:S(2)}, u32[]{:S(2)}) collective-permute-start(bf16[2,128,512]{2,1,0:T(8,128)(2,1)S(1)} %get-tuple-element.53), channel_id=1, source_target_pairs={{0,1},{1,0},{2,3},{3,2},{4,5},{5,4},{6,7},{7,6},{8,9},{9,8},{10,11... | collective-permute-start | bytes 786440 | tf_op jit(solution)/shard_map/ppermute | solution.py:11
  151.9 9.2 %collective-permute-start.29 = (bf16[256,512]{1,0:T(8,128)(2,1)S(1)}, bf16[256,512]{1,0:T(8,128)(2,1)S(1)}, u32[]{:S(2)}, u32[]{:S(2)}) collective-permute-start(bf16[256,512]{1,0:T(8,128)(2,1)S(1)} %get-tuple-element.35), channel_id=1, source_target_pairs={{0,8},{8,0},{16,24},{24,16},{1,9},{9,1},{17,25},{25,17},{2,10},{10... | collective-permute-start | bytes 786440 | tf_op jit(solution)/shard_map/ppermute | solution.py:11
  153.5 14.0 %collective-permute-start.30 = (bf16[256,512]{1,0:T(8,128)(2,1)S(1)}, bf16[256,512]{1,0:T(8,128)(2,1)S(1)}, u32[]{:S(2)}, u32[]{:S(2)}) collective-permute-start(bf16[256,512]{1,0:T(8,128)(2,1)S(1)} %get-tuple-element.37), channel_id=1, source_target_pairs={{0,16},{8,24},{16,0},{24,8},{1,17},{9,25},{17,1},{25,9},{2,18},{10... | collective-permute-start | bytes 786440 | tf_op jit(solution)/shard_map/ppermute | solution.py:11
  154.8 12.7 %collective-permute-start.31 = (bf16[256,512]{1,0:T(8,128)(2,1)S(1)}, bf16[256,512]{1,0:T(8,128)(2,1)S(1)}, u32[]{:S(2)}, u32[]{:S(2)}) collective-permute-start(bf16[256,512]{1,0:T(8,128)(2,1)S(1)} %get-tuple-element.36), channel_id=1, source_target_pairs={{0,24},{8,16},{16,8},{24,0},{1,25},{9,17},{17,9},{25,1},{2,26},{10... | collective-permute-start | bytes 786440 | tf_op jit(solution)/shard_map/ppermute | solution.py:11
  156.9 15.9 %copy-start.19 = (bf16[2,256,512]{2,1,0:T(8,128)(2,1)S(1)}, bf16[2,256,512]{2,1,0:T(8,128)(2,1)}, u32[]{:S(2)}) copy-start(bf16[2,256,512]{2,1,0:T(8,128)(2,1)} %copy-done.17) | copy-start | bytes 1572868
  167.6 16.9 %copy-start.1 = (bf16[2,512,512]{2,1,0:T(8,128)(2,1)S(1)}, bf16[2,512,512]{2,1,0:T(8,128)(2,1)}, u32[]{:S(2)}) copy-start(bf16[2,512,512]{2,1,0:T(8,128)(2,1)} %param.11) | copy-start | bytes 3145732
  169.2 9.3 %collective-permute-start.36 = (bf16[1,256,512]{2,1,0:T(8,128)(2,1)S(1)}, bf16[1,256,512]{2,1,0:T(8,128)(2,1)S(1)}, u32[]{:S(2)}, u32[]{:S(2)}) collective-permute-start(bf16[1,256,512]{2,1,0:T(8,128)(2,1)S(1)} %get-tuple-element.69), channel_id=1, source_target_pairs={{0,8},{8,0},{16,24},{24,16},{1,9},{9,1},{17,25},{25,17},{2,10},{10... | collective-permute-start | bytes 786440 | tf_op jit(solution)/shard_map/ppermute | solution.py:11
  170.3 13.3 %collective-permute-start.37 = (bf16[1,256,512]{2,1,0:T(8,128)(2,1)S(1)}, bf16[1,256,512]{2,1,0:T(8,128)(2,1)S(1)}, u32[]{:S(2)}, u32[]{:S(2)}) collective-permute-start(bf16[1,256,512]{2,1,0:T(8,128)(2,1)S(1)} %get-tuple-element.69), channel_id=1, source_target_pairs={{0,16},{8,24},{16,0},{24,8},{1,17},{9,25},{17,1},{25,9},{2,18},{10... | collective-permute-start | bytes 786440 | tf_op jit(solution)/shard_map/ppermute | solution.py:11
  171.1 12.5 %collective-permute-start.38 = (bf16[1,256,512]{2,1,0:T(8,128)(2,1)S(1)}, bf16[1,256,512]{2,1,0:T(8,128)(2,1)S(1)}, u32[]{:S(2)}, u32[]{:S(2)}) collective-permute-start(bf16[1,256,512]{2,1,0:T(8,128)(2,1)S(1)} %get-tuple-element.69), channel_id=1, source_target_pairs={{0,24},{8,16},{16,8},{24,0},{1,25},{9,17},{17,9},{25,1},{2,26},{10... | collective-permute-start | bytes 786440 | tf_op jit(solution)/shard_map/ppermute | solution.py:11
  (23 other events, 76.3 us)

commit v2 on v1

v2 whole, which is shorter than its diff:
```python
import jax
import jax.numpy as jnp
from jax import lax
from jax.experimental import pallas as pl
from jax.experimental.pallas import tpu as pltpu
from jax.sharding import PartitionSpec as P

F32 = jnp.float32
BF16 = jnp.bfloat16
CORES = 2


def swap(block, axis, bits):
    return lax.ppermute(block, axis, [(i, i ^ bits) for i in range(lax.axis_size(axis))])


def dot(a, b):
    return jnp.dot(a, b, preferred_element_type=F32)


def shaped(shape, dtype=BF16):
    return jax.ShapeDtypeStruct(tuple(shape), dtype)


class Picked:
    def __init__(self, array, block, index):
        self.array, self.block, self.index = array, block, index


def on_device(right_side, panels, tile_counts, diag_leaf, diag_pair, diag_root, sup_rows):
    right, panels, counts = right_side[0], panels[:, 0], tile_counts[:, 0]
    levels, here, width, _ = panels.shape
    n_row, n_leaf = lax.axis_size("row"), lax.axis_size("leaf")
    chips = min(n_row // CORES, 4)
    outer = [1 << b for b in range(n_row.bit_length()) if CORES * chips <= 1 << b < n_row]
    height = right.shape[1]
    half_r, half_w = height // CORES, width // CORES
    part_r, part_w = half_r // chips, width // chips

    meta = jnp.concatenate(
        [
            jnp.stack([lax.axis_index("leaf"), lax.axis_index("row")]).astype(jnp.int32),
            sup_rows,
            counts.reshape(-1),
        ]
    )

    def leaf_of(meta):
        return meta[0]

    def core_of(meta):
        return meta[1] & (CORES - 1)

    def chip_of(meta):
        return (meta[1] // CORES) & (chips - 1)

    def spot(meta, level):
        return lax.rem(meta[2 + level], here)

    def owns(meta, level):
        return lax.div(meta[2 + level], here) == meta[1]

    def live(meta, level, a):
        kept = meta[2 + levels + level * here + a]
        for m in range(level + 1):
            kept = jnp.where(meta[1] * here + a == meta[2 + m], 0, kept)
        return kept

    def live_owned(meta, of, level):
        return jnp.where(owns(meta, level), live(meta, of, spot(meta, level)), 0)

    def keep(limit):
        ids = lax.broadcasted_iota(jnp.int32, (1, width), 1)
        return (ids < limit).astype(F32).astype(BF16)

    def side(level, other):
        return Picked(
            right,
            (None, half_r, width),
            lambda i, meta: (spot(meta, level), core_of(meta) ^ other, 0),
        )

    def side_value(meta, ref, level):
        return ref[...] * keep(jnp.where(owns(meta, level), width, 0))

    def tile(of, level, other=None):
        if other is None:
            return Picked(
                panels, (None, None, width, width), lambda i, meta: (of, spot(meta, level), 0, 0)
            )
        return Picked(
            panels,
            (None, None, half_w, width),
            lambda i, meta: (of, spot(meta, level), core_of(meta) ^ other, 0),
        )

    def tile_value(meta, ref, of, level):
        return ref[...] * keep(live_owned(meta, of, level))

    def run(body, operands, outs, scratch=(), steps=1, flops=0):
        arrays, specs, moved = [], [], 0
        for operand in operands:
            if not isinstance(operand, Picked):
                zeros = (0,) * operand.ndim
                operand = Picked(operand, operand.shape, lambda i, meta, zeros=zeros: zeros)
            arrays.append(operand.array)
            specs.append(pl.BlockSpec(operand.block, operand.index))
            size = operand.array.dtype.itemsize
            for n in operand.block:
                size *= n or 1
            moved += size * steps
        single = not isinstance(outs, (list, tuple))
        listed = [outs] if single else list(outs)
        out_specs = [
            pl.BlockSpec(out.shape, lambda i, meta, zeros=(0,) * len(out.shape): zeros)
            for out in listed
        ]
        moved += sum(out.size * out.dtype.itemsize for out in listed)
        results = pl.pallas_call(
            body,
            grid_spec=pltpu.PrefetchScalarGridSpec(
                num_scalar_prefetch=1,
                grid=(steps,),
                in_specs=specs,
                out_specs=out_specs,
                scratch_shapes=list(scratch),
            ),
            out_shape=listed,
            compiler_params=pltpu.CompilerParams(vmem_limit_bytes=40 * 1024 * 1024),
            cost_estimate=pl.CostEstimate(flops=flops, bytes_accessed=moved, transcendentals=0),
        )(meta, *arrays)
        return results[0] if single else results

    def spread(block):
        for bits in outer:
            block = block + swap(block, "row", bits)
        return block

    steps_up = [CORES * m for m in range(1, chips)]

    def b0_send(meta, ref, out):
        out[...] = side_value(meta, ref, 0)

    def b0_sum(meta, ref, got, out):
        out[...] = side_value(meta, ref, 0) + got[...]

    rows_half = shaped((half_r, width))
    b0 = run(b0_sum, [side(0, 0), swap(run(b0_send, [side(0, 1)], rows_half), "row", 1)], rows_half)
    b0 = spread(b0)
    bits = CORES
    while bits < CORES * chips // 2:
        b0 = b0 + swap(b0, "row", bits)
        bits *= 2
    b0_far = swap(b0, "row", bits)

    def first_send(meta, p, b, out):
        out[:half_w] = tile_value(meta, p, 0, 1)
        out[half_w:] = side_value(meta, b, 1)

    first = shaped((half_w + half_r, width))
    first_got = swap(run(first_send, [tile(0, 1, 1), side(1, 1)], first), "row", 1)

    def first_split(meta, p, b, got, *refs):
        outs, whole = refs[:-1], refs[-1]
        whole[:half_w] = tile_value(meta, p, 0, 1) + got[:half_w]
        whole[half_w:] = side_value(meta, b, 1) + got[half_w:]
        for m, out in enumerate(outs):
            start = pl.multiple_of((chip_of(meta) ^ m) * part_w, part_w)
            out[...] = whole[:, pl.ds(start, part_w)]

    columns = shaped((half_w + half_r, part_w))
    split = run(
        first_split,
        [tile(0, 1, 0), side(1, 0), first_got],
        [columns] * chips,
        [pltpu.VMEM((half_w + half_r, width), BF16)],
    )
    level1 = split[0]
    for piece, step in zip(split[1:], steps_up):
        level1 = level1 + swap(piece, "row", step)
    level1 = spread(level1)
    p01, b1 = level1[:half_w], level1[half_w:]
    p01_other = swap(p01, "row", 1)

    later = [(0, 2), (1, 2), (0, 3), (1, 3)]
    rest_rows = half_w + 2 * half_r + len(later) * width

    def rest_send(meta, p23, b2, b3, *refs):
        tiles, out = refs[:-1], refs[-1]
        out[:half_w] = tile_value(meta, p23, 2, 3)
        out[half_w : half_w + half_r] = side_value(meta, b2, 2)
        out[half_w + half_r : half_w + 2 * half_r] = side_value(meta, b3, 3)
        for i, (of, level) in enumerate(later):
            start = half_w + 2 * half_r + i * width
            out[start : start + width] = tile_value(meta, tiles[i], of, level)

    rest_got = swap(
        run(
            rest_send,
            [tile(2, 3, 1), side(2, 1), side(3, 1)] + [tile(*which) for which in later],
            shaped((rest_rows, width)),
        ),
        "row",
        1,
    )

    def x0_t1(meta, near, far, diag, p, p_other, b, x0, t1, whole):
        core = core_of(meta)
        x = dot(near[...] + far[...], diag[0]).astype(BF16)
        x0[...] = x
        whole[pl.ds(pl.multiple_of(core * half_w, half_w), half_w)] = p[...]
        whole[pl.ds(pl.multiple_of((1 - core) * half_w, half_w), half_w)] = p_other[...]
        t1[...] = b[...].astype(F32) - dot(x, whole[...])

    x0, t1 = run(
        x0_t1,
        [b0, b0_far, diag_leaf, p01, p01_other, b1],
        [rows_half, shaped((half_r, part_w), F32)],
        [pltpu.VMEM((width, part_w), BF16)],
    )
    m1 = (t1 + swap(t1, "leaf", 1)).astype(BF16)
    m1_parts = [m1] + [swap(m1, "row", step) for step in steps_up]

    def early(meta, p23, b2, b3, *refs):
        tiles, (got, x0), (p23_out, u, linked) = refs[:4], refs[4:6], refs[6:]
        p23_out[...] = tile_value(meta, p23, 2, 3) + got[:half_w]
        for i, b in enumerate((b2, b3)):
            rows = pl.ds(half_w + i * half_r, half_r)
            value = (side_value(meta, b, 2 + i) + got[rows]).astype(F32)
            start = half_w + 2 * half_r + 2 * i * width
            p0 = tile_value(meta, tiles[2 * i], 0, 2 + i) + got[start : start + width]
            u[:, i * width : (i + 1) * width] = value - dot(x0[...], p0)
            start += width
            linked[i] = tile_value(meta, tiles[2 * i + 1], 1, 2 + i) + got[start : start + width]

    p23, u, linked = run(
        early,
        [tile(2, 3, 0), side(2, 0), side(3, 0)]
        + [tile(*which) for which in later]
        + [rest_got, x0],
        [
            shaped((half_w, width)),
            shaped((half_r, 2 * width), F32),
            shaped((2, width, width)),
        ],
    )

    bits = 1
    while bits < n_leaf:
        p23 = (p23.astype(F32) + swap(p23, "leaf", bits).astype(F32)).astype(BF16)
        bits *= 2
    p23 = spread(p23)
    bits = CORES
    while bits < CORES * chips:
        p23 = p23 + swap(p23, "row", bits)
        bits *= 2
    p23_other = swap(p23, "row", 1)

    def x1_t23(meta, *refs):
        parts, (diag, u, linked, x1), rest = refs[:chips], refs[chips : chips + 4], refs[chips + 4 :]
        outs, whole = rest[:-1], rest[-1]
        chip = chip_of(meta)
        x = jnp.zeros((half_r, width), F32)
        for m, part in enumerate(parts):
            start = pl.multiple_of((chip ^ m) * part_w, part_w)
            x = x + dot(part[...], diag[pl.ds(start, part_w)])
        x = x.astype(BF16)
        x1[...] = x
        for i in range(2):
            cols = slice(i * width, (i + 1) * width)
            whole[:, cols] = u[:, cols] - dot(x, linked[i])
        for m, out in enumerate(outs):
            start = pl.multiple_of((chip ^ m) * part_r, part_r)
            out[...] = whole[pl.ds(start, part_r)].astype(BF16)

    pair = Picked(diag_pair, (None, width, width), lambda i, meta: (leaf_of(meta) // 2, 0, 0))
    strip = shaped((part_r, 2 * width))
    x1, *strips = run(
        x1_t23,
        m1_parts + [pair, u, linked],
        [rows_half] + [strip] * chips,
        [pltpu.VMEM((half_r, 2 * width), F32)],
    )
    t23 = strips[0]
    for piece, step in zip(strips[1:], steps_up):
        t23 = t23 + swap(piece, "row", step)
    t23 = spread(t23)
    total = t23.astype(F32)
    for m in range(1, n_leaf):
        total = total + swap(t23, "leaf", m).astype(F32)
    m23 = total.astype(BF16)
    m23_parts = [m23] + [swap(m23, "row", step) for step in steps_up]

    def x2_x3(meta, *refs):
        parts, (diag, p, p_other, out, whole, tile23) = refs[:chips], refs[chips:]
        chip, core = chip_of(meta), core_of(meta)
        for m, part in enumerate(parts):
            start = pl.multiple_of((chip ^ m) * part_r, part_r)
            whole[pl.ds(start, part_r)] = part[...]
        tile23[pl.ds(pl.multiple_of(core * half_w, half_w), half_w)] = p[...]
        tile23[pl.ds(pl.multiple_of((1 - core) * half_w, half_w), half_w)] = p_other[...]
        x = dot(whole[:, :width], diag[0]).astype(BF16)
        out[0] = x
        merged = whole[:, width:].astype(F32) - dot(x, tile23[...])
        out[1] = dot(merged.astype(BF16), diag[1]).astype(BF16)

    x23 = run(
        x2_x3,
        m23_parts + [diag_root, p23, p23_other],
        shaped((2, half_r, width)),
        [pltpu.VMEM((half_r, 2 * width), BF16), pltpu.VMEM((width, width), BF16)],
    )
    x01_other = [swap(x, "row", 1) for x in (x0, x1)]
    x23_other = swap(x23, "row", 1)

    def leaf_tile(array, level):
        if level is None:
            return Picked(
                array,
                (None, height, width),
                lambda i, meta: (leaf_of(meta) ^ lax.rem(i + 1, n_leaf), 0, 0),
            )
        return Picked(
            array,
            (None, None, width, width),
            lambda i, meta: (level, leaf_of(meta) ^ lax.rem(i + 1, n_leaf), 0, 0),
        )

    def update01(meta, b, pa, pb, x0, x1, x0_other, x1_other, *refs):
        outs, whole = refs[:-1], refs[-1]
        step = pl.program_id(0)
        core = core_of(meta)
        a = leaf_of(meta) ^ lax.rem(step + 1, n_leaf)

        @pl.when(step == 0)
        def _():
            for i, (mine, other) in enumerate(((x0, x0_other), (x1, x1_other))):
                whole[i, pl.ds(pl.multiple_of(core * half_r, half_r), half_r)] = mine[...]
                whole[i, pl.ds(pl.multiple_of((1 - core) * half_r, half_r), half_r)] = other[...]

        value = b[...].astype(F32)
        for i, p in enumerate((pa, pb)):
            value = value - dot(whole[i], p[...] * keep(live(meta, i, a)))
        for m in range(n_leaf):
            @pl.when(lax.rem(step + 1, n_leaf) == m)
            def _(m=m):
                outs[m][...] = value.astype(outs[m].dtype)

    block = shaped((height, width))
    shares = run(
        update01,
        [leaf_tile(right, None), leaf_tile(panels, 0), leaf_tile(panels, 1), x0, x1] + x01_other,
        [shaped((height, width), F32)] + [block] * (n_leaf - 1),
        [pltpu.VMEM((2, height, width), BF16)],
        steps=n_leaf,
    )
    shares_got = [swap(shares[m], "leaf", m) for m in range(1, n_leaf)]

    def panel_of(level, m):
        return Picked(
            panels,
            (None, None, width, width),
            lambda i, meta: (level, leaf_of(meta) ^ m, 0, 0),
        )

    def panel_value(meta, ref, level, m):
        return ref[...] * keep(live(meta, level, leaf_of(meta) ^ m))

    panels_got = []
    for m in range(1, n_leaf):
        def panel_send(meta, pa, pb, out, m=m):
            out[0] = panel_value(meta, pa, 2, m)
            out[1] = panel_value(meta, pb, 3, m)

        sent = run(panel_send, [panel_of(2, m), panel_of(3, m)], shaped((2, width, width)))
        panels_got.append(swap(sent, "leaf", m))

    def leaf_sums(meta, pa, pb, share, *refs):
        got, (panel_out, share_out) = refs[:-2], refs[-2:]
        panels_in, shares_in = got[: n_leaf - 1], got[n_leaf - 1 :]
        for i, p in enumerate((pa, pb)):
            value = panel_value(meta, p, 2 + i, 0).astype(F32)
            for ref in panels_in:
                value = value + ref[i].astype(F32)
            panel_out[i] = value.astype(BF16)
        value = share[...]
        for ref in shares_in:
            value = value + ref[...].astype(F32)
        share_out[...] = value

    panel_sum, share_sum = run(
        leaf_sums,
        [panel_of(2, 0), panel_of(3, 0), shares[0]] + panels_got + shares_got,
        [shaped((2, width, width)), shaped((height, width), F32)],
    )

    def final(meta, x0, x1, x0_other, x1_other, x23, x23_other, panel, share, solved, out):
        core = core_of(meta)
        mine = pl.ds(pl.multiple_of(core * half_r, half_r), half_r)
        other = pl.ds(pl.multiple_of((1 - core) * half_r, half_r), half_r)
        for i, (a, b) in enumerate(((x0, x0_other), (x1, x1_other))):
            solved[i, mine] = a[...]
            solved[i, other] = b[...]
        value = share[...]
        for i in range(2):
            solved[2 + i, mine] = x23[i]
            solved[2 + i, other] = x23_other[i]
            value = value - dot(solved[2 + i], panel[i])
        value = value.astype(BF16)
        for i in range(n_leaf):
            out[i] = value

    solved, done = run(
        final,
        [x0, x1] + x01_other + [x23, x23_other, panel_sum, share_sum],
        [shaped((levels, height, width)), shaped((n_leaf, height, width))],
    )
    updated = lax.all_to_all(done, "leaf", 0, 0, tiled=True)
    return solved[:, None], updated


def solution(mesh):
    return jax.shard_map(
        on_device,
        mesh=mesh,
        in_specs=(
            P("leaf", "row", None, None),
            P(None, "leaf", "row", None, None),
            P(None, "leaf", "row"),
            P("leaf", None, None),
            P(),
            P(),
            P(),
        ),
        out_specs=(P(None, "leaf", None, None), P("row", None, None)),
        check_vma=False,
    )
```

time: 185 us -> 167 us (0.903)
  other arithmetic: 26 us -> 2.47 us
  waiting for transfers between devices: 62.3 us -> 81.7 us
  matrix products: 16.4 us -> 0 us
  Pallas kernels: 0 us -> 16.4 us
  blocking collectives: 0 us -> 15.3 us
  local copies, waits for them, and re-layouts: 20.9 us -> 9.44 us
  between operations: 11.8 us -> 0.96 us
  starting transfers between devices: 47.1 us -> 40.4 us
    ppermute x39 -> x36, waiting for transfers between devices: 62.3 us -> 81.7 us  [swap(): lax.ppermute(block, axis, [(i, i ^ bits) for i in range(lax.axis_size(axi...]
    dot_general x13 -> x0, matrix products: 16.4 us -> none  [the longest x11 9.59 us: dot(): return jnp.dot(a, b, preferred_element_type=F32)]
    pallas_call x0 -> x15, Pallas kernels: none -> 16.4 us  [run(): pl.pallas_call(body, grid_spec=pltpu.PrefetchScalarGridSpec(num_scalar_pr...]
    all_to_all x0 -> x1, blocking collectives: none -> 15.3 us  [on_device(): updated = lax.all_to_all(done, 'leaf', 0, 0, tiled=True)]
    slice x3 -> x2, local copies, waits for them, and re-layouts: 7.5 us -> 0.01 us  [on_device(): p01, b1 = (level1[:half_w], level1[half_w:])]
    ppermute x39 -> x36, starting transfers between devices: 47.1 us -> 40.4 us  [swap(): lax.ppermute(block, axis, [(i, i ^ bits) for i in range(lax.axis_size(axi...]
    add x8 -> x5, other arithmetic: 6.57 us -> 0.21 us  [the longest x2 0.13 us: on_device(): p23 = p23 + swap(p23, 'row', bits)]
    select_n x5 -> x0, other arithmetic: 5.7 us -> none  [the longest x3 3.11 us: tile(): return jnp.where(mask[None, :] & owned[level], block, jnp.zeros_like(block))]
  transfers between devices with their start and end apart: 39 -> 36, of which waited for: 16 -> 17; matrix products, arithmetic and copies ran while one was open for 23% -> 0% of each run, Pallas kernels for 0% -> 7%
where the time goes in v2:
time: 167 us
  waiting for transfers between devices  81.7 us (49%)
  starting transfers between devices  40.4 us (24%)
  Pallas kernels  16.4 us (10%)
  blocking collectives  15.3 us (9%)
  local copies, waits for them, and re-layouts  9.44 us (6%)
  other arithmetic  2.47 us (1%)
    ppermute x36, waiting for transfers between devices, swap(): lax.ppermute(block, axis, [(i, i ^ bits) for i in range(lax.axis_size(axi...  81.7 us
    ppermute x36, starting transfers between devices, swap(): lax.ppermute(block, axis, [(i, i ^ bits) for i in range(lax.axis_size(axi...  40.4 us
    pallas_call x15, Pallas kernels, run(): pl.pallas_call(body, grid_spec=pltpu.PrefetchScalarGridSpec(num_scalar_pr...  16.4 us
    all_to_all x1, blocking collectives, on_device(): updated = lax.all_to_all(done, 'leaf', 0, 0, tiled=True)  15.3 us
    unnamed x20, local copies, waits for them, and re-layouts  9.35 us
  transfers between devices with their start and end apart: 36, of which 17 were waited for; matrix products, arithmetic and copies ran while one was open for 0% of the time, Pallas kernels for 7%

profile of v2, /device:TPU:0, one launch (start us, length us, event | category | flops | bytes accessed | tf_op | source)
XLA Modules:
  0.0 166.6 jit_solution(5005320072218332169)
XLA Ops:
  1.1 1.3 reduce.3
  3.3 3.4 %copy-done = bf16[4,1,4,512,512]{4,3,2,1,0:T(8,128)(2,1)S(1)} copy-done((bf16[4,1,4,512,512]{4,3,2,1,0:T(8,128)(2,1)S(1)}, bf16[4,1,4,512,512]{4,3,2,1,0:T(8,128)(2,1)}, u32[]{:S(2)}) %copy-start) | copy-done | bytes 8388632
  6.7 1.2 copy-done.2
  7.9 2.2 %shard_map.91 = bf16[2560,512]{1,0:T(8,128)(2,1)} custom-call(s32[22]{0:T(128)S(1)} %pad_add_fusion.meta, bf16[4,4,512,512]{3,2,1,0:T(8,128)(2,1)S(1)} %bitcast.7, bf16[4,256,512]{2,1,0:T(8,128)(2,1)S(1)} %bitcast.29, bf16[4,256,512]{2,1,0:T(8,128)(2,1)S(1)} %bitcast.30, bf16[4,4,512,512]{3,2,1,0:T(8,128)(2,1)S(1)} %bitcast.8, ...), custom_call_target="tpu_custom_call" | custom-call | bytes 5242880 | tf_op jit(solution)/shard_map/pallas_call | solution.py:119
  12.4 3.5 %collective-permute-done.got = bf16[128,512]{1,0:T(8,128)(2,1)S(1)} collective-permute-done((bf16[128,512]{1,0:T(8,128)(2,1)S(1)}, bf16[128,512]{1,0:T(8,128)(2,1)S(1)}, u32[]{:S(2)}, u32[]{:S(2)}) %collective-permute-start) | collective-permute-done | bytes 131104 | tf_op jit(solution)/shard_map/ppermute | solution.py:14
  16.5 3.0 %collective-permute-start.1 = (bf16[128,512]{1,0:T(8,128)(2,1)S(1)}, bf16[128,512]{1,0:T(8,128)(2,1)S(1)}, u32[]{:S(2)}, u32[]{:S(2)}) collective-permute-start(bf16[128,512]{1,0:T(8,128)(2,1)S(1)} %shard_map.87), channel_id=1, source_target_pairs={{0,2},{1,3},{2,0},{3,1},{4,6},{5,7},{6,4},{7,5},{8,10},{9,11},{10,... | collective-permute-start | bytes 393224 | tf_op jit(solution)/shard_map/ppermute | solution.py:14
  20.2 2.5 %collective-permute-start.6 = (bf16[384,128]{1,0:T(8,128)(2,1)S(1)}, bf16[384,128]{1,0:T(8,128)(2,1)S(1)}, u32[]{:S(2)}, u32[]{:S(2)}) collective-permute-start(bf16[384,128]{1,0:T(8,128)(2,1)S(1)} %get-tuple-element.27), channel_id=1, source_target_pairs={{0,6},{1,7},{2,4},{3,5},{4,2},{5,3},{6,0},{7,1},{8,14},{9,15},{10,... | collective-permute-start | bytes 294920 | tf_op jit(solution)/shard_map/ppermute | solution.py:14
  22.9 1.7 %collective-permute-start.4 = (bf16[384,128]{1,0:T(8,128)(2,1)S(1)}, bf16[384,128]{1,0:T(8,128)(2,1)S(1)}, u32[]{:S(2)}, u32[]{:S(2)}) collective-permute-start(bf16[384,128]{1,0:T(8,128)(2,1)S(1)} %get-tuple-element.25), channel_id=1, source_target_pairs={{0,2},{1,3},{2,0},{3,1},{4,6},{5,7},{6,4},{7,5},{8,10},{9,11},{10,... | collective-permute-start | bytes 294920 | tf_op jit(solution)/shard_map/ppermute | solution.py:14
  24.7 2.3 %collective-permute-start.2 = (bf16[128,512]{1,0:T(8,128)(2,1)S(1)}, bf16[128,512]{1,0:T(8,128)(2,1)S(1)}, u32[]{:S(2)}, u32[]{:S(2)}) collective-permute-start(bf16[128,512]{1,0:T(8,128)(2,1)S(1)} %add.45.near), channel_id=1, source_target_pairs={{0,4},{1,5},{2,6},{3,7},{4,0},{5,1},{6,2},{7,3},{8,12},{9,13},{10,... | collective-permute-start | bytes 393224 | tf_op jit(solution)/shard_map/ppermute | solution.py:14
  26.9 1.5 collective-permute-done.6
  28.5 6.7 %collective-permute-done.5 = bf16[384,128]{1,0:T(8,128)(2,1)S(1)} collective-permute-done((bf16[384,128]{1,0:T(8,128)(2,1)S(1)}, bf16[384,128]{1,0:T(8,128)(2,1)S(1)}, u32[]{:S(2)}, u32[]{:S(2)}) %collective-permute-start.5) | collective-permute-done | bytes 98336 | tf_op jit(solution)/shard_map/ppermute | solution.py:14
  35.3 2.3 %collective-permute-done.2.far = bf16[128,512]{1,0:T(8,128)(2,1)S(1)} collective-permute-done((bf16[128,512]{1,0:T(8,128)(2,1)S(1)}, bf16[128,512]{1,0:T(8,128)(2,1)S(1)}, u32[]{:S(2)}, u32[]{:S(2)}) %collective-permute-start.2) | collective-permute-done | bytes 131104 | tf_op jit(solution)/shard_map/ppermute | solution.py:14
  38.5 1.5 copy-done.4
  40.0 1.7 %copy-done.5 = bf16[2560,512]{1,0:T(8,128)(2,1)S(1)} copy-done((bf16[2560,512]{1,0:T(8,128)(2,1)S(1)}, bf16[2560,512]{1,0:T(8,128)(2,1)}, u32[]{:S(2)}) %copy-start.5) | copy-done | bytes 2621464
  41.7 1.0 shard_map.92
  42.8 1.6 collective-permute-start.24
  44.3 6.5 %collective-permute-done.24 = bf16[256,512]{1,0:T(8,128)(2,1)S(1)} collective-permute-done((bf16[256,512]{1,0:T(8,128)(2,1)S(1)}, bf16[256,512]{1,0:T(8,128)(2,1)S(1)}, u32[]{:S(2)}, u32[]{:S(2)}) %collective-permute-start.24) | collective-permute-done | bytes 262176 | tf_op jit(solution)/shard_map/ppermute | solution.py:14
  50.9 1.6 collective-permute-start.25
  53.1 1.6 collective-permute-start.30
  56.4 3.3 %collective-permute-done.25 = bf16[256,512]{1,0:T(8,128)(2,1)S(1)} collective-permute-done((bf16[256,512]{1,0:T(8,128)(2,1)S(1)}, bf16[256,512]{1,0:T(8,128)(2,1)S(1)}, u32[]{:S(2)}, u32[]{:S(2)}) %collective-permute-start.25) | collective-permute-done | bytes 262176 | tf_op jit(solution)/shard_map/ppermute | solution.py:14
  59.8 18.4 %collective-permute-done.8 = f32[128,128]{1,0:T(8,128)S(1)} collective-permute-done((f32[128,128]{1,0:T(8,128)S(1)}, f32[128,128]{1,0:T(8,128)S(1)}, u32[]{:S(2)}, u32[]{:S(2)}) %collective-permute-start.8) | collective-permute-done | bytes 65568 | tf_op jit(solution)/shard_map/ppermute | solution.py:14
  78.3 2.9 %collective-permute-start.10 = (bf16[128,128]{1,0:T(8,128)(2,1)S(1)}, bf16[128,128]{1,0:T(8,128)(2,1)S(1)}, u32[]{:S(2)}, u32[]{:S(2)}) collective-permute-start(bf16[128,128]{1,0:T(8,128)(2,1)S(1)} %add_convert_fusion.3.refs_0_), channel_id=1, source_target_pairs={{0,4},{1,5},{2,6},{3,7},{4,0},{5,1},{6,2},{7,3},{8,12},{9,13},{10,... | collective-permute-start | bytes 98312 | tf_op jit(solution)/shard_map/ppermute | solution.py:14
  81.2 1.0 collective-permute-done.9.refs_1_
  82.2 2.3 %collective-permute-start.11 = (bf16[128,128]{1,0:T(8,128)(2,1)S(1)}, bf16[128,128]{1,0:T(8,128)(2,1)S(1)}, u32[]{:S(2)}, u32[]{:S(2)}) collective-permute-start(bf16[128,128]{1,0:T(8,128)(2,1)S(1)} %add_convert_fusion.3.refs_0_), channel_id=1, source_target_pairs={{0,6},{1,7},{2,4},{3,5},{4,2},{5,3},{6,0},{7,1},{8,14},{9,15},{10,... | collective-permute-start | bytes 98312 | tf_op jit(solution)/shard_map/ppermute | solution.py:14
  84.5 3.4 %collective-permute-done.11.refs_3_ = bf16[128,128]{1,0:T(8,128)(2,1)S(1)} collective-permute-done((bf16[128,128]{1,0:T(8,128)(2,1)S(1)}, bf16[128,128]{1,0:T(8,128)(2,1)S(1)}, u32[]{:S(2)}, u32[]{:S(2)}) %collective-permute-start.11) | collective-permute-done | bytes 32800 | tf_op jit(solution)/shard_map/ppermute | solution.py:14
  87.9 1.1 shard_map.93
  89.0 2.4 %collective-permute-start.17 = (bf16[32,1024]{1,0:T(8,128)(2,1)S(1)}, bf16[32,1024]{1,0:T(8,128)(2,1)S(1)}, u32[]{:S(2)}, u32[]{:S(2)}) collective-permute-start(bf16[32,1024]{1,0:T(8,128)(2,1)S(1)} %get-tuple-element.36), channel_id=1, source_target_pairs={{0,6},{1,7},{2,4},{3,5},{4,2},{5,3},{6,0},{7,1},{8,14},{9,15},{10,... | collective-permute-start | bytes 196616 | tf_op jit(solution)/shard_map/ppermute | solution.py:14
  91.4 3.7 %collective-permute-done.17 = bf16[32,1024]{1,0:T(8,128)(2,1)S(1)} collective-permute-done((bf16[32,1024]{1,0:T(8,128)(2,1)S(1)}, bf16[32,1024]{1,0:T(8,128)(2,1)S(1)}, u32[]{:S(2)}, u32[]{:S(2)}) %collective-permute-start.17) | collective-permute-done | bytes 65568 | tf_op jit(solution)/shard_map/ppermute | solution.py:14
  95.8 1.5 collective-permute-start.32
  97.5 2.0 %collective-permute-done.15 = bf16[32,1024]{1,0:T(8,128)(2,1)S(1)} collective-permute-done((bf16[32,1024]{1,0:T(8,128)(2,1)S(1)}, bf16[32,1024]{1,0:T(8,128)(2,1)S(1)}, u32[]{:S(2)}, u32[]{:S(2)}) %collective-permute-start.15) | collective-permute-done | bytes 65568 | tf_op jit(solution)/shard_map/ppermute | solution.py:14
  100.5 1.6 collective-permute-start.20
  102.0 16.4 %collective-permute-done.20 = bf16[32,1024]{1,0:T(8,128)(2,1)S(1)} collective-permute-done((bf16[32,1024]{1,0:T(8,128)(2,1)S(1)}, bf16[32,1024]{1,0:T(8,128)(2,1)S(1)}, u32[]{:S(2)}, u32[]{:S(2)}) %collective-permute-start.20) | collective-permute-done | bytes 65568 | tf_op jit(solution)/shard_map/ppermute | solution.py:14
  118.9 1.5 collective-permute-start.18
  120.5 2.2 %collective-permute-done.19 = bf16[32,1024]{1,0:T(8,128)(2,1)S(1)} collective-permute-done((bf16[32,1024]{1,0:T(8,128)(2,1)S(1)}, bf16[32,1024]{1,0:T(8,128)(2,1)S(1)}, u32[]{:S(2)}, u32[]{:S(2)}) %collective-permute-start.19) | collective-permute-done | bytes 65568 | tf_op jit(solution)/shard_map/ppermute | solution.py:14
  123.3 1.8 %collective-permute-start.21 = (bf16[32,1024]{1,0:T(8,128)(2,1)S(1)}, bf16[32,1024]{1,0:T(8,128)(2,1)S(1)}, u32[]{:S(2)}, u32[]{:S(2)}) collective-permute-start(bf16[32,1024]{1,0:T(8,128)(2,1)S(1)} %add_convert_fusion.2.refs_0_), channel_id=1, source_target_pairs={{0,2},{1,3},{2,0},{3,1},{4,6},{5,7},{6,4},{7,5},{8,10},{9,11},{10,... | collective-permute-start | bytes 196616 | tf_op jit(solution)/shard_map/ppermute | solution.py:14
  125.1 1.4 collective-permute-start.22
  126.5 1.3 collective-permute-done.21.refs_1_
  127.8 2.2 %collective-permute-start.23 = (bf16[32,1024]{1,0:T(8,128)(2,1)S(1)}, bf16[32,1024]{1,0:T(8,128)(2,1)S(1)}, u32[]{:S(2)}, u32[]{:S(2)}) collective-permute-start(bf16[32,1024]{1,0:T(8,128)(2,1)S(1)} %add_convert_fusion.2.refs_0_), channel_id=1, source_target_pairs={{0,6},{1,7},{2,4},{3,5},{4,2},{5,3},{6,0},{7,1},{8,14},{9,15},{10,... | collective-permute-start | bytes 196616 | tf_op jit(solution)/shard_map/ppermute | solution.py:14
  130.1 2.6 %shard_map.95 = (f32[256,512]{1,0:T(8,128)S(1)}, bf16[256,512]{1,0:T(8,128)(2,1)S(1)}, bf16[256,512]{1,0:T(8,128)(2,1)S(1)}, bf16[256,512]{1,0:T(8,128)(2,1)S(1)}) custom-call(s32[22]{0:T(128)S(1)} %pad_add_fusion.meta, bf16[4,256,512]{2,1,0:T(8,128)(2,1)S(1)} %bitcast.37, bf16[4,4,512,512]{3,2,1,0:T(8,128)(2,1)S(1)} %bitcast.25, ...), custom_call_target="tpu_custom_call" | custom-call | bytes 8650752 | tf_op jit(solution)/shard_map/pallas_call | solution.py:119
  132.7 1.6 collective-permute-start.33
  134.2 1.5 collective-permute-start.34
  135.8 1.2 collective-permute-start.35
  136.9 1.1 shard_map.94.x23
  138.2 3.8 %collective-permute-done.33.refs_3_ = bf16[256,512]{1,0:T(8,128)(2,1)S(1)} collective-permute-done((bf16[256,512]{1,0:T(8,128)(2,1)S(1)}, bf16[256,512]{1,0:T(8,128)(2,1)S(1)}, u32[]{:S(2)}, u32[]{:S(2)}) %collective-permute-start.33) | collective-permute-done | bytes 262176 | tf_op jit(solution)/shard_map/ppermute | solution.py:14
  142.0 5.2 %collective-permute-done.34.refs_4_ = bf16[256,512]{1,0:T(8,128)(2,1)S(1)} collective-permute-done((bf16[256,512]{1,0:T(8,128)(2,1)S(1)}, bf16[256,512]{1,0:T(8,128)(2,1)S(1)}, u32[]{:S(2)}, u32[]{:S(2)}) %collective-permute-start.34) | collective-permute-done | bytes 262176 | tf_op jit(solution)/shard_map/ppermute | solution.py:14
  147.2 1.2 shard_map.99
  148.4 2.0 %shard_map.100 = (bf16[4,256,512]{2,1,0:T(8,128)(2,1)}, bf16[4,256,512]{2,1,0:T(8,128)(2,1)S(1)}) custom-call(s32[22]{0:T(128)S(1)} %pad_add_fusion.meta, bf16[128,512]{1,0:T(8,128)(2,1)S(1)} %get-tuple-element.28.refs_5_.x0, bf16[128,512]{1,0:T(8,128)(2,1)S(1)} %get-tuple-element.32.x1, bf16[128,512]{1,0:T(8,128)(2,1)S(1)} %collective-permute-done.13.x0_other, ...), custom_call_target="tpu_custom_call" | custom-call | bytes 4718592 | tf_op jit(solution)/shard_map/pallas_call | solution.py:119
  150.4 15.3 %all_to_all.5 = bf16[4,256,512]{2,1,0:T(8,128)(2,1)S(1)} all-to-all(bf16[4,256,512]{2,1,0:T(8,128)(2,1)S(1)} %get-tuple-element.45), channel_id=1, replica_groups=mesh['leaf'=4,'row'=8] {'leaf'}, dimensions={0} | all-to-all | bytes 2097152 | tf_op jit(solution)/shard_map/all_to_all | solution.py:418
  (74 shorter events, 12.7 us)
Async XLA Ops:
  3.3 3.4 %copy-start = (bf16[4,1,4,512,512]{4,3,2,1,0:T(8,128)(2,1)S(1)}, bf16[4,1,4,512,512]{4,3,2,1,0:T(8,128)(2,1)}, u32[]{:S(2)}) copy-start(bf16[4,1,4,512,512]{4,3,2,1,0:T(8,128)(2,1)} %param.8) | copy-start | bytes 25165828
  6.7 1.2 copy-start.2
  10.1 28.4 %collective-permute-start.12 = (bf16[2560,512]{1,0:T(8,128)(2,1)}, bf16[2560,512]{1,0:T(8,128)(2,1)S(1)}, u32[]{:S(2)}, u32[]{:S(2)}) collective-permute-start(bf16[2560,512]{1,0:T(8,128)(2,1)} %shard_map.91), channel_id=1, source_target_pairs={{0,1},{1,0},{2,3},{3,2},{4,5},{5,4},{6,7},{7,6},{8,9},{9,8},{10,11... | collective-permute-start | bytes 7864328 | tf_op jit(solution)/shard_map/ppermute | solution.py:14
  10.6 8.9 %copy-start.1 = (bf16[4,1,4,512,512]{4,3,2,1,0:T(8,128)(2,1)S(1)}, bf16[4,1,4,512,512]{4,3,2,1,0:T(8,128)(2,1)}, u32[]{:S(2)}) copy-start(bf16[4,1,4,512,512]{4,3,2,1,0:T(8,128)(2,1)} %param.8) | copy-start | bytes 25165828
  11.2 8.3 %collective-permute-start.3 = (bf16[384,512]{1,0:T(8,128)(2,1)S(1)}, bf16[384,512]{1,0:T(8,128)(2,1)S(1)}, u32[]{:S(2)}, u32[]{:S(2)}) collective-permute-start(bf16[384,512]{1,0:T(8,128)(2,1)S(1)} %shard_map.88), channel_id=1, source_target_pairs={{0,1},{1,0},{2,3},{3,2},{4,5},{5,4},{6,7},{7,6},{8,9},{9,8},{10,11... | collective-permute-start | bytes 1179656 | tf_op jit(solution)/shard_map/ppermute | solution.py:14
  11.9 4.0 %collective-permute-start = (bf16[128,512]{1,0:T(8,128)(2,1)S(1)}, bf16[128,512]{1,0:T(8,128)(2,1)S(1)}, u32[]{:S(2)}, u32[]{:S(2)}) collective-permute-start(bf16[128,512]{1,0:T(8,128)(2,1)S(1)} %shard_map.86), channel_id=1, source_target_pairs={{0,1},{1,0},{2,3},{3,2},{4,5},{5,4},{6,7},{7,6},{8,9},{9,8},{10,11... | collective-permute-start | bytes 393224 | tf_op jit(solution)/shard_map/ppermute | solution.py:14
  16.4 21.1 %copy-start.8 = (bf16[1,512,512]{2,1,0:T(8,128)(2,1)S(1)}, bf16[1,512,512]{2,1,0:T(8,128)(2,1)}, u32[]{:S(2)}) copy-start(bf16[1,512,512]{2,1,0:T(8,128)(2,1)} %diag.1) | copy-start | bytes 1572868
  16.5 8.2 %collective-permute-start.1 = (bf16[128,512]{1,0:T(8,128)(2,1)S(1)}, bf16[128,512]{1,0:T(8,128)(2,1)S(1)}, u32[]{:S(2)}, u32[]{:S(2)}) collective-permute-start(bf16[128,512]{1,0:T(8,128)(2,1)S(1)} %shard_map.87), channel_id=1, source_target_pairs={{0,2},{1,3},{2,0},{3,1},{4,6},{5,7},{6,4},{7,5},{8,10},{9,11},{10,... | collective-permute-start | bytes 393224 | tf_op jit(solution)/shard_map/ppermute | solution.py:14
  20.2 19.8 %copy-start.3 = (bf16[1,4,256,512]{3,2,1,0:T(8,128)(2,1)S(1)}, bf16[1,4,256,512]{3,2,1,0:T(8,128)(2,1)}, u32[]{:S(2)}) copy-start(bf16[1,4,256,512]{3,2,1,0:T(8,128)(2,1)} %param.7) | copy-start | bytes 3145732
  20.2 8.3 %collective-permute-start.6 = (bf16[384,128]{1,0:T(8,128)(2,1)S(1)}, bf16[384,128]{1,0:T(8,128)(2,1)S(1)}, u32[]{:S(2)}, u32[]{:S(2)}) collective-permute-start(bf16[384,128]{1,0:T(8,128)(2,1)S(1)} %get-tuple-element.27), channel_id=1, source_target_pairs={{0,6},{1,7},{2,4},{3,5},{4,2},{5,3},{6,0},{7,1},{8,14},{9,15},{10,... | collective-permute-start | bytes 294920 | tf_op jit(solution)/shard_map/ppermute | solution.py:14
  22.7 12.4 %collective-permute-start.5 = (bf16[384,128]{1,0:T(8,128)(2,1)S(1)}, bf16[384,128]{1,0:T(8,128)(2,1)S(1)}, u32[]{:S(2)}, u32[]{:S(2)}) collective-permute-start(bf16[384,128]{1,0:T(8,128)(2,1)S(1)} %get-tuple-element.26), channel_id=1, source_target_pairs={{0,4},{1,5},{2,6},{3,7},{4,0},{5,1},{6,2},{7,3},{8,12},{9,13},{10,... | collective-permute-start | bytes 294920 | tf_op jit(solution)/shard_map/ppermute | solution.py:14
  22.9 12.2 %collective-permute-start.4 = (bf16[384,128]{1,0:T(8,128)(2,1)S(1)}, bf16[384,128]{1,0:T(8,128)(2,1)S(1)}, u32[]{:S(2)}, u32[]{:S(2)}) collective-permute-start(bf16[384,128]{1,0:T(8,128)(2,1)S(1)} %get-tuple-element.25), channel_id=1, source_target_pairs={{0,2},{1,3},{2,0},{3,1},{4,6},{5,7},{6,4},{7,5},{8,10},{9,11},{10,... | collective-permute-start | bytes 294920 | tf_op jit(solution)/shard_map/ppermute | solution.py:14
  24.7 12.9 %collective-permute-start.2 = (bf16[128,512]{1,0:T(8,128)(2,1)S(1)}, bf16[128,512]{1,0:T(8,128)(2,1)S(1)}, u32[]{:S(2)}, u32[]{:S(2)}) collective-permute-start(bf16[128,512]{1,0:T(8,128)(2,1)S(1)} %add.45.near), channel_id=1, source_target_pairs={{0,4},{1,5},{2,6},{3,7},{4,0},{5,1},{6,2},{7,3},{8,12},{9,13},{10,... | collective-permute-start | bytes 393224 | tf_op jit(solution)/shard_map/ppermute | solution.py:14
  35.2 2.4 %collective-permute-start.7 = (bf16[256,128]{1,0:T(8,128)(2,1)S(1)}, bf16[256,128]{1,0:T(8,128)(2,1)S(1)}, u32[]{:S(2)}, u32[]{:S(2)}) collective-permute-start(bf16[256,128]{1,0:T(8,128)(2,1)S(1)} %slice.8.p), channel_id=1, source_target_pairs={{0,1},{1,0},{2,3},{3,2},{4,5},{5,4},{6,7},{7,6},{8,9},{9,8},{10,11... | collective-permute-start | bytes 196616 | tf_op jit(solution)/shard_map/ppermute | solution.py:14
  38.5 1.5 copy-start.4
  40.0 1.7 %copy-start.5 = (bf16[2560,512]{1,0:T(8,128)(2,1)S(1)}, bf16[2560,512]{1,0:T(8,128)(2,1)}, u32[]{:S(2)}) copy-start(bf16[2560,512]{1,0:T(8,128)(2,1)} %copy-done.4) | copy-start | bytes 7864324
  42.8 8.0 %collective-permute-start.24 = (bf16[256,512]{1,0:T(8,128)(2,1)S(1)}, bf16[256,512]{1,0:T(8,128)(2,1)S(1)}, u32[]{:S(2)}, u32[]{:S(2)}) collective-permute-start(bf16[256,512]{1,0:T(8,128)(2,1)S(1)} %get-tuple-element.37), channel_id=1, source_target_pairs={{0,8},{8,0},{16,24},{24,16},{1,9},{9,1},{17,25},{25,17},{2,10},{10... | collective-permute-start | bytes 786440 | tf_op jit(solution)/shard_map/ppermute | solution.py:14
  50.9 8.8 %collective-permute-start.25 = (bf16[256,512]{1,0:T(8,128)(2,1)S(1)}, bf16[256,512]{1,0:T(8,128)(2,1)S(1)}, u32[]{:S(2)}, u32[]{:S(2)}) collective-permute-start(bf16[256,512]{1,0:T(8,128)(2,1)S(1)} %add_convert_fusion.1), channel_id=1, source_target_pairs={{0,16},{8,24},{16,0},{24,8},{1,17},{9,25},{17,1},{25,9},{2,18},{10... | collective-permute-start | bytes 786440 | tf_op jit(solution)/shard_map/ppermute | solution.py:14
  53.1 34.8 %copy-start.7 = (bf16[2,512,512]{2,1,0:T(8,128)(2,1)S(1)}, bf16[2,512,512]{2,1,0:T(8,128)(2,1)}, u32[]{:S(2)}) copy-start(bf16[2,512,512]{2,1,0:T(8,128)(2,1)} %refs_4_.2) | copy-start | bytes 3145732
  53.1 70.2 %collective-permute-start.30 = (bf16[2,512,512]{2,1,0:T(8,128)(2,1)S(1)}, bf16[2,512,512]{2,1,0:T(8,128)(2,1)S(1)}, u32[]{:S(2)}, u32[]{:S(2)}) collective-permute-start(bf16[2,512,512]{2,1,0:T(8,128)(2,1)S(1)} %shard_map.96), channel_id=1, source_target_pairs={{0,8},{8,0},{16,24},{24,16},{1,9},{9,1},{17,25},{25,17},{2,10},{10... | collective-permute-start | bytes 3145736 | tf_op jit(solution)/shard_map/ppermute | solution.py:14
  55.3 82.8 %collective-permute-start.31 = (bf16[2,512,512]{2,1,0:T(8,128)(2,1)S(1)}, bf16[2,512,512]{2,1,0:T(8,128)(2,1)S(1)}, u32[]{:S(2)}, u32[]{:S(2)}) collective-permute-start(bf16[2,512,512]{2,1,0:T(8,128)(2,1)S(1)} %shard_map.97), channel_id=1, source_target_pairs={{0,16},{8,24},{16,0},{24,8},{1,17},{9,25},{17,1},{25,9},{2,18},{10... | collective-permute-start | bytes 3145736 | tf_op jit(solution)/shard_map/ppermute | solution.py:14
  55.8 22.4 %collective-permute-start.8 = (f32[128,128]{1,0:T(8,128)S(1)}, f32[128,128]{1,0:T(8,128)S(1)}, u32[]{:S(2)}, u32[]{:S(2)}) collective-permute-start(f32[128,128]{1,0:T(8,128)S(1)} %get-tuple-element.29), channel_id=1, source_target_pairs={{0,8},{8,0},{16,24},{24,16},{1,9},{9,1},{17,25},{25,17},{2,10},{10... | collective-permute-start | bytes 196616 | tf_op jit(solution)/shard_map/ppermute | solution.py:14
  59.8 36.0 %collective-permute-start.26 = (bf16[256,512]{1,0:T(8,128)(2,1)S(1)}, bf16[256,512]{1,0:T(8,128)(2,1)S(1)}, u32[]{:S(2)}, u32[]{:S(2)}) collective-permute-start(bf16[256,512]{1,0:T(8,128)(2,1)S(1)} %add_convert_fusion), channel_id=1, source_target_pairs={{0,2},{1,3},{2,0},{3,1},{4,6},{5,7},{6,4},{7,5},{8,10},{9,11},{10,... | collective-permute-start | bytes 786440 | tf_op jit(solution)/shard_map/ppermute | solution.py:14
  78.2 4.0 %collective-permute-start.9 = (bf16[128,128]{1,0:T(8,128)(2,1)S(1)}, bf16[128,128]{1,0:T(8,128)(2,1)S(1)}, u32[]{:S(2)}, u32[]{:S(2)}) collective-permute-start(bf16[128,128]{1,0:T(8,128)(2,1)S(1)} %add_convert_fusion.3.refs_0_), channel_id=1, source_target_pairs={{0,2},{1,3},{2,0},{3,1},{4,6},{5,7},{6,4},{7,5},{8,10},{9,11},{10,... | collective-permute-start | bytes 98312 | tf_op jit(solution)/shard_map/ppermute | solution.py:14
  78.3 6.2 %collective-permute-start.10 = (bf16[128,128]{1,0:T(8,128)(2,1)S(1)}, bf16[128,128]{1,0:T(8,128)(2,1)S(1)}, u32[]{:S(2)}, u32[]{:S(2)}) collective-permute-start(bf16[128,128]{1,0:T(8,128)(2,1)S(1)} %add_convert_fusion.3.refs_0_), channel_id=1, source_target_pairs={{0,4},{1,5},{2,6},{3,7},{4,0},{5,1},{6,2},{7,3},{8,12},{9,13},{10,... | collective-permute-start | bytes 98312 | tf_op jit(solution)/shard_map/ppermute | solution.py:14
  82.2 5.7 %collective-permute-start.11 = (bf16[128,128]{1,0:T(8,128)(2,1)S(1)}, bf16[128,128]{1,0:T(8,128)(2,1)S(1)}, u32[]{:S(2)}, u32[]{:S(2)}) collective-permute-start(bf16[128,128]{1,0:T(8,128)(2,1)S(1)} %add_convert_fusion.3.refs_0_), channel_id=1, source_target_pairs={{0,6},{1,7},{2,4},{3,5},{4,2},{5,3},{6,0},{7,1},{8,14},{9,15},{10,... | collective-permute-start | bytes 98312 | tf_op jit(solution)/shard_map/ppermute | solution.py:14
  89.0 6.1 %collective-permute-start.17 = (bf16[32,1024]{1,0:T(8,128)(2,1)S(1)}, bf16[32,1024]{1,0:T(8,128)(2,1)S(1)}, u32[]{:S(2)}, u32[]{:S(2)}) collective-permute-start(bf16[32,1024]{1,0:T(8,128)(2,1)S(1)} %get-tuple-element.36), channel_id=1, source_target_pairs={{0,6},{1,7},{2,4},{3,5},{4,2},{5,3},{6,0},{7,1},{8,14},{9,15},{10,... | collective-permute-start | bytes 196616 | tf_op jit(solution)/shard_map/ppermute | solution.py:14
  91.4 5.9 %collective-permute-start.16 = (bf16[32,1024]{1,0:T(8,128)(2,1)S(1)}, bf16[32,1024]{1,0:T(8,128)(2,1)S(1)}, u32[]{:S(2)}, u32[]{:S(2)}) collective-permute-start(bf16[32,1024]{1,0:T(8,128)(2,1)S(1)} %get-tuple-element.35), channel_id=1, source_target_pairs={{0,4},{1,5},{2,6},{3,7},{4,0},{5,1},{6,2},{7,3},{8,12},{9,13},{10,... | collective-permute-start | bytes 196616 | tf_op jit(solution)/shard_map/ppermute | solution.py:14
  95.2 4.3 %collective-permute-start.15 = (bf16[32,1024]{1,0:T(8,128)(2,1)S(1)}, bf16[32,1024]{1,0:T(8,128)(2,1)S(1)}, u32[]{:S(2)}, u32[]{:S(2)}) collective-permute-start(bf16[32,1024]{1,0:T(8,128)(2,1)S(1)} %get-tuple-element.34), channel_id=1, source_target_pairs={{0,2},{1,3},{2,0},{3,1},{4,6},{5,7},{6,4},{7,5},{8,10},{9,11},{10,... | collective-permute-start | bytes 196616 | tf_op jit(solution)/shard_map/ppermute | solution.py:14
  95.8 42.4 %collective-permute-start.32 = (bf16[2,512,512]{2,1,0:T(8,128)(2,1)S(1)}, bf16[2,512,512]{2,1,0:T(8,128)(2,1)S(1)}, u32[]{:S(2)}, u32[]{:S(2)}) collective-permute-start(bf16[2,512,512]{2,1,0:T(8,128)(2,1)S(1)} %shard_map.98), channel_id=1, source_target_pairs={{0,24},{8,16},{16,8},{24,0},{1,25},{9,17},{17,9},{25,1},{2,26},{10... | collective-permute-start | bytes 3145736 | tf_op jit(solution)/shard_map/ppermute | solution.py:14
  97.4 3.1 %collective-permute-start.13 = (bf16[128,512]{1,0:T(8,128)(2,1)S(1)}, bf16[128,512]{1,0:T(8,128)(2,1)S(1)}, u32[]{:S(2)}, u32[]{:S(2)}) collective-permute-start(bf16[128,512]{1,0:T(8,128)(2,1)S(1)} %get-tuple-element.28.refs_5_.x0), channel_id=1, source_target_pairs={{0,1},{1,0},{2,3},{3,2},{4,5},{5,4},{6,7},{7,6},{8,9},{9,8},{10,11... | collective-permute-start | bytes 393224 | tf_op jit(solution)/shard_map/ppermute | solution.py:14
  99.4 19.5 %collective-permute-start.27 = (bf16[256,512]{1,0:T(8,128)(2,1)S(1)}, bf16[256,512]{1,0:T(8,128)(2,1)S(1)}, u32[]{:S(2)}, u32[]{:S(2)}) collective-permute-start(bf16[256,512]{1,0:T(8,128)(2,1)S(1)} %add.58), channel_id=1, source_target_pairs={{0,4},{1,5},{2,6},{3,7},{4,0},{5,1},{6,2},{7,3},{8,12},{9,13},{10,... | collective-permute-start | bytes 786440 | tf_op jit(solution)/shard_map/ppermute | solution.py:14
  100.5 18.0 %collective-permute-start.20 = (bf16[32,1024]{1,0:T(8,128)(2,1)S(1)}, bf16[32,1024]{1,0:T(8,128)(2,1)S(1)}, u32[]{:S(2)}, u32[]{:S(2)}) collective-permute-start(bf16[32,1024]{1,0:T(8,128)(2,1)S(1)} %add_add_fusion.1), channel_id=1, source_target_pairs={{0,24},{8,16},{16,8},{24,0},{1,25},{9,17},{17,9},{25,1},{2,26},{10... | collective-permute-start | bytes 196616 | tf_op jit(solution)/shard_map/ppermute | solution.py:14
  118.5 4.3 %collective-permute-start.19 = (bf16[32,1024]{1,0:T(8,128)(2,1)S(1)}, bf16[32,1024]{1,0:T(8,128)(2,1)S(1)}, u32[]{:S(2)}, u32[]{:S(2)}) collective-permute-start(bf16[32,1024]{1,0:T(8,128)(2,1)S(1)} %add_add_fusion.1), channel_id=1, source_target_pairs={{0,16},{8,24},{16,0},{24,8},{1,17},{9,25},{17,1},{25,9},{2,18},{10... | collective-permute-start | bytes 196616 | tf_op jit(solution)/shard_map/ppermute | solution.py:14
  118.9 4.3 %collective-permute-start.18 = (bf16[32,1024]{1,0:T(8,128)(2,1)S(1)}, bf16[32,1024]{1,0:T(8,128)(2,1)S(1)}, u32[]{:S(2)}, u32[]{:S(2)}) collective-permute-start(bf16[32,1024]{1,0:T(8,128)(2,1)S(1)} %add_add_fusion.1), channel_id=1, source_target_pairs={{0,8},{8,0},{16,24},{24,16},{1,9},{9,1},{17,25},{25,17},{2,10},{10... | collective-permute-start | bytes 196616 | tf_op jit(solution)/shard_map/ppermute | solution.py:14
  122.7 2.4 %collective-permute-start.14 = (bf16[128,512]{1,0:T(8,128)(2,1)S(1)}, bf16[128,512]{1,0:T(8,128)(2,1)S(1)}, u32[]{:S(2)}, u32[]{:S(2)}) collective-permute-start(bf16[128,512]{1,0:T(8,128)(2,1)S(1)} %get-tuple-element.32.x1), channel_id=1, source_target_pairs={{0,1},{1,0},{2,3},{3,2},{4,5},{5,4},{6,7},{7,6},{8,9},{9,8},{10,11... | collective-permute-start | bytes 393224 | tf_op jit(solution)/shard_map/ppermute | solution.py:14
  123.2 12.6 %collective-permute-start.28 = (bf16[256,512]{1,0:T(8,128)(2,1)S(1)}, bf16[256,512]{1,0:T(8,128)(2,1)S(1)}, u32[]{:S(2)}, u32[]{:S(2)}) collective-permute-start(bf16[256,512]{1,0:T(8,128)(2,1)S(1)} %add.59.refs_5_), channel_id=1, source_target_pairs={{0,1},{1,0},{2,3},{3,2},{4,5},{5,4},{6,7},{7,6},{8,9},{9,8},{10,11... | collective-permute-start | bytes 786440 | tf_op jit(solution)/shard_map/ppermute | solution.py:14
  123.3 13.7 %copy-start.6 = (bf16[2,512,512]{2,1,0:T(8,128)(2,1)S(1)}, bf16[2,512,512]{2,1,0:T(8,128)(2,1)}, u32[]{:S(2)}) copy-start(bf16[2,512,512]{2,1,0:T(8,128)(2,1)} %refs_4_.3) | copy-start | bytes 3145732
  123.3 4.5 %collective-permute-start.21 = (bf16[32,1024]{1,0:T(8,128)(2,1)S(1)}, bf16[32,1024]{1,0:T(8,128)(2,1)S(1)}, u32[]{:S(2)}, u32[]{:S(2)}) collective-permute-start(bf16[32,1024]{1,0:T(8,128)(2,1)S(1)} %add_convert_fusion.2.refs_0_), channel_id=1, source_target_pairs={{0,2},{1,3},{2,0},{3,1},{4,6},{5,7},{6,4},{7,5},{8,10},{9,11},{10,... | collective-permute-start | bytes 196616 | tf_op jit(solution)/shard_map/ppermute | solution.py:14
  125.1 7.6 %collective-permute-start.22 = (bf16[32,1024]{1,0:T(8,128)(2,1)S(1)}, bf16[32,1024]{1,0:T(8,128)(2,1)S(1)}, u32[]{:S(2)}, u32[]{:S(2)}) collective-permute-start(bf16[32,1024]{1,0:T(8,128)(2,1)S(1)} %add_convert_fusion.2.refs_0_), channel_id=1, source_target_pairs={{0,4},{1,5},{2,6},{3,7},{4,0},{5,1},{6,2},{7,3},{8,12},{9,13},{10,... | collective-permute-start | bytes 196616 | tf_op jit(solution)/shard_map/ppermute | solution.py:14
  127.8 6.4 %collective-permute-start.23 = (bf16[32,1024]{1,0:T(8,128)(2,1)S(1)}, bf16[32,1024]{1,0:T(8,128)(2,1)S(1)}, u32[]{:S(2)}, u32[]{:S(2)}) collective-permute-start(bf16[32,1024]{1,0:T(8,128)(2,1)S(1)} %add_convert_fusion.2.refs_0_), channel_id=1, source_target_pairs={{0,6},{1,7},{2,4},{3,5},{4,2},{5,3},{6,0},{7,1},{8,14},{9,15},{10,... | collective-permute-start | bytes 196616 | tf_op jit(solution)/shard_map/ppermute | solution.py:14
  132.7 9.3 %collective-permute-start.33 = (bf16[256,512]{1,0:T(8,128)(2,1)S(1)}, bf16[256,512]{1,0:T(8,128)(2,1)S(1)}, u32[]{:S(2)}, u32[]{:S(2)}) collective-permute-start(bf16[256,512]{1,0:T(8,128)(2,1)S(1)} %get-tuple-element.39), channel_id=1, source_target_pairs={{0,8},{8,0},{16,24},{24,16},{1,9},{9,1},{17,25},{25,17},{2,10},{10... | collective-permute-start | bytes 786440 | tf_op jit(solution)/shard_map/ppermute | solution.py:14
  134.2 13.0 %collective-permute-start.34 = (bf16[256,512]{1,0:T(8,128)(2,1)S(1)}, bf16[256,512]{1,0:T(8,128)(2,1)S(1)}, u32[]{:S(2)}, u32[]{:S(2)}) collective-permute-start(bf16[256,512]{1,0:T(8,128)(2,1)S(1)} %get-tuple-element.40), channel_id=1, source_target_pairs={{0,16},{8,24},{16,0},{24,8},{1,17},{9,25},{17,1},{25,9},{2,18},{10... | collective-permute-start | bytes 786440 | tf_op jit(solution)/shard_map/ppermute | solution.py:14
  135.8 11.4 %collective-permute-start.35 = (bf16[256,512]{1,0:T(8,128)(2,1)S(1)}, bf16[256,512]{1,0:T(8,128)(2,1)S(1)}, u32[]{:S(2)}, u32[]{:S(2)}) collective-permute-start(bf16[256,512]{1,0:T(8,128)(2,1)S(1)} %get-tuple-element.41), channel_id=1, source_target_pairs={{0,24},{8,16},{16,8},{24,0},{1,25},{9,17},{17,9},{25,1},{2,26},{10... | collective-permute-start | bytes 786440 | tf_op jit(solution)/shard_map/ppermute | solution.py:14
  138.1 10.3 %collective-permute-start.29 = (bf16[2,128,512]{2,1,0:T(8,128)(2,1)S(1)}, bf16[2,128,512]{2,1,0:T(8,128)(2,1)S(1)}, u32[]{:S(2)}, u32[]{:S(2)}) collective-permute-start(bf16[2,128,512]{2,1,0:T(8,128)(2,1)S(1)} %shard_map.94.x23), channel_id=1, source_target_pairs={{0,1},{1,0},{2,3},{3,2},{4,5},{5,4},{6,7},{7,6},{8,9},{9,8},{10,11... | collective-permute-start | bytes 786440 | tf_op jit(solution)/shard_map/ppermute | solution.py:14

commit v3 on v2

v3 whole, which is shorter than its diff:
```python
import jax
import jax.numpy as jnp
from jax import lax
from jax.experimental import pallas as pl
from jax.experimental.pallas import tpu as pltpu
from jax.sharding import PartitionSpec as P

F32 = jnp.float32
BF16 = jnp.bfloat16
CORES = 2


def swap(block, axis, bits):
    return lax.ppermute(block, axis, [(i, i ^ bits) for i in range(lax.axis_size(axis))])


def dot(a, b):
    return jnp.dot(a, b, preferred_element_type=F32)


def shaped(shape, dtype=BF16):
    return jax.ShapeDtypeStruct(tuple(shape), dtype)


class Picked:
    def __init__(self, array, block, index):
        self.array, self.block, self.index = array, block, index


def on_device(right_side, panels, tile_counts, diag_leaf, diag_pair, diag_root, sup_rows):
    right, panels, counts = right_side[0], panels[:, 0], tile_counts[:, 0]
    levels, here, width, _ = panels.shape
    n_row, n_leaf = lax.axis_size("row"), lax.axis_size("leaf")
    chips = min(n_row // CORES, 4)
    outer = [1 << b for b in range(n_row.bit_length()) if CORES * chips <= 1 << b < n_row]
    height = right.shape[1]
    half_r, half_w = height // CORES, width // CORES
    part_r, part_w = half_r // chips, width // chips

    meta = jnp.concatenate(
        [
            jnp.stack([lax.axis_index("leaf"), lax.axis_index("row")]).astype(jnp.int32),
            sup_rows,
            counts.reshape(-1),
        ]
    )

    def leaf_of(meta):
        return meta[0]

    def core_of(meta):
        return meta[1] & (CORES - 1)

    def chip_of(meta):
        return (meta[1] // CORES) & (chips - 1)

    def spot(meta, level):
        return lax.rem(meta[2 + level], here)

    def owns(meta, level):
        return lax.div(meta[2 + level], here) == meta[1]

    def live(meta, level, a):
        kept = meta[2 + levels + level * here + a]
        for m in range(level + 1):
            kept = jnp.where(meta[1] * here + a == meta[2 + m], 0, kept)
        return kept

    def live_owned(meta, of, level):
        return jnp.where(owns(meta, level), live(meta, of, spot(meta, level)), 0)

    def keep(limit):
        ids = lax.broadcasted_iota(jnp.int32, (1, width), 1)
        return (ids < limit).astype(F32).astype(BF16)

    def side(level, other):
        return Picked(
            right,
            (None, half_r, width),
            lambda i, meta: (spot(meta, level), core_of(meta) ^ other, 0),
        )

    def side_value(meta, ref, level):
        return ref[...] * keep(jnp.where(owns(meta, level), width, 0))

    def tile(of, level, other=None):
        if other is None:
            return Picked(
                panels, (None, None, width, width), lambda i, meta: (of, spot(meta, level), 0, 0)
            )
        return Picked(
            panels,
            (None, None, half_w, width),
            lambda i, meta: (of, spot(meta, level), core_of(meta) ^ other, 0),
        )

    def tile_value(meta, ref, of, level):
        return ref[...] * keep(live_owned(meta, of, level))

    def run(body, operands, outs, scratch=(), steps=1, after=(), limit=40):
        arrays, specs, moved = [], [], 0
        for operand in operands:
            if not isinstance(operand, Picked):
                zeros = (0,) * operand.ndim
                operand = Picked(operand, operand.shape, lambda i, meta, zeros=zeros: zeros)
            arrays.append(operand.array)
            specs.append(pl.BlockSpec(operand.block, operand.index))
            size = operand.array.dtype.itemsize
            for n in operand.block:
                size *= n or 1
            moved += size * steps
        taken = len(arrays)
        arrays += after
        specs += [pl.BlockSpec(memory_space=pl.ANY)] * len(after)

        def kernel(meta, *refs):
            body(meta, *refs[:taken], *refs[taken + len(after) :])

        single = not isinstance(outs, (list, tuple))
        listed = [outs] if single else list(outs)
        out_specs = [
            pl.BlockSpec(out.shape, lambda i, meta, zeros=(0,) * len(out.shape): zeros)
            for out in listed
        ]
        moved += sum(out.size * out.dtype.itemsize for out in listed)
        results = pl.pallas_call(
            kernel,
            grid_spec=pltpu.PrefetchScalarGridSpec(
                num_scalar_prefetch=1,
                grid=(steps,),
                in_specs=specs,
                out_specs=out_specs,
                scratch_shapes=list(scratch),
            ),
            out_shape=listed,
            compiler_params=pltpu.CompilerParams(vmem_limit_bytes=limit * 1024 * 1024),
            cost_estimate=pl.CostEstimate(flops=0, bytes_accessed=moved, transcendentals=0),
        )(meta, *arrays)
        return results[0] if single else results

    def spread(block):
        for bits in outer:
            block = block + swap(block, "row", bits)
        return block

    steps_up = [CORES * m for m in range(1, chips)]
    rows_half = shaped((half_r, width))
    lanes = part_w
    blocks = width // lanes

    def at(index, size):
        return pl.ds(pl.multiple_of(index * size, size), size)

    first_rows = 2 * half_r + half_w

    def first_half(meta, out, b0, b1, p01, other):
        core = core_of(meta) ^ other
        out[:half_r] = b0[at(core, half_r)] * keep(jnp.where(owns(meta, 0), width, 0))
        out[half_r : 2 * half_r] = b1[at(core, half_r)] * keep(jnp.where(owns(meta, 1), width, 0))
        out[2 * half_r :] = p01[at(core, half_w)] * keep(live_owned(meta, 0, 1))

    def first_send(meta, b0, b1, p01, out):
        first_half(meta, out, b0, b1, p01, 1)

    def full_side(level):
        return Picked(right, (None, height, width), lambda i, meta: (spot(meta, level), 0, 0))

    first_in = [full_side(0), full_side(1), tile(0, 1)]
    first_got = swap(run(first_send, first_in, shaped((first_rows, width)), limit=60), "row", 1)

    b0_rows, column_rows = blocks * half_r, half_r + half_w
    near, far = (CORES, 2 * CORES)

    def first_split(meta, b0, b1, p01, got, send, kept, whole):
        first_half(meta, whole, b0, b1, p01, 0)
        whole[...] = whole[...] + got[...]
        for i in range(blocks):
            send[i * half_r : (i + 1) * half_r] = whole[:half_r, i * lanes : (i + 1) * lanes]
        kept[:b0_rows] = send[:b0_rows]
        chip = chip_of(meta)
        for i, (mine, other) in enumerate(((0, 1), (2, 3))):
            rows = slice(b0_rows + i * column_rows, b0_rows + (i + 1) * column_rows)
            send[rows] = whole[half_r:, at(chip ^ other, lanes)]
            kept[rows] = whole[half_r:, at(chip ^ mine, lanes)]

    near_shape = shaped((b0_rows + 2 * column_rows, lanes))
    near_send, near_kept = run(
        first_split,
        first_in + [first_got],
        [near_shape, near_shape],
        [pltpu.VMEM((first_rows, width), BF16)],
    )
    near_got = swap(spread(near_send), "row", near)
    near_kept = spread(near_kept)

    def first_join(meta, kept, got, send, own):
        send[:b0_rows] = kept[:b0_rows] + got[:b0_rows]
        middle = b0_rows + column_rows
        own[...] = kept[b0_rows:middle] + got[b0_rows:middle]
        send[b0_rows:] = kept[middle:] + got[middle:]

    far_send, columns_own = run(
        first_join,
        [near_kept, near_got],
        [shaped((b0_rows + column_rows, lanes)), shaped((column_rows, lanes))],
    )
    far_got = swap(far_send, "row", far)

    def panel_of(level, m):
        return Picked(
            panels,
            (None, None, width, width),
            lambda i, meta: (level, leaf_of(meta) ^ m, 0, 0),
        )

    def panel_value(meta, ref, level, m):
        return ref[...] * keep(live(meta, level, leaf_of(meta) ^ m))

    orders = ((2, 1, 2), (3, 2, 1))
    panel_got = []
    for level, one, two in orders:
        def panel_send(meta, pa, pb, out, level=level, one=one, two=two):
            out[0] = panel_value(meta, pa, level, one)
            out[1] = panel_value(meta, pb, level, one ^ two)

        sent = run(
            panel_send,
            [panel_of(level, one), panel_of(level, one ^ two)],
            shaped((2, width, width)),
            after=[near_send],
        )
        panel_got.append(swap(sent, "leaf", one))

    later = [(0, 2), (1, 2), (0, 3), (1, 3)]
    rest_rows = half_w + 2 * half_r + len(later) * width

    def rest_send(meta, p23, b2, b3, *refs):
        tiles, out = refs[:-1], refs[-1]
        out[:half_w] = tile_value(meta, p23, 2, 3)
        out[half_w : half_w + half_r] = side_value(meta, b2, 2)
        out[half_w + half_r : half_w + 2 * half_r] = side_value(meta, b3, 3)
        for i, (of, level) in enumerate(later):
            start = half_w + 2 * half_r + i * width
            out[start : start + width] = tile_value(meta, tiles[i], of, level)

    rest_got = swap(
        run(
            rest_send,
            [tile(2, 3, 1), side(2, 1), side(3, 1)] + [tile(*which) for which in later],
            shaped((rest_rows, width)),
            after=[near_send],
        ),
        "row",
        1,
    )

    def solve0(meta, sent, got, own, diag, x0, p, b):
        x = jnp.zeros((half_r, width), F32)
        for i in range(blocks):
            rows = slice(i * half_r, (i + 1) * half_r)
            x = x + dot(sent[rows] + got[rows], diag[0, i * lanes : (i + 1) * lanes])
        x0[...] = x.astype(BF16)
        b[...] = own[:half_r] + got[b0_rows : b0_rows + half_r]
        p[...] = own[half_r:] + got[b0_rows + half_r :]

    x0, p01, b1 = run(
        solve0,
        [far_send, far_got, columns_own, diag_leaf],
        [rows_half, shaped((half_w, lanes)), shaped((half_r, lanes))],
    )
    p01_other = swap(p01, "row", 1)

    def term1(meta, x0, p, p_other, b, t1, whole):
        core = core_of(meta)
        whole[at(core, half_w)] = p[...]
        whole[at(1 - core, half_w)] = p_other[...]
        t1[...] = b[...].astype(F32) - dot(x0[...], whole[...])

    t1 = run(
        term1,
        [x0, p01, p01_other, b1],
        shaped((half_r, lanes), F32),
        [pltpu.VMEM((width, lanes), BF16)],
    )
    m1 = (t1 + swap(t1, "leaf", 1)).astype(BF16)
    m1_parts = [m1] + [swap(m1, "row", step) for step in steps_up]

    def early(meta, p23, b2, b3, *refs):
        tiles, (got, x0), (p23_send, p23_kept, u, linked, whole) = refs[:4], refs[4:6], refs[6:]
        whole[...] = tile_value(meta, p23, 2, 3) + got[:half_w]
        chip = chip_of(meta)
        for i, (mine, other) in enumerate(((0, 1), (2, 3))):
            rows = slice(i * half_w, (i + 1) * half_w)
            p23_send[rows] = whole[:, at(chip ^ other, lanes)]
            p23_kept[rows] = whole[:, at(chip ^ mine, lanes)]
        for i, b in enumerate((b2, b3)):
            rows = slice(half_w + i * half_r, half_w + (i + 1) * half_r)
            value = (side_value(meta, b, 2 + i) + got[rows]).astype(F32)
            start = half_w + 2 * half_r + 2 * i * width
            p0 = tile_value(meta, tiles[2 * i], 0, 2 + i) + got[start : start + width]
            u[:, i * width : (i + 1) * width] = value - dot(x0[...], p0)
            start += width
            linked[i] = tile_value(meta, tiles[2 * i + 1], 1, 2 + i) + got[start : start + width]

    p23_pair = shaped((2 * half_w, lanes))
    p23_send, p23_kept, u, linked = run(
        early,
        [tile(2, 3, 0), side(2, 0), side(3, 0)]
        + [tile(*which) for which in later]
        + [rest_got, x0],
        [p23_pair, p23_pair, shaped((half_r, 2 * width), F32), shaped((2, width, width))],
        [pltpu.VMEM((half_w, width), BF16)],
        after=[t1],
    )

    p23_near = swap(spread(p23_send), "row", near)

    def p23_join(meta, kept, got, send, own):
        own[...] = kept[:half_w] + got[:half_w]
        send[...] = kept[half_w:] + got[half_w:]

    p23_block = shaped((half_w, lanes))
    p23_send, p23_own = run(p23_join, [spread(p23_kept), p23_near], [p23_block, p23_block])
    p23 = p23_own + swap(p23_send, "row", far)
    bits = 1
    while bits < n_leaf:
        p23 = (p23.astype(F32) + swap(p23, "leaf", bits).astype(F32)).astype(BF16)
        bits *= 2
    p23_parts = [p23] + [swap(p23, "row", step) for step in steps_up]

    def p23_place(meta, *refs):
        parts, out = refs[:-1], refs[-1]
        for m, part in enumerate(parts):
            out[:, at(chip_of(meta) ^ m, lanes)] = part[...]

    p23_half = run(p23_place, p23_parts, shaped((half_w, width)))
    p23_other = swap(p23_half, "row", 1)

    def x1_t23(meta, *refs):
        parts, (diag, u, linked, x1), rest = refs[:chips], refs[chips : chips + 4], refs[chips + 4 :]
        outs, whole = rest[:-1], rest[-1]
        chip = chip_of(meta)
        x = jnp.zeros((half_r, width), F32)
        for m, part in enumerate(parts):
            x = x + dot(part[...], diag[at(chip ^ m, lanes)])
        x = x.astype(BF16)
        x1[...] = x
        for i in range(2):
            cols = slice(i * width, (i + 1) * width)
            whole[:, cols] = u[:, cols] - dot(x, linked[i])
        for m, out in enumerate(outs):
            out[...] = whole[at(chip ^ m, part_r)].astype(BF16)

    pair = Picked(diag_pair, (None, width, width), lambda i, meta: (leaf_of(meta) // 2, 0, 0))
    strip = shaped((part_r, 2 * width))
    x1, *strips = run(
        x1_t23,
        m1_parts + [pair, u, linked],
        [rows_half] + [strip] * chips,
        [pltpu.VMEM((half_r, 2 * width), F32)],
    )
    t23 = strips[0]
    for piece, step in zip(strips[1:], steps_up):
        t23 = t23 + swap(piece, "row", step)
    t23 = spread(t23)
    total = t23.astype(F32)
    for m in range(1, n_leaf):
        total = total + swap(t23, "leaf", m).astype(F32)
    m23 = total.astype(BF16)
    m23_parts = [m23] + [swap(m23, "row", step) for step in steps_up]

    panel_far = []
    for (level, one, two), got in zip(orders, panel_got):
        def panel_join(meta, p, got, out, level=level, two=two):
            value = panel_value(meta, p, level, two).astype(F32) + got[1].astype(F32)
            out[...] = value.astype(BF16)

        sent = run(
            panel_join, [panel_of(level, two), got], shaped((width, width)), after=[p23_own, m1]
        )
        panel_far.append(swap(sent, "leaf", two))

    def x2_x3(meta, *refs):
        parts, (diag, p, p_other, out, whole, tile23) = refs[:chips], refs[chips:]
        chip, core = chip_of(meta), core_of(meta)
        for m, part in enumerate(parts):
            whole[at(chip ^ m, part_r)] = part[...]
        tile23[at(core, half_w)] = p[...]
        tile23[at(1 - core, half_w)] = p_other[...]
        x = dot(whole[:, :width], diag[0]).astype(BF16)
        out[0] = x
        merged = whole[:, width:].astype(F32) - dot(x, tile23[...])
        out[1] = dot(merged.astype(BF16), diag[1]).astype(BF16)

    x23 = run(
        x2_x3,
        m23_parts + [diag_root, p23_half, p23_other],
        shaped((2, half_r, width)),
        [pltpu.VMEM((half_r, 2 * width), BF16), pltpu.VMEM((width, width), BF16)],
    )
    x01_other = [swap(x, "row", 1) for x in (x0, x1)]
    x23_other = swap(x23, "row", 1)

    ways = ((1, 2), (2, 1))

    def leaf_tile(array, level):
        if level is None:
            return Picked(array, (None, height, width), lambda i, meta: (leaf_of(meta) ^ i, 0, 0))
        return Picked(
            array, (None, None, width, width), lambda i, meta: (level, leaf_of(meta) ^ i, 0, 0)
        )

    def update01(meta, b, pa, pb, x0, x1, x0_other, x1_other, *refs):
        sends, kept, whole = refs[:2], refs[2:4], refs[4]
        step = pl.program_id(0)
        core = core_of(meta)
        a = leaf_of(meta) ^ step

        @pl.when(step == 0)
        def _():
            for i, (mine, other) in enumerate(((x0, x0_other), (x1, x1_other))):
                whole[i, at(core, half_r)] = mine[...]
                whole[i, at(1 - core, half_r)] = other[...]

        value = b[...].astype(F32)
        for i, p in enumerate((pa, pb)):
            value = value - dot(whole[i], p[...] * keep(live(meta, i, a)))
        for half, (one, two) in enumerate(ways):
            part = value[half * half_r : (half + 1) * half_r]
            for i, m in enumerate((one, one ^ two)):
                @pl.when(step == m)
                def _(half=half, i=i, part=part):
                    sends[half][i] = part.astype(BF16)
            for i, m in enumerate((0, two)):
                @pl.when(step == m)
                def _(half=half, i=i, part=part):
                    kept[half][i] = part

    share_pair = (2, half_r, width)
    share_send0, share_send1, share_kept0, share_kept1 = run(
        update01,
        [leaf_tile(right, None), leaf_tile(panels, 0), leaf_tile(panels, 1), x0, x1] + x01_other,
        [shaped(share_pair)] * 2 + [shaped(share_pair, F32)] * 2,
        [pltpu.VMEM((2, height, width), BF16)],
        steps=n_leaf,
        after=[t23],
    )
    share_got = [swap(share_send0, "leaf", ways[0][0]), swap(share_send1, "leaf", ways[1][0])]

    def share_join(meta, kept0, kept1, got0, got1, out0, out1):
        for kept, got, out in ((kept0, got0, out0), (kept1, got1, out1)):
            out[...] = (kept[1] + got[1].astype(F32)).astype(BF16)

    share_sent = run(
        share_join, [share_kept0, share_kept1] + share_got, [shaped((half_r, width))] * 2
    )
    share_far = [swap(sent, "leaf", way[1]) for sent, way in zip(share_sent, ways)]

    def leaf_sums(meta, pa, pb, ga, gb, fa, fb, k0, k1, g0, g1, f0, f1, panel_out, share_out):
        for i, (p, got, far) in enumerate(((pa, ga, fa), (pb, gb, fb))):
            value = panel_value(meta, p, 2 + i, 0).astype(F32)
            panel_out[i] = (value + got[0].astype(F32) + far[...].astype(F32)).astype(BF16)
        for i, (kept, got, far) in enumerate(((k0, g0, f0), (k1, g1, f1))):
            value = kept[0] + got[0].astype(F32) + far[...].astype(F32)
            share_out[i * half_r : (i + 1) * half_r] = value

    panel_sum, share_sum = run(
        leaf_sums,
        [panel_of(2, 0), panel_of(3, 0)]
        + panel_got
        + panel_far
        + [share_kept0, share_kept1]
        + share_got
        + share_far,
        [shaped((2, width, width)), shaped((height, width), F32)],
    )

    def final(meta, x0, x1, x0_other, x1_other, x23, x23_other, panel, share, solved, out):
        core = core_of(meta)
        mine, other = at(core, half_r), at(1 - core, half_r)
        for i, (a, b) in enumerate(((x0, x0_other), (x1, x1_other))):
            solved[i, mine] = a[...]
            solved[i, other] = b[...]
        value = share[...]
        for i in range(2):
            solved[2 + i, mine] = x23[i]
            solved[2 + i, other] = x23_other[i]
            value = value - dot(solved[2 + i], panel[i])
        value = value.astype(BF16)
        for i in range(n_leaf):
            out[i] = value

    solved, done = run(
        final,
        [x0, x1] + x01_other + [x23, x23_other, panel_sum, share_sum],
        [shaped((levels, height, width)), shaped((n_leaf, height, width))],
    )
    updated = lax.all_to_all(done, "leaf", 0, 0, tiled=True)
    return solved[:, None], updated


def solution(mesh):
    return jax.shard_map(
        on_device,
        mesh=mesh,
        in_specs=(
            P("leaf", "row", None, None),
            P(None, "leaf", "row", None, None),
            P(None, "leaf", "row"),
            P("leaf", None, None),
            P(),
            P(),
            P(),
        ),
        out_specs=(P(None, "leaf", None, None), P("row", None, None)),
        check_vma=False,
    )
```

time: 167 us -> 142 us (0.85)
  waiting for transfers between devices: 81.7 us -> 55.4 us
  Pallas kernels: 16.4 us -> 21 us
  local copies, waits for them, and re-layouts: 9.44 us -> 4.99 us
    ppermute x36 -> x37, waiting for transfers between devices: 81.7 us -> 55.4 us  [swap(): lax.ppermute(block, axis, [(i, i ^ bits) for i in range(lax.axis_size(axi...]
    pallas_call x15 -> x19, Pallas kernels: 16.4 us -> 21 us  [run(): pl.pallas_call(kernel, grid_spec=pltpu.PrefetchScalarGridSpec(num_scalar_...]
    unnamed x20 -> x18, local copies, waits for them, and re-layouts: 9.35 us -> 4.91 us
    ppermute x36 -> x37, starting transfers between devices: 40.4 us -> 41 us  [swap(): lax.ppermute(block, axis, [(i, i ^ bits) for i in range(lax.axis_size(axi...]
  transfers between devices with their start and end apart: 36 -> 37, of which waited for: 17 -> 18; matrix products, arithmetic and copies ran while one was open for 0% -> 0% of each run, Pallas kernels for 7% -> 10%
where the time goes in v3:
time: 142 us
  waiting for transfers between devices  55.4 us (39%)
  starting transfers between devices  41 us (29%)
  Pallas kernels  21 us (15%)
  blocking collectives  15.5 us (11%)
  local copies, waits for them, and re-layouts  4.99 us (4%)
  other arithmetic  2.74 us (2%)
    ppermute x37, waiting for transfers between devices, swap(): lax.ppermute(block, axis, [(i, i ^ bits) for i in range(lax.axis_size(axi...  55.4 us
    ppermute x37, starting transfers between devices, swap(): lax.ppermute(block, axis, [(i, i ^ bits) for i in range(lax.axis_size(axi...  41 us
    pallas_call x19, Pallas kernels, run(): pl.pallas_call(kernel, grid_spec=pltpu.PrefetchScalarGridSpec(num_scalar_...  21 us
    all_to_all x1, blocking collectives, on_device(): updated = lax.all_to_all(done, 'leaf', 0, 0, tiled=True)  15.5 us
    unnamed x18, local copies, waits for them, and re-layouts  4.91 us
  transfers between devices with their start and end apart: 37, of which 18 were waited for; matrix products, arithmetic and copies ran while one was open for 0% of the time, Pallas kernels for 10%

profile of v3, /device:TPU:0, one launch (start us, length us, event | category | flops | bytes accessed | tf_op | source)
XLA Modules:
  0.0 141.7 jit_solution(7032484630520519968)
XLA Ops:
  1.1 1.3 reduce.3
  2.6 1.3 pad_add_fusion.meta
  3.9 2.8 %shard_map.86 = bf16[512,512]{1,0:T(8,128)(2,1)} custom-call(s32[22]{0:T(128)} %pad_add_fusion.meta, bf16[4,256,512]{2,1,0:T(8,128)(2,1)} %bitcast.31, bf16[4,256,512]{2,1,0:T(8,128)(2,1)} %bitcast.32, bf16[4,4,512,512]{3,2,1,0:T(8,128)(2,1)} %bitcast.7), custom_call_target="tpu_custom_call" | custom-call | bytes 1572864 | tf_op jit(solution)/shard_map/pallas_call | solution.py:126
  7.1 1.7 %collective-permute-done.refs_3_ = bf16[512,512]{1,0:T(8,128)(2,1)S(1)} collective-permute-done((bf16[512,512]{1,0:T(8,128)(2,1)}, bf16[512,512]{1,0:T(8,128)(2,1)S(1)}, u32[]{:S(2)}, u32[]{:S(2)}) %collective-permute-start) | collective-permute-done | bytes 524320 | tf_op jit(solution)/shard_map/ppermute | solution.py:14
  8.9 3.4 %copy-done = bf16[4,1,4,512,512]{4,3,2,1,0:T(8,128)(2,1)S(1)} copy-done((bf16[4,1,4,512,512]{4,3,2,1,0:T(8,128)(2,1)S(1)}, bf16[4,1,4,512,512]{4,3,2,1,0:T(8,128)(2,1)}, u32[]{:S(2)}) %copy-start) | copy-done | bytes 8388632
  12.3 0.7 shard_map.87
  13.1 0.7 shard_map.91
  14.2 2.7 %collective-permute-start.1 = (bf16[1280,128]{1,0:T(8,128)(2,1)S(1)}, bf16[1280,128]{1,0:T(8,128)(2,1)S(1)}, u32[]{:S(2)}, u32[]{:S(2)}) collective-permute-start(bf16[1280,128]{1,0:T(8,128)(2,1)S(1)} %get-tuple-element.31.refs_7_.refs_2_), channel_id=1, source_target_pairs={{0,2},{1,3},{2,0},{3,1},{4,6},{5,7},{6,4},{7,5},{8,10},{9,11},{10,... | collective-permute-start | bytes 983048 | tf_op jit(solution)/shard_map/ppermute | solution.py:14
  17.0 8.2 %collective-permute-done.1.refs_1_ = bf16[1280,128]{1,0:T(8,128)(2,1)S(1)} collective-permute-done((bf16[1280,128]{1,0:T(8,128)(2,1)S(1)}, bf16[1280,128]{1,0:T(8,128)(2,1)S(1)}, u32[]{:S(2)}, u32[]{:S(2)}) %collective-permute-start.1) | collective-permute-done | bytes 327712 | tf_op jit(solution)/shard_map/ppermute | solution.py:14
  25.8 2.8 %collective-permute-start.2 = (bf16[896,128]{1,0:T(8,128)(2,1)S(1)}, bf16[896,128]{1,0:T(8,128)(2,1)S(1)}, u32[]{:S(2)}, u32[]{:S(2)}) collective-permute-start(bf16[896,128]{1,0:T(8,128)(2,1)S(1)} %get-tuple-element.32.refs_0_), channel_id=1, source_target_pairs={{0,4},{1,5},{2,6},{3,7},{4,0},{5,1},{6,2},{7,3},{8,12},{9,13},{10,... | collective-permute-start | bytes 688136 | tf_op jit(solution)/shard_map/ppermute | solution.py:14
  28.6 10.4 %collective-permute-done.2.refs_1_ = bf16[896,128]{1,0:T(8,128)(2,1)S(1)} collective-permute-done((bf16[896,128]{1,0:T(8,128)(2,1)S(1)}, bf16[896,128]{1,0:T(8,128)(2,1)S(1)}, u32[]{:S(2)}, u32[]{:S(2)}) %collective-permute-start.2) | collective-permute-done | bytes 229408 | tf_op jit(solution)/shard_map/ppermute | solution.py:14
  39.0 0.8 shard_map.89
  39.9 1.2 collective-permute-done.3.refs_2_
  41.1 0.7 shard_map.90.refs_9_
  41.9 1.1 shard_map.92
  43.6 1.5 %collective-permute-start.4 = (f32[128,128]{1,0:T(8,128)S(1)}, f32[128,128]{1,0:T(8,128)S(1)}, u32[]{:S(2)}, u32[]{:S(2)}) collective-permute-start(f32[128,128]{1,0:T(8,128)S(1)} %shard_map.90.refs_9_), channel_id=1, source_target_pairs={{0,8},{8,0},{16,24},{24,16},{1,9},{9,1},{17,25},{25,17},{2,10},{10... | collective-permute-start | bytes 196616 | tf_op jit(solution)/shard_map/ppermute | solution.py:14
  45.8 1.6 %collective-permute-start.30 = (bf16[2,512,512]{2,1,0:T(8,128)(2,1)S(1)}, bf16[2,512,512]{2,1,0:T(8,128)(2,1)S(1)}, u32[]{:S(2)}, u32[]{:S(2)}) collective-permute-start(bf16[2,512,512]{2,1,0:T(8,128)(2,1)S(1)} %shard_map.98), channel_id=1, source_target_pairs={{0,16},{8,24},{16,0},{24,8},{1,17},{9,25},{17,1},{25,9},{2,18},{10... | collective-permute-start | bytes 3145736 | tf_op jit(solution)/shard_map/ppermute | solution.py:14
  49.2 3.4 %collective-permute-start.21 = (bf16[256,128]{1,0:T(8,128)(2,1)S(1)}, bf16[256,128]{1,0:T(8,128)(2,1)S(1)}, u32[]{:S(2)}, u32[]{:S(2)}) collective-permute-start(bf16[256,128]{1,0:T(8,128)(2,1)S(1)} %get-tuple-element.47), channel_id=1, source_target_pairs={{0,4},{1,5},{2,6},{3,7},{4,0},{5,1},{6,2},{7,3},{8,12},{9,13},{10,... | collective-permute-start | bytes 196616 | tf_op jit(solution)/shard_map/ppermute | solution.py:14
  53.3 2.3 %collective-permute-done.21 = bf16[256,128]{1,0:T(8,128)(2,1)S(1)} collective-permute-done((bf16[256,128]{1,0:T(8,128)(2,1)S(1)}, bf16[256,128]{1,0:T(8,128)(2,1)S(1)}, u32[]{:S(2)}, u32[]{:S(2)}) %collective-permute-start.21) | collective-permute-done | bytes 65568 | tf_op jit(solution)/shard_map/ppermute | solution.py:14
  55.6 1.5 %collective-permute-start.22 = (bf16[256,128]{1,0:T(8,128)(2,1)S(1)}, bf16[256,128]{1,0:T(8,128)(2,1)S(1)}, u32[]{:S(2)}, u32[]{:S(2)}) collective-permute-start(bf16[256,128]{1,0:T(8,128)(2,1)S(1)} %add.37), channel_id=1, source_target_pairs={{0,8},{8,0},{16,24},{24,16},{1,9},{9,1},{17,25},{25,17},{2,10},{10... | collective-permute-start | bytes 196616 | tf_op jit(solution)/shard_map/ppermute | solution.py:14
  57.1 2.2 %collective-permute-start.6 = (bf16[128,128]{1,0:T(8,128)(2,1)S(1)}, bf16[128,128]{1,0:T(8,128)(2,1)S(1)}, u32[]{:S(2)}, u32[]{:S(2)}) collective-permute-start(bf16[128,128]{1,0:T(8,128)(2,1)S(1)} %add_convert_fusion.3.refs_0_.refs_3_), channel_id=1, source_target_pairs={{0,4},{1,5},{2,6},{3,7},{4,0},{5,1},{6,2},{7,3},{8,12},{9,13},{10,... | collective-permute-start | bytes 98312 | tf_op jit(solution)/shard_map/ppermute | solution.py:14
  59.8 2.4 %collective-permute-done.6.refs_2_ = bf16[128,128]{1,0:T(8,128)(2,1)S(1)} collective-permute-done((bf16[128,128]{1,0:T(8,128)(2,1)S(1)}, bf16[128,128]{1,0:T(8,128)(2,1)S(1)}, u32[]{:S(2)}, u32[]{:S(2)}) %collective-permute-start.6) | collective-permute-done | bytes 32800 | tf_op jit(solution)/shard_map/ppermute | solution.py:14
  62.2 3.0 %collective-permute-done.7.refs_3_ = bf16[128,128]{1,0:T(8,128)(2,1)S(1)} collective-permute-done((bf16[128,128]{1,0:T(8,128)(2,1)S(1)}, bf16[128,128]{1,0:T(8,128)(2,1)S(1)}, u32[]{:S(2)}, u32[]{:S(2)}) %collective-permute-start.7) | collective-permute-done | bytes 32800 | tf_op jit(solution)/shard_map/ppermute | solution.py:14
  65.2 1.1 shard_map.93
  66.4 0.9 collective-permute-start.12
  67.3 6.5 %collective-permute-done.22 = bf16[256,128]{1,0:T(8,128)(2,1)S(1)} collective-permute-done((bf16[256,128]{1,0:T(8,128)(2,1)S(1)}, bf16[256,128]{1,0:T(8,128)(2,1)S(1)}, u32[]{:S(2)}, u32[]{:S(2)}) %collective-permute-start.22) | collective-permute-done | bytes 65568 | tf_op jit(solution)/shard_map/ppermute | solution.py:14
  73.8 3.2 %collective-permute-start.13 = (bf16[32,1024]{1,0:T(8,128)(2,1)S(1)}, bf16[32,1024]{1,0:T(8,128)(2,1)S(1)}, u32[]{:S(2)}, u32[]{:S(2)}) collective-permute-start(bf16[32,1024]{1,0:T(8,128)(2,1)S(1)} %get-tuple-element.43), channel_id=1, source_target_pairs={{0,6},{1,7},{2,4},{3,5},{4,2},{5,3},{6,0},{7,1},{8,14},{9,15},{10,... | collective-permute-start | bytes 196616 | tf_op jit(solution)/shard_map/ppermute | solution.py:14
  77.6 2.4 %collective-permute-done.13 = bf16[32,1024]{1,0:T(8,128)(2,1)S(1)} collective-permute-done((bf16[32,1024]{1,0:T(8,128)(2,1)S(1)}, bf16[32,1024]{1,0:T(8,128)(2,1)S(1)}, u32[]{:S(2)}, u32[]{:S(2)}) %collective-permute-start.13) | collective-permute-done | bytes 65568 | tf_op jit(solution)/shard_map/ppermute | solution.py:14
  81.6 2.0 %collective-permute-start.16 = (bf16[32,1024]{1,0:T(8,128)(2,1)S(1)}, bf16[32,1024]{1,0:T(8,128)(2,1)S(1)}, u32[]{:S(2)}, u32[]{:S(2)}) collective-permute-start(bf16[32,1024]{1,0:T(8,128)(2,1)S(1)} %add_add_fusion.refs_7_), channel_id=1, source_target_pairs={{0,24},{8,16},{16,8},{24,0},{1,25},{9,17},{17,9},{25,1},{2,26},{10... | collective-permute-start | bytes 196616 | tf_op jit(solution)/shard_map/ppermute | solution.py:14
  85.1 2.9 %collective-permute-start.25 = (bf16[256,128]{1,0:T(8,128)(2,1)S(1)}, bf16[256,128]{1,0:T(8,128)(2,1)S(1)}, u32[]{:S(2)}, u32[]{:S(2)}) collective-permute-start(bf16[256,128]{1,0:T(8,128)(2,1)S(1)} %add_convert_fusion.refs_0_), channel_id=1, source_target_pairs={{0,4},{1,5},{2,6},{3,7},{4,0},{5,1},{6,2},{7,3},{8,12},{9,13},{10,... | collective-permute-start | bytes 196616 | tf_op jit(solution)/shard_map/ppermute | solution.py:14
  88.0 1.4 collective-permute-start.26
  90.9 1.7 %collective-permute-done.25.refs_2_ = bf16[256,128]{1,0:T(8,128)(2,1)S(1)} collective-permute-done((bf16[256,128]{1,0:T(8,128)(2,1)S(1)}, bf16[256,128]{1,0:T(8,128)(2,1)S(1)}, u32[]{:S(2)}, u32[]{:S(2)}) %collective-permute-start.25) | collective-permute-done | bytes 65568 | tf_op jit(solution)/shard_map/ppermute | solution.py:14
  92.6 0.8 collective-permute-start.32
  93.4 0.8 collective-permute-done.26.refs_3_
  95.4 1.1 collective-permute-start.18
  96.5 2.6 %collective-permute-start.19 = (bf16[32,1024]{1,0:T(8,128)(2,1)S(1)}, bf16[32,1024]{1,0:T(8,128)(2,1)S(1)}, u32[]{:S(2)}, u32[]{:S(2)}) collective-permute-start(bf16[32,1024]{1,0:T(8,128)(2,1)S(1)} %add_convert_fusion.2.refs_0_), channel_id=1, source_target_pairs={{0,6},{1,7},{2,4},{3,5},{4,2},{5,3},{6,0},{7,1},{8,14},{9,15},{10,... | collective-permute-start | bytes 196616 | tf_op jit(solution)/shard_map/ppermute | solution.py:14
  99.1 2.6 %shard_map.101 = (bf16[2,128,512]{2,1,0:T(8,128)(2,1)S(1)}, bf16[2,128,512]{2,1,0:T(8,128)(2,1)S(1)}, f32[2,128,512]{2,1,0:T(8,128)S(1)}, f32[2,128,512]{2,1,0:T(8,128)S(1)}) custom-call(s32[22]{0:T(128)S(1)} %copy-done.5, bf16[4,256,512]{2,1,0:T(8,128)(2,1)S(1)} %bitcast.39, bf16[4,4,512,512]{3,2,1,0:T(8,128)(2,1)S(1)} %bitcast.29, ...), custom_call_target="tpu_custom_call" | custom-call | bytes 8912896 | tf_op jit(solution)/shard_map/pallas_call | solution.py:126
  101.8 2.2 %collective-permute-done.18.refs_2_ = bf16[32,1024]{1,0:T(8,128)(2,1)S(1)} collective-permute-done((bf16[32,1024]{1,0:T(8,128)(2,1)S(1)}, bf16[32,1024]{1,0:T(8,128)(2,1)S(1)}, u32[]{:S(2)}, u32[]{:S(2)}) %collective-permute-start.18) | collective-permute-done | bytes 65568 | tf_op jit(solution)/shard_map/ppermute | solution.py:14
  104.7 1.3 collective-permute-start.34
  106.0 1.1 shard_map.96.refs_4_
  107.2 3.2 %collective-permute-done.33.refs_2_.refs_8_ = bf16[2,128,512]{2,1,0:T(8,128)(2,1)S(1)} collective-permute-done((bf16[2,128,512]{2,1,0:T(8,128)(2,1)S(1)}, bf16[2,128,512]{2,1,0:T(8,128)(2,1)S(1)}, u32[]{:S(2)}, u32[]{:S(2)}) %collective-permute-start.33) | collective-permute-done | bytes 262176 | tf_op jit(solution)/shard_map/ppermute | solution.py:14
  110.4 4.5 %collective-permute-done.34.refs_3_.refs_9_ = bf16[2,128,512]{2,1,0:T(8,128)(2,1)S(1)} collective-permute-done((bf16[2,128,512]{2,1,0:T(8,128)(2,1)S(1)}, bf16[2,128,512]{2,1,0:T(8,128)(2,1)S(1)}, u32[]{:S(2)}, u32[]{:S(2)}) %collective-permute-start.34) | collective-permute-done | bytes 262176 | tf_op jit(solution)/shard_map/ppermute | solution.py:14
  116.0 0.8 collective-permute-start.36
  116.8 3.8 %collective-permute-done.35.refs_10_ = bf16[128,512]{1,0:T(8,128)(2,1)S(1)} collective-permute-done((bf16[128,512]{1,0:T(8,128)(2,1)S(1)}, bf16[128,512]{1,0:T(8,128)(2,1)S(1)}, u32[]{:S(2)}, u32[]{:S(2)}) %collective-permute-start.35) | collective-permute-done | bytes 131104 | tf_op jit(solution)/shard_map/ppermute | solution.py:14
  121.0 2.3 %shard_map.103 = (bf16[2,512,512]{2,1,0:T(8,128)(2,1)S(1)}, f32[256,512]{1,0:T(8,128)S(1)}) custom-call(s32[22]{0:T(128)S(1)} %copy-done.5, bf16[4,4,512,512]{3,2,1,0:T(8,128)(2,1)} %bitcast.8, bf16[4,4,512,512]{3,2,1,0:T(8,128)(2,1)} %bitcast.9, bf16[2,512,512]{2,1,0:T(8,128)(2,1)S(1)} %collective-permute-done.29.refs_1_.refs_2_, ...), custom_call_target="tpu_custom_call" | custom-call | bytes 7602176 | tf_op jit(solution)/shard_map/pallas_call | solution.py:126
  123.2 1.9 %shard_map.104 = (bf16[4,256,512]{2,1,0:T(8,128)(2,1)}, bf16[4,256,512]{2,1,0:T(8,128)(2,1)S(1)}) custom-call(s32[22]{0:T(128)S(1)} %copy-done.5, bf16[128,512]{1,0:T(8,128)(2,1)S(1)} %get-tuple-element.34.refs_0_.refs_8_.refs_3_, bf16[128,512]{1,0:T(8,128)(2,1)S(1)} %get-tuple-element.39.refs_4_.refs_1_, ...), custom_call_target="tpu_custom_call" | custom-call | bytes 4718592 | tf_op jit(solution)/shard_map/pallas_call | solution.py:126
  125.2 15.5 %all_to_all.5 = bf16[4,256,512]{2,1,0:T(8,128)(2,1)S(1)} all-to-all(bf16[4,256,512]{2,1,0:T(8,128)(2,1)S(1)} %get-tuple-element.57), channel_id=1, replica_groups=mesh['leaf'=4,'row'=8] {'leaf'}, dimensions={0} | all-to-all | bytes 2097152 | tf_op jit(solution)/shard_map/all_to_all | solution.py:498
  140.7 1.0 copy.11
  (74 shorter events, 15.1 us)
Async XLA Ops:
  3.9 5.0 %copy-start.1 = (bf16[1,4,256,512]{3,2,1,0:T(8,128)(2,1)S(1)}, bf16[1,4,256,512]{3,2,1,0:T(8,128)(2,1)}, u32[]{:S(2)}) copy-start(bf16[1,4,256,512]{3,2,1,0:T(8,128)(2,1)} %param.7) | copy-start | bytes 3145732
  3.9 5.0 %copy-start.5 = (s32[22]{0:T(128)S(1)}, s32[22]{0:T(128)}, u32[]{:S(2)}) copy-start(s32[22]{0:T(128)} %pad_add_fusion.meta) | copy-start | bytes 268
  6.7 2.2 %collective-permute-start = (bf16[512,512]{1,0:T(8,128)(2,1)}, bf16[512,512]{1,0:T(8,128)(2,1)S(1)}, u32[]{:S(2)}, u32[]{:S(2)}) collective-permute-start(bf16[512,512]{1,0:T(8,128)(2,1)} %shard_map.86), channel_id=1, source_target_pairs={{0,1},{1,0},{2,3},{3,2},{4,5},{5,4},{6,7},{7,6},{8,9},{9,8},{10,11... | collective-permute-start | bytes 1572872 | tf_op jit(solution)/shard_map/ppermute | solution.py:14
  8.9 3.4 %copy-start = (bf16[4,1,4,512,512]{4,3,2,1,0:T(8,128)(2,1)S(1)}, bf16[4,1,4,512,512]{4,3,2,1,0:T(8,128)(2,1)}, u32[]{:S(2)}) copy-start(bf16[4,1,4,512,512]{4,3,2,1,0:T(8,128)(2,1)} %param.8) | copy-start | bytes 25165828
  13.0 28.9 %slice-start = ((s8[8388608]{0:T(1024)(128)(4,1)}), s8[4194304]{0:T(1024)(128)(4,1)S(1)}, s32[]{:S(2)}) async-start(s8[8388608]{0:T(1024)(128)(4,1)} %bitcast.16), calls=%async_computation.1 | async-start | bytes 8388608
  13.0 26.0 %copy-start.4 = (bf16[1,512,512]{2,1,0:T(8,128)(2,1)S(1)}, bf16[1,512,512]{2,1,0:T(8,128)(2,1)}, u32[]{:S(2)}) copy-start(bf16[1,512,512]{2,1,0:T(8,128)(2,1)} %refs_3_.1) | copy-start | bytes 1572868
  13.0 28.9 %slice-start.1 = ((s8[8388608]{0:T(1024)(128)(4,1)}), s8[4194304]{0:T(1024)(128)(4,1)S(1)}, s32[]{:S(2)}) async-start(s8[8388608]{0:T(1024)(128)(4,1)} %bitcast.16), calls=%async_computation.2 | async-start | bytes 8388608
  13.8 28.1 %collective-permute-start.8 = (bf16[2560,512]{1,0:T(8,128)(2,1)S(1)}, bf16[2560,512]{1,0:T(8,128)(2,1)S(1)}, u32[]{:S(2)}, u32[]{:S(2)}) collective-permute-start(bf16[2560,512]{1,0:T(8,128)(2,1)S(1)} %shard_map.91), channel_id=1, source_target_pairs={{0,1},{1,0},{2,3},{3,2},{4,5},{5,4},{6,7},{7,6},{8,9},{9,8},{10,11... | collective-permute-start | bytes 7864328 | tf_op jit(solution)/shard_map/ppermute | solution.py:14
  14.2 11.0 %collective-permute-start.1 = (bf16[1280,128]{1,0:T(8,128)(2,1)S(1)}, bf16[1280,128]{1,0:T(8,128)(2,1)S(1)}, u32[]{:S(2)}, u32[]{:S(2)}) collective-permute-start(bf16[1280,128]{1,0:T(8,128)(2,1)S(1)} %get-tuple-element.31.refs_7_.refs_2_), channel_id=1, source_target_pairs={{0,2},{1,3},{2,0},{3,1},{4,6},{5,7},{6,4},{7,5},{8,10},{9,11},{10,... | collective-permute-start | bytes 983048 | tf_op jit(solution)/shard_map/ppermute | solution.py:14
  25.8 13.2 %collective-permute-start.2 = (bf16[896,128]{1,0:T(8,128)(2,1)S(1)}, bf16[896,128]{1,0:T(8,128)(2,1)S(1)}, u32[]{:S(2)}, u32[]{:S(2)}) collective-permute-start(bf16[896,128]{1,0:T(8,128)(2,1)S(1)} %get-tuple-element.32.refs_0_), channel_id=1, source_target_pairs={{0,4},{1,5},{2,6},{3,7},{4,0},{5,1},{6,2},{7,3},{8,12},{9,13},{10,... | collective-permute-start | bytes 688136 | tf_op jit(solution)/shard_map/ppermute | solution.py:14
  39.8 1.3 collective-permute-start.3
  43.0 5.6 %collective-permute-start.20 = (bf16[512,128]{1,0:T(8,128)(2,1)S(1)}, bf16[512,128]{1,0:T(8,128)(2,1)S(1)}, u32[]{:S(2)}, u32[]{:S(2)}) collective-permute-start(bf16[512,128]{1,0:T(8,128)(2,1)S(1)} %get-tuple-element.45), channel_id=1, source_target_pairs={{0,2},{1,3},{2,0},{3,1},{4,6},{5,7},{6,4},{7,5},{8,10},{9,11},{10,... | collective-permute-start | bytes 393224 | tf_op jit(solution)/shard_map/ppermute | solution.py:14
  43.6 9.0 %collective-permute-start.4 = (f32[128,128]{1,0:T(8,128)S(1)}, f32[128,128]{1,0:T(8,128)S(1)}, u32[]{:S(2)}, u32[]{:S(2)}) collective-permute-start(f32[128,128]{1,0:T(8,128)S(1)} %shard_map.90.refs_9_), channel_id=1, source_target_pairs={{0,8},{8,0},{16,24},{24,16},{1,9},{9,1},{17,25},{25,17},{2,10},{10... | collective-permute-start | bytes 196616 | tf_op jit(solution)/shard_map/ppermute | solution.py:14
  45.8 19.4 %copy-start.3 = (bf16[2,512,512]{2,1,0:T(8,128)(2,1)S(1)}, bf16[2,512,512]{2,1,0:T(8,128)(2,1)}, u32[]{:S(2)}) copy-start(bf16[2,512,512]{2,1,0:T(8,128)(2,1)} %refs_4_.2) | copy-start | bytes 3145732
  45.8 37.8 %collective-permute-start.30 = (bf16[2,512,512]{2,1,0:T(8,128)(2,1)S(1)}, bf16[2,512,512]{2,1,0:T(8,128)(2,1)S(1)}, u32[]{:S(2)}, u32[]{:S(2)}) collective-permute-start(bf16[2,512,512]{2,1,0:T(8,128)(2,1)S(1)} %shard_map.98), channel_id=1, source_target_pairs={{0,16},{8,24},{16,0},{24,8},{1,17},{9,25},{17,1},{25,9},{2,18},{10... | collective-permute-start | bytes 3145736 | tf_op jit(solution)/shard_map/ppermute | solution.py:14
  48.0 35.7 %collective-permute-start.29 = (bf16[2,512,512]{2,1,0:T(8,128)(2,1)S(1)}, bf16[2,512,512]{2,1,0:T(8,128)(2,1)S(1)}, u32[]{:S(2)}, u32[]{:S(2)}) collective-permute-start(bf16[2,512,512]{2,1,0:T(8,128)(2,1)S(1)} %shard_map.97), channel_id=1, source_target_pairs={{0,8},{8,0},{16,24},{24,16},{1,9},{9,1},{17,25},{25,17},{2,10},{10... | collective-permute-start | bytes 3145736 | tf_op jit(solution)/shard_map/ppermute | solution.py:14
  49.2 6.4 %collective-permute-start.21 = (bf16[256,128]{1,0:T(8,128)(2,1)S(1)}, bf16[256,128]{1,0:T(8,128)(2,1)S(1)}, u32[]{:S(2)}, u32[]{:S(2)}) collective-permute-start(bf16[256,128]{1,0:T(8,128)(2,1)S(1)} %get-tuple-element.47), channel_id=1, source_target_pairs={{0,4},{1,5},{2,6},{3,7},{4,0},{5,1},{6,2},{7,3},{8,12},{9,13},{10,... | collective-permute-start | bytes 196616 | tf_op jit(solution)/shard_map/ppermute | solution.py:14
  52.6 6.7 %collective-permute-start.5 = (bf16[128,128]{1,0:T(8,128)(2,1)S(1)}, bf16[128,128]{1,0:T(8,128)(2,1)S(1)}, u32[]{:S(2)}, u32[]{:S(2)}) collective-permute-start(bf16[128,128]{1,0:T(8,128)(2,1)S(1)} %add_convert_fusion.3.refs_0_.refs_3_), channel_id=1, source_target_pairs={{0,2},{1,3},{2,0},{3,1},{4,6},{5,7},{6,4},{7,5},{8,10},{9,11},{10,... | collective-permute-start | bytes 98312 | tf_op jit(solution)/shard_map/ppermute | solution.py:14
  55.6 18.2 %collective-permute-start.22 = (bf16[256,128]{1,0:T(8,128)(2,1)S(1)}, bf16[256,128]{1,0:T(8,128)(2,1)S(1)}, u32[]{:S(2)}, u32[]{:S(2)}) collective-permute-start(bf16[256,128]{1,0:T(8,128)(2,1)S(1)} %add.37), channel_id=1, source_target_pairs={{0,8},{8,0},{16,24},{24,16},{1,9},{9,1},{17,25},{25,17},{2,10},{10... | collective-permute-start | bytes 196616 | tf_op jit(solution)/shard_map/ppermute | solution.py:14
  57.1 5.1 %collective-permute-start.6 = (bf16[128,128]{1,0:T(8,128)(2,1)S(1)}, bf16[128,128]{1,0:T(8,128)(2,1)S(1)}, u32[]{:S(2)}, u32[]{:S(2)}) collective-permute-start(bf16[128,128]{1,0:T(8,128)(2,1)S(1)} %add_convert_fusion.3.refs_0_.refs_3_), channel_id=1, source_target_pairs={{0,4},{1,5},{2,6},{3,7},{4,0},{5,1},{6,2},{7,3},{8,12},{9,13},{10,... | collective-permute-start | bytes 98312 | tf_op jit(solution)/shard_map/ppermute | solution.py:14
  59.4 5.8 %collective-permute-start.7 = (bf16[128,128]{1,0:T(8,128)(2,1)S(1)}, bf16[128,128]{1,0:T(8,128)(2,1)S(1)}, u32[]{:S(2)}, u32[]{:S(2)}) collective-permute-start(bf16[128,128]{1,0:T(8,128)(2,1)S(1)} %add_convert_fusion.3.refs_0_.refs_3_), channel_id=1, source_target_pairs={{0,6},{1,7},{2,4},{3,5},{4,2},{5,3},{6,0},{7,1},{8,14},{9,15},{10,... | collective-permute-start | bytes 98312 | tf_op jit(solution)/shard_map/ppermute | solution.py:14
  66.3 10.7 %collective-permute-start.11 = (bf16[32,1024]{1,0:T(8,128)(2,1)S(1)}, bf16[32,1024]{1,0:T(8,128)(2,1)S(1)}, u32[]{:S(2)}, u32[]{:S(2)}) collective-permute-start(bf16[32,1024]{1,0:T(8,128)(2,1)S(1)} %get-tuple-element.41), channel_id=1, source_target_pairs={{0,2},{1,3},{2,0},{3,1},{4,6},{5,7},{6,4},{7,5},{8,10},{9,11},{10,... | collective-permute-start | bytes 196616 | tf_op jit(solution)/shard_map/ppermute | solution.py:14
  66.4 11.2 %collective-permute-start.12 = (bf16[32,1024]{1,0:T(8,128)(2,1)S(1)}, bf16[32,1024]{1,0:T(8,128)(2,1)S(1)}, u32[]{:S(2)}, u32[]{:S(2)}) collective-permute-start(bf16[32,1024]{1,0:T(8,128)(2,1)S(1)} %get-tuple-element.42), channel_id=1, source_target_pairs={{0,4},{1,5},{2,6},{3,7},{4,0},{5,1},{6,2},{7,3},{8,12},{9,13},{10,... | collective-permute-start | bytes 196616 | tf_op jit(solution)/shard_map/ppermute | solution.py:14
  73.8 6.2 %collective-permute-start.13 = (bf16[32,1024]{1,0:T(8,128)(2,1)S(1)}, bf16[32,1024]{1,0:T(8,128)(2,1)S(1)}, u32[]{:S(2)}, u32[]{:S(2)}) collective-permute-start(bf16[32,1024]{1,0:T(8,128)(2,1)S(1)} %get-tuple-element.43), channel_id=1, source_target_pairs={{0,6},{1,7},{2,4},{3,5},{4,2},{5,3},{6,0},{7,1},{8,14},{9,15},{10,... | collective-permute-start | bytes 196616 | tf_op jit(solution)/shard_map/ppermute | solution.py:14
  77.0 4.6 %collective-permute-start.23 = (bf16[256,128]{1,0:T(8,128)(2,1)S(1)}, bf16[256,128]{1,0:T(8,128)(2,1)S(1)}, u32[]{:S(2)}, u32[]{:S(2)}) collective-permute-start(bf16[256,128]{1,0:T(8,128)(2,1)S(1)} %add_convert_fusion.1), channel_id=1, source_target_pairs={{0,16},{8,24},{16,0},{24,8},{1,17},{9,25},{17,1},{25,9},{2,18},{10... | collective-permute-start | bytes 196616 | tf_op jit(solution)/shard_map/ppermute | solution.py:14
  80.0 4.3 %collective-permute-start.14 = (bf16[32,1024]{1,0:T(8,128)(2,1)S(1)}, bf16[32,1024]{1,0:T(8,128)(2,1)S(1)}, u32[]{:S(2)}, u32[]{:S(2)}) collective-permute-start(bf16[32,1024]{1,0:T(8,128)(2,1)S(1)} %add_add_fusion.refs_7_), channel_id=1, source_target_pairs={{0,8},{8,0},{16,24},{24,16},{1,9},{9,1},{17,25},{25,17},{2,10},{10... | collective-permute-start | bytes 196616 | tf_op jit(solution)/shard_map/ppermute | solution.py:14
  80.6 4.4 %collective-permute-start.15 = (bf16[32,1024]{1,0:T(8,128)(2,1)S(1)}, bf16[32,1024]{1,0:T(8,128)(2,1)S(1)}, u32[]{:S(2)}, u32[]{:S(2)}) collective-permute-start(bf16[32,1024]{1,0:T(8,128)(2,1)S(1)} %add_add_fusion.refs_7_), channel_id=1, source_target_pairs={{0,16},{8,24},{16,0},{24,8},{1,17},{9,25},{17,1},{25,9},{2,18},{10... | collective-permute-start | bytes 196616 | tf_op jit(solution)/shard_map/ppermute | solution.py:14
  81.6 6.4 %collective-permute-start.16 = (bf16[32,1024]{1,0:T(8,128)(2,1)S(1)}, bf16[32,1024]{1,0:T(8,128)(2,1)S(1)}, u32[]{:S(2)}, u32[]{:S(2)}) collective-permute-start(bf16[32,1024]{1,0:T(8,128)(2,1)S(1)} %add_add_fusion.refs_7_), channel_id=1, source_target_pairs={{0,24},{8,16},{16,8},{24,0},{1,25},{9,17},{17,9},{25,1},{2,26},{10... | collective-permute-start | bytes 196616 | tf_op jit(solution)/shard_map/ppermute | solution.py:14
  83.6 11.3 %collective-permute-start.9 = (bf16[128,512]{1,0:T(8,128)(2,1)S(1)}, bf16[128,512]{1,0:T(8,128)(2,1)S(1)}, u32[]{:S(2)}, u32[]{:S(2)}) collective-permute-start(bf16[128,512]{1,0:T(8,128)(2,1)S(1)} %get-tuple-element.34.refs_0_.refs_8_.refs_3_), channel_id=1, source_target_pairs={{0,1},{1,0},{2,3},{3,2},{4,5},{5,4},{6,7},{7,6},{8,9},{9,8},{10,11... | collective-permute-start | bytes 393224 | tf_op jit(solution)/shard_map/ppermute | solution.py:14
  83.7 11.7 %collective-permute-start.10 = (bf16[128,512]{1,0:T(8,128)(2,1)S(1)}, bf16[128,512]{1,0:T(8,128)(2,1)S(1)}, u32[]{:S(2)}, u32[]{:S(2)}) collective-permute-start(bf16[128,512]{1,0:T(8,128)(2,1)S(1)} %get-tuple-element.39.refs_4_.refs_1_), channel_id=1, source_target_pairs={{0,1},{1,0},{2,3},{3,2},{4,5},{5,4},{6,7},{7,6},{8,9},{9,8},{10,11... | collective-permute-start | bytes 393224 | tf_op jit(solution)/shard_map/ppermute | solution.py:14
  84.3 5.1 %collective-permute-start.24 = (bf16[256,128]{1,0:T(8,128)(2,1)S(1)}, bf16[256,128]{1,0:T(8,128)(2,1)S(1)}, u32[]{:S(2)}, u32[]{:S(2)}) collective-permute-start(bf16[256,128]{1,0:T(8,128)(2,1)S(1)} %add_convert_fusion.refs_0_), channel_id=1, source_target_pairs={{0,2},{1,3},{2,0},{3,1},{4,6},{5,7},{6,4},{7,5},{8,10},{9,11},{10,... | collective-permute-start | bytes 196616 | tf_op jit(solution)/shard_map/ppermute | solution.py:14
  85.1 7.6 %collective-permute-start.25 = (bf16[256,128]{1,0:T(8,128)(2,1)S(1)}, bf16[256,128]{1,0:T(8,128)(2,1)S(1)}, u32[]{:S(2)}, u32[]{:S(2)}) collective-permute-start(bf16[256,128]{1,0:T(8,128)(2,1)S(1)} %add_convert_fusion.refs_0_), channel_id=1, source_target_pairs={{0,4},{1,5},{2,6},{3,7},{4,0},{5,1},{6,2},{7,3},{8,12},{9,13},{10,... | collective-permute-start | bytes 196616 | tf_op jit(solution)/shard_map/ppermute | solution.py:14
  88.0 6.2 %collective-permute-start.26 = (bf16[256,128]{1,0:T(8,128)(2,1)S(1)}, bf16[256,128]{1,0:T(8,128)(2,1)S(1)}, u32[]{:S(2)}, u32[]{:S(2)}) collective-permute-start(bf16[256,128]{1,0:T(8,128)(2,1)S(1)} %add_convert_fusion.refs_0_), channel_id=1, source_target_pairs={{0,6},{1,7},{2,4},{3,5},{4,2},{5,3},{6,0},{7,1},{8,14},{9,15},{10,... | collective-permute-start | bytes 196616 | tf_op jit(solution)/shard_map/ppermute | solution.py:14
  89.4 7.1 %collective-permute-start.17 = (bf16[32,1024]{1,0:T(8,128)(2,1)S(1)}, bf16[32,1024]{1,0:T(8,128)(2,1)S(1)}, u32[]{:S(2)}, u32[]{:S(2)}) collective-permute-start(bf16[32,1024]{1,0:T(8,128)(2,1)S(1)} %add_convert_fusion.2.refs_0_), channel_id=1, source_target_pairs={{0,2},{1,3},{2,0},{3,1},{4,6},{5,7},{6,4},{7,5},{8,10},{9,11},{10,... | collective-permute-start | bytes 196616 | tf_op jit(solution)/shard_map/ppermute | solution.py:14
  92.6 28.3 %collective-permute-start.32 = (bf16[512,512]{1,0:T(8,128)(2,1)S(1)}, bf16[512,512]{1,0:T(8,128)(2,1)S(1)}, u32[]{:S(2)}, u32[]{:S(2)}) collective-permute-start(bf16[512,512]{1,0:T(8,128)(2,1)S(1)} %shard_map.100), channel_id=1, source_target_pairs={{0,8},{8,0},{16,24},{24,16},{1,9},{9,1},{17,25},{25,17},{2,10},{10... | collective-permute-start | bytes 1572872 | tf_op jit(solution)/shard_map/ppermute | solution.py:14
  94.8 11.2 %copy-start.2 = (bf16[2,512,512]{2,1,0:T(8,128)(2,1)S(1)}, bf16[2,512,512]{2,1,0:T(8,128)(2,1)}, u32[]{:S(2)}) copy-start(bf16[2,512,512]{2,1,0:T(8,128)(2,1)} %refs_4_.3) | copy-start | bytes 3145732
  94.8 11.1 %collective-permute-start.27 = (bf16[256,512]{1,0:T(8,128)(2,1)S(1)}, bf16[256,512]{1,0:T(8,128)(2,1)S(1)}, u32[]{:S(2)}, u32[]{:S(2)}) collective-permute-start(bf16[256,512]{1,0:T(8,128)(2,1)S(1)} %shard_map.95.refs_5_), channel_id=1, source_target_pairs={{0,1},{1,0},{2,3},{3,2},{4,5},{5,4},{6,7},{7,6},{8,9},{9,8},{10,11... | collective-permute-start | bytes 786440 | tf_op jit(solution)/shard_map/ppermute | solution.py:14
  94.9 26.0 %collective-permute-start.31 = (bf16[512,512]{1,0:T(8,128)(2,1)S(1)}, bf16[512,512]{1,0:T(8,128)(2,1)S(1)}, u32[]{:S(2)}, u32[]{:S(2)}) collective-permute-start(bf16[512,512]{1,0:T(8,128)(2,1)S(1)} %shard_map.99), channel_id=1, source_target_pairs={{0,16},{8,24},{16,0},{24,8},{1,17},{9,25},{17,1},{25,9},{2,18},{10... | collective-permute-start | bytes 1572872 | tf_op jit(solution)/shard_map/ppermute | solution.py:14
  95.4 8.6 %collective-permute-start.18 = (bf16[32,1024]{1,0:T(8,128)(2,1)S(1)}, bf16[32,1024]{1,0:T(8,128)(2,1)S(1)}, u32[]{:S(2)}, u32[]{:S(2)}) collective-permute-start(bf16[32,1024]{1,0:T(8,128)(2,1)S(1)} %add_convert_fusion.2.refs_0_), channel_id=1, source_target_pairs={{0,4},{1,5},{2,6},{3,7},{4,0},{5,1},{6,2},{7,3},{8,12},{9,13},{10,... | collective-permute-start | bytes 196616 | tf_op jit(solution)/shard_map/ppermute | solution.py:14
  96.5 8.2 %collective-permute-start.19 = (bf16[32,1024]{1,0:T(8,128)(2,1)S(1)}, bf16[32,1024]{1,0:T(8,128)(2,1)S(1)}, u32[]{:S(2)}, u32[]{:S(2)}) collective-permute-start(bf16[32,1024]{1,0:T(8,128)(2,1)S(1)} %add_convert_fusion.2.refs_0_), channel_id=1, source_target_pairs={{0,6},{1,7},{2,4},{3,5},{4,2},{5,3},{6,0},{7,1},{8,14},{9,15},{10,... | collective-permute-start | bytes 196616 | tf_op jit(solution)/shard_map/ppermute | solution.py:14
  104.0 6.4 %collective-permute-start.33 = (bf16[2,128,512]{2,1,0:T(8,128)(2,1)S(1)}, bf16[2,128,512]{2,1,0:T(8,128)(2,1)S(1)}, u32[]{:S(2)}, u32[]{:S(2)}) collective-permute-start(bf16[2,128,512]{2,1,0:T(8,128)(2,1)S(1)} %get-tuple-element.50), channel_id=1, source_target_pairs={{0,8},{8,0},{16,24},{24,16},{1,9},{9,1},{17,25},{25,17},{2,10},{10... | collective-permute-start | bytes 786440 | tf_op jit(solution)/shard_map/ppermute | solution.py:14
  104.7 10.2 %collective-permute-start.34 = (bf16[2,128,512]{2,1,0:T(8,128)(2,1)S(1)}, bf16[2,128,512]{2,1,0:T(8,128)(2,1)S(1)}, u32[]{:S(2)}, u32[]{:S(2)}) collective-permute-start(bf16[2,128,512]{2,1,0:T(8,128)(2,1)S(1)} %get-tuple-element.51), channel_id=1, source_target_pairs={{0,16},{8,24},{16,0},{24,8},{1,17},{9,25},{17,1},{25,9},{2,18},{10... | collective-permute-start | bytes 786440 | tf_op jit(solution)/shard_map/ppermute | solution.py:14
  107.1 16.1 %collective-permute-start.28 = (bf16[2,128,512]{2,1,0:T(8,128)(2,1)S(1)}, bf16[2,128,512]{2,1,0:T(8,128)(2,1)S(1)}, u32[]{:S(2)}, u32[]{:S(2)}) collective-permute-start(bf16[2,128,512]{2,1,0:T(8,128)(2,1)S(1)} %shard_map.96.refs_4_), channel_id=1, source_target_pairs={{0,1},{1,0},{2,3},{3,2},{4,5},{5,4},{6,7},{7,6},{8,9},{9,8},{10,11... | collective-permute-start | bytes 786440 | tf_op jit(solution)/shard_map/ppermute | solution.py:14
  115.5 5.1 %collective-permute-start.35 = (bf16[128,512]{1,0:T(8,128)(2,1)S(1)}, bf16[128,512]{1,0:T(8,128)(2,1)S(1)}, u32[]{:S(2)}, u32[]{:S(2)}) collective-permute-start(bf16[128,512]{1,0:T(8,128)(2,1)S(1)} %get-tuple-element.52), channel_id=1, source_target_pairs={{0,16},{8,24},{16,0},{24,8},{1,17},{9,25},{17,1},{25,9},{2,18},{10... | collective-permute-start | bytes 393224 | tf_op jit(solution)/shard_map/ppermute | solution.py:14
  116.0 5.0 %collective-permute-start.36 = (bf16[128,512]{1,0:T(8,128)(2,1)S(1)}, bf16[128,512]{1,0:T(8,128)(2,1)S(1)}, u32[]{:S(2)}, u32[]{:S(2)}) collective-permute-start(bf16[128,512]{1,0:T(8,128)(2,1)S(1)} %get-tuple-element.53), channel_id=1, source_target_pairs={{0,8},{8,0},{16,24},{24,16},{1,9},{9,1},{17,25},{25,17},{2,10},{10... | collective-permute-start | bytes 393224 | tf_op jit(solution)/shard_map/ppermute | solution.py:14

commit v4 on v3

v4 whole, which is shorter than its diff:
```python
import jax
import jax.numpy as jnp
from jax import lax
from jax.experimental import pallas as pl
from jax.experimental.pallas import tpu as pltpu
from jax.sharding import PartitionSpec as P

F32 = jnp.float32
BF16 = jnp.bfloat16
CORES = 2


def swap(block, axis, bits):
    return lax.ppermute(block, axis, [(i, i ^ bits) for i in range(lax.axis_size(axis))])


def dot(a, b):
    return jnp.dot(a, b, preferred_element_type=F32)


def shaped(shape, dtype=BF16):
    return jax.ShapeDtypeStruct(tuple(shape), dtype)


class Picked:
    def __init__(self, array, block, index):
        self.array, self.block, self.index = array, block, index


def on_device(right_side, panels, tile_counts, diag_leaf, diag_pair, diag_root, sup_rows):
    right, panels, counts = right_side[0], panels[:, 0], tile_counts[:, 0]
    levels, here, width, _ = panels.shape
    n_row, n_leaf = lax.axis_size("row"), lax.axis_size("leaf")
    chips = min(n_row // CORES, 4)
    outer = [1 << b for b in range(n_row.bit_length()) if CORES * chips <= 1 << b < n_row]
    height = right.shape[1]
    half_r, half_w = height // CORES, width // CORES
    part_r, part_w = half_r // chips, width // chips

    def row_of(meta):
        return lax.axis_index("row")

    def leaf_of(meta):
        return lax.axis_index("leaf")

    def core_of(meta):
        return row_of(meta) & (CORES - 1)

    def chip_of(meta):
        return lax.div(row_of(meta), CORES) & (chips - 1)

    def spot(meta, level):
        return lax.rem(meta[0][level], here)

    def owns(meta, level):
        return lax.div(meta[0][level], here) == row_of(meta)

    def live(meta, level, a):
        kept = meta[1][level, a]
        for m in range(level + 1):
            kept = jnp.where(row_of(meta) * here + a == meta[0][m], 0, kept)
        return kept

    def live_owned(meta, of, level):
        return jnp.where(owns(meta, level), live(meta, of, spot(meta, level)), 0)

    def keep(limit):
        ids = lax.broadcasted_iota(jnp.int32, (1, width), 1)
        return (ids < limit).astype(F32).astype(BF16)

    def side(level, other):
        return Picked(
            right,
            (None, half_r, width),
            lambda i, *meta: (spot(meta, level), core_of(meta) ^ other, 0),
        )

    def side_value(meta, ref, level):
        return ref[...] * keep(jnp.where(owns(meta, level), width, 0))

    def tile(of, level, other=None):
        if other is None:
            return Picked(
                panels, (None, None, width, width), lambda i, *meta: (of, spot(meta, level), 0, 0)
            )
        return Picked(
            panels,
            (None, None, half_w, width),
            lambda i, *meta: (of, spot(meta, level), core_of(meta) ^ other, 0),
        )

    def tile_value(meta, ref, of, level):
        return ref[...] * keep(live_owned(meta, of, level))

    def run(body, operands, outs, scratch=(), steps=1, after=(), limit=32):
        arrays, specs, moved = [], [], 0
        for operand in operands:
            if not isinstance(operand, Picked):
                zeros = (0,) * operand.ndim
                operand = Picked(operand, operand.shape, lambda i, sup, live_counts, zeros=zeros: zeros)
            arrays.append(operand.array)
            specs.append(pl.BlockSpec(operand.block, operand.index))
            size = operand.array.dtype.itemsize
            for n in operand.block:
                size *= n or 1
            moved += size * steps
        taken = len(arrays)
        arrays += list(after)
        specs += [pl.BlockSpec(memory_space=pl.ANY)] * len(after)

        def kernel(sup, live_counts, *refs):
            body((sup, live_counts), *refs[:taken], *refs[taken + len(after) :])

        single = not isinstance(outs, (list, tuple))
        listed = [outs] if single else list(outs)
        out_specs = [
            pl.BlockSpec(out.shape, lambda i, sup, live_counts, zeros=(0,) * len(out.shape): zeros)
            for out in listed
        ]
        moved += sum(out.size * out.dtype.itemsize for out in listed)
        results = pl.pallas_call(
            kernel,
            grid_spec=pltpu.PrefetchScalarGridSpec(
                num_scalar_prefetch=2,
                grid=(steps,),
                in_specs=specs,
                out_specs=out_specs,
                scratch_shapes=list(scratch),
            ),
            out_shape=listed,
            name=body.__name__,
            compiler_params=pltpu.CompilerParams(vmem_limit_bytes=limit * 1024 * 1024),
            cost_estimate=pl.CostEstimate(flops=0, bytes_accessed=moved, transcendentals=0),
        )(sup_rows, counts, *arrays)
        return results[0] if single else results

    def spread(block):
        for bits in outer:
            block = block + swap(block, "row", bits)
        return block

    steps_up = [CORES * m for m in range(1, chips)]
    rows_half = shaped((half_r, width))
    lanes = part_w
    blocks = width // lanes

    def at(index, size):
        return pl.ds(pl.multiple_of(index * size, size), size)

    first_rows = 2 * half_r + 2 * half_w

    def first_half(meta, out, b0, b1, p01, p23):
        out[:half_r] = side_value(meta, b0, 0)
        out[half_r : 2 * half_r] = side_value(meta, b1, 1)
        out[2 * half_r : 2 * half_r + half_w] = tile_value(meta, p01, 0, 1)
        out[2 * half_r + half_w :] = tile_value(meta, p23, 2, 3)

    def first_send(meta, b0, b1, p01, p23, out):
        first_half(meta, out, b0, b1, p01, p23)

    def first_in(other):
        return [side(0, other), side(1, other), tile(0, 1, other), tile(2, 3, other)]

    first_got = swap(run(first_send, first_in(1), shaped((first_rows, width)), limit=60), "row", 1)

    b0_rows, column_rows = blocks * half_r, half_r + half_w
    near, far = (CORES, 2 * CORES)

    def first_split(meta, b0, b1, p01, p23, got, send, kept, p23_send, p23_kept, whole):
        first_half(meta, whole, b0, b1, p01, p23)
        whole[...] = whole[...] + got[...]
        for i in range(blocks):
            send[i * half_r : (i + 1) * half_r] = whole[:half_r, i * lanes : (i + 1) * lanes]
        kept[:b0_rows] = send[:b0_rows]
        chip = chip_of(meta)
        for i, (mine, other) in enumerate(((0, 1), (2, 3))):
            rows = slice(b0_rows + i * column_rows, b0_rows + (i + 1) * column_rows)
            source = slice(half_r, half_r + column_rows)
            send[rows] = whole[source, at(chip ^ other, lanes)]
            kept[rows] = whole[source, at(chip ^ mine, lanes)]
            rows = slice(i * half_w, (i + 1) * half_w)
            source = slice(half_r + column_rows, first_rows)
            p23_send[rows] = whole[source, at(chip ^ other, lanes)]
            p23_kept[rows] = whole[source, at(chip ^ mine, lanes)]

    near_shape, p23_pair = (
        shaped((b0_rows + 2 * column_rows, lanes)),
        shaped((2 * half_w, lanes)),
    )
    near_send, near_kept, p23_send, p23_kept = run(
        first_split,
        first_in(0) + [first_got],
        [near_shape, near_shape, p23_pair, p23_pair],
        [pltpu.VMEM((first_rows, width), BF16)],
    )
    near_got = swap(spread(near_send), "row", near)
    near_kept = spread(near_kept)
    p23_got = swap(spread(p23_send), "row", near)
    p23_kept = spread(p23_kept)

    def first_join(meta, kept, got, send, own):
        send[:b0_rows] = kept[:b0_rows] + got[:b0_rows]
        middle = b0_rows + column_rows
        own[...] = kept[b0_rows:middle] + got[b0_rows:middle]
        send[b0_rows:] = kept[middle:] + got[middle:]

    far_send, columns_own = run(
        first_join,
        [near_kept, near_got],
        [shaped((b0_rows + column_rows, lanes)), shaped((column_rows, lanes))],
    )
    far_got = swap(far_send, "row", far)

    def p23_join(meta, kept, got, send, own):
        own[...] = kept[:half_w] + got[:half_w]
        send[...] = kept[half_w:] + got[half_w:]

    p23_block = shaped((half_w, lanes))
    p23_send, p23_own = run(
        p23_join, [p23_kept, p23_got], [p23_block, p23_block], after=[far_send]
    )
    p23_far = swap(p23_send, "row", far)

    def panel_of(level, m):
        return Picked(
            panels,
            (None, None, width, width),
            lambda i, *meta: (level, leaf_of(meta) ^ m, 0, 0),
        )

    def panel_value(meta, ref, level, m):
        return ref[...] * keep(live(meta, level, leaf_of(meta) ^ m))

    orders = ((2, 1, 2), (3, 2, 1))
    panel_got = []
    for level, one, two in orders:
        def panel_send(meta, pa, pb, out, level=level, one=one, two=two):
            out[0] = panel_value(meta, pa, level, one)
            out[1] = panel_value(meta, pb, level, one ^ two)

        sent = run(
            panel_send,
            [panel_of(level, one), panel_of(level, one ^ two)],
            shaped((2, width, width)),
            after=[near_send],
        )
        panel_got.append(swap(sent, "leaf", one))

    later = [(0, 2), (1, 2), (0, 3), (1, 3)]
    rest_rows = 2 * half_r + len(later) * width

    def rest_send(meta, b2, b3, *refs):
        tiles, out = refs[:-1], refs[-1]
        out[:half_r] = side_value(meta, b2, 2)
        out[half_r : 2 * half_r] = side_value(meta, b3, 3)
        for i, (of, level) in enumerate(later):
            start = 2 * half_r + i * width
            out[start : start + width] = tile_value(meta, tiles[i], of, level)

    rest_got = swap(
        run(
            rest_send,
            [side(2, 1), side(3, 1)] + [tile(*which) for which in later],
            shaped((rest_rows, width)),
            after=[near_send],
        ),
        "row",
        1,
    )

    def solve0(meta, sent, got, own, diag, x0, p, b):
        x = jnp.zeros((half_r, width), F32)
        for i in range(blocks):
            rows = slice(i * half_r, (i + 1) * half_r)
            x = x + dot(sent[rows] + got[rows], diag[0, i * lanes : (i + 1) * lanes])
        x0[...] = x.astype(BF16)
        b[...] = own[:half_r] + got[b0_rows : b0_rows + half_r]
        p[...] = own[half_r:] + got[b0_rows + half_r :]

    x0, p01, b1 = run(
        solve0,
        [far_send, far_got, columns_own, diag_leaf],
        [rows_half, shaped((half_w, lanes)), shaped((half_r, lanes))],
        after=[p23_send],
    )
    p01_other = swap(p01, "row", 1)

    def term1(meta, x0, p, p_other, b, t1, whole):
        core = core_of(meta)
        whole[at(core, half_w)] = p[...]
        whole[at(1 - core, half_w)] = p_other[...]
        t1[...] = b[...].astype(F32) - dot(x0[...], whole[...])

    t1 = run(
        term1,
        [x0, p01, p01_other, b1],
        shaped((half_r, lanes), F32),
        [pltpu.VMEM((width, lanes), BF16)],
        after=[p23_far],
    )
    panel_far, panel_sent = [], []
    for (level, one, two), got in zip(orders, panel_got):
        def panel_join(meta, p, got, out, level=level, two=two):
            value = panel_value(meta, p, level, two).astype(F32) + got[1].astype(F32)
            out[...] = value.astype(BF16)

        sent = run(
            panel_join, [panel_of(level, two), got], shaped((width, width)), after=[t1]
        )
        panel_sent.append(sent)
        panel_far.append(swap(sent, "leaf", two))

    p23 = p23_own + p23_far
    p23 = (p23.astype(F32) + swap(p23, "leaf", 1).astype(F32)).astype(BF16)
    p23_turned = swap(p23, "leaf", 2)

    def m1_sum(meta, a, b, out):
        out[...] = (a[...] + b[...]).astype(BF16)

    m1 = run(m1_sum, [t1, swap(t1, "leaf", 1)], shaped((half_r, lanes)), after=panel_sent)
    m1 = jnp.concatenate([m1, swap(m1, "row", near)])
    m1_far = swap(m1, "row", far)
    p23 = (p23.astype(F32) + p23_turned.astype(F32)).astype(BF16)
    p23 = jnp.concatenate([p23, swap(p23, "row", near)])
    p23_far = swap(p23, "row", far)

    def p23_place(meta, near_two, far_two, out):
        for m in range(chips):
            source = (near_two, far_two)[m // 2]
            rows = slice((m % 2) * half_w, (m % 2 + 1) * half_w)
            out[:, at(chip_of(meta) ^ m, lanes)] = source[rows]

    p23_half = run(p23_place, [p23, p23_far], shaped((half_w, width)))
    p23_other = swap(p23_half, "row", 1)

    def early(meta, b2, b3, *refs):
        tiles, (got, x0, u, linked) = refs[:4], refs[4:]
        for i, b in enumerate((b2, b3)):
            rows = slice(i * half_r, (i + 1) * half_r)
            value = (side_value(meta, b, 2 + i) + got[rows]).astype(F32)
            start = 2 * half_r + 2 * i * width
            p0 = tile_value(meta, tiles[2 * i], 0, 2 + i) + got[start : start + width]
            u[:, i * width : (i + 1) * width] = value - dot(x0[...], p0)
            start += width
            linked[i] = tile_value(meta, tiles[2 * i + 1], 1, 2 + i) + got[start : start + width]

    u, linked = run(
        early,
        [side(2, 0), side(3, 0)] + [tile(*which) for which in later] + [rest_got, x0],
        [shaped((half_r, 2 * width), F32), shaped((2, width, width))],
        after=[t1],
    )

    def x1_t23(meta, *refs):
        (near_two, far_two, diag, u, linked, x1), outs, whole = refs[:6], refs[6:-1], refs[-1]
        chip = chip_of(meta)
        x = jnp.zeros((half_r, width), F32)
        for m in range(chips):
            part = (near_two, far_two)[m // 2][(m % 2) * half_r : (m % 2 + 1) * half_r]
            x = x + dot(part, diag[at(chip ^ m, lanes)])
        x = x.astype(BF16)
        x1[...] = x
        for i in range(2):
            cols = slice(i * width, (i + 1) * width)
            whole[:, cols] = u[:, cols] - dot(x, linked[i])
        for m, out in enumerate(outs):
            out[...] = whole[at(chip ^ m, part_r)].astype(BF16)

    pair = Picked(diag_pair, (None, width, width), lambda i, *meta: (lax.div(leaf_of(meta), 2), 0, 0))
    strip = shaped((part_r, 2 * width))
    x1, *strips = run(
        x1_t23,
        [m1, m1_far, pair, u, linked],
        [rows_half] + [strip] * chips,
        [pltpu.VMEM((half_r, 2 * width), F32)],
    )
    strips[1:] = [swap(piece, "row", step) for piece, step in zip(strips[1:], steps_up)]
    x01_other = [swap(x, "row", 1) for x in (x0, x1)]

    ways = ((1, 2), (2, 1))

    def leaf_tile(array, level):
        if level is None:
            return Picked(array, (None, height, width), lambda i, *meta: (leaf_of(meta) ^ i, 0, 0))
        return Picked(
            array, (None, None, width, width), lambda i, *meta: (level, leaf_of(meta) ^ i, 0, 0)
        )

    def update01(meta, b, pa, pb, x0, x1, x0_other, x1_other, *refs):
        sends, kept, whole = refs[:2], refs[2:4], refs[4]
        step = pl.program_id(0)
        core = core_of(meta)
        a = leaf_of(meta) ^ step

        @pl.when(step == 0)
        def _():
            for i, (mine, other) in enumerate(((x0, x0_other), (x1, x1_other))):
                whole[i, at(core, half_r)] = mine[...]
                whole[i, at(1 - core, half_r)] = other[...]

        value = b[...].astype(F32)
        for i, p in enumerate((pa, pb)):
            value = value - dot(whole[i], p[...] * keep(live(meta, i, a)))
        for half, (one, two) in enumerate(ways):
            part = value[half * half_r : (half + 1) * half_r]
            for i, m in enumerate((one, one ^ two)):
                @pl.when(step == m)
                def _(half=half, i=i, part=part):
                    sends[half][i] = part.astype(BF16)
            for i, m in enumerate((0, two)):
                @pl.when(step == m)
                def _(half=half, i=i, part=part):
                    kept[half][i] = part

    share_pair = (2, half_r, width)
    share_send0, share_send1, share_kept0, share_kept1 = run(
        update01,
        [leaf_tile(right, None), leaf_tile(panels, 0), leaf_tile(panels, 1), x0, x1] + x01_other,
        [shaped(share_pair)] * 2 + [shaped(share_pair, F32)] * 2,
        [pltpu.VMEM((2, height, width), BF16)],
        steps=n_leaf,
    )
    share_got = [swap(share_send0, "leaf", ways[0][0]), swap(share_send1, "leaf", ways[1][0])]

    def share_join(meta, kept0, kept1, got0, got1, out0, out1):
        for kept, got, out in ((kept0, got0, out0), (kept1, got1, out1)):
            out[...] = (kept[1] + got[1].astype(F32)).astype(BF16)

    share_sent = run(
        share_join, [share_kept0, share_kept1] + share_got, [shaped((half_r, width))] * 2
    )
    share_far = [swap(sent, "leaf", way[1]) for sent, way in zip(share_sent, ways)]

    def t23_sum(meta, *refs):
        value = refs[0][...]
        for ref in refs[1:-1]:
            value = value + ref[...]
        refs[-1][...] = value

    t23 = spread(run(t23_sum, strips, strip, after=[share_send0]))
    t23 = t23.astype(F32) + swap(t23, "leaf", 1).astype(F32)
    t23_far = swap(t23, "leaf", 2)

    def m23_sum(meta, a, b, out):
        out[...] = (a[...] + b[...]).astype(BF16)

    m23 = run(
        m23_sum,
        [t23, t23_far],
        strip,
        after=[p23_half, *share_sent, *panel_far],
    )
    m23_parts = [m23] + [swap(m23, "row", step) for step in steps_up]

    def leaf_sums(meta, pa, pb, ga, gb, fa, fb, k0, k1, g0, g1, f0, f1, panel_out, share_out):
        for i, (p, got, far) in enumerate(((pa, ga, fa), (pb, gb, fb))):
            value = panel_value(meta, p, 2 + i, 0).astype(F32)
            panel_out[i] = (value + got[0].astype(F32) + far[...].astype(F32)).astype(BF16)
        for i, (kept, got, far) in enumerate(((k0, g0, f0), (k1, g1, f1))):
            value = kept[0] + got[0].astype(F32) + far[...].astype(F32)
            share_out[i * half_r : (i + 1) * half_r] = value

    panel_sum, share_sum = run(
        leaf_sums,
        [panel_of(2, 0), panel_of(3, 0)]
        + panel_got
        + panel_far
        + [share_kept0, share_kept1]
        + share_got
        + share_far,
        [shaped((2, width, width)), shaped((height, width), F32)],
    )

    def x2_x3(meta, *refs):
        parts, (diag, p, p_other, out, whole, tile23) = refs[:chips], refs[chips:]
        chip, core = chip_of(meta), core_of(meta)
        for m, part in enumerate(parts):
            whole[at(chip ^ m, part_r)] = part[...]
        tile23[at(core, half_w)] = p[...]
        tile23[at(1 - core, half_w)] = p_other[...]
        x = dot(whole[:, :width], diag[0]).astype(BF16)
        out[0] = x
        merged = whole[:, width:].astype(F32) - dot(x, tile23[...])
        out[1] = dot(merged.astype(BF16), diag[1]).astype(BF16)

    x23 = run(
        x2_x3,
        m23_parts + [diag_root, p23_half, p23_other],
        shaped((2, half_r, width)),
        [pltpu.VMEM((half_r, 2 * width), BF16), pltpu.VMEM((width, width), BF16)],
        after=[share_sum],
    )
    x23_other = swap(x23, "row", 1)

    def final(meta, x0, x1, x0_other, x1_other, x23, x23_other, panel, share, solved, out):
        core = core_of(meta)
        mine, other = at(core, half_r), at(1 - core, half_r)
        for i, (a, b) in enumerate(((x0, x0_other), (x1, x1_other))):
            solved[i, mine] = a[...]
            solved[i, other] = b[...]
        value = share[...]
        for i in range(2):
            solved[2 + i, mine] = x23[i]
            solved[2 + i, other] = x23_other[i]
            value = value - dot(solved[2 + i], panel[i])
        value = value.astype(BF16)
        for i in range(n_leaf):
            out[i] = value

    solved, done = run(
        final,
        [x0, x1] + x01_other + [x23, x23_other, panel_sum, share_sum],
        [shaped((levels, height, width)), shaped((n_leaf, height, width))],
    )
    updated = lax.all_to_all(done, "leaf", 0, 0, tiled=True)
    return solved[:, None], updated


def solution(mesh):
    return jax.shard_map(
        on_device,
        mesh=mesh,
        in_specs=(
            P("leaf", "row", None, None),
            P(None, "leaf", "row", None, None),
            P(None, "leaf", "row"),
            P("leaf", None, None),
            P(),
            P(),
            P(),
        ),
        out_specs=(P(None, "leaf", None, None), P("row", None, None)),
        check_vma=False,
    )
```

time: 142 us -> 124 us (0.87)
  waiting for transfers between devices: 55.4 us -> 35 us
  other arithmetic: 2.74 us -> 0.09 us
  starting transfers between devices: 41 us -> 42.7 us
  blocking collectives: 15.5 us -> 17.2 us
    ppermute x37 -> x34, waiting for transfers between devices: 55.4 us -> 35 us  [swap(): lax.ppermute(block, axis, [(i, i ^ bits) for i in range(lax.axis_size(axi...]
    ppermute x37 -> x34, starting transfers between devices: 41 us -> 42.7 us  [swap(): lax.ppermute(block, axis, [(i, i ^ bits) for i in range(lax.axis_size(axi...]
    all_to_all x1, blocking collectives: 15.5 us -> 17.2 us  [on_device(): updated = lax.all_to_all(done, 'leaf', 0, 0, tiled=True)]
    pallas_call x19 -> x22, Pallas kernels: 21 us -> 22.2 us  [run(): pl.pallas_call(kernel, grid_spec=pltpu.PrefetchScalarGridSpec(num_scalar_...]
    unnamed x18 -> x19, local copies, waits for them, and re-layouts: 4.91 us -> 5.98 us
  transfers between devices with their start and end apart: 37 -> 34, of which waited for: 18 -> 15; matrix products, arithmetic and copies ran while one was open for 0% -> 0% of each run, Pallas kernels for 10% -> 12%
where the time goes in v4:
time: 124 us
  starting transfers between devices  42.7 us (34%)
  waiting for transfers between devices  35 us (28%)
  Pallas kernels  22.2 us (18%)
  blocking collectives  17.2 us (14%)
  local copies, waits for them, and re-layouts  5.98 us (5%)
    ppermute x34, starting transfers between devices, swap(): lax.ppermute(block, axis, [(i, i ^ bits) for i in range(lax.axis_size(axi...  42.7 us
    ppermute x34, waiting for transfers between devices, swap(): lax.ppermute(block, axis, [(i, i ^ bits) for i in range(lax.axis_size(axi...  35 us
    pallas_call x22, Pallas kernels, run(): pl.pallas_call(kernel, grid_spec=pltpu.PrefetchScalarGridSpec(num_scalar_...  22.2 us
    all_to_all x1, blocking collectives, on_device(): updated = lax.all_to_all(done, 'leaf', 0, 0, tiled=True)  17.2 us
    unnamed x19, local copies, waits for them, and re-layouts  5.98 us
  transfers between devices with their start and end apart: 34, of which 15 were waited for; matrix products, arithmetic and copies ran while one was open for 0% of the time, Pallas kernels for 12%

profile of v4, /device:TPU:0, one launch (start us, length us, event | category | flops | bytes accessed | tf_op | source)
XLA Modules:
  0.0 124.1 jit_solution(15024370376332091418)
XLA Ops:
  0.7 2.9 %first_send.1 = bf16[768,512]{1,0:T(8,128)(2,1)} custom-call(s32[4]{0:T(128)} %sup.43, s32[4,4]{1,0:T(4,128)} %bitcast.39, bf16[4,256,512]{2,1,0:T(8,128)(2,1)} %bitcast.30, bf16[4,256,512]{2,1,0:T(8,128)(2,1)} %bitcast.31, bf16[4,4,512,512]{3,2,1,0:T(8,128)(2,1)} %bitcast.6, bf16[4,4,512,512]{3,2,1,0:T(8,128)(2,1)} %bitcast.7), custom_call_target="tpu_custom_call" | custom-call | bytes 1572864 | tf_op jit(solution)/shard_map/first_send/pallas_call | solution.py:121
  4.1 2.1 %collective-permute-done.refs_4_ = bf16[768,512]{1,0:T(8,128)(2,1)S(1)} collective-permute-done((bf16[768,512]{1,0:T(8,128)(2,1)}, bf16[768,512]{1,0:T(8,128)(2,1)S(1)}, u32[]{:S(2)}, u32[]{:S(2)}) %collective-permute-start) | collective-permute-done | bytes 786464 | tf_op jit(solution)/shard_map/ppermute | solution.py:14
  6.2 3.4 %copy-done = bf16[4,1,4,512,512]{4,3,2,1,0:T(8,128)(2,1)S(1)} copy-done((bf16[4,1,4,512,512]{4,3,2,1,0:T(8,128)(2,1)S(1)}, bf16[4,1,4,512,512]{4,3,2,1,0:T(8,128)(2,1)}, u32[]{:S(2)}) %copy-start) | copy-done | bytes 8388632
  9.6 0.9 first_split.1
  10.5 0.7 rest_send.1
  11.8 1.5 %slice-done.1 = s8[4194304]{0:T(1024)(128)(4,1)S(1)} async-done(((s8[8388608]{0:T(1024)(128)(4,1)}), s8[4194304]{0:T(1024)(128)(4,1)S(1)}, s32[]{:S(2)}) %slice-start.1) | async-done | bytes 4194328
  13.9 3.0 %collective-permute-start.8 = (bf16[2,512,512]{2,1,0:T(8,128)(2,1)S(1)}, bf16[2,512,512]{2,1,0:T(8,128)(2,1)S(1)}, u32[]{:S(2)}, u32[]{:S(2)}) collective-permute-start(bf16[2,512,512]{2,1,0:T(8,128)(2,1)S(1)} %panel_send.3), channel_id=1, source_target_pairs={{0,16},{8,24},{16,0},{24,8},{1,17},{9,25},{17,1},{25,9},{2,18},{10... | collective-permute-start | bytes 3145736 | tf_op jit(solution)/shard_map/ppermute | solution.py:14
  17.6 1.6 %collective-permute-start.7 = (bf16[2,512,512]{2,1,0:T(8,128)(2,1)S(1)}, bf16[2,512,512]{2,1,0:T(8,128)(2,1)S(1)}, u32[]{:S(2)}, u32[]{:S(2)}) collective-permute-start(bf16[2,512,512]{2,1,0:T(8,128)(2,1)S(1)} %panel_send.2), channel_id=1, source_target_pairs={{0,8},{8,0},{16,24},{24,16},{1,9},{9,1},{17,25},{25,17},{2,10},{10... | collective-permute-start | bytes 3145736 | tf_op jit(solution)/shard_map/ppermute | solution.py:14
  19.1 1.6 %collective-permute-start.1 = (bf16[1280,128]{1,0:T(8,128)(2,1)S(1)}, bf16[1280,128]{1,0:T(8,128)(2,1)S(1)}, u32[]{:S(2)}, u32[]{:S(2)}) collective-permute-start(bf16[1280,128]{1,0:T(8,128)(2,1)S(1)} %get-tuple-element.31.refs_2_.refs_6_), channel_id=1, source_target_pairs={{0,2},{1,3},{2,0},{3,1},{4,6},{5,7},{6,4},{7,5},{8,10},{9,11},{10,... | collective-permute-start | bytes 983048 | tf_op jit(solution)/shard_map/ppermute | solution.py:14
  20.7 7.6 %collective-permute-done.1.refs_1_ = bf16[1280,128]{1,0:T(8,128)(2,1)S(1)} collective-permute-done((bf16[1280,128]{1,0:T(8,128)(2,1)S(1)}, bf16[1280,128]{1,0:T(8,128)(2,1)S(1)}, u32[]{:S(2)}, u32[]{:S(2)}) %collective-permute-start.1) | collective-permute-done | bytes 327712 | tf_op jit(solution)/shard_map/ppermute | solution.py:14
  28.9 2.7 %collective-permute-start.2 = (bf16[896,128]{1,0:T(8,128)(2,1)S(1)}, bf16[896,128]{1,0:T(8,128)(2,1)S(1)}, u32[]{:S(2)}, u32[]{:S(2)}) collective-permute-start(bf16[896,128]{1,0:T(8,128)(2,1)S(1)} %get-tuple-element.32.refs_2_.refs_0_), channel_id=1, source_target_pairs={{0,4},{1,5},{2,6},{3,7},{4,0},{5,1},{6,2},{7,3},{8,12},{9,13},{10,... | collective-permute-start | bytes 688136 | tf_op jit(solution)/shard_map/ppermute | solution.py:14
  31.6 1.6 %collective-permute-start.3 = (bf16[512,128]{1,0:T(8,128)(2,1)S(1)}, bf16[512,128]{1,0:T(8,128)(2,1)S(1)}, u32[]{:S(2)}, u32[]{:S(2)}) collective-permute-start(bf16[512,128]{1,0:T(8,128)(2,1)S(1)} %get-tuple-element.35), channel_id=1, source_target_pairs={{0,2},{1,3},{2,0},{3,1},{4,6},{5,7},{6,4},{7,5},{8,10},{9,11},{10,... | collective-permute-start | bytes 393224 | tf_op jit(solution)/shard_map/ppermute | solution.py:14
  33.2 5.0 %collective-permute-done.3.refs_1_ = bf16[512,128]{1,0:T(8,128)(2,1)S(1)} collective-permute-done((bf16[512,128]{1,0:T(8,128)(2,1)S(1)}, bf16[512,128]{1,0:T(8,128)(2,1)S(1)}, u32[]{:S(2)}, u32[]{:S(2)}) %collective-permute-start.3) | collective-permute-done | bytes 131104 | tf_op jit(solution)/shard_map/ppermute | solution.py:14
  38.7 2.4 %collective-permute-start.5 = (bf16[256,128]{1,0:T(8,128)(2,1)S(1)}, bf16[256,128]{1,0:T(8,128)(2,1)S(1)}, u32[]{:S(2)}, u32[]{:S(2)}) collective-permute-start(bf16[256,128]{1,0:T(8,128)(2,1)S(1)} %get-tuple-element.36.refs_4_), channel_id=1, source_target_pairs={{0,4},{1,5},{2,6},{3,7},{4,0},{5,1},{6,2},{7,3},{8,12},{9,13},{10,... | collective-permute-start | bytes 196616 | tf_op jit(solution)/shard_map/ppermute | solution.py:14
  41.7 0.8 solve0.1
  42.6 1.3 %collective-permute-done.5.refs_4_ = bf16[256,128]{1,0:T(8,128)(2,1)S(1)} collective-permute-done((bf16[256,128]{1,0:T(8,128)(2,1)S(1)}, bf16[256,128]{1,0:T(8,128)(2,1)S(1)}, u32[]{:S(2)}, u32[]{:S(2)}) %collective-permute-start.5) | collective-permute-done | bytes 65568 | tf_op jit(solution)/shard_map/ppermute | solution.py:14
  44.0 0.8 term1.1.refs_2_.refs_0_.refs_8_
  45.4 1.6 %collective-permute-start.19 = (bf16[256,128]{1,0:T(8,128)(2,1)S(1)}, bf16[256,128]{1,0:T(8,128)(2,1)S(1)}, u32[]{:S(2)}, u32[]{:S(2)}) collective-permute-start(bf16[256,128]{1,0:T(8,128)(2,1)S(1)} %add.13), channel_id=1, source_target_pairs={{0,8},{8,0},{16,24},{24,16},{1,9},{9,1},{17,25},{25,17},{2,10},{10... | collective-permute-start | bytes 196616 | tf_op jit(solution)/shard_map/ppermute | solution.py:14
  48.4 1.1 collective-permute-done.6.refs_1_
  50.1 2.1 %collective-permute-start.9 = (bf16[128,128]{1,0:T(8,128)(2,1)S(1)}, bf16[128,128]{1,0:T(8,128)(2,1)S(1)}, u32[]{:S(2)}, u32[]{:S(2)}) collective-permute-start(bf16[128,128]{1,0:T(8,128)(2,1)S(1)} %m1_sum.1), channel_id=1, source_target_pairs={{0,2},{1,3},{2,0},{3,1},{4,6},{5,7},{6,4},{7,5},{8,10},{9,11},{10,... | collective-permute-start | bytes 98312 | tf_op jit(solution)/shard_map/ppermute | solution.py:14
  52.8 1.3 %collective-permute-done.9 = bf16[128,128]{1,0:T(8,128)(2,1)S(1)} collective-permute-done((bf16[128,128]{1,0:T(8,128)(2,1)S(1)}, bf16[128,128]{1,0:T(8,128)(2,1)S(1)}, u32[]{:S(2)}, u32[]{:S(2)}) %collective-permute-start.9) | collective-permute-done | bytes 32800 | tf_op jit(solution)/shard_map/ppermute | solution.py:14
  54.1 2.1 %collective-permute-start.10 = (bf16[256,128]{1,0:T(8,128)(2,1)S(1)}, bf16[256,128]{1,0:T(8,128)(2,1)S(1)}, u32[]{:S(2)}, u32[]{:S(2)}) collective-permute-start(bf16[256,128]{1,0:T(8,128)(2,1)S(1)} %pad_maximum_fusion.1.refs_0_), channel_id=1, source_target_pairs={{0,4},{1,5},{2,6},{3,7},{4,0},{5,1},{6,2},{7,3},{8,12},{9,13},{10,... | collective-permute-start | bytes 196616 | tf_op jit(solution)/shard_map/ppermute | solution.py:14
  56.6 1.8 %collective-permute-start.21 = (bf16[256,128]{1,0:T(8,128)(2,1)S(1)}, bf16[256,128]{1,0:T(8,128)(2,1)S(1)}, u32[]{:S(2)}, u32[]{:S(2)}) collective-permute-start(bf16[256,128]{1,0:T(8,128)(2,1)S(1)} %add_convert_fusion), channel_id=1, source_target_pairs={{0,2},{1,3},{2,0},{3,1},{4,6},{5,7},{6,4},{7,5},{8,10},{9,11},{10,... | collective-permute-start | bytes 196616 | tf_op jit(solution)/shard_map/ppermute | solution.py:14
  58.6 1.1 early.1
  59.7 1.1 x1_t23.1
  61.2 1.3 %collective-permute-start.14 = (bf16[32,1024]{1,0:T(8,128)(2,1)S(1)}, bf16[32,1024]{1,0:T(8,128)(2,1)S(1)}, u32[]{:S(2)}, u32[]{:S(2)}) collective-permute-start(bf16[32,1024]{1,0:T(8,128)(2,1)S(1)} %get-tuple-element.44), channel_id=1, source_target_pairs={{0,2},{1,3},{2,0},{3,1},{4,6},{5,7},{6,4},{7,5},{8,10},{9,11},{10,... | collective-permute-start | bytes 196616 | tf_op jit(solution)/shard_map/ppermute | solution.py:14
  62.6 2.5 %collective-permute-start.22 = (bf16[512,128]{1,0:T(8,128)(2,1)S(1)}, bf16[512,128]{1,0:T(8,128)(2,1)S(1)}, u32[]{:S(2)}, u32[]{:S(2)}) collective-permute-start(bf16[512,128]{1,0:T(8,128)(2,1)S(1)} %pad_maximum_fusion.refs_0_), channel_id=1, source_target_pairs={{0,4},{1,5},{2,6},{3,7},{4,0},{5,1},{6,2},{7,3},{8,12},{9,13},{10,... | collective-permute-start | bytes 393224 | tf_op jit(solution)/shard_map/ppermute | solution.py:14
  65.6 2.6 %collective-permute-start.15 = (bf16[32,1024]{1,0:T(8,128)(2,1)S(1)}, bf16[32,1024]{1,0:T(8,128)(2,1)S(1)}, u32[]{:S(2)}, u32[]{:S(2)}) collective-permute-start(bf16[32,1024]{1,0:T(8,128)(2,1)S(1)} %get-tuple-element.45), channel_id=1, source_target_pairs={{0,4},{1,5},{2,6},{3,7},{4,0},{5,1},{6,2},{7,3},{8,12},{9,13},{10,... | collective-permute-start | bytes 196616 | tf_op jit(solution)/shard_map/ppermute | solution.py:14
  68.2 1.9 %collective-permute-start.16 = (bf16[32,1024]{1,0:T(8,128)(2,1)S(1)}, bf16[32,1024]{1,0:T(8,128)(2,1)S(1)}, u32[]{:S(2)}, u32[]{:S(2)}) collective-permute-start(bf16[32,1024]{1,0:T(8,128)(2,1)S(1)} %get-tuple-element.46), channel_id=1, source_target_pairs={{0,6},{1,7},{2,4},{3,5},{4,2},{5,3},{6,0},{7,1},{8,14},{9,15},{10,... | collective-permute-start | bytes 196616 | tf_op jit(solution)/shard_map/ppermute | solution.py:14
  70.1 2.7 %update01.1 = (bf16[2,128,512]{2,1,0:T(8,128)(2,1)S(1)}, bf16[2,128,512]{2,1,0:T(8,128)(2,1)S(1)}, f32[2,128,512]{2,1,0:T(8,128)S(1)}, f32[2,128,512]{2,1,0:T(8,128)S(1)}) custom-call(s32[4]{0:T(128)S(1)} %copy-done.6, s32[4,4]{1,0:T(4,128)S(1)} %bitcast.53, bf16[4,256,512]{2,1,0:T(8,128)(2,1)S(1)} %bitcast.38, bf16[4,4,512,512]{3,2,1,0:T(8,128)(2,1)S(1)} %bitcast.26, ...), custom_call_target="tpu_custom_call" | custom-call | bytes 8912896 | tf_op jit(solution)/shard_map/update01/pallas_call | solution.py:121
  72.8 4.0 %collective-permute-done.15.refs_2_ = bf16[32,1024]{1,0:T(8,128)(2,1)S(1)} collective-permute-done((bf16[32,1024]{1,0:T(8,128)(2,1)S(1)}, bf16[32,1024]{1,0:T(8,128)(2,1)S(1)}, u32[]{:S(2)}, u32[]{:S(2)}) %collective-permute-start.15) | collective-permute-done | bytes 65568 | tf_op jit(solution)/shard_map/ppermute | solution.py:14
  78.1 1.4 %collective-permute-start.23 = (bf16[2,128,512]{2,1,0:T(8,128)(2,1)S(1)}, bf16[2,128,512]{2,1,0:T(8,128)(2,1)S(1)}, u32[]{:S(2)}, u32[]{:S(2)}) collective-permute-start(bf16[2,128,512]{2,1,0:T(8,128)(2,1)S(1)} %get-tuple-element.47.refs_4_), channel_id=1, source_target_pairs={{0,8},{8,0},{16,24},{24,16},{1,9},{9,1},{17,25},{25,17},{2,10},{10... | collective-permute-start | bytes 786440 | tf_op jit(solution)/shard_map/ppermute | solution.py:14
  80.6 1.9 %collective-permute-done.17 = bf16[32,1024]{1,0:T(8,128)(2,1)S(1)} collective-permute-done((bf16[32,1024]{1,0:T(8,128)(2,1)S(1)}, bf16[32,1024]{1,0:T(8,128)(2,1)S(1)}, u32[]{:S(2)}, u32[]{:S(2)}) %collective-permute-start.17) | collective-permute-done | bytes 65568 | tf_op jit(solution)/shard_map/ppermute | solution.py:14
  82.5 3.4 %collective-permute-done.23.refs_2_.refs_8_ = bf16[2,128,512]{2,1,0:T(8,128)(2,1)S(1)} collective-permute-done((bf16[2,128,512]{2,1,0:T(8,128)(2,1)S(1)}, bf16[2,128,512]{2,1,0:T(8,128)(2,1)S(1)}, u32[]{:S(2)}, u32[]{:S(2)}) %collective-permute-start.23) | collective-permute-done | bytes 262176 | tf_op jit(solution)/shard_map/ppermute | solution.py:14
  87.0 1.6 %collective-permute-start.31 = (bf16[128,512]{1,0:T(8,128)(2,1)S(1)}, bf16[128,512]{1,0:T(8,128)(2,1)S(1)}, u32[]{:S(2)}, u32[]{:S(2)}) collective-permute-start(bf16[128,512]{1,0:T(8,128)(2,1)S(1)} %get-tuple-element.52.refs_3_), channel_id=1, source_target_pairs={{0,16},{8,24},{16,0},{24,8},{1,17},{9,25},{17,1},{25,9},{2,18},{10... | collective-permute-start | bytes 393224 | tf_op jit(solution)/shard_map/ppermute | solution.py:14
  88.6 1.0 collective-permute-start.32
  89.7 1.2 collective-permute-done.18.refs_1_
  91.5 2.4 %collective-permute-start.27 = (bf16[32,1024]{1,0:T(8,128)(2,1)S(1)}, bf16[32,1024]{1,0:T(8,128)(2,1)S(1)}, u32[]{:S(2)}, u32[]{:S(2)}) collective-permute-start(bf16[32,1024]{1,0:T(8,128)(2,1)S(1)} %m23_sum.1.refs_0_), channel_id=1, source_target_pairs={{0,2},{1,3},{2,0},{3,1},{4,6},{5,7},{6,4},{7,5},{8,10},{9,11},{10,... | collective-permute-start | bytes 196616 | tf_op jit(solution)/shard_map/ppermute | solution.py:14
  93.9 1.2 collective-permute-start.28
  95.1 1.4 %collective-permute-start.29 = (bf16[32,1024]{1,0:T(8,128)(2,1)S(1)}, bf16[32,1024]{1,0:T(8,128)(2,1)S(1)}, u32[]{:S(2)}, u32[]{:S(2)}) collective-permute-start(bf16[32,1024]{1,0:T(8,128)(2,1)S(1)} %m23_sum.1.refs_0_), channel_id=1, source_target_pairs={{0,6},{1,7},{2,4},{3,5},{4,2},{5,3},{6,0},{7,1},{8,14},{9,15},{10,... | collective-permute-start | bytes 196616 | tf_op jit(solution)/shard_map/ppermute | solution.py:14
  96.5 1.1 leaf_sums.1
  97.5 2.2 %collective-permute-done.28.refs_2_ = bf16[32,1024]{1,0:T(8,128)(2,1)S(1)} collective-permute-done((bf16[32,1024]{1,0:T(8,128)(2,1)S(1)}, bf16[32,1024]{1,0:T(8,128)(2,1)S(1)}, u32[]{:S(2)}, u32[]{:S(2)}) %collective-permute-start.28) | collective-permute-done | bytes 65568 | tf_op jit(solution)/shard_map/ppermute | solution.py:14
  99.7 1.5 %collective-permute-done.29.refs_3_ = bf16[32,1024]{1,0:T(8,128)(2,1)S(1)} collective-permute-done((bf16[32,1024]{1,0:T(8,128)(2,1)S(1)}, bf16[32,1024]{1,0:T(8,128)(2,1)S(1)}, u32[]{:S(2)}, u32[]{:S(2)}) %collective-permute-start.29) | collective-permute-done | bytes 65568 | tf_op jit(solution)/shard_map/ppermute | solution.py:14
  101.2 1.2 x2_x3.1.refs_4_
  102.5 1.5 %collective-permute-done.33.refs_5_ = bf16[2,128,512]{2,1,0:T(8,128)(2,1)S(1)} collective-permute-done((bf16[2,128,512]{2,1,0:T(8,128)(2,1)S(1)}, bf16[2,128,512]{2,1,0:T(8,128)(2,1)S(1)}, u32[]{:S(2)}, u32[]{:S(2)}) %collective-permute-start.33) | collective-permute-done | bytes 262176 | tf_op jit(solution)/shard_map/ppermute | solution.py:14
  104.0 2.0 %final.1 = (bf16[4,256,512]{2,1,0:T(8,128)(2,1)}, bf16[4,256,512]{2,1,0:T(8,128)(2,1)S(1)}) custom-call(s32[4]{0:T(128)S(1)} %copy-done.6, s32[4,4]{1,0:T(4,128)S(1)} %bitcast.60, bf16[128,512]{1,0:T(8,128)(2,1)S(1)} %get-tuple-element.37.refs_0_.refs_7_.refs_3_, bf16[128,512]{1,0:T(8,128)(2,1)S(1)} %get-tuple-element.42.refs_4_.refs_1_, ...), custom_call_target="tpu_custom_call" | custom-call | bytes 4718592 | tf_op jit(solution)/shard_map/final/pallas_call | solution.py:121
  106.0 17.2 %all_to_all.5 = bf16[4,256,512]{2,1,0:T(8,128)(2,1)S(1)} all-to-all(bf16[4,256,512]{2,1,0:T(8,128)(2,1)S(1)} %get-tuple-element.57), channel_id=1, replica_groups=mesh['leaf'=4,'row'=8] {'leaf'}, dimensions={0} | all-to-all | bytes 2097152 | tf_op jit(solution)/shard_map/all_to_all | solution.py:515
  123.1 1.0 copy.11
  (69 shorter events, 13.0 us)
Async XLA Ops:
  0.6 5.6 %copy-start.1 = (bf16[1,4,256,512]{3,2,1,0:T(8,128)(2,1)S(1)}, bf16[1,4,256,512]{3,2,1,0:T(8,128)(2,1)}, u32[]{:S(2)}) copy-start(bf16[1,4,256,512]{3,2,1,0:T(8,128)(2,1)} %param.7) | copy-start | bytes 3145732
  0.6 5.5 %copy-start.4 = (s32[4,1,4]{2,1,0:T(1,128)S(1)}, s32[4,1,4]{2,1,0:T(1,128)}, u32[]{:S(2)}) copy-start(s32[4,1,4]{2,1,0:T(1,128)} %param.9) | copy-start | bytes 196
  0.6 5.5 %copy-start.6 = (s32[4]{0:T(128)S(1)}, s32[4]{0:T(128)}, u32[]{:S(2)}) copy-start(s32[4]{0:T(128)} %sup.43) | copy-start | bytes 52
  3.6 2.6 %collective-permute-start = (bf16[768,512]{1,0:T(8,128)(2,1)}, bf16[768,512]{1,0:T(8,128)(2,1)S(1)}, u32[]{:S(2)}, u32[]{:S(2)}) collective-permute-start(bf16[768,512]{1,0:T(8,128)(2,1)} %first_send.1), channel_id=1, source_target_pairs={{0,1},{1,0},{2,3},{3,2},{4,5},{5,4},{6,7},{7,6},{8,9},{9,8},{10,11... | collective-permute-start | bytes 2359304 | tf_op jit(solution)/shard_map/ppermute | solution.py:14
  6.2 3.4 %copy-start = (bf16[4,1,4,512,512]{4,3,2,1,0:T(8,128)(2,1)S(1)}, bf16[4,1,4,512,512]{4,3,2,1,0:T(8,128)(2,1)}, u32[]{:S(2)}) copy-start(bf16[4,1,4,512,512]{4,3,2,1,0:T(8,128)(2,1)} %param.8) | copy-start | bytes 25165828
  9.6 2.2 %slice-start = ((s8[8388608]{0:T(1024)(128)(4,1)}), s8[4194304]{0:T(1024)(128)(4,1)S(1)}, s32[]{:S(2)}) async-start(s8[8388608]{0:T(1024)(128)(4,1)} %bitcast.14), calls=%async_computation.1 | async-start | bytes 8388608
  10.5 2.8 %slice-start.1 = ((s8[8388608]{0:T(1024)(128)(4,1)}), s8[4194304]{0:T(1024)(128)(4,1)S(1)}, s32[]{:S(2)}) async-start(s8[8388608]{0:T(1024)(128)(4,1)} %bitcast.14), calls=%async_computation.2 | async-start | bytes 8388608
  11.2 47.4 %collective-permute-start.11 = (bf16[2304,512]{1,0:T(8,128)(2,1)S(1)}, bf16[2304,512]{1,0:T(8,128)(2,1)S(1)}, u32[]{:S(2)}, u32[]{:S(2)}) collective-permute-start(bf16[2304,512]{1,0:T(8,128)(2,1)S(1)} %rest_send.1), channel_id=1, source_target_pairs={{0,1},{1,0},{2,3},{3,2},{4,5},{5,4},{6,7},{7,6},{8,9},{9,8},{10,11... | collective-permute-start | bytes 7077896 | tf_op jit(solution)/shard_map/ppermute | solution.py:14
  13.9 27.8 %copy-start.5 = (bf16[1,512,512]{2,1,0:T(8,128)(2,1)S(1)}, bf16[1,512,512]{2,1,0:T(8,128)(2,1)}, u32[]{:S(2)}) copy-start(bf16[1,512,512]{2,1,0:T(8,128)(2,1)} %refs_3_.1) | copy-start | bytes 1572868
  13.9 33.0 %collective-permute-start.8 = (bf16[2,512,512]{2,1,0:T(8,128)(2,1)S(1)}, bf16[2,512,512]{2,1,0:T(8,128)(2,1)S(1)}, u32[]{:S(2)}, u32[]{:S(2)}) collective-permute-start(bf16[2,512,512]{2,1,0:T(8,128)(2,1)S(1)} %panel_send.3), channel_id=1, source_target_pairs={{0,16},{8,24},{16,0},{24,8},{1,17},{9,25},{17,1},{25,9},{2,18},{10... | collective-permute-start | bytes 3145736 | tf_op jit(solution)/shard_map/ppermute | solution.py:14
  17.6 30.1 %collective-permute-start.7 = (bf16[2,512,512]{2,1,0:T(8,128)(2,1)S(1)}, bf16[2,512,512]{2,1,0:T(8,128)(2,1)S(1)}, u32[]{:S(2)}, u32[]{:S(2)}) collective-permute-start(bf16[2,512,512]{2,1,0:T(8,128)(2,1)S(1)} %panel_send.2), channel_id=1, source_target_pairs={{0,8},{8,0},{16,24},{24,16},{1,9},{9,1},{17,25},{25,17},{2,10},{10... | collective-permute-start | bytes 3145736 | tf_op jit(solution)/shard_map/ppermute | solution.py:14
  19.1 9.2 %collective-permute-start.1 = (bf16[1280,128]{1,0:T(8,128)(2,1)S(1)}, bf16[1280,128]{1,0:T(8,128)(2,1)S(1)}, u32[]{:S(2)}, u32[]{:S(2)}) collective-permute-start(bf16[1280,128]{1,0:T(8,128)(2,1)S(1)} %get-tuple-element.31.refs_2_.refs_6_), channel_id=1, source_target_pairs={{0,2},{1,3},{2,0},{3,1},{4,6},{5,7},{6,4},{7,5},{8,10},{9,11},{10,... | collective-permute-start | bytes 983048 | tf_op jit(solution)/shard_map/ppermute | solution.py:14
  28.9 12.8 %collective-permute-start.2 = (bf16[896,128]{1,0:T(8,128)(2,1)S(1)}, bf16[896,128]{1,0:T(8,128)(2,1)S(1)}, u32[]{:S(2)}, u32[]{:S(2)}) collective-permute-start(bf16[896,128]{1,0:T(8,128)(2,1)S(1)} %get-tuple-element.32.refs_2_.refs_0_), channel_id=1, source_target_pairs={{0,4},{1,5},{2,6},{3,7},{4,0},{5,1},{6,2},{7,3},{8,12},{9,13},{10,... | collective-permute-start | bytes 688136 | tf_op jit(solution)/shard_map/ppermute | solution.py:14
  31.6 6.5 %collective-permute-start.3 = (bf16[512,128]{1,0:T(8,128)(2,1)S(1)}, bf16[512,128]{1,0:T(8,128)(2,1)S(1)}, u32[]{:S(2)}, u32[]{:S(2)}) collective-permute-start(bf16[512,128]{1,0:T(8,128)(2,1)S(1)} %get-tuple-element.35), channel_id=1, source_target_pairs={{0,2},{1,3},{2,0},{3,1},{4,6},{5,7},{6,4},{7,5},{8,10},{9,11},{10,... | collective-permute-start | bytes 393224 | tf_op jit(solution)/shard_map/ppermute | solution.py:14
  38.7 5.2 %collective-permute-start.5 = (bf16[256,128]{1,0:T(8,128)(2,1)S(1)}, bf16[256,128]{1,0:T(8,128)(2,1)S(1)}, u32[]{:S(2)}, u32[]{:S(2)}) collective-permute-start(bf16[256,128]{1,0:T(8,128)(2,1)S(1)} %get-tuple-element.36.refs_4_), channel_id=1, source_target_pairs={{0,4},{1,5},{2,6},{3,7},{4,0},{5,1},{6,2},{7,3},{8,12},{9,13},{10,... | collective-permute-start | bytes 196616 | tf_op jit(solution)/shard_map/ppermute | solution.py:14
  42.6 1.4 %collective-permute-start.4 = (bf16[256,128]{1,0:T(8,128)(2,1)S(1)}, bf16[256,128]{1,0:T(8,128)(2,1)S(1)}, u32[]{:S(2)}, u32[]{:S(2)}) collective-permute-start(bf16[256,128]{1,0:T(8,128)(2,1)S(1)} %get-tuple-element.38.refs_1_), channel_id=1, source_target_pairs={{0,1},{1,0},{2,3},{3,2},{4,5},{5,4},{6,7},{7,6},{8,9},{9,8},{10,11... | collective-permute-start | bytes 196616 | tf_op jit(solution)/shard_map/ppermute | solution.py:14
  44.7 4.8 %collective-permute-start.6 = (f32[128,128]{1,0:T(8,128)S(1)}, f32[128,128]{1,0:T(8,128)S(1)}, u32[]{:S(2)}, u32[]{:S(2)}) collective-permute-start(f32[128,128]{1,0:T(8,128)S(1)} %term1.1.refs_2_.refs_0_.refs_8_), channel_id=1, source_target_pairs={{0,8},{8,0},{16,24},{24,16},{1,9},{9,1},{17,25},{25,17},{2,10},{10... | collective-permute-start | bytes 196616 | tf_op jit(solution)/shard_map/ppermute | solution.py:14
  45.4 6.8 %collective-permute-start.19 = (bf16[256,128]{1,0:T(8,128)(2,1)S(1)}, bf16[256,128]{1,0:T(8,128)(2,1)S(1)}, u32[]{:S(2)}, u32[]{:S(2)}) collective-permute-start(bf16[256,128]{1,0:T(8,128)(2,1)S(1)} %add.13), channel_id=1, source_target_pairs={{0,8},{8,0},{16,24},{24,16},{1,9},{9,1},{17,25},{25,17},{2,10},{10... | collective-permute-start | bytes 196616 | tf_op jit(solution)/shard_map/ppermute | solution.py:14
  50.1 4.0 %collective-permute-start.9 = (bf16[128,128]{1,0:T(8,128)(2,1)S(1)}, bf16[128,128]{1,0:T(8,128)(2,1)S(1)}, u32[]{:S(2)}, u32[]{:S(2)}) collective-permute-start(bf16[128,128]{1,0:T(8,128)(2,1)S(1)} %m1_sum.1), channel_id=1, source_target_pairs={{0,2},{1,3},{2,0},{3,1},{4,6},{5,7},{6,4},{7,5},{8,10},{9,11},{10,... | collective-permute-start | bytes 98312 | tf_op jit(solution)/shard_map/ppermute | solution.py:14
  52.2 4.3 %collective-permute-start.20 = (bf16[256,128]{1,0:T(8,128)(2,1)S(1)}, bf16[256,128]{1,0:T(8,128)(2,1)S(1)}, u32[]{:S(2)}, u32[]{:S(2)}) collective-permute-start(bf16[256,128]{1,0:T(8,128)(2,1)S(1)} %add_convert_fusion.1), channel_id=1, source_target_pairs={{0,16},{8,24},{16,0},{24,8},{1,17},{9,25},{17,1},{25,9},{2,18},{10... | collective-permute-start | bytes 196616 | tf_op jit(solution)/shard_map/ppermute | solution.py:14
  54.1 5.5 %collective-permute-start.10 = (bf16[256,128]{1,0:T(8,128)(2,1)S(1)}, bf16[256,128]{1,0:T(8,128)(2,1)S(1)}, u32[]{:S(2)}, u32[]{:S(2)}) collective-permute-start(bf16[256,128]{1,0:T(8,128)(2,1)S(1)} %pad_maximum_fusion.1.refs_0_), channel_id=1, source_target_pairs={{0,4},{1,5},{2,6},{3,7},{4,0},{5,1},{6,2},{7,3},{8,12},{9,13},{10,... | collective-permute-start | bytes 196616 | tf_op jit(solution)/shard_map/ppermute | solution.py:14
  56.6 3.1 %copy-start.3 = (bf16[2,512,512]{2,1,0:T(8,128)(2,1)S(1)}, bf16[2,512,512]{2,1,0:T(8,128)(2,1)}, u32[]{:S(2)}) copy-start(bf16[2,512,512]{2,1,0:T(8,128)(2,1)} %refs_2_.1) | copy-start | bytes 3145732
  56.6 6.0 %collective-permute-start.21 = (bf16[256,128]{1,0:T(8,128)(2,1)S(1)}, bf16[256,128]{1,0:T(8,128)(2,1)S(1)}, u32[]{:S(2)}, u32[]{:S(2)}) collective-permute-start(bf16[256,128]{1,0:T(8,128)(2,1)S(1)} %add_convert_fusion), channel_id=1, source_target_pairs={{0,2},{1,3},{2,0},{3,1},{4,6},{5,7},{6,4},{7,5},{8,10},{9,11},{10,... | collective-permute-start | bytes 196616 | tf_op jit(solution)/shard_map/ppermute | solution.py:14
  58.4 6.7 %collective-permute-start.12 = (bf16[128,512]{1,0:T(8,128)(2,1)S(1)}, bf16[128,512]{1,0:T(8,128)(2,1)S(1)}, u32[]{:S(2)}, u32[]{:S(2)}) collective-permute-start(bf16[128,512]{1,0:T(8,128)(2,1)S(1)} %get-tuple-element.37.refs_0_.refs_7_.refs_3_), channel_id=1, source_target_pairs={{0,1},{1,0},{2,3},{3,2},{4,5},{5,4},{6,7},{7,6},{8,9},{9,8},{10,11... | collective-permute-start | bytes 393224 | tf_op jit(solution)/shard_map/ppermute | solution.py:14
  58.4 30.2 %collective-permute-start.26 = (bf16[512,512]{1,0:T(8,128)(2,1)S(1)}, bf16[512,512]{1,0:T(8,128)(2,1)S(1)}, u32[]{:S(2)}, u32[]{:S(2)}) collective-permute-start(bf16[512,512]{1,0:T(8,128)(2,1)S(1)} %panel_join.3.refs_3_), channel_id=1, source_target_pairs={{0,8},{8,0},{16,24},{24,16},{1,9},{9,1},{17,25},{25,17},{2,10},{10... | collective-permute-start | bytes 1572872 | tf_op jit(solution)/shard_map/ppermute | solution.py:14
  60.8 7.4 %collective-permute-start.13 = (bf16[128,512]{1,0:T(8,128)(2,1)S(1)}, bf16[128,512]{1,0:T(8,128)(2,1)S(1)}, u32[]{:S(2)}, u32[]{:S(2)}) collective-permute-start(bf16[128,512]{1,0:T(8,128)(2,1)S(1)} %get-tuple-element.42.refs_4_.refs_1_), channel_id=1, source_target_pairs={{0,1},{1,0},{2,3},{3,2},{4,5},{5,4},{6,7},{7,6},{8,9},{9,8},{10,11... | collective-permute-start | bytes 393224 | tf_op jit(solution)/shard_map/ppermute | solution.py:14
  61.2 4.4 %collective-permute-start.14 = (bf16[32,1024]{1,0:T(8,128)(2,1)S(1)}, bf16[32,1024]{1,0:T(8,128)(2,1)S(1)}, u32[]{:S(2)}, u32[]{:S(2)}) collective-permute-start(bf16[32,1024]{1,0:T(8,128)(2,1)S(1)} %get-tuple-element.44), channel_id=1, source_target_pairs={{0,2},{1,3},{2,0},{3,1},{4,6},{5,7},{6,4},{7,5},{8,10},{9,11},{10,... | collective-permute-start | bytes 196616 | tf_op jit(solution)/shard_map/ppermute | solution.py:14
  62.6 16.9 %collective-permute-start.22 = (bf16[512,128]{1,0:T(8,128)(2,1)S(1)}, bf16[512,128]{1,0:T(8,128)(2,1)S(1)}, u32[]{:S(2)}, u32[]{:S(2)}) collective-permute-start(bf16[512,128]{1,0:T(8,128)(2,1)S(1)} %pad_maximum_fusion.refs_0_), channel_id=1, source_target_pairs={{0,4},{1,5},{2,6},{3,7},{4,0},{5,1},{6,2},{7,3},{8,12},{9,13},{10,... | collective-permute-start | bytes 393224 | tf_op jit(solution)/shard_map/ppermute | solution.py:14
  65.1 24.6 %collective-permute-start.25 = (bf16[512,512]{1,0:T(8,128)(2,1)S(1)}, bf16[512,512]{1,0:T(8,128)(2,1)S(1)}, u32[]{:S(2)}, u32[]{:S(2)}) collective-permute-start(bf16[512,512]{1,0:T(8,128)(2,1)S(1)} %panel_join.2.refs_2_), channel_id=1, source_target_pairs={{0,16},{8,24},{16,0},{24,8},{1,17},{9,25},{17,1},{25,9},{2,18},{10... | collective-permute-start | bytes 1572872 | tf_op jit(solution)/shard_map/ppermute | solution.py:14
  65.6 11.2 %collective-permute-start.15 = (bf16[32,1024]{1,0:T(8,128)(2,1)S(1)}, bf16[32,1024]{1,0:T(8,128)(2,1)S(1)}, u32[]{:S(2)}, u32[]{:S(2)}) collective-permute-start(bf16[32,1024]{1,0:T(8,128)(2,1)S(1)} %get-tuple-element.45), channel_id=1, source_target_pairs={{0,4},{1,5},{2,6},{3,7},{4,0},{5,1},{6,2},{7,3},{8,12},{9,13},{10,... | collective-permute-start | bytes 196616 | tf_op jit(solution)/shard_map/ppermute | solution.py:14
  68.2 8.6 %collective-permute-start.16 = (bf16[32,1024]{1,0:T(8,128)(2,1)S(1)}, bf16[32,1024]{1,0:T(8,128)(2,1)S(1)}, u32[]{:S(2)}, u32[]{:S(2)}) collective-permute-start(bf16[32,1024]{1,0:T(8,128)(2,1)S(1)} %get-tuple-element.46), channel_id=1, source_target_pairs={{0,6},{1,7},{2,4},{3,5},{4,2},{5,3},{6,0},{7,1},{8,14},{9,15},{10,... | collective-permute-start | bytes 196616 | tf_op jit(solution)/shard_map/ppermute | solution.py:14
  77.4 5.1 %collective-permute-start.17 = (bf16[32,1024]{1,0:T(8,128)(2,1)S(1)}, bf16[32,1024]{1,0:T(8,128)(2,1)S(1)}, u32[]{:S(2)}, u32[]{:S(2)}) collective-permute-start(bf16[32,1024]{1,0:T(8,128)(2,1)S(1)} %t23_sum.1), channel_id=1, source_target_pairs={{0,8},{8,0},{16,24},{24,16},{1,9},{9,1},{17,25},{25,17},{2,10},{10... | collective-permute-start | bytes 196616 | tf_op jit(solution)/shard_map/ppermute | solution.py:14
  78.1 7.8 %collective-permute-start.23 = (bf16[2,128,512]{2,1,0:T(8,128)(2,1)S(1)}, bf16[2,128,512]{2,1,0:T(8,128)(2,1)S(1)}, u32[]{:S(2)}, u32[]{:S(2)}) collective-permute-start(bf16[2,128,512]{2,1,0:T(8,128)(2,1)S(1)} %get-tuple-element.47.refs_4_), channel_id=1, source_target_pairs={{0,8},{8,0},{16,24},{24,16},{1,9},{9,1},{17,25},{25,17},{2,10},{10... | collective-permute-start | bytes 786440 | tf_op jit(solution)/shard_map/ppermute | solution.py:14
  79.5 6.9 %collective-permute-start.24 = (bf16[2,128,512]{2,1,0:T(8,128)(2,1)S(1)}, bf16[2,128,512]{2,1,0:T(8,128)(2,1)S(1)}, u32[]{:S(2)}, u32[]{:S(2)}) collective-permute-start(bf16[2,128,512]{2,1,0:T(8,128)(2,1)S(1)} %get-tuple-element.51), channel_id=1, source_target_pairs={{0,16},{8,24},{16,0},{24,8},{1,17},{9,25},{17,1},{25,9},{2,18},{10... | collective-permute-start | bytes 786440 | tf_op jit(solution)/shard_map/ppermute | solution.py:14
  82.5 15.0 %collective-permute-start.30 = (bf16[256,512]{1,0:T(8,128)(2,1)S(1)}, bf16[256,512]{1,0:T(8,128)(2,1)S(1)}, u32[]{:S(2)}, u32[]{:S(2)}) collective-permute-start(bf16[256,512]{1,0:T(8,128)(2,1)S(1)} %p23_place.1.refs_2_.refs_5_), channel_id=1, source_target_pairs={{0,1},{1,0},{2,3},{3,2},{4,5},{5,4},{6,7},{7,6},{8,9},{9,8},{10,11... | collective-permute-start | bytes 786440 | tf_op jit(solution)/shard_map/ppermute | solution.py:14
  85.9 5.0 %collective-permute-start.18 = (f32[32,1024]{1,0:T(8,128)S(1)}, f32[32,1024]{1,0:T(8,128)S(1)}, u32[]{:S(2)}, u32[]{:S(2)}) collective-permute-start(f32[32,1024]{1,0:T(8,128)S(1)} %convert_add_fusion.refs_0_), channel_id=1, source_target_pairs={{0,16},{8,24},{16,0},{24,8},{1,17},{9,25},{17,1},{25,9},{2,18},{10... | collective-permute-start | bytes 393224 | tf_op jit(solution)/shard_map/ppermute | solution.py:14
  87.0 8.0 %collective-permute-start.31 = (bf16[128,512]{1,0:T(8,128)(2,1)S(1)}, bf16[128,512]{1,0:T(8,128)(2,1)S(1)}, u32[]{:S(2)}, u32[]{:S(2)}) collective-permute-start(bf16[128,512]{1,0:T(8,128)(2,1)S(1)} %get-tuple-element.52.refs_3_), channel_id=1, source_target_pairs={{0,16},{8,24},{16,0},{24,8},{1,17},{9,25},{17,1},{25,9},{2,18},{10... | collective-permute-start | bytes 393224 | tf_op jit(solution)/shard_map/ppermute | solution.py:14
  88.6 7.8 %collective-permute-start.32 = (bf16[128,512]{1,0:T(8,128)(2,1)S(1)}, bf16[128,512]{1,0:T(8,128)(2,1)S(1)}, u32[]{:S(2)}, u32[]{:S(2)}) collective-permute-start(bf16[128,512]{1,0:T(8,128)(2,1)S(1)} %get-tuple-element.53.refs_4_), channel_id=1, source_target_pairs={{0,8},{8,0},{16,24},{24,16},{1,9},{9,1},{17,25},{25,17},{2,10},{10... | collective-permute-start | bytes 393224 | tf_op jit(solution)/shard_map/ppermute | solution.py:14
  91.4 9.8 %copy-start.2 = (bf16[2,512,512]{2,1,0:T(8,128)(2,1)S(1)}, bf16[2,512,512]{2,1,0:T(8,128)(2,1)}, u32[]{:S(2)}) copy-start(bf16[2,512,512]{2,1,0:T(8,128)(2,1)} %refs_4_.1) | copy-start | bytes 3145732
  91.5 6.1 %collective-permute-start.27 = (bf16[32,1024]{1,0:T(8,128)(2,1)S(1)}, bf16[32,1024]{1,0:T(8,128)(2,1)S(1)}, u32[]{:S(2)}, u32[]{:S(2)}) collective-permute-start(bf16[32,1024]{1,0:T(8,128)(2,1)S(1)} %m23_sum.1.refs_0_), channel_id=1, source_target_pairs={{0,2},{1,3},{2,0},{3,1},{4,6},{5,7},{6,4},{7,5},{8,10},{9,11},{10,... | collective-permute-start | bytes 196616 | tf_op jit(solution)/shard_map/ppermute | solution.py:14
  93.9 5.9 %collective-permute-start.28 = (bf16[32,1024]{1,0:T(8,128)(2,1)S(1)}, bf16[32,1024]{1,0:T(8,128)(2,1)S(1)}, u32[]{:S(2)}, u32[]{:S(2)}) collective-permute-start(bf16[32,1024]{1,0:T(8,128)(2,1)S(1)} %m23_sum.1.refs_0_), channel_id=1, source_target_pairs={{0,4},{1,5},{2,6},{3,7},{4,0},{5,1},{6,2},{7,3},{8,12},{9,13},{10,... | collective-permute-start | bytes 196616 | tf_op jit(solution)/shard_map/ppermute | solution.py:14
  95.1 6.2 %collective-permute-start.29 = (bf16[32,1024]{1,0:T(8,128)(2,1)S(1)}, bf16[32,1024]{1,0:T(8,128)(2,1)S(1)}, u32[]{:S(2)}, u32[]{:S(2)}) collective-permute-start(bf16[32,1024]{1,0:T(8,128)(2,1)S(1)} %m23_sum.1.refs_0_), channel_id=1, source_target_pairs={{0,6},{1,7},{2,4},{3,5},{4,2},{5,3},{6,0},{7,1},{8,14},{9,15},{10,... | collective-permute-start | bytes 196616 | tf_op jit(solution)/shard_map/ppermute | solution.py:14
  102.4 1.6 %collective-permute-start.33 = (bf16[2,128,512]{2,1,0:T(8,128)(2,1)S(1)}, bf16[2,128,512]{2,1,0:T(8,128)(2,1)S(1)}, u32[]{:S(2)}, u32[]{:S(2)}) collective-permute-start(bf16[2,128,512]{2,1,0:T(8,128)(2,1)S(1)} %x2_x3.1.refs_4_), channel_id=1, source_target_pairs={{0,1},{1,0},{2,3},{3,2},{4,5},{5,4},{6,7},{7,6},{8,9},{9,8},{10,11... | collective-permute-start | bytes 786440 | tf_op jit(solution)/shard_map/ppermute | solution.py:14

commit v5 on v4

--- a/solution.py
+++ b/solution.py
@@ -25,6 +25,11 @@
 class Picked:
     def __init__(self, array, block, index):
         self.array, self.block, self.index = array, block, index
+
+
+class InHbm:
+    def __init__(self, array):
+        self.array = array
 
 
 def on_device(right_side, panels, tile_counts, diag_leaf, diag_pair, diag_root, sup_rows):
@@ -95,6 +100,10 @@
     def run(body, operands, outs, scratch=(), steps=1, after=(), limit=32):
         arrays, specs, moved = [], [], 0
         for operand in operands:
+            if isinstance(operand, InHbm):
+                arrays.append(operand.array)
+                specs.append(pl.BlockSpec(memory_space=pltpu.HBM))
+                continue
             if not isinstance(operand, Picked):
                 zeros = (0,) * operand.ndim
                 operand = Picked(operand, operand.shape, lambda i, sup, live_counts, zeros=zeros: zeros)
@@ -132,7 +141,7 @@
             compiler_params=pltpu.CompilerParams(vmem_limit_bytes=limit * 1024 * 1024),
             cost_estimate=pl.CostEstimate(flops=0, bytes_accessed=moved, transcendentals=0),
         )(sup_rows, counts, *arrays)
-        return results[0] if single else results
+        return results[0] if single else list(results)
 
     def spread(block):
         for bits in outer:
@@ -149,26 +158,48 @@
 
     first_rows = 2 * half_r + 2 * half_w
 
-    def first_half(meta, out, b0, b1, p01, p23):
-        out[:half_r] = side_value(meta, b0, 0)
-        out[half_r : 2 * half_r] = side_value(meta, b1, 1)
-        out[2 * half_r : 2 * half_r + half_w] = tile_value(meta, p01, 0, 1)
-        out[2 * half_r + half_w :] = tile_value(meta, p23, 2, 3)
-
-    def first_send(meta, b0, b1, p01, p23, out):
-        first_half(meta, out, b0, b1, p01, p23)
-
-    def first_in(other):
-        return [side(0, other), side(1, other), tile(0, 1, other), tile(2, 3, other)]
-
-    first_got = swap(run(first_send, first_in(1), shaped((first_rows, width)), limit=60), "row", 1)
+    def first_send(meta, sides, tiles, send, kept, sem):
+        core = core_of(meta)
+        copies, start = [], 0
+        for source, level in ((None, 0), (None, 1), (0, 1), (2, 3)):
+            size = half_r if source is None else half_w
+            whole = sides if source is None else tiles.at[source]
+            for out, side_of in ((send, 1 - core), (kept, core)):
+                copies.append(
+                    pltpu.make_async_copy(
+                        whole.at[spot(meta, level), at(side_of, size)],
+                        out.at[start : start + size],
+                        sem.at[len(copies)],
+                    )
+                )
+            start += size
+        for copy in copies:
+            copy.start()
+        for copy in copies:
+            copy.wait()
+        for out in (send, kept):
+            for level in range(2):
+                rows = slice(level * half_r, (level + 1) * half_r)
+                out[rows] = out[rows] * keep(jnp.where(owns(meta, level), width, 0))
+            for i, (of, level) in enumerate(((0, 1), (2, 3))):
+                rows = slice(2 * half_r + i * half_w, 2 * half_r + (i + 1) * half_w)
+                out[rows] = out[rows] * keep(live_owned(meta, of, level))
+
+    first_shape = shaped((first_rows, width))
+    first_out, first_kept = run(
+        first_send,
+        [InHbm(right), InHbm(panels)],
+        [first_shape, first_shape],
+        [pltpu.SemaphoreType.DMA((8,))],
+        limit=60,
+    )
+    first_got = swap(first_out, "row", 1)
 
     b0_rows, column_rows = blocks * half_r, half_r + half_w
     near, far = (CORES, 2 * CORES)
 
-    def first_split(meta, b0, b1, p01, p23, got, send, kept, p23_send, p23_kept, whole):
-        first_half(meta, whole, b0, b1, p01, p23)
-        whole[...] = whole[...] + got[...]
+    def first_split(meta, own, got, send, kept, p23_send, p23_kept, whole):
+        whole[...] = own[...] + got[...]
         for i in range(blocks):
             send[i * half_r : (i + 1) * half_r] = whole[:half_r, i * lanes : (i + 1) * lanes]
         kept[:b0_rows] = send[:b0_rows]
@@ -189,7 +220,7 @@
     )
     near_send, near_kept, p23_send, p23_kept = run(
         first_split,
-        first_in(0) + [first_got],
+        [first_kept, first_got],
         [near_shape, near_shape, p23_pair, p23_pair],
         [pltpu.VMEM((first_rows, width), BF16)],
     )
@@ -197,6 +228,32 @@
     near_kept = spread(near_kept)
     p23_got = swap(spread(p23_send), "row", near)
     p23_kept = spread(p23_kept)
+
+    def panel_of(level, m):
+        return Picked(
+            panels,
+            (None, None, width, width),
+            lambda i, *meta: (level, leaf_of(meta) ^ m, 0, 0),
+        )
+
+    def panel_value(meta, ref, level, m):
+        return ref[...] * keep(live(meta, level, leaf_of(meta) ^ m))
+
+    orders = ((2, 1, 2), (3, 2, 1))
+    panel_got, first_sent = [], []
+    for level, one, two in orders:
+        def panel_send(meta, pa, pb, out, level=level, one=one, two=two):
+            out[0] = panel_value(meta, pa, level, one)
+            out[1] = panel_value(meta, pb, level, one ^ two)
+
+        sent = run(
+            panel_send,
+            [panel_of(level, one), panel_of(level, one ^ two)],
+            shaped((2, width, width)),
+            after=[near_send],
+        )
+        first_sent.append(sent)
+        panel_got.append(swap(sent, "leaf", one))
 
     def first_join(meta, kept, got, send, own):
         send[:b0_rows] = kept[:b0_rows] + got[:b0_rows]
@@ -208,6 +265,7 @@
         first_join,
         [near_kept, near_got],
         [shaped((b0_rows + column_rows, lanes)), shaped((column_rows, lanes))],
+        after=first_sent,
     )
     far_got = swap(far_send, "row", far)
 
@@ -221,52 +279,21 @@
     )
     p23_far = swap(p23_send, "row", far)
 
-    def panel_of(level, m):
-        return Picked(
-            panels,
-            (None, None, width, width),
-            lambda i, *meta: (level, leaf_of(meta) ^ m, 0, 0),
-        )
-
-    def panel_value(meta, ref, level, m):
-        return ref[...] * keep(live(meta, level, leaf_of(meta) ^ m))
-
-    orders = ((2, 1, 2), (3, 2, 1))
-    panel_got = []
-    for level, one, two in orders:
-        def panel_send(meta, pa, pb, out, level=level, one=one, two=two):
-            out[0] = panel_value(meta, pa, level, one)
-            out[1] = panel_value(meta, pb, level, one ^ two)
-
-        sent = run(
-            panel_send,
-            [panel_of(level, one), panel_of(level, one ^ two)],
-            shaped((2, width, width)),
+    rest_got, linked_got = [], []
+    for level in (2, 3):
+        def rest_send(meta, b, p0, p1, out, linked_out, level=level):
+            out[:half_r] = side_value(meta, b, level)
+            out[half_r:] = tile_value(meta, p0, 0, level)
+            linked_out[...] = tile_value(meta, p1, 1, level)
+
+        rest_sent, linked_sent = run(
+            rest_send,
+            [side(level, 1), tile(0, level), tile(1, level)],
+            [shaped((half_r + width, width)), shaped((width, width))],
             after=[near_send],
         )
-        panel_got.append(swap(sent, "leaf", one))
-
-    later = [(0, 2), (1, 2), (0, 3), (1, 3)]
-    rest_rows = 2 * half_r + len(later) * width
-
-    def rest_send(meta, b2, b3, *refs):
-        tiles, out = refs[:-1], refs[-1]
-        out[:half_r] = side_value(meta, b2, 2)
-        out[half_r : 2 * half_r] = side_value(meta, b3, 3)
-        for i, (of, level) in enumerate(later):
-            start = 2 * half_r + i * width
-            out[start : start + width] = tile_value(meta, tiles[i], of, level)
-
-    rest_got = swap(
-        run(
-            rest_send,
-            [side(2, 1), side(3, 1)] + [tile(*which) for which in later],
-            shaped((rest_rows, width)),
-            after=[near_send],
-        ),
-        "row",
-        1,
-    )
+        rest_got.append(swap(rest_sent, "row", 1))
+        linked_got.append(swap(linked_sent, "row", 1))
 
     def solve0(meta, sent, got, own, diag, x0, p, b):
         x = jnp.zeros((half_r, width), F32)
@@ -317,42 +344,29 @@
     def m1_sum(meta, a, b, out):
         out[...] = (a[...] + b[...]).astype(BF16)
 
-    m1 = run(m1_sum, [t1, swap(t1, "leaf", 1)], shaped((half_r, lanes)), after=panel_sent)
+    m1 = run(m1_sum, [t1, swap(t1, "leaf", 1)], shaped((half_r, lanes)))
     m1 = jnp.concatenate([m1, swap(m1, "row", near)])
     m1_far = swap(m1, "row", far)
     p23 = (p23.astype(F32) + p23_turned.astype(F32)).astype(BF16)
-    p23 = jnp.concatenate([p23, swap(p23, "row", near)])
-    p23_far = swap(p23, "row", far)
-
-    def p23_place(meta, near_two, far_two, out):
-        for m in range(chips):
-            source = (near_two, far_two)[m // 2]
-            rows = slice((m % 2) * half_w, (m % 2 + 1) * half_w)
-            out[:, at(chip_of(meta) ^ m, lanes)] = source[rows]
-
-    p23_half = run(p23_place, [p23, p23_far], shaped((half_w, width)))
-    p23_other = swap(p23_half, "row", 1)
-
-    def early(meta, b2, b3, *refs):
-        tiles, (got, x0, u, linked) = refs[:4], refs[4:]
-        for i, b in enumerate((b2, b3)):
-            rows = slice(i * half_r, (i + 1) * half_r)
-            value = (side_value(meta, b, 2 + i) + got[rows]).astype(F32)
-            start = 2 * half_r + 2 * i * width
-            p0 = tile_value(meta, tiles[2 * i], 0, 2 + i) + got[start : start + width]
-            u[:, i * width : (i + 1) * width] = value - dot(x0[...], p0)
-            start += width
-            linked[i] = tile_value(meta, tiles[2 * i + 1], 1, 2 + i) + got[start : start + width]
-
-    u, linked = run(
+    p23_next = swap(p23, "row", near)
+
+    def early(meta, *refs):
+        x0, us = refs[6], refs[7:]
+        for i in range(2):
+            b, p0, got = refs[3 * i : 3 * i + 3]
+            value = (side_value(meta, b, 2 + i) + got[:half_r]).astype(F32)
+            us[i][...] = value - dot(x0[...], tile_value(meta, p0, 0, 2 + i) + got[half_r:])
+
+    us = run(
         early,
-        [side(2, 0), side(3, 0)] + [tile(*which) for which in later] + [rest_got, x0],
-        [shaped((half_r, 2 * width), F32), shaped((2, width, width))],
+        [side(2, 0), tile(0, 2), rest_got[0], side(3, 0), tile(0, 3), rest_got[1], x0],
+        [shaped((half_r, width), F32)] * 2,
         after=[t1],
     )
 
     def x1_t23(meta, *refs):
-        (near_two, far_two, diag, u, linked, x1), outs, whole = refs[:6], refs[6:-1], refs[-1]
+        (near_two, far_two, diag), us, ps, got = refs[:3], refs[3:5], refs[5:7], refs[7:9]
+        x1, outs, whole = refs[9], refs[10:-1], refs[-1]
         chip = chip_of(meta)
         x = jnp.zeros((half_r, width), F32)
         for m in range(chips):
@@ -362,7 +376,7 @@
         x1[...] = x
         for i in range(2):
             cols = slice(i * width, (i + 1) * width)
-            whole[:, cols] = u[:, cols] - dot(x, linked[i])
+            whole[:, cols] = us[i][...] - dot(x, tile_value(meta, ps[i], 1, 2 + i) + got[i][...])
         for m, out in enumerate(outs):
             out[...] = whole[at(chip ^ m, part_r)].astype(BF16)
 
@@ -370,9 +384,10 @@
     strip = shaped((part_r, 2 * width))
     x1, *strips = run(
         x1_t23,
-        [m1, m1_far, pair, u, linked],
+        [m1, m1_far, pair] + us + [tile(1, 2), tile(1, 3)] + linked_got,
         [rows_half] + [strip] * chips,
         [pltpu.VMEM((half_r, 2 * width), F32)],
+        after=panel_sent,
     )
     strips[1:] = [swap(piece, "row", step) for piece, step in zip(strips[1:], steps_up)]
     x01_other = [swap(x, "row", 1) for x in (x0, x1)]
@@ -438,6 +453,22 @@
         refs[-1][...] = value
 
     t23 = spread(run(t23_sum, strips, strip, after=[share_send0]))
+    def p23_stack(meta, a, b, out):
+        out[:half_w] = a[...]
+        out[half_w:] = b[...]
+
+    p23 = run(p23_stack, [p23, p23_next], p23_pair, after=[t23])
+    p23_far = swap(p23, "row", far)
+
+    def p23_place(meta, near_two, far_two, out):
+        for m in range(chips):
+            source = (near_two, far_two)[m // 2]
+            rows = slice((m % 2) * half_w, (m % 2 + 1) * half_w)
+            out[:, at(chip_of(meta) ^ m, lanes)] = source[rows]
+
+    p23_half = run(p23_place, [p23, p23_far], shaped((half_w, width)))
+    p23_other = swap(p23_half, "row", 1)
+
     t23 = t23.astype(F32) + swap(t23, "leaf", 1).astype(F32)
     t23_far = swap(t23, "leaf", 2)
 
@@ -448,7 +479,7 @@
         m23_sum,
         [t23, t23_far],
         strip,
-        after=[p23_half, *share_sent, *panel_far],
+        after=[p23_half, *panel_far],
     )
     m23_parts = [m23] + [swap(m23, "row", step) for step in steps_up]
 
@@ -492,27 +523,57 @@
     )
     x23_other = swap(x23, "row", 1)
 
-    def final(meta, x0, x1, x0_other, x1_other, x23, x23_other, panel, share, solved, out):
+    def final(meta, x23, x23_other, panel, share, top, bottom, whole):
+        core = core_of(meta)
+        value = share[...]
+        for i in range(2):
+            whole[i, at(core, half_r)] = x23[i]
+            whole[i, at(1 - core, half_r)] = x23_other[i]
+            value = value - dot(whole[i], panel[i])
+        top[...] = value[:half_r].astype(BF16)
+        bottom[...] = value[half_r:].astype(BF16)
+
+    top, bottom = run(
+        final,
+        [x23, x23_other, panel_sum, share_sum],
+        [rows_half, rows_half],
+        [pltpu.VMEM((2, height, width), BF16)],
+    )
+
+    def write_solved(meta, x0, x1, x0_other, x1_other, x23, x23_other, out):
         core = core_of(meta)
         mine, other = at(core, half_r), at(1 - core, half_r)
         for i, (a, b) in enumerate(((x0, x0_other), (x1, x1_other))):
-            solved[i, mine] = a[...]
-            solved[i, other] = b[...]
-        value = share[...]
+            out[i, mine] = a[...]
+            out[i, other] = b[...]
         for i in range(2):
-            solved[2 + i, mine] = x23[i]
-            solved[2 + i, other] = x23_other[i]
-            value = value - dot(solved[2 + i], panel[i])
-        value = value.astype(BF16)
-        for i in range(n_leaf):
-            out[i] = value
-
-    solved, done = run(
-        final,
-        [x0, x1] + x01_other + [x23, x23_other, panel_sum, share_sum],
-        [shaped((levels, height, width)), shaped((n_leaf, height, width))],
-    )
-    updated = lax.all_to_all(done, "leaf", 0, 0, tiled=True)
+            out[2 + i, mine] = x23[i]
+            out[2 + i, other] = x23_other[i]
+
+    solved = run(
+        write_solved,
+        [x0, x1] + x01_other + [x23, x23_other],
+        shaped((levels, height, width)),
+        after=[top],
+    )
+
+    top_1, bottom_2 = swap(top, "leaf", 1), swap(bottom, "leaf", 2)
+    bottom_1, top_2 = swap(bottom, "leaf", 1), swap(top, "leaf", 2)
+    top_3, bottom_3 = swap(top_1, "leaf", 2), swap(bottom_2, "leaf", 1)
+
+    def write_updated(meta, *refs):
+        parts, out = refs[:-1], refs[-1]
+        for m in range(n_leaf):
+            for half in range(2):
+                rows = slice(half * half_r, (half + 1) * half_r)
+                out[leaf_of(meta) ^ m, rows] = parts[2 * m + half][...]
+
+    updated = run(
+        write_updated,
+        [top, bottom, top_1, bottom_1, top_2, bottom_2, top_3, bottom_3],
+        shaped((n_leaf, height, width)),
+        after=[solved],
+    )
     return solved[:, None], updated
 
 

time: 124 us -> 121 us (0.976)
  blocking collectives: 17.2 us -> 0 us
  waiting for transfers between devices: 35 us -> 38.9 us
  Pallas kernels: 22.2 us -> 26 us
  starting transfers between devices: 42.7 us -> 46 us
  local copies, waits for them, and re-layouts: 5.98 us -> 8.4 us
    all_to_all x1 -> x0, blocking collectives: 17.2 us -> none  [on_device(): updated = lax.all_to_all(done, 'leaf', 0, 0, tiled=True)]
    ppermute x34 -> x43, waiting for transfers between devices: 35 us -> 38.9 us  [swap(): lax.ppermute(block, axis, [(i, i ^ bits) for i in range(lax.axis_size(axi...]
    pallas_call x22 -> x26, Pallas kernels: 22.2 us -> 26 us  [run(): pl.pallas_call(kernel, grid_spec=pltpu.PrefetchScalarGridSpec(num_scalar_...]
    ppermute x34 -> x43, starting transfers between devices: 42.7 us -> 46 us  [swap(): lax.ppermute(block, axis, [(i, i ^ bits) for i in range(lax.axis_size(axi...]
    unnamed x19 -> x20, local copies, waits for them, and re-layouts: 5.98 us -> 8.4 us
  transfers between devices with their start and end apart: 34 -> 43, of which waited for: 15 -> 18; matrix products, arithmetic and copies ran while one was open for 0% -> 0% of each run, Pallas kernels for 12% -> 15%
where the time goes in v5:
time: 121 us; the launch traced here: 120 us
  starting transfers between devices  46 us (38%)
  waiting for transfers between devices  38.9 us (32%)
  Pallas kernels  26 us (21%)
  local copies, waits for them, and re-layouts  8.4 us (7%)
    ppermute x43, starting transfers between devices, swap(): lax.ppermute(block, axis, [(i, i ^ bits) for i in range(lax.axis_size(axi...  46 us
    ppermute x43, waiting for transfers between devices, swap(): lax.ppermute(block, axis, [(i, i ^ bits) for i in range(lax.axis_size(axi...  38.9 us
    pallas_call x26, Pallas kernels, run(): pl.pallas_call(kernel, grid_spec=pltpu.PrefetchScalarGridSpec(num_scalar_...  26 us
    unnamed x20, local copies, waits for them, and re-layouts  8.4 us
  transfers between devices with their start and end apart: 43, of which 18 were waited for; matrix products, arithmetic and copies ran while one was open for 0% of the time, Pallas kernels for 15%

profile of v5, /device:TPU:0, one launch (start us, length us, event | category | flops | bytes accessed | tf_op | source)
XLA Modules:
  0.0 120.4 jit_solution(13115771353447414849)
XLA Ops:
  0.7 3.6 %first_send.1 = (bf16[768,512]{1,0:T(8,128)(2,1)}, bf16[768,512]{1,0:T(8,128)(2,1)}) custom-call(s32[4]{0:T(128)} %sup.51, s32[4,4]{1,0:T(4,128)} %bitcast.32, bf16[4,256,512]{2,1,0:T(8,128)(2,1)} %bitcast.25, bf16[4,4,512,512]{3,2,1,0:T(8,128)(2,1)} %bitcast.6), custom_call_target="tpu_custom_call" | custom-call | bytes 1572864 | tf_op jit(solution)/shard_map/first_send/pallas_call | solution.py:130
  4.7 2.1 %collective-permute-done.refs_1_ = bf16[768,512]{1,0:T(8,128)(2,1)S(1)} collective-permute-done((bf16[768,512]{1,0:T(8,128)(2,1)}, bf16[768,512]{1,0:T(8,128)(2,1)S(1)}, u32[]{:S(2)}, u32[]{:S(2)}) %collective-permute-start) | collective-permute-done | bytes 786464 | tf_op jit(solution)/shard_map/ppermute | solution.py:14
  6.9 1.1 copy-done.7
  8.8 3.0 %collective-permute-start.1 = (bf16[1280,128]{1,0:T(8,128)(2,1)S(1)}, bf16[1280,128]{1,0:T(8,128)(2,1)S(1)}, u32[]{:S(2)}, u32[]{:S(2)}) collective-permute-start(bf16[1280,128]{1,0:T(8,128)(2,1)S(1)} %get-tuple-element.39.refs_2_.refs_3_), channel_id=1, source_target_pairs={{0,2},{1,3},{2,0},{3,1},{4,6},{5,7},{6,4},{7,5},{8,10},{9,11},{10,... | collective-permute-start | bytes 983048 | tf_op jit(solution)/shard_map/ppermute | solution.py:14
  11.8 3.4 %copy-done = bf16[4,1,4,512,512]{4,3,2,1,0:T(8,128)(2,1)S(1)} copy-done((bf16[4,1,4,512,512]{4,3,2,1,0:T(8,128)(2,1)S(1)}, bf16[4,1,4,512,512]{4,3,2,1,0:T(8,128)(2,1)}, u32[]{:S(2)}) %copy-start) | copy-done | bytes 8388632
  16.0 2.6 %copy-done.1 = bf16[4,1,4,512,512]{4,3,2,1,0:T(8,128)(2,1)S(1)} copy-done((bf16[4,1,4,512,512]{4,3,2,1,0:T(8,128)(2,1)S(1)}, bf16[4,1,4,512,512]{4,3,2,1,0:T(8,128)(2,1)}, u32[]{:S(2)}) %copy-start.1) | copy-done | bytes 8388632
  19.3 1.6 %collective-permute-start.13 = (bf16[2,512,512]{2,1,0:T(8,128)(2,1)S(1)}, bf16[2,512,512]{2,1,0:T(8,128)(2,1)S(1)}, u32[]{:S(2)}, u32[]{:S(2)}) collective-permute-start(bf16[2,512,512]{2,1,0:T(8,128)(2,1)S(1)} %panel_send.2.refs_2_), channel_id=1, source_target_pairs={{0,8},{8,0},{16,24},{24,16},{1,9},{9,1},{17,25},{25,17},{2,10},{10... | collective-permute-start | bytes 3145736 | tf_op jit(solution)/shard_map/ppermute | solution.py:14
  21.5 1.6 %collective-permute-start.14 = (bf16[2,512,512]{2,1,0:T(8,128)(2,1)S(1)}, bf16[2,512,512]{2,1,0:T(8,128)(2,1)S(1)}, u32[]{:S(2)}, u32[]{:S(2)}) collective-permute-start(bf16[2,512,512]{2,1,0:T(8,128)(2,1)S(1)} %panel_send.3.refs_3_), channel_id=1, source_target_pairs={{0,16},{8,24},{16,0},{24,8},{1,17},{9,25},{17,1},{25,9},{2,18},{10... | collective-permute-start | bytes 3145736 | tf_op jit(solution)/shard_map/ppermute | solution.py:14
  23.7 2.7 %collective-permute-start.2 = (bf16[896,128]{1,0:T(8,128)(2,1)S(1)}, bf16[896,128]{1,0:T(8,128)(2,1)S(1)}, u32[]{:S(2)}, u32[]{:S(2)}) collective-permute-start(bf16[896,128]{1,0:T(8,128)(2,1)S(1)} %get-tuple-element.40.refs_2_.refs_0_), channel_id=1, source_target_pairs={{0,4},{1,5},{2,6},{3,7},{4,0},{5,1},{6,2},{7,3},{8,12},{9,13},{10,... | collective-permute-start | bytes 688136 | tf_op jit(solution)/shard_map/ppermute | solution.py:14
  26.8 6.7 %collective-permute-done.3.refs_1_ = bf16[512,128]{1,0:T(8,128)(2,1)S(1)} collective-permute-done((bf16[512,128]{1,0:T(8,128)(2,1)S(1)}, bf16[512,128]{1,0:T(8,128)(2,1)S(1)}, u32[]{:S(2)}, u32[]{:S(2)}) %collective-permute-start.3) | collective-permute-done | bytes 131104 | tf_op jit(solution)/shard_map/ppermute | solution.py:14
  34.2 1.3 %collective-permute-start.5 = (bf16[256,128]{1,0:T(8,128)(2,1)S(1)}, bf16[256,128]{1,0:T(8,128)(2,1)S(1)}, u32[]{:S(2)}, u32[]{:S(2)}) collective-permute-start(bf16[256,128]{1,0:T(8,128)(2,1)S(1)} %get-tuple-element.44.refs_4_), channel_id=1, source_target_pairs={{0,4},{1,5},{2,6},{3,7},{4,0},{5,1},{6,2},{7,3},{8,12},{9,13},{10,... | collective-permute-start | bytes 196616 | tf_op jit(solution)/shard_map/ppermute | solution.py:14
  37.2 2.2 %collective-permute-done.5.refs_4_ = bf16[256,128]{1,0:T(8,128)(2,1)S(1)} collective-permute-done((bf16[256,128]{1,0:T(8,128)(2,1)S(1)}, bf16[256,128]{1,0:T(8,128)(2,1)S(1)}, u32[]{:S(2)}, u32[]{:S(2)}) %collective-permute-start.5) | collective-permute-done | bytes 65568 | tf_op jit(solution)/shard_map/ppermute | solution.py:14
  39.5 1.3 %collective-permute-done.4.refs_2_ = bf16[256,128]{1,0:T(8,128)(2,1)S(1)} collective-permute-done((bf16[256,128]{1,0:T(8,128)(2,1)S(1)}, bf16[256,128]{1,0:T(8,128)(2,1)S(1)}, u32[]{:S(2)}, u32[]{:S(2)}) %collective-permute-start.4) | collective-permute-done | bytes 65568 | tf_op jit(solution)/shard_map/ppermute | solution.py:14
  42.1 3.7 %collective-permute-done.6.refs_1_ = f32[128,128]{1,0:T(8,128)S(1)} collective-permute-done((f32[128,128]{1,0:T(8,128)S(1)}, f32[128,128]{1,0:T(8,128)S(1)}, u32[]{:S(2)}, u32[]{:S(2)}) %collective-permute-start.6) | collective-permute-done | bytes 65568 | tf_op jit(solution)/shard_map/ppermute | solution.py:14
  46.4 2.5 %collective-permute-start.7 = (bf16[128,128]{1,0:T(8,128)(2,1)S(1)}, bf16[128,128]{1,0:T(8,128)(2,1)S(1)}, u32[]{:S(2)}, u32[]{:S(2)}) collective-permute-start(bf16[128,128]{1,0:T(8,128)(2,1)S(1)} %m1_sum.1), channel_id=1, source_target_pairs={{0,2},{1,3},{2,0},{3,1},{4,6},{5,7},{6,4},{7,5},{8,10},{9,11},{10,... | collective-permute-start | bytes 98312 | tf_op jit(solution)/shard_map/ppermute | solution.py:14
  48.9 1.9 %collective-permute-done.7 = bf16[128,128]{1,0:T(8,128)(2,1)S(1)} collective-permute-done((bf16[128,128]{1,0:T(8,128)(2,1)S(1)}, bf16[128,128]{1,0:T(8,128)(2,1)S(1)}, u32[]{:S(2)}, u32[]{:S(2)}) %collective-permute-start.7) | collective-permute-done | bytes 32800 | tf_op jit(solution)/shard_map/ppermute | solution.py:14
  50.8 2.1 %collective-permute-start.8 = (bf16[256,128]{1,0:T(8,128)(2,1)S(1)}, bf16[256,128]{1,0:T(8,128)(2,1)S(1)}, u32[]{:S(2)}, u32[]{:S(2)}) collective-permute-start(bf16[256,128]{1,0:T(8,128)(2,1)S(1)} %pad_maximum_fusion.refs_0_), channel_id=1, source_target_pairs={{0,4},{1,5},{2,6},{3,7},{4,0},{5,1},{6,2},{7,3},{8,12},{9,13},{10,... | collective-permute-start | bytes 196616 | tf_op jit(solution)/shard_map/ppermute | solution.py:14
  52.9 1.6 %collective-permute-start.22 = (bf16[256,128]{1,0:T(8,128)(2,1)S(1)}, bf16[256,128]{1,0:T(8,128)(2,1)S(1)}, u32[]{:S(2)}, u32[]{:S(2)}) collective-permute-start(bf16[256,128]{1,0:T(8,128)(2,1)S(1)} %add.13), channel_id=1, source_target_pairs={{0,8},{8,0},{16,24},{24,16},{1,9},{9,1},{17,25},{25,17},{2,10},{10... | collective-permute-start | bytes 196616 | tf_op jit(solution)/shard_map/ppermute | solution.py:14
  57.0 1.2 x1_t23.1
  58.8 1.6 %collective-permute-start.23 = (bf16[256,128]{1,0:T(8,128)(2,1)S(1)}, bf16[256,128]{1,0:T(8,128)(2,1)S(1)}, u32[]{:S(2)}, u32[]{:S(2)}) collective-permute-start(bf16[256,128]{1,0:T(8,128)(2,1)S(1)} %add_convert_fusion.1), channel_id=1, source_target_pairs={{0,16},{8,24},{16,0},{24,8},{1,17},{9,25},{17,1},{25,9},{2,18},{10... | collective-permute-start | bytes 196616 | tf_op jit(solution)/shard_map/ppermute | solution.py:14
  60.8 1.1 collective-permute-start.27
  62.0 1.5 %collective-permute-done.23 = bf16[256,128]{1,0:T(8,128)(2,1)S(1)} collective-permute-done((bf16[256,128]{1,0:T(8,128)(2,1)S(1)}, bf16[256,128]{1,0:T(8,128)(2,1)S(1)}, u32[]{:S(2)}, u32[]{:S(2)}) %collective-permute-start.23) | collective-permute-done | bytes 65568 | tf_op jit(solution)/shard_map/ppermute | solution.py:14
  64.5 2.1 %collective-permute-start.18 = (bf16[32,1024]{1,0:T(8,128)(2,1)S(1)}, bf16[32,1024]{1,0:T(8,128)(2,1)S(1)}, u32[]{:S(2)}, u32[]{:S(2)}) collective-permute-start(bf16[32,1024]{1,0:T(8,128)(2,1)S(1)} %get-tuple-element.57), channel_id=1, source_target_pairs={{0,4},{1,5},{2,6},{3,7},{4,0},{5,1},{6,2},{7,3},{8,12},{9,13},{10,... | collective-permute-start | bytes 196616 | tf_op jit(solution)/shard_map/ppermute | solution.py:14
  66.6 1.2 %collective-permute-start.19 = (bf16[32,1024]{1,0:T(8,128)(2,1)S(1)}, bf16[32,1024]{1,0:T(8,128)(2,1)S(1)}, u32[]{:S(2)}, u32[]{:S(2)}) collective-permute-start(bf16[32,1024]{1,0:T(8,128)(2,1)S(1)} %get-tuple-element.58), channel_id=1, source_target_pairs={{0,6},{1,7},{2,4},{3,5},{4,2},{5,3},{6,0},{7,1},{8,14},{9,15},{10,... | collective-permute-start | bytes 196616 | tf_op jit(solution)/shard_map/ppermute | solution.py:14
  67.9 2.7 %update01.1 = (bf16[2,128,512]{2,1,0:T(8,128)(2,1)S(1)}, bf16[2,128,512]{2,1,0:T(8,128)(2,1)S(1)}, f32[2,128,512]{2,1,0:T(8,128)S(1)}, f32[2,128,512]{2,1,0:T(8,128)S(1)}) custom-call(s32[4]{0:T(128)S(1)} %copy-done.9, s32[4,4]{1,0:T(4,128)S(1)} %bitcast.47, bf16[4,256,512]{2,1,0:T(8,128)(2,1)S(1)} %bitcast.30, bf16[4,4,512,512]{3,2,1,0:T(8,128)(2,1)S(1)} %bitcast.21, ...), custom_call_target="tpu_custom_call" | custom-call | bytes 8912896 | tf_op jit(solution)/shard_map/update01/pallas_call | solution.py:130
  71.1 1.8 %collective-permute-done.19.refs_3_ = bf16[32,1024]{1,0:T(8,128)(2,1)S(1)} collective-permute-done((bf16[32,1024]{1,0:T(8,128)(2,1)S(1)}, bf16[32,1024]{1,0:T(8,128)(2,1)S(1)}, u32[]{:S(2)}, u32[]{:S(2)}) %collective-permute-start.19) | collective-permute-done | bytes 65568 | tf_op jit(solution)/shard_map/ppermute | solution.py:14
  74.5 1.1 collective-permute-start.32
  75.6 1.3 %collective-permute-start.33 = (bf16[2,128,512]{2,1,0:T(8,128)(2,1)S(1)}, bf16[2,128,512]{2,1,0:T(8,128)(2,1)S(1)}, u32[]{:S(2)}, u32[]{:S(2)}) collective-permute-start(bf16[2,128,512]{2,1,0:T(8,128)(2,1)S(1)} %get-tuple-element.63), channel_id=1, source_target_pairs={{0,16},{8,24},{16,0},{24,8},{1,17},{9,25},{17,1},{25,9},{2,18},{10... | collective-permute-start | bytes 786440 | tf_op jit(solution)/shard_map/ppermute | solution.py:14
  78.4 1.1 collective-permute-start.25
  79.5 5.6 %collective-permute-done.25.refs_1_ = bf16[512,128]{1,0:T(8,128)(2,1)S(1)} collective-permute-done((bf16[512,128]{1,0:T(8,128)(2,1)S(1)}, bf16[512,128]{1,0:T(8,128)(2,1)S(1)}, u32[]{:S(2)}, u32[]{:S(2)}) %collective-permute-start.25) | collective-permute-done | bytes 131104 | tf_op jit(solution)/shard_map/ppermute | solution.py:14
  85.1 1.8 %collective-permute-start.21 = (f32[32,1024]{1,0:T(8,128)S(1)}, f32[32,1024]{1,0:T(8,128)S(1)}, u32[]{:S(2)}, u32[]{:S(2)}) collective-permute-start(f32[32,1024]{1,0:T(8,128)S(1)} %convert_add_fusion.refs_0_), channel_id=1, source_target_pairs={{0,16},{8,24},{16,0},{24,8},{1,17},{9,25},{17,1},{25,9},{2,18},{10... | collective-permute-start | bytes 393224 | tf_op jit(solution)/shard_map/ppermute | solution.py:14
  88.5 1.5 %collective-permute-done.21.refs_1_ = f32[32,1024]{1,0:T(8,128)S(1)} collective-permute-done((f32[32,1024]{1,0:T(8,128)S(1)}, f32[32,1024]{1,0:T(8,128)S(1)}, u32[]{:S(2)}, u32[]{:S(2)}) %collective-permute-start.21) | collective-permute-done | bytes 131104 | tf_op jit(solution)/shard_map/ppermute | solution.py:14
  90.1 1.2 collective-permute-start.35
  91.9 2.5 %collective-permute-start.29 = (bf16[32,1024]{1,0:T(8,128)(2,1)S(1)}, bf16[32,1024]{1,0:T(8,128)(2,1)S(1)}, u32[]{:S(2)}, u32[]{:S(2)}) collective-permute-start(bf16[32,1024]{1,0:T(8,128)(2,1)S(1)} %m23_sum.1.refs_0_), channel_id=1, source_target_pairs={{0,4},{1,5},{2,6},{3,7},{4,0},{5,1},{6,2},{7,3},{8,12},{9,13},{10,... | collective-permute-start | bytes 196616 | tf_op jit(solution)/shard_map/ppermute | solution.py:14
  94.4 1.8 %collective-permute-start.30 = (bf16[32,1024]{1,0:T(8,128)(2,1)S(1)}, bf16[32,1024]{1,0:T(8,128)(2,1)S(1)}, u32[]{:S(2)}, u32[]{:S(2)}) collective-permute-start(bf16[32,1024]{1,0:T(8,128)(2,1)S(1)} %m23_sum.1.refs_0_), channel_id=1, source_target_pairs={{0,6},{1,7},{2,4},{3,5},{4,2},{5,3},{6,0},{7,1},{8,14},{9,15},{10,... | collective-permute-start | bytes 196616 | tf_op jit(solution)/shard_map/ppermute | solution.py:14
  97.4 3.1 %collective-permute-done.30.refs_3_ = bf16[32,1024]{1,0:T(8,128)(2,1)S(1)} collective-permute-done((bf16[32,1024]{1,0:T(8,128)(2,1)S(1)}, bf16[32,1024]{1,0:T(8,128)(2,1)S(1)}, u32[]{:S(2)}, u32[]{:S(2)}) %collective-permute-start.30) | collective-permute-done | bytes 65568 | tf_op jit(solution)/shard_map/ppermute | solution.py:14
  100.5 1.2 x2_x3.1.refs_0_.refs_4_
  101.7 1.5 %collective-permute-done.36.refs_1_.refs_5_ = bf16[2,128,512]{2,1,0:T(8,128)(2,1)S(1)} collective-permute-done((bf16[2,128,512]{2,1,0:T(8,128)(2,1)S(1)}, bf16[2,128,512]{2,1,0:T(8,128)(2,1)S(1)}, u32[]{:S(2)}, u32[]{:S(2)}) %collective-permute-start.36) | collective-permute-done | bytes 262176 | tf_op jit(solution)/shard_map/ppermute | solution.py:14
  104.3 1.2 collective-permute-start.37
  105.4 1.8 %collective-permute-start.40 = (bf16[128,512]{1,0:T(8,128)(2,1)S(1)}, bf16[128,512]{1,0:T(8,128)(2,1)S(1)}, u32[]{:S(2)}, u32[]{:S(2)}) collective-permute-start(bf16[128,512]{1,0:T(8,128)(2,1)S(1)} %get-tuple-element.69.refs_1_), channel_id=1, source_target_pairs={{0,16},{8,24},{16,0},{24,8},{1,17},{9,25},{17,1},{25,9},{2,18},{10... | collective-permute-start | bytes 393224 | tf_op jit(solution)/shard_map/ppermute | solution.py:14
  107.2 1.1 collective-permute-start.38
  108.4 1.9 %collective-permute-done.37.refs_2_ = bf16[128,512]{1,0:T(8,128)(2,1)S(1)} collective-permute-done((bf16[128,512]{1,0:T(8,128)(2,1)S(1)}, bf16[128,512]{1,0:T(8,128)(2,1)S(1)}, u32[]{:S(2)}, u32[]{:S(2)}) %collective-permute-start.37) | collective-permute-done | bytes 131104 | tf_op jit(solution)/shard_map/ppermute | solution.py:14
  110.3 2.3 %collective-permute-start.41 = (bf16[128,512]{1,0:T(8,128)(2,1)S(1)}, bf16[128,512]{1,0:T(8,128)(2,1)S(1)}, u32[]{:S(2)}, u32[]{:S(2)}) collective-permute-start(bf16[128,512]{1,0:T(8,128)(2,1)S(1)} %collective-permute-done.37.refs_2_), channel_id=1, source_target_pairs={{0,16},{8,24},{16,0},{24,8},{1,17},{9,25},{17,1},{25,9},{2,18},{10... | collective-permute-start | bytes 393224 | tf_op jit(solution)/shard_map/ppermute | solution.py:14
  113.5 1.6 %write_solved.1.refs_8_ = bf16[4,256,512]{2,1,0:T(8,128)(2,1)} custom-call(s32[4]{0:T(128)S(1)} %copy-done.9, s32[4,4]{1,0:T(4,128)S(1)} %bitcast.56, bf16[128,512]{1,0:T(8,128)(2,1)S(1)} %get-tuple-element.45.refs_0_.refs_6_.refs_3_, bf16[128,512]{1,0:T(8,128)(2,1)S(1)} %get-tuple-element.54.refs_4_.refs_1_, ...), custom_call_target="tpu_custom_call" | custom-call | bytes 2097152 | tf_op jit(solution)/shard_map/write_solved/pallas_call | solution.py:130
  115.1 1.2 collective-permute-done.41.refs_6_
  116.3 1.3 %collective-permute-done.42.refs_7_ = bf16[128,512]{1,0:T(8,128)(2,1)S(1)} collective-permute-done((bf16[128,512]{1,0:T(8,128)(2,1)S(1)}, bf16[128,512]{1,0:T(8,128)(2,1)S(1)}, u32[]{:S(2)}, u32[]{:S(2)}) %collective-permute-start.42) | collective-permute-done | bytes 131104 | tf_op jit(solution)/shard_map/ppermute | solution.py:14
  117.6 1.2 %copy-done.3 = bf16[4,256,512]{2,1,0:T(8,128)(2,1)S(1)} copy-done((bf16[4,256,512]{2,1,0:T(8,128)(2,1)S(1)}, bf16[4,256,512]{2,1,0:T(8,128)(2,1)}, u32[]{:S(2)}) %copy-start.3) | copy-done | bytes 1048600
  118.8 1.6 %write_updated.1 = bf16[4,256,512]{2,1,0:T(8,128)(2,1)} custom-call(s32[4]{0:T(128)S(1)} %copy-done.9, s32[4,4]{1,0:T(4,128)S(1)} %bitcast.57, bf16[128,512]{1,0:T(8,128)(2,1)S(1)} %get-tuple-element.68.refs_6_.refs_0_, bf16[128,512]{1,0:T(8,128)(2,1)S(1)} %get-tuple-element.69.refs_1_, bf16[128,512]{1,0:T(8,128)(2,1)S(1)} %collective-permute-done.37.refs_2_, ...), custom_call_target="tpu_custom_call" | custom-call | bytes 2097152 | tf_op jit(solution)/shard_map/write_updated/pallas_call | solution.py:130
  (89 shorter events, 22.4 us)
Async XLA Ops:
  0.6 6.2 %copy-start.4 = (s32[4,1,4]{2,1,0:T(1,128)S(1)}, s32[4,1,4]{2,1,0:T(1,128)}, u32[]{:S(2)}) copy-start(s32[4,1,4]{2,1,0:T(1,128)} %param.9) | copy-start | bytes 196
  0.6 11.2 %copy-start.2 = (bf16[1,4,256,512]{3,2,1,0:T(8,128)(2,1)S(1)}, bf16[1,4,256,512]{3,2,1,0:T(8,128)(2,1)}, u32[]{:S(2)}) copy-start(bf16[1,4,256,512]{3,2,1,0:T(8,128)(2,1)} %param.7) | copy-start | bytes 3145732
  0.6 6.2 %copy-start.9 = (s32[4]{0:T(128)S(1)}, s32[4]{0:T(128)}, u32[]{:S(2)}) copy-start(s32[4]{0:T(128)} %sup.51) | copy-start | bytes 52
  4.2 2.6 %collective-permute-start = (bf16[768,512]{1,0:T(8,128)(2,1)}, bf16[768,512]{1,0:T(8,128)(2,1)S(1)}, u32[]{:S(2)}, u32[]{:S(2)}) collective-permute-start(bf16[768,512]{1,0:T(8,128)(2,1)} %get-tuple-element.37), channel_id=1, source_target_pairs={{0,1},{1,0},{2,3},{3,2},{4,5},{5,4},{6,7},{7,6},{8,9},{9,8},{10,11... | collective-permute-start | bytes 2359304 | tf_op jit(solution)/shard_map/ppermute | solution.py:14
  8.8 14.2 %collective-permute-start.1 = (bf16[1280,128]{1,0:T(8,128)(2,1)S(1)}, bf16[1280,128]{1,0:T(8,128)(2,1)S(1)}, u32[]{:S(2)}, u32[]{:S(2)}) collective-permute-start(bf16[1280,128]{1,0:T(8,128)(2,1)S(1)} %get-tuple-element.39.refs_2_.refs_3_), channel_id=1, source_target_pairs={{0,2},{1,3},{2,0},{3,1},{4,6},{5,7},{6,4},{7,5},{8,10},{9,11},{10,... | collective-permute-start | bytes 983048 | tf_op jit(solution)/shard_map/ppermute | solution.py:14
  11.8 3.4 %copy-start = (bf16[4,1,4,512,512]{4,3,2,1,0:T(8,128)(2,1)S(1)}, bf16[4,1,4,512,512]{4,3,2,1,0:T(8,128)(2,1)}, u32[]{:S(2)}) copy-start(bf16[4,1,4,512,512]{4,3,2,1,0:T(8,128)(2,1)} %param.8) | copy-start | bytes 25165828
  15.9 33.0 %collective-permute-start.10 = (bf16[640,512]{1,0:T(8,128)(2,1)S(1)}, bf16[640,512]{1,0:T(8,128)(2,1)S(1)}, u32[]{:S(2)}, u32[]{:S(2)}) collective-permute-start(bf16[640,512]{1,0:T(8,128)(2,1)S(1)} %get-tuple-element.49), channel_id=1, source_target_pairs={{0,1},{1,0},{2,3},{3,2},{4,5},{5,4},{6,7},{7,6},{8,9},{9,8},{10,11... | collective-permute-start | bytes 1966088 | tf_op jit(solution)/shard_map/ppermute | solution.py:14
  19.3 33.7 %collective-permute-start.13 = (bf16[2,512,512]{2,1,0:T(8,128)(2,1)S(1)}, bf16[2,512,512]{2,1,0:T(8,128)(2,1)S(1)}, u32[]{:S(2)}, u32[]{:S(2)}) collective-permute-start(bf16[2,512,512]{2,1,0:T(8,128)(2,1)S(1)} %panel_send.2.refs_2_), channel_id=1, source_target_pairs={{0,8},{8,0},{16,24},{24,16},{1,9},{9,1},{17,25},{25,17},{2,10},{10... | collective-permute-start | bytes 3145736 | tf_op jit(solution)/shard_map/ppermute | solution.py:14
  21.5 34.7 %collective-permute-start.14 = (bf16[2,512,512]{2,1,0:T(8,128)(2,1)S(1)}, bf16[2,512,512]{2,1,0:T(8,128)(2,1)S(1)}, u32[]{:S(2)}, u32[]{:S(2)}) collective-permute-start(bf16[2,512,512]{2,1,0:T(8,128)(2,1)S(1)} %panel_send.3.refs_3_), channel_id=1, source_target_pairs={{0,16},{8,24},{16,0},{24,8},{1,17},{9,25},{17,1},{25,9},{2,18},{10... | collective-permute-start | bytes 3145736 | tf_op jit(solution)/shard_map/ppermute | solution.py:14
  23.7 12.7 %collective-permute-start.2 = (bf16[896,128]{1,0:T(8,128)(2,1)S(1)}, bf16[896,128]{1,0:T(8,128)(2,1)S(1)}, u32[]{:S(2)}, u32[]{:S(2)}) collective-permute-start(bf16[896,128]{1,0:T(8,128)(2,1)S(1)} %get-tuple-element.40.refs_2_.refs_0_), channel_id=1, source_target_pairs={{0,4},{1,5},{2,6},{3,7},{4,0},{5,1},{6,2},{7,3},{8,12},{9,13},{10,... | collective-permute-start | bytes 688136 | tf_op jit(solution)/shard_map/ppermute | solution.py:14
  26.4 7.2 %collective-permute-start.3 = (bf16[512,128]{1,0:T(8,128)(2,1)S(1)}, bf16[512,128]{1,0:T(8,128)(2,1)S(1)}, u32[]{:S(2)}, u32[]{:S(2)}) collective-permute-start(bf16[512,128]{1,0:T(8,128)(2,1)S(1)} %get-tuple-element.43), channel_id=1, source_target_pairs={{0,2},{1,3},{2,0},{3,1},{4,6},{5,7},{6,4},{7,5},{8,10},{9,11},{10,... | collective-permute-start | bytes 393224 | tf_op jit(solution)/shard_map/ppermute | solution.py:14
  34.2 5.3 %collective-permute-start.5 = (bf16[256,128]{1,0:T(8,128)(2,1)S(1)}, bf16[256,128]{1,0:T(8,128)(2,1)S(1)}, u32[]{:S(2)}, u32[]{:S(2)}) collective-permute-start(bf16[256,128]{1,0:T(8,128)(2,1)S(1)} %get-tuple-element.44.refs_4_), channel_id=1, source_target_pairs={{0,4},{1,5},{2,6},{3,7},{4,0},{5,1},{6,2},{7,3},{8,12},{9,13},{10,... | collective-permute-start | bytes 196616 | tf_op jit(solution)/shard_map/ppermute | solution.py:14
  36.4 14.4 %collective-permute-start.9 = (bf16[640,512]{1,0:T(8,128)(2,1)S(1)}, bf16[640,512]{1,0:T(8,128)(2,1)S(1)}, u32[]{:S(2)}, u32[]{:S(2)}) collective-permute-start(bf16[640,512]{1,0:T(8,128)(2,1)S(1)} %get-tuple-element.48), channel_id=1, source_target_pairs={{0,1},{1,0},{2,3},{3,2},{4,5},{5,4},{6,7},{7,6},{8,9},{9,8},{10,11... | collective-permute-start | bytes 1966088 | tf_op jit(solution)/shard_map/ppermute | solution.py:14
  39.5 1.3 %collective-permute-start.4 = (bf16[256,128]{1,0:T(8,128)(2,1)S(1)}, bf16[256,128]{1,0:T(8,128)(2,1)S(1)}, u32[]{:S(2)}, u32[]{:S(2)}) collective-permute-start(bf16[256,128]{1,0:T(8,128)(2,1)S(1)} %get-tuple-element.46.refs_1_), channel_id=1, source_target_pairs={{0,1},{1,0},{2,3},{3,2},{4,5},{5,4},{6,7},{7,6},{8,9},{9,8},{10,11... | collective-permute-start | bytes 196616 | tf_op jit(solution)/shard_map/ppermute | solution.py:14
  41.5 4.3 %collective-permute-start.6 = (f32[128,128]{1,0:T(8,128)S(1)}, f32[128,128]{1,0:T(8,128)S(1)}, u32[]{:S(2)}, u32[]{:S(2)}) collective-permute-start(f32[128,128]{1,0:T(8,128)S(1)} %term1.1.refs_0_.refs_7_.refs_2_), channel_id=1, source_target_pairs={{0,8},{8,0},{16,24},{24,16},{1,9},{9,1},{17,25},{25,17},{2,10},{10... | collective-permute-start | bytes 196616 | tf_op jit(solution)/shard_map/ppermute | solution.py:14
  46.4 4.4 %collective-permute-start.7 = (bf16[128,128]{1,0:T(8,128)(2,1)S(1)}, bf16[128,128]{1,0:T(8,128)(2,1)S(1)}, u32[]{:S(2)}, u32[]{:S(2)}) collective-permute-start(bf16[128,128]{1,0:T(8,128)(2,1)S(1)} %m1_sum.1), channel_id=1, source_target_pairs={{0,2},{1,3},{2,0},{3,1},{4,6},{5,7},{6,4},{7,5},{8,10},{9,11},{10,... | collective-permute-start | bytes 98312 | tf_op jit(solution)/shard_map/ppermute | solution.py:14
  48.9 8.1 %collective-permute-start.11 = (bf16[512,512]{1,0:T(8,128)(2,1)S(1)}, bf16[512,512]{1,0:T(8,128)(2,1)S(1)}, u32[]{:S(2)}, u32[]{:S(2)}) collective-permute-start(bf16[512,512]{1,0:T(8,128)(2,1)S(1)} %get-tuple-element.52), channel_id=1, source_target_pairs={{0,1},{1,0},{2,3},{3,2},{4,5},{5,4},{6,7},{7,6},{8,9},{9,8},{10,11... | collective-permute-start | bytes 1572872 | tf_op jit(solution)/shard_map/ppermute | solution.py:14
  50.8 6.2 %collective-permute-start.12 = (bf16[512,512]{1,0:T(8,128)(2,1)S(1)}, bf16[512,512]{1,0:T(8,128)(2,1)S(1)}, u32[]{:S(2)}, u32[]{:S(2)}) collective-permute-start(bf16[512,512]{1,0:T(8,128)(2,1)S(1)} %get-tuple-element.53), channel_id=1, source_target_pairs={{0,1},{1,0},{2,3},{3,2},{4,5},{5,4},{6,7},{7,6},{8,9},{9,8},{10,11... | collective-permute-start | bytes 1572872 | tf_op jit(solution)/shard_map/ppermute | solution.py:14
  50.8 6.2 %collective-permute-start.8 = (bf16[256,128]{1,0:T(8,128)(2,1)S(1)}, bf16[256,128]{1,0:T(8,128)(2,1)S(1)}, u32[]{:S(2)}, u32[]{:S(2)}) collective-permute-start(bf16[256,128]{1,0:T(8,128)(2,1)S(1)} %pad_maximum_fusion.refs_0_), channel_id=1, source_target_pairs={{0,4},{1,5},{2,6},{3,7},{4,0},{5,1},{6,2},{7,3},{8,12},{9,13},{10,... | collective-permute-start | bytes 196616 | tf_op jit(solution)/shard_map/ppermute | solution.py:14
  52.9 5.8 %collective-permute-start.22 = (bf16[256,128]{1,0:T(8,128)(2,1)S(1)}, bf16[256,128]{1,0:T(8,128)(2,1)S(1)}, u32[]{:S(2)}, u32[]{:S(2)}) collective-permute-start(bf16[256,128]{1,0:T(8,128)(2,1)S(1)} %add.13), channel_id=1, source_target_pairs={{0,8},{8,0},{16,24},{24,16},{1,9},{9,1},{17,25},{25,17},{2,10},{10... | collective-permute-start | bytes 196616 | tf_op jit(solution)/shard_map/ppermute | solution.py:14
  56.1 8.4 %collective-permute-start.15 = (bf16[128,512]{1,0:T(8,128)(2,1)S(1)}, bf16[128,512]{1,0:T(8,128)(2,1)S(1)}, u32[]{:S(2)}, u32[]{:S(2)}) collective-permute-start(bf16[128,512]{1,0:T(8,128)(2,1)S(1)} %get-tuple-element.45.refs_0_.refs_6_.refs_3_), channel_id=1, source_target_pairs={{0,1},{1,0},{2,3},{3,2},{4,5},{5,4},{6,7},{7,6},{8,9},{9,8},{10,11... | collective-permute-start | bytes 393224 | tf_op jit(solution)/shard_map/ppermute | solution.py:14
  58.2 8.5 %collective-permute-start.16 = (bf16[128,512]{1,0:T(8,128)(2,1)S(1)}, bf16[128,512]{1,0:T(8,128)(2,1)S(1)}, u32[]{:S(2)}, u32[]{:S(2)}) collective-permute-start(bf16[128,512]{1,0:T(8,128)(2,1)S(1)} %get-tuple-element.54.refs_4_.refs_1_), channel_id=1, source_target_pairs={{0,1},{1,0},{2,3},{3,2},{4,5},{5,4},{6,7},{7,6},{8,9},{9,8},{10,11... | collective-permute-start | bytes 393224 | tf_op jit(solution)/shard_map/ppermute | solution.py:14
  58.8 4.7 %collective-permute-start.23 = (bf16[256,128]{1,0:T(8,128)(2,1)S(1)}, bf16[256,128]{1,0:T(8,128)(2,1)S(1)}, u32[]{:S(2)}, u32[]{:S(2)}) collective-permute-start(bf16[256,128]{1,0:T(8,128)(2,1)S(1)} %add_convert_fusion.1), channel_id=1, source_target_pairs={{0,16},{8,24},{16,0},{24,8},{1,17},{9,25},{17,1},{25,9},{2,18},{10... | collective-permute-start | bytes 196616 | tf_op jit(solution)/shard_map/ppermute | solution.py:14
  60.3 30.9 %collective-permute-start.26 = (bf16[512,512]{1,0:T(8,128)(2,1)S(1)}, bf16[512,512]{1,0:T(8,128)(2,1)S(1)}, u32[]{:S(2)}, u32[]{:S(2)}) collective-permute-start(bf16[512,512]{1,0:T(8,128)(2,1)S(1)} %panel_join.2.refs_9_), channel_id=1, source_target_pairs={{0,16},{8,24},{16,0},{24,8},{1,17},{9,25},{17,1},{25,9},{2,18},{10... | collective-permute-start | bytes 1572872 | tf_op jit(solution)/shard_map/ppermute | solution.py:14
  60.8 30.4 %collective-permute-start.27 = (bf16[512,512]{1,0:T(8,128)(2,1)S(1)}, bf16[512,512]{1,0:T(8,128)(2,1)S(1)}, u32[]{:S(2)}, u32[]{:S(2)}) collective-permute-start(bf16[512,512]{1,0:T(8,128)(2,1)S(1)} %panel_join.3.refs_10_), channel_id=1, source_target_pairs={{0,8},{8,0},{16,24},{24,16},{1,9},{9,1},{17,25},{25,17},{2,10},{10... | collective-permute-start | bytes 1572872 | tf_op jit(solution)/shard_map/ppermute | solution.py:14
  63.5 7.1 %collective-permute-start.17 = (bf16[32,1024]{1,0:T(8,128)(2,1)S(1)}, bf16[32,1024]{1,0:T(8,128)(2,1)S(1)}, u32[]{:S(2)}, u32[]{:S(2)}) collective-permute-start(bf16[32,1024]{1,0:T(8,128)(2,1)S(1)} %get-tuple-element.56), channel_id=1, source_target_pairs={{0,2},{1,3},{2,0},{3,1},{4,6},{5,7},{6,4},{7,5},{8,10},{9,11},{10,... | collective-permute-start | bytes 196616 | tf_op jit(solution)/shard_map/ppermute | solution.py:14
  64.5 6.6 %collective-permute-start.18 = (bf16[32,1024]{1,0:T(8,128)(2,1)S(1)}, bf16[32,1024]{1,0:T(8,128)(2,1)S(1)}, u32[]{:S(2)}, u32[]{:S(2)}) collective-permute-start(bf16[32,1024]{1,0:T(8,128)(2,1)S(1)} %get-tuple-element.57), channel_id=1, source_target_pairs={{0,4},{1,5},{2,6},{3,7},{4,0},{5,1},{6,2},{7,3},{8,12},{9,13},{10,... | collective-permute-start | bytes 196616 | tf_op jit(solution)/shard_map/ppermute | solution.py:14
  66.6 6.3 %collective-permute-start.19 = (bf16[32,1024]{1,0:T(8,128)(2,1)S(1)}, bf16[32,1024]{1,0:T(8,128)(2,1)S(1)}, u32[]{:S(2)}, u32[]{:S(2)}) collective-permute-start(bf16[32,1024]{1,0:T(8,128)(2,1)S(1)} %get-tuple-element.58), channel_id=1, source_target_pairs={{0,6},{1,7},{2,4},{3,5},{4,2},{5,3},{6,0},{7,1},{8,14},{9,15},{10,... | collective-permute-start | bytes 196616 | tf_op jit(solution)/shard_map/ppermute | solution.py:14
  70.6 5.0 %collective-permute-start.24 = (bf16[256,128]{1,0:T(8,128)(2,1)S(1)}, bf16[256,128]{1,0:T(8,128)(2,1)S(1)}, u32[]{:S(2)}, u32[]{:S(2)}) collective-permute-start(bf16[256,128]{1,0:T(8,128)(2,1)S(1)} %add_convert_fusion.refs_0_), channel_id=1, source_target_pairs={{0,2},{1,3},{2,0},{3,1},{4,6},{5,7},{6,4},{7,5},{8,10},{9,11},{10,... | collective-permute-start | bytes 196616 | tf_op jit(solution)/shard_map/ppermute | solution.py:14
  73.5 4.9 %collective-permute-start.20 = (bf16[32,1024]{1,0:T(8,128)(2,1)S(1)}, bf16[32,1024]{1,0:T(8,128)(2,1)S(1)}, u32[]{:S(2)}, u32[]{:S(2)}) collective-permute-start(bf16[32,1024]{1,0:T(8,128)(2,1)S(1)} %t23_sum.1.refs_2_), channel_id=1, source_target_pairs={{0,8},{8,0},{16,24},{24,16},{1,9},{9,1},{17,25},{25,17},{2,10},{10... | collective-permute-start | bytes 196616 | tf_op jit(solution)/shard_map/ppermute | solution.py:14
  74.5 13.0 %collective-permute-start.32 = (bf16[2,128,512]{2,1,0:T(8,128)(2,1)S(1)}, bf16[2,128,512]{2,1,0:T(8,128)(2,1)S(1)}, u32[]{:S(2)}, u32[]{:S(2)}) collective-permute-start(bf16[2,128,512]{2,1,0:T(8,128)(2,1)S(1)} %get-tuple-element.59.refs_4_), channel_id=1, source_target_pairs={{0,8},{8,0},{16,24},{24,16},{1,9},{9,1},{17,25},{25,17},{2,10},{10... | collective-permute-start | bytes 786440 | tf_op jit(solution)/shard_map/ppermute | solution.py:14
  75.6 12.0 %collective-permute-start.33 = (bf16[2,128,512]{2,1,0:T(8,128)(2,1)S(1)}, bf16[2,128,512]{2,1,0:T(8,128)(2,1)S(1)}, u32[]{:S(2)}, u32[]{:S(2)}) collective-permute-start(bf16[2,128,512]{2,1,0:T(8,128)(2,1)S(1)} %get-tuple-element.63), channel_id=1, source_target_pairs={{0,16},{8,24},{16,0},{24,8},{1,17},{9,25},{17,1},{25,9},{2,18},{10... | collective-permute-start | bytes 786440 | tf_op jit(solution)/shard_map/ppermute | solution.py:14
  78.4 6.7 %collective-permute-start.25 = (bf16[512,128]{1,0:T(8,128)(2,1)S(1)}, bf16[512,128]{1,0:T(8,128)(2,1)S(1)}, u32[]{:S(2)}, u32[]{:S(2)}) collective-permute-start(bf16[512,128]{1,0:T(8,128)(2,1)S(1)} %p23_stack.1.refs_0_), channel_id=1, source_target_pairs={{0,4},{1,5},{2,6},{3,7},{4,0},{5,1},{6,2},{7,3},{8,12},{9,13},{10,... | collective-permute-start | bytes 393224 | tf_op jit(solution)/shard_map/ppermute | solution.py:14
  85.1 5.0 %collective-permute-start.21 = (f32[32,1024]{1,0:T(8,128)S(1)}, f32[32,1024]{1,0:T(8,128)S(1)}, u32[]{:S(2)}, u32[]{:S(2)}) collective-permute-start(f32[32,1024]{1,0:T(8,128)S(1)} %convert_add_fusion.refs_0_), channel_id=1, source_target_pairs={{0,16},{8,24},{16,0},{24,8},{1,17},{9,25},{17,1},{25,9},{2,18},{10... | collective-permute-start | bytes 393224 | tf_op jit(solution)/shard_map/ppermute | solution.py:14
  87.5 9.8 %collective-permute-start.31 = (bf16[256,512]{1,0:T(8,128)(2,1)S(1)}, bf16[256,512]{1,0:T(8,128)(2,1)S(1)}, u32[]{:S(2)}, u32[]{:S(2)}) collective-permute-start(bf16[256,512]{1,0:T(8,128)(2,1)S(1)} %p23_place.1.refs_2_.refs_5_), channel_id=1, source_target_pairs={{0,1},{1,0},{2,3},{3,2},{4,5},{5,4},{6,7},{7,6},{8,9},{9,8},{10,11... | collective-permute-start | bytes 786440 | tf_op jit(solution)/shard_map/ppermute | solution.py:14
  88.2 6.2 %collective-permute-start.34 = (bf16[128,512]{1,0:T(8,128)(2,1)S(1)}, bf16[128,512]{1,0:T(8,128)(2,1)S(1)}, u32[]{:S(2)}, u32[]{:S(2)}) collective-permute-start(bf16[128,512]{1,0:T(8,128)(2,1)S(1)} %get-tuple-element.64), channel_id=1, source_target_pairs={{0,16},{8,24},{16,0},{24,8},{1,17},{9,25},{17,1},{25,9},{2,18},{10... | collective-permute-start | bytes 393224 | tf_op jit(solution)/shard_map/ppermute | solution.py:14
  90.1 6.2 %collective-permute-start.35 = (bf16[128,512]{1,0:T(8,128)(2,1)S(1)}, bf16[128,512]{1,0:T(8,128)(2,1)S(1)}, u32[]{:S(2)}, u32[]{:S(2)}) collective-permute-start(bf16[128,512]{1,0:T(8,128)(2,1)S(1)} %get-tuple-element.65), channel_id=1, source_target_pairs={{0,8},{8,0},{16,24},{24,16},{1,9},{9,1},{17,25},{25,17},{2,10},{10... | collective-permute-start | bytes 393224 | tf_op jit(solution)/shard_map/ppermute | solution.py:14
  91.8 8.7 %copy-start.6 = (bf16[2,512,512]{2,1,0:T(8,128)(2,1)S(1)}, bf16[2,512,512]{2,1,0:T(8,128)(2,1)}, u32[]{:S(2)}) copy-start(bf16[2,512,512]{2,1,0:T(8,128)(2,1)} %refs_4_.1) | copy-start | bytes 3145732
  91.8 5.5 %collective-permute-start.28 = (bf16[32,1024]{1,0:T(8,128)(2,1)S(1)}, bf16[32,1024]{1,0:T(8,128)(2,1)S(1)}, u32[]{:S(2)}, u32[]{:S(2)}) collective-permute-start(bf16[32,1024]{1,0:T(8,128)(2,1)S(1)} %m23_sum.1.refs_0_), channel_id=1, source_target_pairs={{0,2},{1,3},{2,0},{3,1},{4,6},{5,7},{6,4},{7,5},{8,10},{9,11},{10,... | collective-permute-start | bytes 196616 | tf_op jit(solution)/shard_map/ppermute | solution.py:14
  91.9 5.5 %collective-permute-start.29 = (bf16[32,1024]{1,0:T(8,128)(2,1)S(1)}, bf16[32,1024]{1,0:T(8,128)(2,1)S(1)}, u32[]{:S(2)}, u32[]{:S(2)}) collective-permute-start(bf16[32,1024]{1,0:T(8,128)(2,1)S(1)} %m23_sum.1.refs_0_), channel_id=1, source_target_pairs={{0,4},{1,5},{2,6},{3,7},{4,0},{5,1},{6,2},{7,3},{8,12},{9,13},{10,... | collective-permute-start | bytes 196616 | tf_op jit(solution)/shard_map/ppermute | solution.py:14
  94.4 6.1 %collective-permute-start.30 = (bf16[32,1024]{1,0:T(8,128)(2,1)S(1)}, bf16[32,1024]{1,0:T(8,128)(2,1)S(1)}, u32[]{:S(2)}, u32[]{:S(2)}) collective-permute-start(bf16[32,1024]{1,0:T(8,128)(2,1)S(1)} %m23_sum.1.refs_0_), channel_id=1, source_target_pairs={{0,6},{1,7},{2,4},{3,5},{4,2},{5,3},{6,0},{7,1},{8,14},{9,15},{10,... | collective-permute-start | bytes 196616 | tf_op jit(solution)/shard_map/ppermute | solution.py:14
  101.7 1.6 %collective-permute-start.36 = (bf16[2,128,512]{2,1,0:T(8,128)(2,1)S(1)}, bf16[2,128,512]{2,1,0:T(8,128)(2,1)S(1)}, u32[]{:S(2)}, u32[]{:S(2)}) collective-permute-start(bf16[2,128,512]{2,1,0:T(8,128)(2,1)S(1)} %x2_x3.1.refs_0_.refs_4_), channel_id=1, source_target_pairs={{0,1},{1,0},{2,3},{3,2},{4,5},{5,4},{6,7},{7,6},{8,9},{9,8},{10,11... | collective-permute-start | bytes 786440 | tf_op jit(solution)/shard_map/ppermute | solution.py:14
  104.3 6.1 %collective-permute-start.37 = (bf16[128,512]{1,0:T(8,128)(2,1)S(1)}, bf16[128,512]{1,0:T(8,128)(2,1)S(1)}, u32[]{:S(2)}, u32[]{:S(2)}) collective-permute-start(bf16[128,512]{1,0:T(8,128)(2,1)S(1)} %get-tuple-element.68.refs_6_.refs_0_), channel_id=1, source_target_pairs={{0,8},{8,0},{16,24},{24,16},{1,9},{9,1},{17,25},{25,17},{2,10},{10... | collective-permute-start | bytes 393224 | tf_op jit(solution)/shard_map/ppermute | solution.py:14
  105.4 7.2 %collective-permute-start.40 = (bf16[128,512]{1,0:T(8,128)(2,1)S(1)}, bf16[128,512]{1,0:T(8,128)(2,1)S(1)}, u32[]{:S(2)}, u32[]{:S(2)}) collective-permute-start(bf16[128,512]{1,0:T(8,128)(2,1)S(1)} %get-tuple-element.69.refs_1_), channel_id=1, source_target_pairs={{0,16},{8,24},{16,0},{24,8},{1,17},{9,25},{17,1},{25,9},{2,18},{10... | collective-permute-start | bytes 393224 | tf_op jit(solution)/shard_map/ppermute | solution.py:14
  107.2 8.0 %collective-permute-start.38 = (bf16[128,512]{1,0:T(8,128)(2,1)S(1)}, bf16[128,512]{1,0:T(8,128)(2,1)S(1)}, u32[]{:S(2)}, u32[]{:S(2)}) collective-permute-start(bf16[128,512]{1,0:T(8,128)(2,1)S(1)} %get-tuple-element.69.refs_1_), channel_id=1, source_target_pairs={{0,8},{8,0},{16,24},{24,16},{1,9},{9,1},{17,25},{25,17},{2,10},{10... | collective-permute-start | bytes 393224 | tf_op jit(solution)/shard_map/ppermute | solution.py:14
  108.3 6.8 %collective-permute-start.39 = (bf16[128,512]{1,0:T(8,128)(2,1)S(1)}, bf16[128,512]{1,0:T(8,128)(2,1)S(1)}, u32[]{:S(2)}, u32[]{:S(2)}) collective-permute-start(bf16[128,512]{1,0:T(8,128)(2,1)S(1)} %get-tuple-element.68.refs_6_.refs_0_), channel_id=1, source_target_pairs={{0,16},{8,24},{16,0},{24,8},{1,17},{9,25},{17,1},{25,9},{2,18},{10... | collective-permute-start | bytes 393224 | tf_op jit(solution)/shard_map/ppermute | solution.py:14
  110.3 6.0 %collective-permute-start.41 = (bf16[128,512]{1,0:T(8,128)(2,1)S(1)}, bf16[128,512]{1,0:T(8,128)(2,1)S(1)}, u32[]{:S(2)}, u32[]{:S(2)}) collective-permute-start(bf16[128,512]{1,0:T(8,128)(2,1)S(1)} %collective-permute-done.37.refs_2_), channel_id=1, source_target_pairs={{0,16},{8,24},{16,0},{24,8},{1,17},{9,25},{17,1},{25,9},{2,18},{10... | collective-permute-start | bytes 393224 | tf_op jit(solution)/shard_map/ppermute | solution.py:14
  112.6 5.0 %collective-permute-start.42 = (bf16[128,512]{1,0:T(8,128)(2,1)S(1)}, bf16[128,512]{1,0:T(8,128)(2,1)S(1)}, u32[]{:S(2)}, u32[]{:S(2)}) collective-permute-start(bf16[128,512]{1,0:T(8,128)(2,1)S(1)} %collective-permute-done.40.refs_5_), channel_id=1, source_target_pairs={{0,8},{8,0},{16,24},{24,16},{1,9},{9,1},{17,25},{25,17},{2,10},{10... | collective-permute-start | bytes 393224 | tf_op jit(solution)/shard_map/ppermute | solution.py:14
  (5 other events, 9.6 us)

commit v6 on v5

--- a/solution.py
+++ b/solution.py
@@ -97,7 +97,7 @@
     def tile_value(meta, ref, of, level):
         return ref[...] * keep(live_owned(meta, of, level))
 
-    def run(body, operands, outs, scratch=(), steps=1, after=(), limit=32):
+    def run(body, operands, outs, scratch=(), steps=1, after=(), limit=40):
         arrays, specs, moved = [], [], 0
         for operand in operands:
             if isinstance(operand, InHbm):
@@ -265,7 +265,7 @@
         first_join,
         [near_kept, near_got],
         [shaped((b0_rows + column_rows, lanes)), shaped((column_rows, lanes))],
-        after=first_sent,
+        after=[*first_sent],
     )
     far_got = swap(far_send, "row", far)
 
@@ -310,6 +310,7 @@
         [rows_half, shaped((half_w, lanes)), shaped((half_r, lanes))],
         after=[p23_send],
     )
+    x0_other = swap(x0, "row", 1)
     p01_other = swap(p01, "row", 1)
 
     def term1(meta, x0, p, p_other, b, t1, whole):
@@ -344,7 +345,7 @@
     def m1_sum(meta, a, b, out):
         out[...] = (a[...] + b[...]).astype(BF16)
 
-    m1 = run(m1_sum, [t1, swap(t1, "leaf", 1)], shaped((half_r, lanes)))
+    m1 = run(m1_sum, [t1, swap(t1, "leaf", 1)], shaped((half_r, lanes)), after=[])
     m1 = jnp.concatenate([m1, swap(m1, "row", near)])
     m1_far = swap(m1, "row", far)
     p23 = (p23.astype(F32) + p23_turned.astype(F32)).astype(BF16)
@@ -387,10 +388,10 @@
         [m1, m1_far, pair] + us + [tile(1, 2), tile(1, 3)] + linked_got,
         [rows_half] + [strip] * chips,
         [pltpu.VMEM((half_r, 2 * width), F32)],
-        after=panel_sent,
+        after=[*panel_sent],
     )
     strips[1:] = [swap(piece, "row", step) for piece, step in zip(strips[1:], steps_up)]
-    x01_other = [swap(x, "row", 1) for x in (x0, x1)]
+    x01_other = [x0_other, swap(x1, "row", 1)]
 
     ways = ((1, 2), (2, 1))
 
@@ -457,7 +458,7 @@
         out[:half_w] = a[...]
         out[half_w:] = b[...]
 
-    p23 = run(p23_stack, [p23, p23_next], p23_pair, after=[t23])
+    p23 = run(p23_stack, [p23, p23_next], p23_pair, after=[x1])
     p23_far = swap(p23, "row", far)
 
     def p23_place(meta, near_two, far_two, out):
@@ -479,7 +480,7 @@
         m23_sum,
         [t23, t23_far],
         strip,
-        after=[p23_half, *panel_far],
+        after=[p23_half, *share_sent],
     )
     m23_parts = [m23] + [swap(m23, "row", step) for step in steps_up]
 
@@ -519,7 +520,7 @@
         m23_parts + [diag_root, p23_half, p23_other],
         shaped((2, half_r, width)),
         [pltpu.VMEM((half_r, 2 * width), BF16), pltpu.VMEM((width, width), BF16)],
-        after=[share_sum],
+        after=[panel_sum],
     )
     x23_other = swap(x23, "row", 1)
 
@@ -572,7 +573,7 @@
         write_updated,
         [top, bottom, top_1, bottom_1, top_2, bottom_2, top_3, bottom_3],
         shaped((n_leaf, height, width)),
-        after=[solved],
+        after=[],
     )
     return solved[:, None], updated
 

time: 121 us -> 116 us (0.959)
  waiting for transfers between devices: 38.9 us -> 35.1 us
  Pallas kernels: 26 us -> 27.3 us
  local copies, waits for them, and re-layouts: 8.4 us -> 7.18 us
    ppermute x43, waiting for transfers between devices: 38.9 us -> 35.1 us  [swap(): lax.ppermute(block, axis, [(i, i ^ bits) for i in range(lax.axis_size(axi...]
    unnamed x20 -> x18, local copies, waits for them, and re-layouts: 8.4 us -> 7.18 us
  transfers between devices with their start and end apart: 43 -> 43, of which waited for: 18 -> 19; matrix products, arithmetic and copies ran while one was open for 0% -> 0% of each run, Pallas kernels for 15% -> 17%
where the time goes in v6:
time: 116 us
  starting transfers between devices  45 us (39%)
  waiting for transfers between devices  35.1 us (30%)
  Pallas kernels  27.3 us (24%)
  local copies, waits for them, and re-layouts  7.18 us (6%)
    ppermute x43, starting transfers between devices, swap(): lax.ppermute(block, axis, [(i, i ^ bits) for i in range(lax.axis_size(axi...  45 us
    ppermute x43, waiting for transfers between devices, swap(): lax.ppermute(block, axis, [(i, i ^ bits) for i in range(lax.axis_size(axi...  35.1 us
    pallas_call x26, Pallas kernels, run(): pl.pallas_call(kernel, grid_spec=pltpu.PrefetchScalarGridSpec(num_scalar_...  27.3 us
    unnamed x18, local copies, waits for them, and re-layouts  7.18 us
  transfers between devices with their start and end apart: 43, of which 19 were waited for; matrix products, arithmetic and copies ran while one was open for 0% of the time, Pallas kernels for 17%

profile of v6, /device:TPU:0, one launch (start us, length us, event | category | flops | bytes accessed | tf_op | source)
XLA Modules:
  0.0 115.7 jit_solution(563415629775255293)
XLA Ops:
  0.7 3.6 %first_send.1 = (bf16[768,512]{1,0:T(8,128)(2,1)}, bf16[768,512]{1,0:T(8,128)(2,1)}) custom-call(s32[4]{0:T(128)} %sup.51, s32[4,4]{1,0:T(4,128)} %bitcast.31, bf16[4,256,512]{2,1,0:T(8,128)(2,1)} %bitcast.25, bf16[4,4,512,512]{3,2,1,0:T(8,128)(2,1)} %bitcast.6), custom_call_target="tpu_custom_call" | custom-call | bytes 1572864 | tf_op jit(solution)/shard_map/first_send/pallas_call | solution.py:130
  4.7 2.1 %collective-permute-done.refs_1_ = bf16[768,512]{1,0:T(8,128)(2,1)S(1)} collective-permute-done((bf16[768,512]{1,0:T(8,128)(2,1)}, bf16[768,512]{1,0:T(8,128)(2,1)S(1)}, u32[]{:S(2)}, u32[]{:S(2)}) %collective-permute-start) | collective-permute-done | bytes 786464 | tf_op jit(solution)/shard_map/ppermute | solution.py:14
  6.9 1.1 copy-done.6
  8.8 3.0 %collective-permute-start.1 = (bf16[1280,128]{1,0:T(8,128)(2,1)S(1)}, bf16[1280,128]{1,0:T(8,128)(2,1)S(1)}, u32[]{:S(2)}, u32[]{:S(2)}) collective-permute-start(bf16[1280,128]{1,0:T(8,128)(2,1)S(1)} %get-tuple-element.39.refs_2_.refs_3_), channel_id=1, source_target_pairs={{0,2},{1,3},{2,0},{3,1},{4,6},{5,7},{6,4},{7,5},{8,10},{9,11},{10,... | collective-permute-start | bytes 983048 | tf_op jit(solution)/shard_map/ppermute | solution.py:14
  11.8 3.4 %copy-done = bf16[4,1,4,512,512]{4,3,2,1,0:T(8,128)(2,1)S(1)} copy-done((bf16[4,1,4,512,512]{4,3,2,1,0:T(8,128)(2,1)S(1)}, bf16[4,1,4,512,512]{4,3,2,1,0:T(8,128)(2,1)}, u32[]{:S(2)}) %copy-start) | copy-done | bytes 8388632
  16.0 2.6 %copy-done.1 = bf16[4,1,4,512,512]{4,3,2,1,0:T(8,128)(2,1)S(1)} copy-done((bf16[4,1,4,512,512]{4,3,2,1,0:T(8,128)(2,1)S(1)}, bf16[4,1,4,512,512]{4,3,2,1,0:T(8,128)(2,1)}, u32[]{:S(2)}) %copy-start.1) | copy-done | bytes 8388632
  19.3 1.6 %collective-permute-start.13 = (bf16[2,512,512]{2,1,0:T(8,128)(2,1)S(1)}, bf16[2,512,512]{2,1,0:T(8,128)(2,1)S(1)}, u32[]{:S(2)}, u32[]{:S(2)}) collective-permute-start(bf16[2,512,512]{2,1,0:T(8,128)(2,1)S(1)} %panel_send.2.refs_2_), channel_id=1, source_target_pairs={{0,8},{8,0},{16,24},{24,16},{1,9},{9,1},{17,25},{25,17},{2,10},{10... | collective-permute-start | bytes 3145736 | tf_op jit(solution)/shard_map/ppermute | solution.py:14
  21.5 1.6 %collective-permute-start.14 = (bf16[2,512,512]{2,1,0:T(8,128)(2,1)S(1)}, bf16[2,512,512]{2,1,0:T(8,128)(2,1)S(1)}, u32[]{:S(2)}, u32[]{:S(2)}) collective-permute-start(bf16[2,512,512]{2,1,0:T(8,128)(2,1)S(1)} %panel_send.3.refs_3_), channel_id=1, source_target_pairs={{0,16},{8,24},{16,0},{24,8},{1,17},{9,25},{17,1},{25,9},{2,18},{10... | collective-permute-start | bytes 3145736 | tf_op jit(solution)/shard_map/ppermute | solution.py:14
  23.7 2.7 %collective-permute-start.2 = (bf16[896,128]{1,0:T(8,128)(2,1)S(1)}, bf16[896,128]{1,0:T(8,128)(2,1)S(1)}, u32[]{:S(2)}, u32[]{:S(2)}) collective-permute-start(bf16[896,128]{1,0:T(8,128)(2,1)S(1)} %get-tuple-element.40.refs_2_.refs_0_), channel_id=1, source_target_pairs={{0,4},{1,5},{2,6},{3,7},{4,0},{5,1},{6,2},{7,3},{8,12},{9,13},{10,... | collective-permute-start | bytes 688136 | tf_op jit(solution)/shard_map/ppermute | solution.py:14
  26.8 6.7 %collective-permute-done.3.refs_1_ = bf16[512,128]{1,0:T(8,128)(2,1)S(1)} collective-permute-done((bf16[512,128]{1,0:T(8,128)(2,1)S(1)}, bf16[512,128]{1,0:T(8,128)(2,1)S(1)}, u32[]{:S(2)}, u32[]{:S(2)}) %collective-permute-start.3) | collective-permute-done | bytes 131104 | tf_op jit(solution)/shard_map/ppermute | solution.py:14
  34.2 1.3 %collective-permute-start.5 = (bf16[256,128]{1,0:T(8,128)(2,1)S(1)}, bf16[256,128]{1,0:T(8,128)(2,1)S(1)}, u32[]{:S(2)}, u32[]{:S(2)}) collective-permute-start(bf16[256,128]{1,0:T(8,128)(2,1)S(1)} %get-tuple-element.44.refs_4_), channel_id=1, source_target_pairs={{0,4},{1,5},{2,6},{3,7},{4,0},{5,1},{6,2},{7,3},{8,12},{9,13},{10,... | collective-permute-start | bytes 196616 | tf_op jit(solution)/shard_map/ppermute | solution.py:14
  37.2 2.2 %collective-permute-done.5.refs_4_ = bf16[256,128]{1,0:T(8,128)(2,1)S(1)} collective-permute-done((bf16[256,128]{1,0:T(8,128)(2,1)S(1)}, bf16[256,128]{1,0:T(8,128)(2,1)S(1)}, u32[]{:S(2)}, u32[]{:S(2)}) %collective-permute-start.5) | collective-permute-done | bytes 65568 | tf_op jit(solution)/shard_map/ppermute | solution.py:14
  39.5 1.3 %collective-permute-done.4.refs_2_ = bf16[256,128]{1,0:T(8,128)(2,1)S(1)} collective-permute-done((bf16[256,128]{1,0:T(8,128)(2,1)S(1)}, bf16[256,128]{1,0:T(8,128)(2,1)S(1)}, u32[]{:S(2)}, u32[]{:S(2)}) %collective-permute-start.4) | collective-permute-done | bytes 65568 | tf_op jit(solution)/shard_map/ppermute | solution.py:14
  42.1 3.7 %collective-permute-done.6.refs_1_ = f32[128,128]{1,0:T(8,128)S(1)} collective-permute-done((f32[128,128]{1,0:T(8,128)S(1)}, f32[128,128]{1,0:T(8,128)S(1)}, u32[]{:S(2)}, u32[]{:S(2)}) %collective-permute-start.6) | collective-permute-done | bytes 65568 | tf_op jit(solution)/shard_map/ppermute | solution.py:14
  46.4 2.5 %collective-permute-start.7 = (bf16[128,128]{1,0:T(8,128)(2,1)S(1)}, bf16[128,128]{1,0:T(8,128)(2,1)S(1)}, u32[]{:S(2)}, u32[]{:S(2)}) collective-permute-start(bf16[128,128]{1,0:T(8,128)(2,1)S(1)} %m1_sum.1), channel_id=1, source_target_pairs={{0,2},{1,3},{2,0},{3,1},{4,6},{5,7},{6,4},{7,5},{8,10},{9,11},{10,... | collective-permute-start | bytes 98312 | tf_op jit(solution)/shard_map/ppermute | solution.py:14
  48.9 1.9 %collective-permute-done.7 = bf16[128,128]{1,0:T(8,128)(2,1)S(1)} collective-permute-done((bf16[128,128]{1,0:T(8,128)(2,1)S(1)}, bf16[128,128]{1,0:T(8,128)(2,1)S(1)}, u32[]{:S(2)}, u32[]{:S(2)}) %collective-permute-start.7) | collective-permute-done | bytes 32800 | tf_op jit(solution)/shard_map/ppermute | solution.py:14
  50.8 2.1 %collective-permute-start.8 = (bf16[256,128]{1,0:T(8,128)(2,1)S(1)}, bf16[256,128]{1,0:T(8,128)(2,1)S(1)}, u32[]{:S(2)}, u32[]{:S(2)}) collective-permute-start(bf16[256,128]{1,0:T(8,128)(2,1)S(1)} %pad_maximum_fusion.refs_0_), channel_id=1, source_target_pairs={{0,4},{1,5},{2,6},{3,7},{4,0},{5,1},{6,2},{7,3},{8,12},{9,13},{10,... | collective-permute-start | bytes 196616 | tf_op jit(solution)/shard_map/ppermute | solution.py:14
  52.9 1.6 %collective-permute-start.22 = (bf16[256,128]{1,0:T(8,128)(2,1)S(1)}, bf16[256,128]{1,0:T(8,128)(2,1)S(1)}, u32[]{:S(2)}, u32[]{:S(2)}) collective-permute-start(bf16[256,128]{1,0:T(8,128)(2,1)S(1)} %add.13), channel_id=1, source_target_pairs={{0,8},{8,0},{16,24},{24,16},{1,9},{9,1},{17,25},{25,17},{2,10},{10... | collective-permute-start | bytes 196616 | tf_op jit(solution)/shard_map/ppermute | solution.py:14
  57.0 1.2 %x1_t23.1 = (bf16[128,512]{1,0:T(8,128)(2,1)S(1)}, bf16[32,1024]{1,0:T(8,128)(2,1)S(1)}, bf16[32,1024]{1,0:T(8,128)(2,1)S(1)}, bf16[32,1024]{1,0:T(8,128)(2,1)S(1)}, bf16[32,1024]{1,0:T(8,128)(2,1)S(1)}) custom-call(s32[4]{0:T(128)S(1)} %copy-done.8, s32[4,4]{1,0:T(4,128)S(1)} %bitcast.45, bf16[256,128]{1,0:T(8,128)(2,1)S(1)} %pad_maximum_fusion.refs_0_, ...), custom_call_target="tpu_custom_call" | custom-call | bytes 3670016 | tf_op jit(solution)/shard_map/x1_t23/pallas_call | solution.py:130
  58.8 1.6 %collective-permute-start.23 = (bf16[256,128]{1,0:T(8,128)(2,1)S(1)}, bf16[256,128]{1,0:T(8,128)(2,1)S(1)}, u32[]{:S(2)}, u32[]{:S(2)}) collective-permute-start(bf16[256,128]{1,0:T(8,128)(2,1)S(1)} %add_convert_fusion.1), channel_id=1, source_target_pairs={{0,16},{8,24},{16,0},{24,8},{1,17},{9,25},{17,1},{25,9},{2,18},{10... | collective-permute-start | bytes 196616 | tf_op jit(solution)/shard_map/ppermute | solution.py:14
  60.8 1.1 collective-permute-start.33
  62.0 1.5 %collective-permute-done.23 = bf16[256,128]{1,0:T(8,128)(2,1)S(1)} collective-permute-done((bf16[256,128]{1,0:T(8,128)(2,1)S(1)}, bf16[256,128]{1,0:T(8,128)(2,1)S(1)}, u32[]{:S(2)}, u32[]{:S(2)}) %collective-permute-start.23) | collective-permute-done | bytes 65568 | tf_op jit(solution)/shard_map/ppermute | solution.py:14
  63.5 1.0 collective-permute-start.17
  64.5 2.1 %collective-permute-start.18 = (bf16[32,1024]{1,0:T(8,128)(2,1)S(1)}, bf16[32,1024]{1,0:T(8,128)(2,1)S(1)}, u32[]{:S(2)}, u32[]{:S(2)}) collective-permute-start(bf16[32,1024]{1,0:T(8,128)(2,1)S(1)} %get-tuple-element.57), channel_id=1, source_target_pairs={{0,4},{1,5},{2,6},{3,7},{4,0},{5,1},{6,2},{7,3},{8,12},{9,13},{10,... | collective-permute-start | bytes 196616 | tf_op jit(solution)/shard_map/ppermute | solution.py:14
  66.6 1.2 %collective-permute-start.19 = (bf16[32,1024]{1,0:T(8,128)(2,1)S(1)}, bf16[32,1024]{1,0:T(8,128)(2,1)S(1)}, u32[]{:S(2)}, u32[]{:S(2)}) collective-permute-start(bf16[32,1024]{1,0:T(8,128)(2,1)S(1)} %get-tuple-element.58), channel_id=1, source_target_pairs={{0,6},{1,7},{2,4},{3,5},{4,2},{5,3},{6,0},{7,1},{8,14},{9,15},{10,... | collective-permute-start | bytes 196616 | tf_op jit(solution)/shard_map/ppermute | solution.py:14
  67.9 2.7 %update01.1 = (bf16[2,128,512]{2,1,0:T(8,128)(2,1)S(1)}, bf16[2,128,512]{2,1,0:T(8,128)(2,1)S(1)}, f32[2,128,512]{2,1,0:T(8,128)S(1)}, f32[2,128,512]{2,1,0:T(8,128)S(1)}) custom-call(s32[4]{0:T(128)S(1)} %copy-done.8, s32[4,4]{1,0:T(4,128)S(1)} %bitcast.46, bf16[4,256,512]{2,1,0:T(8,128)(2,1)S(1)} %bitcast.30, bf16[4,4,512,512]{3,2,1,0:T(8,128)(2,1)S(1)} %bitcast.23, ...), custom_call_target="tpu_custom_call" | custom-call | bytes 8912896 | tf_op jit(solution)/shard_map/update01/pallas_call | solution.py:130
  71.1 1.8 %collective-permute-done.19.refs_3_ = bf16[32,1024]{1,0:T(8,128)(2,1)S(1)} collective-permute-done((bf16[32,1024]{1,0:T(8,128)(2,1)S(1)}, bf16[32,1024]{1,0:T(8,128)(2,1)S(1)}, u32[]{:S(2)}, u32[]{:S(2)}) %collective-permute-start.19) | collective-permute-done | bytes 65568 | tf_op jit(solution)/shard_map/ppermute | solution.py:14
  74.5 1.9 %collective-permute-start.27 = (bf16[2,128,512]{2,1,0:T(8,128)(2,1)S(1)}, bf16[2,128,512]{2,1,0:T(8,128)(2,1)S(1)}, u32[]{:S(2)}, u32[]{:S(2)}) collective-permute-start(bf16[2,128,512]{2,1,0:T(8,128)(2,1)S(1)} %get-tuple-element.63), channel_id=1, source_target_pairs={{0,16},{8,24},{16,0},{24,8},{1,17},{9,25},{17,1},{25,9},{2,18},{10... | collective-permute-start | bytes 786440 | tf_op jit(solution)/shard_map/ppermute | solution.py:14
  76.9 1.0 collective-permute-start.25
  78.7 4.8 %collective-permute-done.25.refs_1_ = bf16[512,128]{1,0:T(8,128)(2,1)S(1)} collective-permute-done((bf16[512,128]{1,0:T(8,128)(2,1)S(1)}, bf16[512,128]{1,0:T(8,128)(2,1)S(1)}, u32[]{:S(2)}, u32[]{:S(2)}) %collective-permute-start.25) | collective-permute-done | bytes 131104 | tf_op jit(solution)/shard_map/ppermute | solution.py:14
  85.4 1.6 %collective-permute-start.34 = (bf16[128,512]{1,0:T(8,128)(2,1)S(1)}, bf16[128,512]{1,0:T(8,128)(2,1)S(1)}, u32[]{:S(2)}, u32[]{:S(2)}) collective-permute-start(bf16[128,512]{1,0:T(8,128)(2,1)S(1)} %get-tuple-element.64.refs_3_), channel_id=1, source_target_pairs={{0,16},{8,24},{16,0},{24,8},{1,17},{9,25},{17,1},{25,9},{2,18},{10... | collective-permute-start | bytes 393224 | tf_op jit(solution)/shard_map/ppermute | solution.py:14
  87.0 1.5 %collective-permute-done.21.refs_1_ = f32[32,1024]{1,0:T(8,128)S(1)} collective-permute-done((f32[32,1024]{1,0:T(8,128)S(1)}, f32[32,1024]{1,0:T(8,128)S(1)}, u32[]{:S(2)}, u32[]{:S(2)}) %collective-permute-start.21) | collective-permute-done | bytes 131104 | tf_op jit(solution)/shard_map/ppermute | solution.py:14
  90.1 2.1 %collective-permute-start.30 = (bf16[32,1024]{1,0:T(8,128)(2,1)S(1)}, bf16[32,1024]{1,0:T(8,128)(2,1)S(1)}, u32[]{:S(2)}, u32[]{:S(2)}) collective-permute-start(bf16[32,1024]{1,0:T(8,128)(2,1)S(1)} %m23_sum.1.refs_0_), channel_id=1, source_target_pairs={{0,6},{1,7},{2,4},{3,5},{4,2},{5,3},{6,0},{7,1},{8,14},{9,15},{10,... | collective-permute-start | bytes 196616 | tf_op jit(solution)/shard_map/ppermute | solution.py:14
  92.3 2.3 %collective-permute-start.28 = (bf16[32,1024]{1,0:T(8,128)(2,1)S(1)}, bf16[32,1024]{1,0:T(8,128)(2,1)S(1)}, u32[]{:S(2)}, u32[]{:S(2)}) collective-permute-start(bf16[32,1024]{1,0:T(8,128)(2,1)S(1)} %m23_sum.1.refs_0_), channel_id=1, source_target_pairs={{0,2},{1,3},{2,0},{3,1},{4,6},{5,7},{6,4},{7,5},{8,10},{9,11},{10,... | collective-permute-start | bytes 196616 | tf_op jit(solution)/shard_map/ppermute | solution.py:14
  94.6 2.3 %leaf_sums.1 = (bf16[2,512,512]{2,1,0:T(8,128)(2,1)S(1)}, f32[256,512]{1,0:T(8,128)S(1)}) custom-call(s32[4]{0:T(128)S(1)} %copy-done.8, s32[4,4]{1,0:T(4,128)S(1)} %bitcast.52, bf16[4,4,512,512]{3,2,1,0:T(8,128)(2,1)} %bitcast.7, bf16[4,4,512,512]{3,2,1,0:T(8,128)(2,1)} %bitcast.8, bf16[2,512,512]{2,1,0:T(8,128)(2,1)S(1)} %collective-permute-done.13.refs_1_.refs_2_, ...), custom_call_target="tpu_custom_call" | custom-call | bytes 7602176 | tf_op jit(solution)/shard_map/leaf_sums/pallas_call | solution.py:130
  96.9 1.0 collective-permute-done.29.refs_2_
  97.9 1.2 %x2_x3.1.refs_0_.refs_4_ = bf16[2,128,512]{2,1,0:T(8,128)(2,1)S(1)} custom-call(s32[4]{0:T(128)S(1)} %copy-done.8, s32[4,4]{1,0:T(4,128)S(1)} %bitcast.53, bf16[32,1024]{1,0:T(8,128)(2,1)S(1)} %m23_sum.1.refs_0_, bf16[32,1024]{1,0:T(8,128)(2,1)S(1)} %collective-permute-done.28.refs_1_, bf16[32,1024]{1,0:T(8,128)(2,1)S(1)} %collective-permute-done.29.refs_2_, ...), custom_call_target="tpu_custom_call" | custom-call | bytes 2097152 | tf_op jit(solution)/shard_map/x2_x3/pallas_call | solution.py:130
  99.1 1.5 %collective-permute-done.36.refs_1_.refs_5_ = bf16[2,128,512]{2,1,0:T(8,128)(2,1)S(1)} collective-permute-done((bf16[2,128,512]{2,1,0:T(8,128)(2,1)S(1)}, bf16[2,128,512]{2,1,0:T(8,128)(2,1)S(1)}, u32[]{:S(2)}, u32[]{:S(2)}) %collective-permute-start.36) | collective-permute-done | bytes 262176 | tf_op jit(solution)/shard_map/ppermute | solution.py:14
  100.6 1.0 final.1
  101.6 1.1 collective-permute-start.40
  103.5 1.3 %collective-permute-start.38 = (bf16[128,512]{1,0:T(8,128)(2,1)S(1)}, bf16[128,512]{1,0:T(8,128)(2,1)S(1)}, u32[]{:S(2)}, u32[]{:S(2)}) collective-permute-start(bf16[128,512]{1,0:T(8,128)(2,1)S(1)} %get-tuple-element.69.refs_1_), channel_id=1, source_target_pairs={{0,8},{8,0},{16,24},{24,16},{1,9},{9,1},{17,25},{25,17},{2,10},{10... | collective-permute-start | bytes 393224 | tf_op jit(solution)/shard_map/ppermute | solution.py:14
  104.8 1.0 collective-permute-start.39
  105.8 2.0 %collective-permute-done.40.refs_5_ = bf16[128,512]{1,0:T(8,128)(2,1)S(1)} collective-permute-done((bf16[128,512]{1,0:T(8,128)(2,1)S(1)}, bf16[128,512]{1,0:T(8,128)(2,1)S(1)}, u32[]{:S(2)}, u32[]{:S(2)}) %collective-permute-start.40) | collective-permute-done | bytes 131104 | tf_op jit(solution)/shard_map/ppermute | solution.py:14
  107.8 1.3 %collective-permute-start.42 = (bf16[128,512]{1,0:T(8,128)(2,1)S(1)}, bf16[128,512]{1,0:T(8,128)(2,1)S(1)}, u32[]{:S(2)}, u32[]{:S(2)}) collective-permute-start(bf16[128,512]{1,0:T(8,128)(2,1)S(1)} %collective-permute-done.40.refs_5_), channel_id=1, source_target_pairs={{0,8},{8,0},{16,24},{24,16},{1,9},{9,1},{17,25},{25,17},{2,10},{10... | collective-permute-start | bytes 393224 | tf_op jit(solution)/shard_map/ppermute | solution.py:14
  109.1 1.0 collective-permute-start.41
  110.1 1.6 %write_solved.1 = bf16[4,256,512]{2,1,0:T(8,128)(2,1)} custom-call(s32[4]{0:T(128)S(1)} %copy-done.8, s32[4,4]{1,0:T(4,128)S(1)} %bitcast.55, bf16[128,512]{1,0:T(8,128)(2,1)S(1)} %get-tuple-element.45.refs_0_.refs_6_.refs_3_, bf16[128,512]{1,0:T(8,128)(2,1)S(1)} %get-tuple-element.54.refs_4_.refs_2_.refs_1_, ...), custom_call_target="tpu_custom_call" | custom-call | bytes 2097152 | tf_op jit(solution)/shard_map/write_solved/pallas_call | solution.py:130
  111.9 1.7 %collective-permute-done.42.refs_7_ = bf16[128,512]{1,0:T(8,128)(2,1)S(1)} collective-permute-done((bf16[128,512]{1,0:T(8,128)(2,1)S(1)}, bf16[128,512]{1,0:T(8,128)(2,1)S(1)}, u32[]{:S(2)}, u32[]{:S(2)}) %collective-permute-start.42) | collective-permute-done | bytes 131104 | tf_op jit(solution)/shard_map/ppermute | solution.py:14
  114.1 1.6 %write_updated.1 = bf16[4,256,512]{2,1,0:T(8,128)(2,1)} custom-call(s32[4]{0:T(128)S(1)} %copy-done.8, s32[4,4]{1,0:T(4,128)S(1)} %bitcast.56, bf16[128,512]{1,0:T(8,128)(2,1)S(1)} %get-tuple-element.68.refs_6_.refs_0_, bf16[128,512]{1,0:T(8,128)(2,1)S(1)} %get-tuple-element.69.refs_1_, bf16[128,512]{1,0:T(8,128)(2,1)S(1)} %collective-permute-done.37.refs_2_, ...), custom_call_target="tpu_custom_call" | custom-call | bytes 2097152 | tf_op jit(solution)/shard_map/write_updated/pallas_call | solution.py:130
  (87 shorter events, 20.8 us)
Async XLA Ops:
  0.6 6.2 %copy-start.8 = (s32[4]{0:T(128)S(1)}, s32[4]{0:T(128)}, u32[]{:S(2)}) copy-start(s32[4]{0:T(128)} %sup.51) | copy-start | bytes 52
  0.6 6.2 %copy-start.3 = (s32[4,1,4]{2,1,0:T(1,128)S(1)}, s32[4,1,4]{2,1,0:T(1,128)}, u32[]{:S(2)}) copy-start(s32[4,1,4]{2,1,0:T(1,128)} %param.9) | copy-start | bytes 196
  0.6 11.2 %copy-start.2 = (bf16[1,4,256,512]{3,2,1,0:T(8,128)(2,1)S(1)}, bf16[1,4,256,512]{3,2,1,0:T(8,128)(2,1)}, u32[]{:S(2)}) copy-start(bf16[1,4,256,512]{3,2,1,0:T(8,128)(2,1)} %param.7) | copy-start | bytes 3145732
  4.2 2.6 %collective-permute-start = (bf16[768,512]{1,0:T(8,128)(2,1)}, bf16[768,512]{1,0:T(8,128)(2,1)S(1)}, u32[]{:S(2)}, u32[]{:S(2)}) collective-permute-start(bf16[768,512]{1,0:T(8,128)(2,1)} %get-tuple-element.37), channel_id=1, source_target_pairs={{0,1},{1,0},{2,3},{3,2},{4,5},{5,4},{6,7},{7,6},{8,9},{9,8},{10,11... | collective-permute-start | bytes 2359304 | tf_op jit(solution)/shard_map/ppermute | solution.py:14
  8.8 14.2 %collective-permute-start.1 = (bf16[1280,128]{1,0:T(8,128)(2,1)S(1)}, bf16[1280,128]{1,0:T(8,128)(2,1)S(1)}, u32[]{:S(2)}, u32[]{:S(2)}) collective-permute-start(bf16[1280,128]{1,0:T(8,128)(2,1)S(1)} %get-tuple-element.39.refs_2_.refs_3_), channel_id=1, source_target_pairs={{0,2},{1,3},{2,0},{3,1},{4,6},{5,7},{6,4},{7,5},{8,10},{9,11},{10,... | collective-permute-start | bytes 983048 | tf_op jit(solution)/shard_map/ppermute | solution.py:14
  11.8 3.4 %copy-start = (bf16[4,1,4,512,512]{4,3,2,1,0:T(8,128)(2,1)S(1)}, bf16[4,1,4,512,512]{4,3,2,1,0:T(8,128)(2,1)}, u32[]{:S(2)}) copy-start(bf16[4,1,4,512,512]{4,3,2,1,0:T(8,128)(2,1)} %param.8) | copy-start | bytes 25165828
  15.9 33.0 %collective-permute-start.10 = (bf16[640,512]{1,0:T(8,128)(2,1)S(1)}, bf16[640,512]{1,0:T(8,128)(2,1)S(1)}, u32[]{:S(2)}, u32[]{:S(2)}) collective-permute-start(bf16[640,512]{1,0:T(8,128)(2,1)S(1)} %get-tuple-element.49), channel_id=1, source_target_pairs={{0,1},{1,0},{2,3},{3,2},{4,5},{5,4},{6,7},{7,6},{8,9},{9,8},{10,11... | collective-permute-start | bytes 1966088 | tf_op jit(solution)/shard_map/ppermute | solution.py:14
  19.3 33.7 %collective-permute-start.13 = (bf16[2,512,512]{2,1,0:T(8,128)(2,1)S(1)}, bf16[2,512,512]{2,1,0:T(8,128)(2,1)S(1)}, u32[]{:S(2)}, u32[]{:S(2)}) collective-permute-start(bf16[2,512,512]{2,1,0:T(8,128)(2,1)S(1)} %panel_send.2.refs_2_), channel_id=1, source_target_pairs={{0,8},{8,0},{16,24},{24,16},{1,9},{9,1},{17,25},{25,17},{2,10},{10... | collective-permute-start | bytes 3145736 | tf_op jit(solution)/shard_map/ppermute | solution.py:14
  21.5 34.7 %collective-permute-start.14 = (bf16[2,512,512]{2,1,0:T(8,128)(2,1)S(1)}, bf16[2,512,512]{2,1,0:T(8,128)(2,1)S(1)}, u32[]{:S(2)}, u32[]{:S(2)}) collective-permute-start(bf16[2,512,512]{2,1,0:T(8,128)(2,1)S(1)} %panel_send.3.refs_3_), channel_id=1, source_target_pairs={{0,16},{8,24},{16,0},{24,8},{1,17},{9,25},{17,1},{25,9},{2,18},{10... | collective-permute-start | bytes 3145736 | tf_op jit(solution)/shard_map/ppermute | solution.py:14
  23.7 12.7 %collective-permute-start.2 = (bf16[896,128]{1,0:T(8,128)(2,1)S(1)}, bf16[896,128]{1,0:T(8,128)(2,1)S(1)}, u32[]{:S(2)}, u32[]{:S(2)}) collective-permute-start(bf16[896,128]{1,0:T(8,128)(2,1)S(1)} %get-tuple-element.40.refs_2_.refs_0_), channel_id=1, source_target_pairs={{0,4},{1,5},{2,6},{3,7},{4,0},{5,1},{6,2},{7,3},{8,12},{9,13},{10,... | collective-permute-start | bytes 688136 | tf_op jit(solution)/shard_map/ppermute | solution.py:14
  26.4 7.2 %collective-permute-start.3 = (bf16[512,128]{1,0:T(8,128)(2,1)S(1)}, bf16[512,128]{1,0:T(8,128)(2,1)S(1)}, u32[]{:S(2)}, u32[]{:S(2)}) collective-permute-start(bf16[512,128]{1,0:T(8,128)(2,1)S(1)} %get-tuple-element.43), channel_id=1, source_target_pairs={{0,2},{1,3},{2,0},{3,1},{4,6},{5,7},{6,4},{7,5},{8,10},{9,11},{10,... | collective-permute-start | bytes 393224 | tf_op jit(solution)/shard_map/ppermute | solution.py:14
  34.2 5.3 %collective-permute-start.5 = (bf16[256,128]{1,0:T(8,128)(2,1)S(1)}, bf16[256,128]{1,0:T(8,128)(2,1)S(1)}, u32[]{:S(2)}, u32[]{:S(2)}) collective-permute-start(bf16[256,128]{1,0:T(8,128)(2,1)S(1)} %get-tuple-element.44.refs_4_), channel_id=1, source_target_pairs={{0,4},{1,5},{2,6},{3,7},{4,0},{5,1},{6,2},{7,3},{8,12},{9,13},{10,... | collective-permute-start | bytes 196616 | tf_op jit(solution)/shard_map/ppermute | solution.py:14
  36.4 14.4 %collective-permute-start.9 = (bf16[640,512]{1,0:T(8,128)(2,1)S(1)}, bf16[640,512]{1,0:T(8,128)(2,1)S(1)}, u32[]{:S(2)}, u32[]{:S(2)}) collective-permute-start(bf16[640,512]{1,0:T(8,128)(2,1)S(1)} %get-tuple-element.48), channel_id=1, source_target_pairs={{0,1},{1,0},{2,3},{3,2},{4,5},{5,4},{6,7},{7,6},{8,9},{9,8},{10,11... | collective-permute-start | bytes 1966088 | tf_op jit(solution)/shard_map/ppermute | solution.py:14
  39.5 1.3 %collective-permute-start.4 = (bf16[256,128]{1,0:T(8,128)(2,1)S(1)}, bf16[256,128]{1,0:T(8,128)(2,1)S(1)}, u32[]{:S(2)}, u32[]{:S(2)}) collective-permute-start(bf16[256,128]{1,0:T(8,128)(2,1)S(1)} %get-tuple-element.46.refs_1_), channel_id=1, source_target_pairs={{0,1},{1,0},{2,3},{3,2},{4,5},{5,4},{6,7},{7,6},{8,9},{9,8},{10,11... | collective-permute-start | bytes 196616 | tf_op jit(solution)/shard_map/ppermute | solution.py:14
  41.5 4.3 %collective-permute-start.6 = (f32[128,128]{1,0:T(8,128)S(1)}, f32[128,128]{1,0:T(8,128)S(1)}, u32[]{:S(2)}, u32[]{:S(2)}) collective-permute-start(f32[128,128]{1,0:T(8,128)S(1)} %term1.1.refs_0_.refs_7_.refs_2_), channel_id=1, source_target_pairs={{0,8},{8,0},{16,24},{24,16},{1,9},{9,1},{17,25},{25,17},{2,10},{10... | collective-permute-start | bytes 196616 | tf_op jit(solution)/shard_map/ppermute | solution.py:14
  46.4 4.4 %collective-permute-start.7 = (bf16[128,128]{1,0:T(8,128)(2,1)S(1)}, bf16[128,128]{1,0:T(8,128)(2,1)S(1)}, u32[]{:S(2)}, u32[]{:S(2)}) collective-permute-start(bf16[128,128]{1,0:T(8,128)(2,1)S(1)} %m1_sum.1), channel_id=1, source_target_pairs={{0,2},{1,3},{2,0},{3,1},{4,6},{5,7},{6,4},{7,5},{8,10},{9,11},{10,... | collective-permute-start | bytes 98312 | tf_op jit(solution)/shard_map/ppermute | solution.py:14
  48.9 8.1 %collective-permute-start.12 = (bf16[512,512]{1,0:T(8,128)(2,1)S(1)}, bf16[512,512]{1,0:T(8,128)(2,1)S(1)}, u32[]{:S(2)}, u32[]{:S(2)}) collective-permute-start(bf16[512,512]{1,0:T(8,128)(2,1)S(1)} %get-tuple-element.53), channel_id=1, source_target_pairs={{0,1},{1,0},{2,3},{3,2},{4,5},{5,4},{6,7},{7,6},{8,9},{9,8},{10,11... | collective-permute-start | bytes 1572872 | tf_op jit(solution)/shard_map/ppermute | solution.py:14
  50.8 6.2 %collective-permute-start.11 = (bf16[512,512]{1,0:T(8,128)(2,1)S(1)}, bf16[512,512]{1,0:T(8,128)(2,1)S(1)}, u32[]{:S(2)}, u32[]{:S(2)}) collective-permute-start(bf16[512,512]{1,0:T(8,128)(2,1)S(1)} %get-tuple-element.52), channel_id=1, source_target_pairs={{0,1},{1,0},{2,3},{3,2},{4,5},{5,4},{6,7},{7,6},{8,9},{9,8},{10,11... | collective-permute-start | bytes 1572872 | tf_op jit(solution)/shard_map/ppermute | solution.py:14
  50.8 6.2 %collective-permute-start.8 = (bf16[256,128]{1,0:T(8,128)(2,1)S(1)}, bf16[256,128]{1,0:T(8,128)(2,1)S(1)}, u32[]{:S(2)}, u32[]{:S(2)}) collective-permute-start(bf16[256,128]{1,0:T(8,128)(2,1)S(1)} %pad_maximum_fusion.refs_0_), channel_id=1, source_target_pairs={{0,4},{1,5},{2,6},{3,7},{4,0},{5,1},{6,2},{7,3},{8,12},{9,13},{10,... | collective-permute-start | bytes 196616 | tf_op jit(solution)/shard_map/ppermute | solution.py:14
  52.9 5.8 %collective-permute-start.22 = (bf16[256,128]{1,0:T(8,128)(2,1)S(1)}, bf16[256,128]{1,0:T(8,128)(2,1)S(1)}, u32[]{:S(2)}, u32[]{:S(2)}) collective-permute-start(bf16[256,128]{1,0:T(8,128)(2,1)S(1)} %add.13), channel_id=1, source_target_pairs={{0,8},{8,0},{16,24},{24,16},{1,9},{9,1},{17,25},{25,17},{2,10},{10... | collective-permute-start | bytes 196616 | tf_op jit(solution)/shard_map/ppermute | solution.py:14
  56.1 8.4 %collective-permute-start.15 = (bf16[128,512]{1,0:T(8,128)(2,1)S(1)}, bf16[128,512]{1,0:T(8,128)(2,1)S(1)}, u32[]{:S(2)}, u32[]{:S(2)}) collective-permute-start(bf16[128,512]{1,0:T(8,128)(2,1)S(1)} %get-tuple-element.45.refs_0_.refs_6_.refs_3_), channel_id=1, source_target_pairs={{0,1},{1,0},{2,3},{3,2},{4,5},{5,4},{6,7},{7,6},{8,9},{9,8},{10,11... | collective-permute-start | bytes 393224 | tf_op jit(solution)/shard_map/ppermute | solution.py:14
  58.2 8.5 %collective-permute-start.16 = (bf16[128,512]{1,0:T(8,128)(2,1)S(1)}, bf16[128,512]{1,0:T(8,128)(2,1)S(1)}, u32[]{:S(2)}, u32[]{:S(2)}) collective-permute-start(bf16[128,512]{1,0:T(8,128)(2,1)S(1)} %get-tuple-element.54.refs_4_.refs_2_.refs_1_), channel_id=1, source_target_pairs={{0,1},{1,0},{2,3},{3,2},{4,5},{5,4},{6,7},{7,6},{8,9},{9,8},{10,11... | collective-permute-start | bytes 393224 | tf_op jit(solution)/shard_map/ppermute | solution.py:14
  58.8 4.7 %collective-permute-start.23 = (bf16[256,128]{1,0:T(8,128)(2,1)S(1)}, bf16[256,128]{1,0:T(8,128)(2,1)S(1)}, u32[]{:S(2)}, u32[]{:S(2)}) collective-permute-start(bf16[256,128]{1,0:T(8,128)(2,1)S(1)} %add_convert_fusion.1), channel_id=1, source_target_pairs={{0,16},{8,24},{16,0},{24,8},{1,17},{9,25},{17,1},{25,9},{2,18},{10... | collective-permute-start | bytes 196616 | tf_op jit(solution)/shard_map/ppermute | solution.py:14
  60.3 29.8 %collective-permute-start.32 = (bf16[512,512]{1,0:T(8,128)(2,1)S(1)}, bf16[512,512]{1,0:T(8,128)(2,1)S(1)}, u32[]{:S(2)}, u32[]{:S(2)}) collective-permute-start(bf16[512,512]{1,0:T(8,128)(2,1)S(1)} %panel_join.2.refs_9_), channel_id=1, source_target_pairs={{0,16},{8,24},{16,0},{24,8},{1,17},{9,25},{17,1},{25,9},{2,18},{10... | collective-permute-start | bytes 1572872 | tf_op jit(solution)/shard_map/ppermute | solution.py:14
  60.8 31.4 %collective-permute-start.33 = (bf16[512,512]{1,0:T(8,128)(2,1)S(1)}, bf16[512,512]{1,0:T(8,128)(2,1)S(1)}, u32[]{:S(2)}, u32[]{:S(2)}) collective-permute-start(bf16[512,512]{1,0:T(8,128)(2,1)S(1)} %panel_join.3.refs_10_), channel_id=1, source_target_pairs={{0,8},{8,0},{16,24},{24,16},{1,9},{9,1},{17,25},{25,17},{2,10},{10... | collective-permute-start | bytes 1572872 | tf_op jit(solution)/shard_map/ppermute | solution.py:14
  63.5 7.1 %collective-permute-start.17 = (bf16[32,1024]{1,0:T(8,128)(2,1)S(1)}, bf16[32,1024]{1,0:T(8,128)(2,1)S(1)}, u32[]{:S(2)}, u32[]{:S(2)}) collective-permute-start(bf16[32,1024]{1,0:T(8,128)(2,1)S(1)} %get-tuple-element.56), channel_id=1, source_target_pairs={{0,2},{1,3},{2,0},{3,1},{4,6},{5,7},{6,4},{7,5},{8,10},{9,11},{10,... | collective-permute-start | bytes 196616 | tf_op jit(solution)/shard_map/ppermute | solution.py:14
  64.5 6.6 %collective-permute-start.18 = (bf16[32,1024]{1,0:T(8,128)(2,1)S(1)}, bf16[32,1024]{1,0:T(8,128)(2,1)S(1)}, u32[]{:S(2)}, u32[]{:S(2)}) collective-permute-start(bf16[32,1024]{1,0:T(8,128)(2,1)S(1)} %get-tuple-element.57), channel_id=1, source_target_pairs={{0,4},{1,5},{2,6},{3,7},{4,0},{5,1},{6,2},{7,3},{8,12},{9,13},{10,... | collective-permute-start | bytes 196616 | tf_op jit(solution)/shard_map/ppermute | solution.py:14
  66.6 6.3 %collective-permute-start.19 = (bf16[32,1024]{1,0:T(8,128)(2,1)S(1)}, bf16[32,1024]{1,0:T(8,128)(2,1)S(1)}, u32[]{:S(2)}, u32[]{:S(2)}) collective-permute-start(bf16[32,1024]{1,0:T(8,128)(2,1)S(1)} %get-tuple-element.58), channel_id=1, source_target_pairs={{0,6},{1,7},{2,4},{3,5},{4,2},{5,3},{6,0},{7,1},{8,14},{9,15},{10,... | collective-permute-start | bytes 196616 | tf_op jit(solution)/shard_map/ppermute | solution.py:14
  70.6 5.7 %collective-permute-start.24 = (bf16[256,128]{1,0:T(8,128)(2,1)S(1)}, bf16[256,128]{1,0:T(8,128)(2,1)S(1)}, u32[]{:S(2)}, u32[]{:S(2)}) collective-permute-start(bf16[256,128]{1,0:T(8,128)(2,1)S(1)} %add_convert_fusion.refs_0_), channel_id=1, source_target_pairs={{0,2},{1,3},{2,0},{3,1},{4,6},{5,7},{6,4},{7,5},{8,10},{9,11},{10,... | collective-permute-start | bytes 196616 | tf_op jit(solution)/shard_map/ppermute | solution.py:14
  73.5 4.4 %collective-permute-start.20 = (bf16[32,1024]{1,0:T(8,128)(2,1)S(1)}, bf16[32,1024]{1,0:T(8,128)(2,1)S(1)}, u32[]{:S(2)}, u32[]{:S(2)}) collective-permute-start(bf16[32,1024]{1,0:T(8,128)(2,1)S(1)} %t23_sum.1), channel_id=1, source_target_pairs={{0,8},{8,0},{16,24},{24,16},{1,9},{9,1},{17,25},{25,17},{2,10},{10... | collective-permute-start | bytes 196616 | tf_op jit(solution)/shard_map/ppermute | solution.py:14
  74.5 10.3 %collective-permute-start.27 = (bf16[2,128,512]{2,1,0:T(8,128)(2,1)S(1)}, bf16[2,128,512]{2,1,0:T(8,128)(2,1)S(1)}, u32[]{:S(2)}, u32[]{:S(2)}) collective-permute-start(bf16[2,128,512]{2,1,0:T(8,128)(2,1)S(1)} %get-tuple-element.63), channel_id=1, source_target_pairs={{0,16},{8,24},{16,0},{24,8},{1,17},{9,25},{17,1},{25,9},{2,18},{10... | collective-permute-start | bytes 786440 | tf_op jit(solution)/shard_map/ppermute | solution.py:14
  76.9 6.7 %collective-permute-start.25 = (bf16[512,128]{1,0:T(8,128)(2,1)S(1)}, bf16[512,128]{1,0:T(8,128)(2,1)S(1)}, u32[]{:S(2)}, u32[]{:S(2)}) collective-permute-start(bf16[512,128]{1,0:T(8,128)(2,1)S(1)} %p23_stack.1.refs_0_), channel_id=1, source_target_pairs={{0,4},{1,5},{2,6},{3,7},{4,0},{5,1},{6,2},{7,3},{8,12},{9,13},{10,... | collective-permute-start | bytes 393224 | tf_op jit(solution)/shard_map/ppermute | solution.py:14
  77.9 6.9 %collective-permute-start.26 = (bf16[2,128,512]{2,1,0:T(8,128)(2,1)S(1)}, bf16[2,128,512]{2,1,0:T(8,128)(2,1)S(1)}, u32[]{:S(2)}, u32[]{:S(2)}) collective-permute-start(bf16[2,128,512]{2,1,0:T(8,128)(2,1)S(1)} %get-tuple-element.59.refs_4_), channel_id=1, source_target_pairs={{0,8},{8,0},{16,24},{24,16},{1,9},{9,1},{17,25},{25,17},{2,10},{10... | collective-permute-start | bytes 786440 | tf_op jit(solution)/shard_map/ppermute | solution.py:14
  83.6 5.0 %collective-permute-start.21 = (f32[32,1024]{1,0:T(8,128)S(1)}, f32[32,1024]{1,0:T(8,128)S(1)}, u32[]{:S(2)}, u32[]{:S(2)}) collective-permute-start(f32[32,1024]{1,0:T(8,128)S(1)} %convert_add_fusion.refs_0_), channel_id=1, source_target_pairs={{0,16},{8,24},{16,0},{24,8},{1,17},{9,25},{17,1},{25,9},{2,18},{10... | collective-permute-start | bytes 393224 | tf_op jit(solution)/shard_map/ppermute | solution.py:14
  84.7 12.1 %collective-permute-start.31 = (bf16[256,512]{1,0:T(8,128)(2,1)S(1)}, bf16[256,512]{1,0:T(8,128)(2,1)S(1)}, u32[]{:S(2)}, u32[]{:S(2)}) collective-permute-start(bf16[256,512]{1,0:T(8,128)(2,1)S(1)} %p23_place.1.refs_2_.refs_5_), channel_id=1, source_target_pairs={{0,1},{1,0},{2,3},{3,2},{4,5},{5,4},{6,7},{7,6},{8,9},{9,8},{10,11... | collective-permute-start | bytes 786440 | tf_op jit(solution)/shard_map/ppermute | solution.py:14
  85.4 6.8 %collective-permute-start.34 = (bf16[128,512]{1,0:T(8,128)(2,1)S(1)}, bf16[128,512]{1,0:T(8,128)(2,1)S(1)}, u32[]{:S(2)}, u32[]{:S(2)}) collective-permute-start(bf16[128,512]{1,0:T(8,128)(2,1)S(1)} %get-tuple-element.64.refs_3_), channel_id=1, source_target_pairs={{0,16},{8,24},{16,0},{24,8},{1,17},{9,25},{17,1},{25,9},{2,18},{10... | collective-permute-start | bytes 393224 | tf_op jit(solution)/shard_map/ppermute | solution.py:14
  88.6 6.0 %collective-permute-start.35 = (bf16[128,512]{1,0:T(8,128)(2,1)S(1)}, bf16[128,512]{1,0:T(8,128)(2,1)S(1)}, u32[]{:S(2)}, u32[]{:S(2)}) collective-permute-start(bf16[128,512]{1,0:T(8,128)(2,1)S(1)} %get-tuple-element.65.refs_4_), channel_id=1, source_target_pairs={{0,8},{8,0},{16,24},{24,16},{1,9},{9,1},{17,25},{25,17},{2,10},{10... | collective-permute-start | bytes 393224 | tf_op jit(solution)/shard_map/ppermute | solution.py:14
  90.1 7.8 %copy-start.5 = (bf16[2,512,512]{2,1,0:T(8,128)(2,1)S(1)}, bf16[2,512,512]{2,1,0:T(8,128)(2,1)}, u32[]{:S(2)}) copy-start(bf16[2,512,512]{2,1,0:T(8,128)(2,1)} %refs_4_.1) | copy-start | bytes 3145732
  90.1 6.8 %collective-permute-start.30 = (bf16[32,1024]{1,0:T(8,128)(2,1)S(1)}, bf16[32,1024]{1,0:T(8,128)(2,1)S(1)}, u32[]{:S(2)}, u32[]{:S(2)}) collective-permute-start(bf16[32,1024]{1,0:T(8,128)(2,1)S(1)} %m23_sum.1.refs_0_), channel_id=1, source_target_pairs={{0,6},{1,7},{2,4},{3,5},{4,2},{5,3},{6,0},{7,1},{8,14},{9,15},{10,... | collective-permute-start | bytes 196616 | tf_op jit(solution)/shard_map/ppermute | solution.py:14
  92.2 5.6 %collective-permute-start.29 = (bf16[32,1024]{1,0:T(8,128)(2,1)S(1)}, bf16[32,1024]{1,0:T(8,128)(2,1)S(1)}, u32[]{:S(2)}, u32[]{:S(2)}) collective-permute-start(bf16[32,1024]{1,0:T(8,128)(2,1)S(1)} %m23_sum.1.refs_0_), channel_id=1, source_target_pairs={{0,4},{1,5},{2,6},{3,7},{4,0},{5,1},{6,2},{7,3},{8,12},{9,13},{10,... | collective-permute-start | bytes 196616 | tf_op jit(solution)/shard_map/ppermute | solution.py:14
  92.3 5.6 %collective-permute-start.28 = (bf16[32,1024]{1,0:T(8,128)(2,1)S(1)}, bf16[32,1024]{1,0:T(8,128)(2,1)S(1)}, u32[]{:S(2)}, u32[]{:S(2)}) collective-permute-start(bf16[32,1024]{1,0:T(8,128)(2,1)S(1)} %m23_sum.1.refs_0_), channel_id=1, source_target_pairs={{0,2},{1,3},{2,0},{3,1},{4,6},{5,7},{6,4},{7,5},{8,10},{9,11},{10,... | collective-permute-start | bytes 196616 | tf_op jit(solution)/shard_map/ppermute | solution.py:14
  99.0 1.6 %collective-permute-start.36 = (bf16[2,128,512]{2,1,0:T(8,128)(2,1)S(1)}, bf16[2,128,512]{2,1,0:T(8,128)(2,1)S(1)}, u32[]{:S(2)}, u32[]{:S(2)}) collective-permute-start(bf16[2,128,512]{2,1,0:T(8,128)(2,1)S(1)} %x2_x3.1.refs_0_.refs_4_), channel_id=1, source_target_pairs={{0,1},{1,0},{2,3},{3,2},{4,5},{5,4},{6,7},{7,6},{8,9},{9,8},{10,11... | collective-permute-start | bytes 786440 | tf_op jit(solution)/shard_map/ppermute | solution.py:14
  101.6 6.1 %collective-permute-start.40 = (bf16[128,512]{1,0:T(8,128)(2,1)S(1)}, bf16[128,512]{1,0:T(8,128)(2,1)S(1)}, u32[]{:S(2)}, u32[]{:S(2)}) collective-permute-start(bf16[128,512]{1,0:T(8,128)(2,1)S(1)} %get-tuple-element.69.refs_1_), channel_id=1, source_target_pairs={{0,16},{8,24},{16,0},{24,8},{1,17},{9,25},{17,1},{25,9},{2,18},{10... | collective-permute-start | bytes 393224 | tf_op jit(solution)/shard_map/ppermute | solution.py:14
  102.8 6.4 %collective-permute-start.37 = (bf16[128,512]{1,0:T(8,128)(2,1)S(1)}, bf16[128,512]{1,0:T(8,128)(2,1)S(1)}, u32[]{:S(2)}, u32[]{:S(2)}) collective-permute-start(bf16[128,512]{1,0:T(8,128)(2,1)S(1)} %get-tuple-element.68.refs_6_.refs_0_), channel_id=1, source_target_pairs={{0,8},{8,0},{16,24},{24,16},{1,9},{9,1},{17,25},{25,17},{2,10},{10... | collective-permute-start | bytes 393224 | tf_op jit(solution)/shard_map/ppermute | solution.py:14
  103.5 8.4 %collective-permute-start.38 = (bf16[128,512]{1,0:T(8,128)(2,1)S(1)}, bf16[128,512]{1,0:T(8,128)(2,1)S(1)}, u32[]{:S(2)}, u32[]{:S(2)}) collective-permute-start(bf16[128,512]{1,0:T(8,128)(2,1)S(1)} %get-tuple-element.69.refs_1_), channel_id=1, source_target_pairs={{0,8},{8,0},{16,24},{24,16},{1,9},{9,1},{17,25},{25,17},{2,10},{10... | collective-permute-start | bytes 393224 | tf_op jit(solution)/shard_map/ppermute | solution.py:14
  104.8 7.2 %collective-permute-start.39 = (bf16[128,512]{1,0:T(8,128)(2,1)S(1)}, bf16[128,512]{1,0:T(8,128)(2,1)S(1)}, u32[]{:S(2)}, u32[]{:S(2)}) collective-permute-start(bf16[128,512]{1,0:T(8,128)(2,1)S(1)} %get-tuple-element.68.refs_6_.refs_0_), channel_id=1, source_target_pairs={{0,16},{8,24},{16,0},{24,8},{1,17},{9,25},{17,1},{25,9},{2,18},{10... | collective-permute-start | bytes 393224 | tf_op jit(solution)/shard_map/ppermute | solution.py:14
  107.8 5.9 %collective-permute-start.42 = (bf16[128,512]{1,0:T(8,128)(2,1)S(1)}, bf16[128,512]{1,0:T(8,128)(2,1)S(1)}, u32[]{:S(2)}, u32[]{:S(2)}) collective-permute-start(bf16[128,512]{1,0:T(8,128)(2,1)S(1)} %collective-permute-done.40.refs_5_), channel_id=1, source_target_pairs={{0,8},{8,0},{16,24},{24,16},{1,9},{9,1},{17,25},{25,17},{2,10},{10... | collective-permute-start | bytes 393224 | tf_op jit(solution)/shard_map/ppermute | solution.py:14
  109.1 5.0 %collective-permute-start.41 = (bf16[128,512]{1,0:T(8,128)(2,1)S(1)}, bf16[128,512]{1,0:T(8,128)(2,1)S(1)}, u32[]{:S(2)}, u32[]{:S(2)}) collective-permute-start(bf16[128,512]{1,0:T(8,128)(2,1)S(1)} %collective-permute-done.37.refs_2_), channel_id=1, source_target_pairs={{0,16},{8,24},{16,0},{24,8},{1,17},{9,25},{17,1},{25,9},{2,18},{10... | collective-permute-start | bytes 393224 | tf_op jit(solution)/shard_map/ppermute | solution.py:14
  (4 other events, 8.3 us)

commit v7 on v6

--- a/solution.py
+++ b/solution.py
@@ -191,7 +191,7 @@
         [InHbm(right), InHbm(panels)],
         [first_shape, first_shape],
         [pltpu.SemaphoreType.DMA((8,))],
-        limit=60,
+        limit=52,
     )
     first_got = swap(first_out, "row", 1)
 

time: 116 us -> 112 us (0.966)
  local copies, waits for them, and re-layouts: 7.18 us -> 1.88 us
  starting transfers between devices: 45 us -> 48.2 us
  Pallas kernels: 27.3 us -> 26.1 us
    unnamed x18, local copies, waits for them, and re-layouts: 7.18 us -> 1.88 us
    ppermute x43, starting transfers between devices: 45 us -> 48.2 us  [swap(): lax.ppermute(block, axis, [(i, i ^ bits) for i in range(lax.axis_size(axi...]
where the time goes in v7:
time: 112 us
  starting transfers between devices  48.2 us (43%)
  waiting for transfers between devices  34.7 us (31%)
  Pallas kernels  26.1 us (23%)
  local copies, waits for them, and re-layouts  1.88 us (2%)
    ppermute x43, starting transfers between devices, swap(): lax.ppermute(block, axis, [(i, i ^ bits) for i in range(lax.axis_size(axi...  48.2 us
    ppermute x43, waiting for transfers between devices, swap(): lax.ppermute(block, axis, [(i, i ^ bits) for i in range(lax.axis_size(axi...  34.7 us
    pallas_call x26, Pallas kernels, run(): pl.pallas_call(kernel, grid_spec=pltpu.PrefetchScalarGridSpec(num_scalar_...  26.1 us
  transfers between devices with their start and end apart: 43, of which 19 were waited for; matrix products, arithmetic and copies ran while one was open for 0% of the time, Pallas kernels for 17%

profile of v7, /device:TPU:0, one launch (start us, length us, event | category | flops | bytes accessed | tf_op | source)
XLA Modules:
  0.0 112.1 jit_solution(2277350907686019277)
XLA Ops:
  1.5 1.0 copy-done.7
  2.5 2.5 %first_send.1 = (bf16[768,512]{1,0:T(8,128)(2,1)S(1)}, bf16[768,512]{1,0:T(8,128)(2,1)S(1)}) custom-call(s32[4]{0:T(128)S(1)} %copy-done.7, s32[4,4]{1,0:T(4,128)S(1)} %bitcast.31, bf16[4,256,512]{2,1,0:T(8,128)(2,1)} %bitcast.25, bf16[4,4,512,512]{3,2,1,0:T(8,128)(2,1)} %bitcast.6), custom_call_target="tpu_custom_call" | custom-call | bytes 1572864 | tf_op jit(solution)/shard_map/first_send/pallas_call | solution.py:130
  5.5 1.9 %collective-permute-done.refs_1_ = bf16[768,512]{1,0:T(8,128)(2,1)S(1)} collective-permute-done((bf16[768,512]{1,0:T(8,128)(2,1)S(1)}, bf16[768,512]{1,0:T(8,128)(2,1)S(1)}, u32[]{:S(2)}, u32[]{:S(2)}) %collective-permute-start) | collective-permute-done | bytes 786464 | tf_op jit(solution)/shard_map/ppermute | solution.py:14
  8.2 3.0 %collective-permute-start.1 = (bf16[1280,128]{1,0:T(8,128)(2,1)S(1)}, bf16[1280,128]{1,0:T(8,128)(2,1)S(1)}, u32[]{:S(2)}, u32[]{:S(2)}) collective-permute-start(bf16[1280,128]{1,0:T(8,128)(2,1)S(1)} %get-tuple-element.39.refs_2_.refs_3_), channel_id=1, source_target_pairs={{0,2},{1,3},{2,0},{3,1},{4,6},{5,7},{6,4},{7,5},{8,10},{9,11},{10,... | collective-permute-start | bytes 983048 | tf_op jit(solution)/shard_map/ppermute | solution.py:14
  12.6 1.6 %collective-permute-start.13 = (bf16[2,512,512]{2,1,0:T(8,128)(2,1)S(1)}, bf16[2,512,512]{2,1,0:T(8,128)(2,1)S(1)}, u32[]{:S(2)}, u32[]{:S(2)}) collective-permute-start(bf16[2,512,512]{2,1,0:T(8,128)(2,1)S(1)} %panel_send.2.refs_2_), channel_id=1, source_target_pairs={{0,8},{8,0},{16,24},{24,16},{1,9},{9,1},{17,25},{25,17},{2,10},{10... | collective-permute-start | bytes 3145736 | tf_op jit(solution)/shard_map/ppermute | solution.py:14
  14.8 1.6 %collective-permute-start.14 = (bf16[2,512,512]{2,1,0:T(8,128)(2,1)S(1)}, bf16[2,512,512]{2,1,0:T(8,128)(2,1)S(1)}, u32[]{:S(2)}, u32[]{:S(2)}) collective-permute-start(bf16[2,512,512]{2,1,0:T(8,128)(2,1)S(1)} %panel_send.3.refs_3_), channel_id=1, source_target_pairs={{0,16},{8,24},{16,0},{24,8},{1,17},{9,25},{17,1},{25,9},{2,18},{10... | collective-permute-start | bytes 3145736 | tf_op jit(solution)/shard_map/ppermute | solution.py:14
  16.4 2.8 %collective-permute-done.1.refs_1_ = bf16[1280,128]{1,0:T(8,128)(2,1)S(1)} collective-permute-done((bf16[1280,128]{1,0:T(8,128)(2,1)S(1)}, bf16[1280,128]{1,0:T(8,128)(2,1)S(1)}, u32[]{:S(2)}, u32[]{:S(2)}) %collective-permute-start.1) | collective-permute-done | bytes 327712 | tf_op jit(solution)/shard_map/ppermute | solution.py:14
  19.9 2.8 %collective-permute-start.2 = (bf16[896,128]{1,0:T(8,128)(2,1)S(1)}, bf16[896,128]{1,0:T(8,128)(2,1)S(1)}, u32[]{:S(2)}, u32[]{:S(2)}) collective-permute-start(bf16[896,128]{1,0:T(8,128)(2,1)S(1)} %get-tuple-element.40.refs_2_.refs_0_), channel_id=1, source_target_pairs={{0,4},{1,5},{2,6},{3,7},{4,0},{5,1},{6,2},{7,3},{8,12},{9,13},{10,... | collective-permute-start | bytes 688136 | tf_op jit(solution)/shard_map/ppermute | solution.py:14
  22.7 1.6 %collective-permute-start.3 = (bf16[512,128]{1,0:T(8,128)(2,1)S(1)}, bf16[512,128]{1,0:T(8,128)(2,1)S(1)}, u32[]{:S(2)}, u32[]{:S(2)}) collective-permute-start(bf16[512,128]{1,0:T(8,128)(2,1)S(1)} %get-tuple-element.43), channel_id=1, source_target_pairs={{0,2},{1,3},{2,0},{3,1},{4,6},{5,7},{6,4},{7,5},{8,10},{9,11},{10,... | collective-permute-start | bytes 393224 | tf_op jit(solution)/shard_map/ppermute | solution.py:14
  24.3 5.6 %collective-permute-done.3.refs_1_ = bf16[512,128]{1,0:T(8,128)(2,1)S(1)} collective-permute-done((bf16[512,128]{1,0:T(8,128)(2,1)S(1)}, bf16[512,128]{1,0:T(8,128)(2,1)S(1)}, u32[]{:S(2)}, u32[]{:S(2)}) %collective-permute-start.3) | collective-permute-done | bytes 131104 | tf_op jit(solution)/shard_map/ppermute | solution.py:14
  30.5 2.4 %collective-permute-start.5 = (bf16[256,128]{1,0:T(8,128)(2,1)S(1)}, bf16[256,128]{1,0:T(8,128)(2,1)S(1)}, u32[]{:S(2)}, u32[]{:S(2)}) collective-permute-start(bf16[256,128]{1,0:T(8,128)(2,1)S(1)} %get-tuple-element.44.refs_4_), channel_id=1, source_target_pairs={{0,4},{1,5},{2,6},{3,7},{4,0},{5,1},{6,2},{7,3},{8,12},{9,13},{10,... | collective-permute-start | bytes 196616 | tf_op jit(solution)/shard_map/ppermute | solution.py:14
  34.6 1.2 %collective-permute-done.5.refs_4_ = bf16[256,128]{1,0:T(8,128)(2,1)S(1)} collective-permute-done((bf16[256,128]{1,0:T(8,128)(2,1)S(1)}, bf16[256,128]{1,0:T(8,128)(2,1)S(1)}, u32[]{:S(2)}, u32[]{:S(2)}) %collective-permute-start.5) | collective-permute-done | bytes 65568 | tf_op jit(solution)/shard_map/ppermute | solution.py:14
  35.8 1.3 %collective-permute-done.4.refs_2_ = bf16[256,128]{1,0:T(8,128)(2,1)S(1)} collective-permute-done((bf16[256,128]{1,0:T(8,128)(2,1)S(1)}, bf16[256,128]{1,0:T(8,128)(2,1)S(1)}, u32[]{:S(2)}, u32[]{:S(2)}) %collective-permute-start.4) | collective-permute-done | bytes 65568 | tf_op jit(solution)/shard_map/ppermute | solution.py:14
  37.8 1.6 %collective-permute-start.6 = (f32[128,128]{1,0:T(8,128)S(1)}, f32[128,128]{1,0:T(8,128)S(1)}, u32[]{:S(2)}, u32[]{:S(2)}) collective-permute-start(f32[128,128]{1,0:T(8,128)S(1)} %term1.1.refs_0_.refs_7_.refs_2_), channel_id=1, source_target_pairs={{0,8},{8,0},{16,24},{24,16},{1,9},{9,1},{17,25},{25,17},{2,10},{10... | collective-permute-start | bytes 196616 | tf_op jit(solution)/shard_map/ppermute | solution.py:14
  39.4 2.8 %collective-permute-done.6.refs_1_ = f32[128,128]{1,0:T(8,128)S(1)} collective-permute-done((f32[128,128]{1,0:T(8,128)S(1)}, f32[128,128]{1,0:T(8,128)S(1)}, u32[]{:S(2)}, u32[]{:S(2)}) %collective-permute-start.6) | collective-permute-done | bytes 65568 | tf_op jit(solution)/shard_map/ppermute | solution.py:14
  42.7 2.5 %collective-permute-start.7 = (bf16[128,128]{1,0:T(8,128)(2,1)S(1)}, bf16[128,128]{1,0:T(8,128)(2,1)S(1)}, u32[]{:S(2)}, u32[]{:S(2)}) collective-permute-start(bf16[128,128]{1,0:T(8,128)(2,1)S(1)} %m1_sum.1), channel_id=1, source_target_pairs={{0,2},{1,3},{2,0},{3,1},{4,6},{5,7},{6,4},{7,5},{8,10},{9,11},{10,... | collective-permute-start | bytes 98312 | tf_op jit(solution)/shard_map/ppermute | solution.py:14
  45.2 1.9 %collective-permute-done.7 = bf16[128,128]{1,0:T(8,128)(2,1)S(1)} collective-permute-done((bf16[128,128]{1,0:T(8,128)(2,1)S(1)}, bf16[128,128]{1,0:T(8,128)(2,1)S(1)}, u32[]{:S(2)}, u32[]{:S(2)}) %collective-permute-start.7) | collective-permute-done | bytes 32800 | tf_op jit(solution)/shard_map/ppermute | solution.py:14
  47.1 2.0 %collective-permute-start.8 = (bf16[256,128]{1,0:T(8,128)(2,1)S(1)}, bf16[256,128]{1,0:T(8,128)(2,1)S(1)}, u32[]{:S(2)}, u32[]{:S(2)}) collective-permute-start(bf16[256,128]{1,0:T(8,128)(2,1)S(1)} %pad_maximum_fusion.refs_0_), channel_id=1, source_target_pairs={{0,4},{1,5},{2,6},{3,7},{4,0},{5,1},{6,2},{7,3},{8,12},{9,13},{10,... | collective-permute-start | bytes 196616 | tf_op jit(solution)/shard_map/ppermute | solution.py:14
  49.2 1.6 %collective-permute-start.22 = (bf16[256,128]{1,0:T(8,128)(2,1)S(1)}, bf16[256,128]{1,0:T(8,128)(2,1)S(1)}, u32[]{:S(2)}, u32[]{:S(2)}) collective-permute-start(bf16[256,128]{1,0:T(8,128)(2,1)S(1)} %add.13), channel_id=1, source_target_pairs={{0,8},{8,0},{16,24},{24,16},{1,9},{9,1},{17,25},{25,17},{2,10},{10... | collective-permute-start | bytes 196616 | tf_op jit(solution)/shard_map/ppermute | solution.py:14
  53.2 1.2 %x1_t23.1 = (bf16[128,512]{1,0:T(8,128)(2,1)S(1)}, bf16[32,1024]{1,0:T(8,128)(2,1)S(1)}, bf16[32,1024]{1,0:T(8,128)(2,1)S(1)}, bf16[32,1024]{1,0:T(8,128)(2,1)S(1)}, bf16[32,1024]{1,0:T(8,128)(2,1)S(1)}) custom-call(s32[4]{0:T(128)S(1)} %copy-done.8, s32[4,4]{1,0:T(4,128)S(1)} %bitcast.45, bf16[256,128]{1,0:T(8,128)(2,1)S(1)} %pad_maximum_fusion.refs_0_, ...), custom_call_target="tpu_custom_call" | custom-call | bytes 3670016 | tf_op jit(solution)/shard_map/x1_t23/pallas_call | solution.py:130
  55.0 1.6 %collective-permute-start.23 = (bf16[256,128]{1,0:T(8,128)(2,1)S(1)}, bf16[256,128]{1,0:T(8,128)(2,1)S(1)}, u32[]{:S(2)}, u32[]{:S(2)}) collective-permute-start(bf16[256,128]{1,0:T(8,128)(2,1)S(1)} %add_convert_fusion.1), channel_id=1, source_target_pairs={{0,16},{8,24},{16,0},{24,8},{1,17},{9,25},{17,1},{25,9},{2,18},{10... | collective-permute-start | bytes 196616 | tf_op jit(solution)/shard_map/ppermute | solution.py:14
  57.6 2.1 %collective-permute-done.23 = bf16[256,128]{1,0:T(8,128)(2,1)S(1)} collective-permute-done((bf16[256,128]{1,0:T(8,128)(2,1)S(1)}, bf16[256,128]{1,0:T(8,128)(2,1)S(1)}, u32[]{:S(2)}, u32[]{:S(2)}) %collective-permute-start.23) | collective-permute-done | bytes 65568 | tf_op jit(solution)/shard_map/ppermute | solution.py:14
  60.6 2.1 %collective-permute-start.18 = (bf16[32,1024]{1,0:T(8,128)(2,1)S(1)}, bf16[32,1024]{1,0:T(8,128)(2,1)S(1)}, u32[]{:S(2)}, u32[]{:S(2)}) collective-permute-start(bf16[32,1024]{1,0:T(8,128)(2,1)S(1)} %get-tuple-element.57), channel_id=1, source_target_pairs={{0,4},{1,5},{2,6},{3,7},{4,0},{5,1},{6,2},{7,3},{8,12},{9,13},{10,... | collective-permute-start | bytes 196616 | tf_op jit(solution)/shard_map/ppermute | solution.py:14
  62.7 1.4 %collective-permute-start.19 = (bf16[32,1024]{1,0:T(8,128)(2,1)S(1)}, bf16[32,1024]{1,0:T(8,128)(2,1)S(1)}, u32[]{:S(2)}, u32[]{:S(2)}) collective-permute-start(bf16[32,1024]{1,0:T(8,128)(2,1)S(1)} %get-tuple-element.58), channel_id=1, source_target_pairs={{0,6},{1,7},{2,4},{3,5},{4,2},{5,3},{6,0},{7,1},{8,14},{9,15},{10,... | collective-permute-start | bytes 196616 | tf_op jit(solution)/shard_map/ppermute | solution.py:14
  64.2 2.7 %update01.1 = (bf16[2,128,512]{2,1,0:T(8,128)(2,1)S(1)}, bf16[2,128,512]{2,1,0:T(8,128)(2,1)S(1)}, f32[2,128,512]{2,1,0:T(8,128)S(1)}, f32[2,128,512]{2,1,0:T(8,128)S(1)}) custom-call(s32[4]{0:T(128)S(1)} %copy-done.8, s32[4,4]{1,0:T(4,128)S(1)} %bitcast.46, bf16[4,256,512]{2,1,0:T(8,128)(2,1)S(1)} %bitcast.30, bf16[4,4,512,512]{3,2,1,0:T(8,128)(2,1)S(1)} %bitcast.23, ...), custom_call_target="tpu_custom_call" | custom-call | bytes 8912896 | tf_op jit(solution)/shard_map/update01/pallas_call | solution.py:130
  67.4 1.4 %collective-permute-done.19.refs_3_ = bf16[32,1024]{1,0:T(8,128)(2,1)S(1)} collective-permute-done((bf16[32,1024]{1,0:T(8,128)(2,1)S(1)}, bf16[32,1024]{1,0:T(8,128)(2,1)S(1)}, u32[]{:S(2)}, u32[]{:S(2)}) %collective-permute-start.19) | collective-permute-done | bytes 65568 | tf_op jit(solution)/shard_map/ppermute | solution.py:14
  69.4 1.6 %collective-permute-start.20 = (bf16[32,1024]{1,0:T(8,128)(2,1)S(1)}, bf16[32,1024]{1,0:T(8,128)(2,1)S(1)}, u32[]{:S(2)}, u32[]{:S(2)}) collective-permute-start(bf16[32,1024]{1,0:T(8,128)(2,1)S(1)} %t23_sum.1), channel_id=1, source_target_pairs={{0,8},{8,0},{16,24},{24,16},{1,9},{9,1},{17,25},{25,17},{2,10},{10... | collective-permute-start | bytes 196616 | tf_op jit(solution)/shard_map/ppermute | solution.py:14
  71.0 1.9 %collective-permute-start.27 = (bf16[2,128,512]{2,1,0:T(8,128)(2,1)S(1)}, bf16[2,128,512]{2,1,0:T(8,128)(2,1)S(1)}, u32[]{:S(2)}, u32[]{:S(2)}) collective-permute-start(bf16[2,128,512]{2,1,0:T(8,128)(2,1)S(1)} %get-tuple-element.63), channel_id=1, source_target_pairs={{0,16},{8,24},{16,0},{24,8},{1,17},{9,25},{17,1},{25,9},{2,18},{10... | collective-permute-start | bytes 786440 | tf_op jit(solution)/shard_map/ppermute | solution.py:14
  74.5 1.2 %collective-permute-start.26 = (bf16[2,128,512]{2,1,0:T(8,128)(2,1)S(1)}, bf16[2,128,512]{2,1,0:T(8,128)(2,1)S(1)}, u32[]{:S(2)}, u32[]{:S(2)}) collective-permute-start(bf16[2,128,512]{2,1,0:T(8,128)(2,1)S(1)} %get-tuple-element.59.refs_4_), channel_id=1, source_target_pairs={{0,8},{8,0},{16,24},{24,16},{1,9},{9,1},{17,25},{25,17},{2,10},{10... | collective-permute-start | bytes 786440 | tf_op jit(solution)/shard_map/ppermute | solution.py:14
  75.7 4.1 %collective-permute-done.25.refs_1_ = bf16[512,128]{1,0:T(8,128)(2,1)S(1)} collective-permute-done((bf16[512,128]{1,0:T(8,128)(2,1)S(1)}, bf16[512,128]{1,0:T(8,128)(2,1)S(1)}, u32[]{:S(2)}, u32[]{:S(2)}) %collective-permute-start.25) | collective-permute-done | bytes 131104 | tf_op jit(solution)/shard_map/ppermute | solution.py:14
  81.7 1.4 %collective-permute-start.34 = (bf16[128,512]{1,0:T(8,128)(2,1)S(1)}, bf16[128,512]{1,0:T(8,128)(2,1)S(1)}, u32[]{:S(2)}, u32[]{:S(2)}) collective-permute-start(bf16[128,512]{1,0:T(8,128)(2,1)S(1)} %get-tuple-element.64.refs_3_), channel_id=1, source_target_pairs={{0,16},{8,24},{16,0},{24,8},{1,17},{9,25},{17,1},{25,9},{2,18},{10... | collective-permute-start | bytes 393224 | tf_op jit(solution)/shard_map/ppermute | solution.py:14
  83.2 1.5 %collective-permute-done.21.refs_1_ = f32[32,1024]{1,0:T(8,128)S(1)} collective-permute-done((f32[32,1024]{1,0:T(8,128)S(1)}, f32[32,1024]{1,0:T(8,128)S(1)}, u32[]{:S(2)}, u32[]{:S(2)}) %collective-permute-start.21) | collective-permute-done | bytes 131104 | tf_op jit(solution)/shard_map/ppermute | solution.py:14
  84.7 1.0 collective-permute-start.35
  86.4 2.3 %collective-permute-start.30 = (bf16[32,1024]{1,0:T(8,128)(2,1)S(1)}, bf16[32,1024]{1,0:T(8,128)(2,1)S(1)}, u32[]{:S(2)}, u32[]{:S(2)}) collective-permute-start(bf16[32,1024]{1,0:T(8,128)(2,1)S(1)} %m23_sum.1.refs_0_), channel_id=1, source_target_pairs={{0,6},{1,7},{2,4},{3,5},{4,2},{5,3},{6,0},{7,1},{8,14},{9,15},{10,... | collective-permute-start | bytes 196616 | tf_op jit(solution)/shard_map/ppermute | solution.py:14
  88.7 2.1 %collective-permute-start.28 = (bf16[32,1024]{1,0:T(8,128)(2,1)S(1)}, bf16[32,1024]{1,0:T(8,128)(2,1)S(1)}, u32[]{:S(2)}, u32[]{:S(2)}) collective-permute-start(bf16[32,1024]{1,0:T(8,128)(2,1)S(1)} %m23_sum.1.refs_0_), channel_id=1, source_target_pairs={{0,2},{1,3},{2,0},{3,1},{4,6},{5,7},{6,4},{7,5},{8,10},{9,11},{10,... | collective-permute-start | bytes 196616 | tf_op jit(solution)/shard_map/ppermute | solution.py:14
  90.8 2.3 %leaf_sums.1 = (bf16[2,512,512]{2,1,0:T(8,128)(2,1)S(1)}, f32[256,512]{1,0:T(8,128)S(1)}) custom-call(s32[4]{0:T(128)S(1)} %copy-done.8, s32[4,4]{1,0:T(4,128)S(1)} %bitcast.52, bf16[4,4,512,512]{3,2,1,0:T(8,128)(2,1)} %bitcast.7, bf16[4,4,512,512]{3,2,1,0:T(8,128)(2,1)} %bitcast.8, bf16[2,512,512]{2,1,0:T(8,128)(2,1)S(1)} %collective-permute-done.13.refs_1_.refs_2_, ...), custom_call_target="tpu_custom_call" | custom-call | bytes 7602176 | tf_op jit(solution)/shard_map/leaf_sums/pallas_call | solution.py:130
  93.1 1.2 %collective-permute-done.29.refs_2_ = bf16[32,1024]{1,0:T(8,128)(2,1)S(1)} collective-permute-done((bf16[32,1024]{1,0:T(8,128)(2,1)S(1)}, bf16[32,1024]{1,0:T(8,128)(2,1)S(1)}, u32[]{:S(2)}, u32[]{:S(2)}) %collective-permute-start.29) | collective-permute-done | bytes 65568 | tf_op jit(solution)/shard_map/ppermute | solution.py:14
  94.3 1.2 %x2_x3.1.refs_0_.refs_4_ = bf16[2,128,512]{2,1,0:T(8,128)(2,1)S(1)} custom-call(s32[4]{0:T(128)S(1)} %copy-done.8, s32[4,4]{1,0:T(4,128)S(1)} %bitcast.53, bf16[32,1024]{1,0:T(8,128)(2,1)S(1)} %m23_sum.1.refs_0_, bf16[32,1024]{1,0:T(8,128)(2,1)S(1)} %collective-permute-done.28.refs_1_, bf16[32,1024]{1,0:T(8,128)(2,1)S(1)} %collective-permute-done.29.refs_2_, ...), custom_call_target="tpu_custom_call" | custom-call | bytes 2097152 | tf_op jit(solution)/shard_map/x2_x3/pallas_call | solution.py:130
  95.6 1.5 %collective-permute-done.36.refs_1_.refs_5_ = bf16[2,128,512]{2,1,0:T(8,128)(2,1)S(1)} collective-permute-done((bf16[2,128,512]{2,1,0:T(8,128)(2,1)S(1)}, bf16[2,128,512]{2,1,0:T(8,128)(2,1)S(1)}, u32[]{:S(2)}, u32[]{:S(2)}) %collective-permute-start.36) | collective-permute-done | bytes 262176 | tf_op jit(solution)/shard_map/ppermute | solution.py:14
  97.1 1.0 final.1
  98.1 1.0 collective-permute-start.40
  100.1 1.1 collective-permute-start.38
  101.1 1.1 collective-permute-start.39
  102.2 2.1 %collective-permute-done.40.refs_5_ = bf16[128,512]{1,0:T(8,128)(2,1)S(1)} collective-permute-done((bf16[128,512]{1,0:T(8,128)(2,1)S(1)}, bf16[128,512]{1,0:T(8,128)(2,1)S(1)}, u32[]{:S(2)}, u32[]{:S(2)}) %collective-permute-start.40) | collective-permute-done | bytes 131104 | tf_op jit(solution)/shard_map/ppermute | solution.py:14
  105.5 1.1 collective-permute-start.41
  106.6 1.6 %write_solved.1 = bf16[4,256,512]{2,1,0:T(8,128)(2,1)} custom-call(s32[4]{0:T(128)S(1)} %copy-done.8, s32[4,4]{1,0:T(4,128)S(1)} %bitcast.55, bf16[128,512]{1,0:T(8,128)(2,1)S(1)} %get-tuple-element.45.refs_0_.refs_6_.refs_3_, bf16[128,512]{1,0:T(8,128)(2,1)S(1)} %get-tuple-element.54.refs_4_.refs_2_.refs_1_, ...), custom_call_target="tpu_custom_call" | custom-call | bytes 2097152 | tf_op jit(solution)/shard_map/write_solved/pallas_call | solution.py:130
  108.3 1.7 %collective-permute-done.42.refs_7_ = bf16[128,512]{1,0:T(8,128)(2,1)S(1)} collective-permute-done((bf16[128,512]{1,0:T(8,128)(2,1)S(1)}, bf16[128,512]{1,0:T(8,128)(2,1)S(1)}, u32[]{:S(2)}, u32[]{:S(2)}) %collective-permute-start.42) | collective-permute-done | bytes 131104 | tf_op jit(solution)/shard_map/ppermute | solution.py:14
  110.5 1.6 %write_updated.1 = bf16[4,256,512]{2,1,0:T(8,128)(2,1)} custom-call(s32[4]{0:T(128)S(1)} %copy-done.8, s32[4,4]{1,0:T(4,128)S(1)} %bitcast.56, bf16[128,512]{1,0:T(8,128)(2,1)S(1)} %get-tuple-element.68.refs_6_.refs_0_, bf16[128,512]{1,0:T(8,128)(2,1)S(1)} %get-tuple-element.69.refs_1_, bf16[128,512]{1,0:T(8,128)(2,1)S(1)} %collective-permute-done.37.refs_2_, ...), custom_call_target="tpu_custom_call" | custom-call | bytes 2097152 | tf_op jit(solution)/shard_map/write_updated/pallas_call | solution.py:130
  (87 shorter events, 21.3 us)
Async XLA Ops:
  0.6 10.6 %copy-start = (bf16[4,1,4,512,512]{4,3,2,1,0:T(8,128)(2,1)S(1)}, bf16[4,1,4,512,512]{4,3,2,1,0:T(8,128)(2,1)}, u32[]{:S(2)}) copy-start(bf16[4,1,4,512,512]{4,3,2,1,0:T(8,128)(2,1)} %param.8) | copy-start | bytes 25165828
  0.6 10.6 %copy-start.1 = (bf16[1,4,256,512]{3,2,1,0:T(8,128)(2,1)S(1)}, bf16[1,4,256,512]{3,2,1,0:T(8,128)(2,1)}, u32[]{:S(2)}) copy-start(bf16[1,4,256,512]{3,2,1,0:T(8,128)(2,1)} %param.7) | copy-start | bytes 3145732
  5.0 2.4 %collective-permute-start = (bf16[768,512]{1,0:T(8,128)(2,1)S(1)}, bf16[768,512]{1,0:T(8,128)(2,1)S(1)}, u32[]{:S(2)}, u32[]{:S(2)}) collective-permute-start(bf16[768,512]{1,0:T(8,128)(2,1)S(1)} %get-tuple-element.37), channel_id=1, source_target_pairs={{0,1},{1,0},{2,3},{3,2},{4,5},{5,4},{6,7},{7,6},{8,9},{9,8},{10,11... | collective-permute-start | bytes 2359304 | tf_op jit(solution)/shard_map/ppermute | solution.py:14
  8.2 11.0 %collective-permute-start.1 = (bf16[1280,128]{1,0:T(8,128)(2,1)S(1)}, bf16[1280,128]{1,0:T(8,128)(2,1)S(1)}, u32[]{:S(2)}, u32[]{:S(2)}) collective-permute-start(bf16[1280,128]{1,0:T(8,128)(2,1)S(1)} %get-tuple-element.39.refs_2_.refs_3_), channel_id=1, source_target_pairs={{0,2},{1,3},{2,0},{3,1},{4,6},{5,7},{6,4},{7,5},{8,10},{9,11},{10,... | collective-permute-start | bytes 983048 | tf_op jit(solution)/shard_map/ppermute | solution.py:14
  11.9 33.3 %collective-permute-start.10 = (bf16[640,512]{1,0:T(8,128)(2,1)S(1)}, bf16[640,512]{1,0:T(8,128)(2,1)S(1)}, u32[]{:S(2)}, u32[]{:S(2)}) collective-permute-start(bf16[640,512]{1,0:T(8,128)(2,1)S(1)} %get-tuple-element.49), channel_id=1, source_target_pairs={{0,1},{1,0},{2,3},{3,2},{4,5},{5,4},{6,7},{7,6},{8,9},{9,8},{10,11... | collective-permute-start | bytes 1966088 | tf_op jit(solution)/shard_map/ppermute | solution.py:14
  12.6 36.5 %collective-permute-start.13 = (bf16[2,512,512]{2,1,0:T(8,128)(2,1)S(1)}, bf16[2,512,512]{2,1,0:T(8,128)(2,1)S(1)}, u32[]{:S(2)}, u32[]{:S(2)}) collective-permute-start(bf16[2,512,512]{2,1,0:T(8,128)(2,1)S(1)} %panel_send.2.refs_2_), channel_id=1, source_target_pairs={{0,8},{8,0},{16,24},{24,16},{1,9},{9,1},{17,25},{25,17},{2,10},{10... | collective-permute-start | bytes 3145736 | tf_op jit(solution)/shard_map/ppermute | solution.py:14
  14.8 37.5 %collective-permute-start.14 = (bf16[2,512,512]{2,1,0:T(8,128)(2,1)S(1)}, bf16[2,512,512]{2,1,0:T(8,128)(2,1)S(1)}, u32[]{:S(2)}, u32[]{:S(2)}) collective-permute-start(bf16[2,512,512]{2,1,0:T(8,128)(2,1)S(1)} %panel_send.3.refs_3_), channel_id=1, source_target_pairs={{0,16},{8,24},{16,0},{24,8},{1,17},{9,25},{17,1},{25,9},{2,18},{10... | collective-permute-start | bytes 3145736 | tf_op jit(solution)/shard_map/ppermute | solution.py:14
  19.9 13.8 %collective-permute-start.2 = (bf16[896,128]{1,0:T(8,128)(2,1)S(1)}, bf16[896,128]{1,0:T(8,128)(2,1)S(1)}, u32[]{:S(2)}, u32[]{:S(2)}) collective-permute-start(bf16[896,128]{1,0:T(8,128)(2,1)S(1)} %get-tuple-element.40.refs_2_.refs_0_), channel_id=1, source_target_pairs={{0,4},{1,5},{2,6},{3,7},{4,0},{5,1},{6,2},{7,3},{8,12},{9,13},{10,... | collective-permute-start | bytes 688136 | tf_op jit(solution)/shard_map/ppermute | solution.py:14
  22.7 7.2 %collective-permute-start.3 = (bf16[512,128]{1,0:T(8,128)(2,1)S(1)}, bf16[512,128]{1,0:T(8,128)(2,1)S(1)}, u32[]{:S(2)}, u32[]{:S(2)}) collective-permute-start(bf16[512,128]{1,0:T(8,128)(2,1)S(1)} %get-tuple-element.43), channel_id=1, source_target_pairs={{0,2},{1,3},{2,0},{3,1},{4,6},{5,7},{6,4},{7,5},{8,10},{9,11},{10,... | collective-permute-start | bytes 393224 | tf_op jit(solution)/shard_map/ppermute | solution.py:14
  30.5 6.5 %copy-start.3 = (s32[4,1,4]{2,1,0:T(1,128)S(1)}, s32[4,1,4]{2,1,0:T(1,128)}, u32[]{:S(2)}) copy-start(s32[4,1,4]{2,1,0:T(1,128)} %param.9) | copy-start | bytes 196
  30.5 6.5 %copy-start.8 = (s32[4]{0:T(128)S(1)}, s32[4]{0:T(128)}, u32[]{:S(2)}) copy-start(s32[4]{0:T(128)} %sup.51) | copy-start | bytes 52
  30.5 5.3 %collective-permute-start.5 = (bf16[256,128]{1,0:T(8,128)(2,1)S(1)}, bf16[256,128]{1,0:T(8,128)(2,1)S(1)}, u32[]{:S(2)}, u32[]{:S(2)}) collective-permute-start(bf16[256,128]{1,0:T(8,128)(2,1)S(1)} %get-tuple-element.44.refs_4_), channel_id=1, source_target_pairs={{0,4},{1,5},{2,6},{3,7},{4,0},{5,1},{6,2},{7,3},{8,12},{9,13},{10,... | collective-permute-start | bytes 196616 | tf_op jit(solution)/shard_map/ppermute | solution.py:14
  33.6 13.5 %collective-permute-start.9 = (bf16[640,512]{1,0:T(8,128)(2,1)S(1)}, bf16[640,512]{1,0:T(8,128)(2,1)S(1)}, u32[]{:S(2)}, u32[]{:S(2)}) collective-permute-start(bf16[640,512]{1,0:T(8,128)(2,1)S(1)} %get-tuple-element.48), channel_id=1, source_target_pairs={{0,1},{1,0},{2,3},{3,2},{4,5},{5,4},{6,7},{7,6},{8,9},{9,8},{10,11... | collective-permute-start | bytes 1966088 | tf_op jit(solution)/shard_map/ppermute | solution.py:14
  35.8 1.3 %collective-permute-start.4 = (bf16[256,128]{1,0:T(8,128)(2,1)S(1)}, bf16[256,128]{1,0:T(8,128)(2,1)S(1)}, u32[]{:S(2)}, u32[]{:S(2)}) collective-permute-start(bf16[256,128]{1,0:T(8,128)(2,1)S(1)} %get-tuple-element.46.refs_1_), channel_id=1, source_target_pairs={{0,1},{1,0},{2,3},{3,2},{4,5},{5,4},{6,7},{7,6},{8,9},{9,8},{10,11... | collective-permute-start | bytes 196616 | tf_op jit(solution)/shard_map/ppermute | solution.py:14
  37.8 4.3 %collective-permute-start.6 = (f32[128,128]{1,0:T(8,128)S(1)}, f32[128,128]{1,0:T(8,128)S(1)}, u32[]{:S(2)}, u32[]{:S(2)}) collective-permute-start(f32[128,128]{1,0:T(8,128)S(1)} %term1.1.refs_0_.refs_7_.refs_2_), channel_id=1, source_target_pairs={{0,8},{8,0},{16,24},{24,16},{1,9},{9,1},{17,25},{25,17},{2,10},{10... | collective-permute-start | bytes 196616 | tf_op jit(solution)/shard_map/ppermute | solution.py:14
  42.7 4.4 %collective-permute-start.7 = (bf16[128,128]{1,0:T(8,128)(2,1)S(1)}, bf16[128,128]{1,0:T(8,128)(2,1)S(1)}, u32[]{:S(2)}, u32[]{:S(2)}) collective-permute-start(bf16[128,128]{1,0:T(8,128)(2,1)S(1)} %m1_sum.1), channel_id=1, source_target_pairs={{0,2},{1,3},{2,0},{3,1},{4,6},{5,7},{6,4},{7,5},{8,10},{9,11},{10,... | collective-permute-start | bytes 98312 | tf_op jit(solution)/shard_map/ppermute | solution.py:14
  45.2 8.0 %collective-permute-start.12 = (bf16[512,512]{1,0:T(8,128)(2,1)S(1)}, bf16[512,512]{1,0:T(8,128)(2,1)S(1)}, u32[]{:S(2)}, u32[]{:S(2)}) collective-permute-start(bf16[512,512]{1,0:T(8,128)(2,1)S(1)} %get-tuple-element.53), channel_id=1, source_target_pairs={{0,1},{1,0},{2,3},{3,2},{4,5},{5,4},{6,7},{7,6},{8,9},{9,8},{10,11... | collective-permute-start | bytes 1572872 | tf_op jit(solution)/shard_map/ppermute | solution.py:14
  47.1 6.1 %collective-permute-start.11 = (bf16[512,512]{1,0:T(8,128)(2,1)S(1)}, bf16[512,512]{1,0:T(8,128)(2,1)S(1)}, u32[]{:S(2)}, u32[]{:S(2)}) collective-permute-start(bf16[512,512]{1,0:T(8,128)(2,1)S(1)} %get-tuple-element.52), channel_id=1, source_target_pairs={{0,1},{1,0},{2,3},{3,2},{4,5},{5,4},{6,7},{7,6},{8,9},{9,8},{10,11... | collective-permute-start | bytes 1572872 | tf_op jit(solution)/shard_map/ppermute | solution.py:14
  47.1 6.1 %collective-permute-start.8 = (bf16[256,128]{1,0:T(8,128)(2,1)S(1)}, bf16[256,128]{1,0:T(8,128)(2,1)S(1)}, u32[]{:S(2)}, u32[]{:S(2)}) collective-permute-start(bf16[256,128]{1,0:T(8,128)(2,1)S(1)} %pad_maximum_fusion.refs_0_), channel_id=1, source_target_pairs={{0,4},{1,5},{2,6},{3,7},{4,0},{5,1},{6,2},{7,3},{8,12},{9,13},{10,... | collective-permute-start | bytes 196616 | tf_op jit(solution)/shard_map/ppermute | solution.py:14
  49.2 5.8 %collective-permute-start.22 = (bf16[256,128]{1,0:T(8,128)(2,1)S(1)}, bf16[256,128]{1,0:T(8,128)(2,1)S(1)}, u32[]{:S(2)}, u32[]{:S(2)}) collective-permute-start(bf16[256,128]{1,0:T(8,128)(2,1)S(1)} %add.13), channel_id=1, source_target_pairs={{0,8},{8,0},{16,24},{24,16},{1,9},{9,1},{17,25},{25,17},{2,10},{10... | collective-permute-start | bytes 196616 | tf_op jit(solution)/shard_map/ppermute | solution.py:14
  52.4 8.3 %collective-permute-start.15 = (bf16[128,512]{1,0:T(8,128)(2,1)S(1)}, bf16[128,512]{1,0:T(8,128)(2,1)S(1)}, u32[]{:S(2)}, u32[]{:S(2)}) collective-permute-start(bf16[128,512]{1,0:T(8,128)(2,1)S(1)} %get-tuple-element.45.refs_0_.refs_6_.refs_3_), channel_id=1, source_target_pairs={{0,1},{1,0},{2,3},{3,2},{4,5},{5,4},{6,7},{7,6},{8,9},{9,8},{10,11... | collective-permute-start | bytes 393224 | tf_op jit(solution)/shard_map/ppermute | solution.py:14
  54.4 8.3 %collective-permute-start.16 = (bf16[128,512]{1,0:T(8,128)(2,1)S(1)}, bf16[128,512]{1,0:T(8,128)(2,1)S(1)}, u32[]{:S(2)}, u32[]{:S(2)}) collective-permute-start(bf16[128,512]{1,0:T(8,128)(2,1)S(1)} %get-tuple-element.54.refs_4_.refs_2_.refs_1_), channel_id=1, source_target_pairs={{0,1},{1,0},{2,3},{3,2},{4,5},{5,4},{6,7},{7,6},{8,9},{9,8},{10,11... | collective-permute-start | bytes 393224 | tf_op jit(solution)/shard_map/ppermute | solution.py:14
  55.0 4.7 %collective-permute-start.23 = (bf16[256,128]{1,0:T(8,128)(2,1)S(1)}, bf16[256,128]{1,0:T(8,128)(2,1)S(1)}, u32[]{:S(2)}, u32[]{:S(2)}) collective-permute-start(bf16[256,128]{1,0:T(8,128)(2,1)S(1)} %add_convert_fusion.1), channel_id=1, source_target_pairs={{0,16},{8,24},{16,0},{24,8},{1,17},{9,25},{17,1},{25,9},{2,18},{10... | collective-permute-start | bytes 196616 | tf_op jit(solution)/shard_map/ppermute | solution.py:14
  56.6 29.8 %collective-permute-start.32 = (bf16[512,512]{1,0:T(8,128)(2,1)S(1)}, bf16[512,512]{1,0:T(8,128)(2,1)S(1)}, u32[]{:S(2)}, u32[]{:S(2)}) collective-permute-start(bf16[512,512]{1,0:T(8,128)(2,1)S(1)} %panel_join.2.refs_9_), channel_id=1, source_target_pairs={{0,16},{8,24},{16,0},{24,8},{1,17},{9,25},{17,1},{25,9},{2,18},{10... | collective-permute-start | bytes 1572872 | tf_op jit(solution)/shard_map/ppermute | solution.py:14
  57.1 31.6 %collective-permute-start.33 = (bf16[512,512]{1,0:T(8,128)(2,1)S(1)}, bf16[512,512]{1,0:T(8,128)(2,1)S(1)}, u32[]{:S(2)}, u32[]{:S(2)}) collective-permute-start(bf16[512,512]{1,0:T(8,128)(2,1)S(1)} %panel_join.3.refs_10_), channel_id=1, source_target_pairs={{0,8},{8,0},{16,24},{24,16},{1,9},{9,1},{17,25},{25,17},{2,10},{10... | collective-permute-start | bytes 1572872 | tf_op jit(solution)/shard_map/ppermute | solution.py:14
  59.7 7.1 %collective-permute-start.17 = (bf16[32,1024]{1,0:T(8,128)(2,1)S(1)}, bf16[32,1024]{1,0:T(8,128)(2,1)S(1)}, u32[]{:S(2)}, u32[]{:S(2)}) collective-permute-start(bf16[32,1024]{1,0:T(8,128)(2,1)S(1)} %get-tuple-element.56), channel_id=1, source_target_pairs={{0,2},{1,3},{2,0},{3,1},{4,6},{5,7},{6,4},{7,5},{8,10},{9,11},{10,... | collective-permute-start | bytes 196616 | tf_op jit(solution)/shard_map/ppermute | solution.py:14
  60.6 6.8 %collective-permute-start.18 = (bf16[32,1024]{1,0:T(8,128)(2,1)S(1)}, bf16[32,1024]{1,0:T(8,128)(2,1)S(1)}, u32[]{:S(2)}, u32[]{:S(2)}) collective-permute-start(bf16[32,1024]{1,0:T(8,128)(2,1)S(1)} %get-tuple-element.57), channel_id=1, source_target_pairs={{0,4},{1,5},{2,6},{3,7},{4,0},{5,1},{6,2},{7,3},{8,12},{9,13},{10,... | collective-permute-start | bytes 196616 | tf_op jit(solution)/shard_map/ppermute | solution.py:14
  62.7 6.1 %collective-permute-start.19 = (bf16[32,1024]{1,0:T(8,128)(2,1)S(1)}, bf16[32,1024]{1,0:T(8,128)(2,1)S(1)}, u32[]{:S(2)}, u32[]{:S(2)}) collective-permute-start(bf16[32,1024]{1,0:T(8,128)(2,1)S(1)} %get-tuple-element.58), channel_id=1, source_target_pairs={{0,6},{1,7},{2,4},{3,5},{4,2},{5,3},{6,0},{7,1},{8,14},{9,15},{10,... | collective-permute-start | bytes 196616 | tf_op jit(solution)/shard_map/ppermute | solution.py:14
  66.9 6.0 %collective-permute-start.24 = (bf16[256,128]{1,0:T(8,128)(2,1)S(1)}, bf16[256,128]{1,0:T(8,128)(2,1)S(1)}, u32[]{:S(2)}, u32[]{:S(2)}) collective-permute-start(bf16[256,128]{1,0:T(8,128)(2,1)S(1)} %add_convert_fusion.refs_0_), channel_id=1, source_target_pairs={{0,2},{1,3},{2,0},{3,1},{4,6},{5,7},{6,4},{7,5},{8,10},{9,11},{10,... | collective-permute-start | bytes 196616 | tf_op jit(solution)/shard_map/ppermute | solution.py:14
  69.4 5.1 %collective-permute-start.20 = (bf16[32,1024]{1,0:T(8,128)(2,1)S(1)}, bf16[32,1024]{1,0:T(8,128)(2,1)S(1)}, u32[]{:S(2)}, u32[]{:S(2)}) collective-permute-start(bf16[32,1024]{1,0:T(8,128)(2,1)S(1)} %t23_sum.1), channel_id=1, source_target_pairs={{0,8},{8,0},{16,24},{24,16},{1,9},{9,1},{17,25},{25,17},{2,10},{10... | collective-permute-start | bytes 196616 | tf_op jit(solution)/shard_map/ppermute | solution.py:14
  71.0 10.0 %collective-permute-start.27 = (bf16[2,128,512]{2,1,0:T(8,128)(2,1)S(1)}, bf16[2,128,512]{2,1,0:T(8,128)(2,1)S(1)}, u32[]{:S(2)}, u32[]{:S(2)}) collective-permute-start(bf16[2,128,512]{2,1,0:T(8,128)(2,1)S(1)} %get-tuple-element.63), channel_id=1, source_target_pairs={{0,16},{8,24},{16,0},{24,8},{1,17},{9,25},{17,1},{25,9},{2,18},{10... | collective-permute-start | bytes 786440 | tf_op jit(solution)/shard_map/ppermute | solution.py:14
  73.5 6.3 %collective-permute-start.25 = (bf16[512,128]{1,0:T(8,128)(2,1)S(1)}, bf16[512,128]{1,0:T(8,128)(2,1)S(1)}, u32[]{:S(2)}, u32[]{:S(2)}) collective-permute-start(bf16[512,128]{1,0:T(8,128)(2,1)S(1)} %p23_stack.1.refs_0_), channel_id=1, source_target_pairs={{0,4},{1,5},{2,6},{3,7},{4,0},{5,1},{6,2},{7,3},{8,12},{9,13},{10,... | collective-permute-start | bytes 393224 | tf_op jit(solution)/shard_map/ppermute | solution.py:14
  74.5 6.6 %collective-permute-start.26 = (bf16[2,128,512]{2,1,0:T(8,128)(2,1)S(1)}, bf16[2,128,512]{2,1,0:T(8,128)(2,1)S(1)}, u32[]{:S(2)}, u32[]{:S(2)}) collective-permute-start(bf16[2,128,512]{2,1,0:T(8,128)(2,1)S(1)} %get-tuple-element.59.refs_4_), channel_id=1, source_target_pairs={{0,8},{8,0},{16,24},{24,16},{1,9},{9,1},{17,25},{25,17},{2,10},{10... | collective-permute-start | bytes 786440 | tf_op jit(solution)/shard_map/ppermute | solution.py:14
  79.7 5.0 %collective-permute-start.21 = (f32[32,1024]{1,0:T(8,128)S(1)}, f32[32,1024]{1,0:T(8,128)S(1)}, u32[]{:S(2)}, u32[]{:S(2)}) collective-permute-start(f32[32,1024]{1,0:T(8,128)S(1)} %convert_add_fusion.refs_0_), channel_id=1, source_target_pairs={{0,16},{8,24},{16,0},{24,8},{1,17},{9,25},{17,1},{25,9},{2,18},{10... | collective-permute-start | bytes 393224 | tf_op jit(solution)/shard_map/ppermute | solution.py:14
  81.0 12.1 %collective-permute-start.31 = (bf16[256,512]{1,0:T(8,128)(2,1)S(1)}, bf16[256,512]{1,0:T(8,128)(2,1)S(1)}, u32[]{:S(2)}, u32[]{:S(2)}) collective-permute-start(bf16[256,512]{1,0:T(8,128)(2,1)S(1)} %p23_place.1.refs_2_.refs_5_), channel_id=1, source_target_pairs={{0,1},{1,0},{2,3},{3,2},{4,5},{5,4},{6,7},{7,6},{8,9},{9,8},{10,11... | collective-permute-start | bytes 786440 | tf_op jit(solution)/shard_map/ppermute | solution.py:14
  81.7 7.0 %collective-permute-start.34 = (bf16[128,512]{1,0:T(8,128)(2,1)S(1)}, bf16[128,512]{1,0:T(8,128)(2,1)S(1)}, u32[]{:S(2)}, u32[]{:S(2)}) collective-permute-start(bf16[128,512]{1,0:T(8,128)(2,1)S(1)} %get-tuple-element.64.refs_3_), channel_id=1, source_target_pairs={{0,16},{8,24},{16,0},{24,8},{1,17},{9,25},{17,1},{25,9},{2,18},{10... | collective-permute-start | bytes 393224 | tf_op jit(solution)/shard_map/ppermute | solution.py:14
  84.7 6.1 %collective-permute-start.35 = (bf16[128,512]{1,0:T(8,128)(2,1)S(1)}, bf16[128,512]{1,0:T(8,128)(2,1)S(1)}, u32[]{:S(2)}, u32[]{:S(2)}) collective-permute-start(bf16[128,512]{1,0:T(8,128)(2,1)S(1)} %get-tuple-element.65.refs_4_), channel_id=1, source_target_pairs={{0,8},{8,0},{16,24},{24,16},{1,9},{9,1},{17,25},{25,17},{2,10},{10... | collective-permute-start | bytes 393224 | tf_op jit(solution)/shard_map/ppermute | solution.py:14
  86.3 8.0 %copy-start.5 = (bf16[2,512,512]{2,1,0:T(8,128)(2,1)S(1)}, bf16[2,512,512]{2,1,0:T(8,128)(2,1)}, u32[]{:S(2)}) copy-start(bf16[2,512,512]{2,1,0:T(8,128)(2,1)} %refs_4_.1) | copy-start | bytes 3145732
  86.4 6.8 %collective-permute-start.30 = (bf16[32,1024]{1,0:T(8,128)(2,1)S(1)}, bf16[32,1024]{1,0:T(8,128)(2,1)S(1)}, u32[]{:S(2)}, u32[]{:S(2)}) collective-permute-start(bf16[32,1024]{1,0:T(8,128)(2,1)S(1)} %m23_sum.1.refs_0_), channel_id=1, source_target_pairs={{0,6},{1,7},{2,4},{3,5},{4,2},{5,3},{6,0},{7,1},{8,14},{9,15},{10,... | collective-permute-start | bytes 196616 | tf_op jit(solution)/shard_map/ppermute | solution.py:14
  88.7 5.6 %collective-permute-start.29 = (bf16[32,1024]{1,0:T(8,128)(2,1)S(1)}, bf16[32,1024]{1,0:T(8,128)(2,1)S(1)}, u32[]{:S(2)}, u32[]{:S(2)}) collective-permute-start(bf16[32,1024]{1,0:T(8,128)(2,1)S(1)} %m23_sum.1.refs_0_), channel_id=1, source_target_pairs={{0,4},{1,5},{2,6},{3,7},{4,0},{5,1},{6,2},{7,3},{8,12},{9,13},{10,... | collective-permute-start | bytes 196616 | tf_op jit(solution)/shard_map/ppermute | solution.py:14
  88.7 5.6 %collective-permute-start.28 = (bf16[32,1024]{1,0:T(8,128)(2,1)S(1)}, bf16[32,1024]{1,0:T(8,128)(2,1)S(1)}, u32[]{:S(2)}, u32[]{:S(2)}) collective-permute-start(bf16[32,1024]{1,0:T(8,128)(2,1)S(1)} %m23_sum.1.refs_0_), channel_id=1, source_target_pairs={{0,2},{1,3},{2,0},{3,1},{4,6},{5,7},{6,4},{7,5},{8,10},{9,11},{10,... | collective-permute-start | bytes 196616 | tf_op jit(solution)/shard_map/ppermute | solution.py:14
  95.5 1.6 %collective-permute-start.36 = (bf16[2,128,512]{2,1,0:T(8,128)(2,1)S(1)}, bf16[2,128,512]{2,1,0:T(8,128)(2,1)S(1)}, u32[]{:S(2)}, u32[]{:S(2)}) collective-permute-start(bf16[2,128,512]{2,1,0:T(8,128)(2,1)S(1)} %x2_x3.1.refs_0_.refs_4_), channel_id=1, source_target_pairs={{0,1},{1,0},{2,3},{3,2},{4,5},{5,4},{6,7},{7,6},{8,9},{9,8},{10,11... | collective-permute-start | bytes 786440 | tf_op jit(solution)/shard_map/ppermute | solution.py:14
  98.1 6.2 %collective-permute-start.40 = (bf16[128,512]{1,0:T(8,128)(2,1)S(1)}, bf16[128,512]{1,0:T(8,128)(2,1)S(1)}, u32[]{:S(2)}, u32[]{:S(2)}) collective-permute-start(bf16[128,512]{1,0:T(8,128)(2,1)S(1)} %get-tuple-element.69.refs_1_), channel_id=1, source_target_pairs={{0,16},{8,24},{16,0},{24,8},{1,17},{9,25},{17,1},{25,9},{2,18},{10... | collective-permute-start | bytes 393224 | tf_op jit(solution)/shard_map/ppermute | solution.py:14
  99.1 6.4 %collective-permute-start.37 = (bf16[128,512]{1,0:T(8,128)(2,1)S(1)}, bf16[128,512]{1,0:T(8,128)(2,1)S(1)}, u32[]{:S(2)}, u32[]{:S(2)}) collective-permute-start(bf16[128,512]{1,0:T(8,128)(2,1)S(1)} %get-tuple-element.68.refs_6_.refs_0_), channel_id=1, source_target_pairs={{0,8},{8,0},{16,24},{24,16},{1,9},{9,1},{17,25},{25,17},{2,10},{10... | collective-permute-start | bytes 393224 | tf_op jit(solution)/shard_map/ppermute | solution.py:14
  100.1 8.2 %collective-permute-start.38 = (bf16[128,512]{1,0:T(8,128)(2,1)S(1)}, bf16[128,512]{1,0:T(8,128)(2,1)S(1)}, u32[]{:S(2)}, u32[]{:S(2)}) collective-permute-start(bf16[128,512]{1,0:T(8,128)(2,1)S(1)} %get-tuple-element.69.refs_1_), channel_id=1, source_target_pairs={{0,8},{8,0},{16,24},{24,16},{1,9},{9,1},{17,25},{25,17},{2,10},{10... | collective-permute-start | bytes 393224 | tf_op jit(solution)/shard_map/ppermute | solution.py:14
  101.1 7.2 %collective-permute-start.39 = (bf16[128,512]{1,0:T(8,128)(2,1)S(1)}, bf16[128,512]{1,0:T(8,128)(2,1)S(1)}, u32[]{:S(2)}, u32[]{:S(2)}) collective-permute-start(bf16[128,512]{1,0:T(8,128)(2,1)S(1)} %get-tuple-element.68.refs_6_.refs_0_), channel_id=1, source_target_pairs={{0,16},{8,24},{16,0},{24,8},{1,17},{9,25},{17,1},{25,9},{2,18},{10... | collective-permute-start | bytes 393224 | tf_op jit(solution)/shard_map/ppermute | solution.py:14
  104.4 5.6 %collective-permute-start.42 = (bf16[128,512]{1,0:T(8,128)(2,1)S(1)}, bf16[128,512]{1,0:T(8,128)(2,1)S(1)}, u32[]{:S(2)}, u32[]{:S(2)}) collective-permute-start(bf16[128,512]{1,0:T(8,128)(2,1)S(1)} %collective-permute-done.40.refs_5_), channel_id=1, source_target_pairs={{0,8},{8,0},{16,24},{24,16},{1,9},{9,1},{17,25},{25,17},{2,10},{10... | collective-permute-start | bytes 393224 | tf_op jit(solution)/shard_map/ppermute | solution.py:14
  105.5 5.0 %collective-permute-start.41 = (bf16[128,512]{1,0:T(8,128)(2,1)S(1)}, bf16[128,512]{1,0:T(8,128)(2,1)S(1)}, u32[]{:S(2)}, u32[]{:S(2)}) collective-permute-start(bf16[128,512]{1,0:T(8,128)(2,1)S(1)} %collective-permute-done.37.refs_2_), channel_id=1, source_target_pairs={{0,16},{8,24},{16,0},{24,8},{1,17},{9,25},{17,1},{25,9},{2,18},{10... | collective-permute-start | bytes 393224 | tf_op jit(solution)/shard_map/ppermute | solution.py:14
  (4 other events, 6.7 us)
